TPU v7x, 32 devices: a whole 2x2x4 slice. The times are simulated.
32 devices in a mesh: span: 4 (over z), xsec: 2 (over x), leaf: 4 (over y, core).
Axes of the slice: x: 2, y: 2, z: 4, core: 2. Of those that a mesh axis runs over, the one named last changes fastest.
Arguments:
- snapshots: float32 [3, 8192, 256], P(None, ('span', 'xsec', 'leaf')), may hold values from -1800 to 1800
- member_ends: int32 [2, 32768], P(None, ('span', 'xsec', 'leaf')), may hold values from 0 to 383, as said below
- member_dir: float32 [3, 32768], P(None, ('span', 'xsec', 'leaf')), may hold values from -3 to 3
- member_stiff: float32 [32768], P(('span', 'xsec', 'leaf')), may hold values from 0.25 to 24
Outputs:
- basis: float32 [3, 8192, 256], P(None, ('span', 'xsec', 'leaf'))
- forces: float32 [3, 8192, 256], P(None, ('span', 'xsec', 'leaf'))
- reduced: float32 [256, 256], replicated
- coef: float32 [256, 256], replicated
- column_energy: float32 [256], replicated
Inputs may be any that keep to these rules, and one draw needn't show every extreme that they name: member_ends[0] names a node of the member's own device block; member_ends[1] names such a node or, from 256 on, a node of the top level of the slab directly below in the same sector; both ends of a member lie on the same or neighbouring levels.
All inputs are finite; a program needn't handle non-finite values.
Results may differ from a plain program's by a relative error of at most 0.0008.
Values sent between devices are 32-bit elements; how exact they have to be, the bound alone decides.
No kernel may reach another device: no remote copies, remote signals or barrier semaphores. Data moves between devices by JAX's collectives and lax.ppermute only.
A program may use at most 64 MiB of HBM per device.

v0:
```python
import math

import jax
import jax.numpy as jnp
from jax import lax
from jax.experimental import pallas as pl
from jax.experimental.pallas import tpu as pltpu
from jax.sharding import PartitionSpec as P

AXES = ("span", "xsec", "leaf")
SEC_NODES = 128
CHUNK = 256
highest = lax.Precision.HIGHEST
VMEM = pl.BlockSpec(memory_space=pltpu.VMEM)
SMEM = pl.BlockSpec(memory_space=pltpu.SMEM)


def dot(a, b, ca=1, cb=0):
    return lax.dot_general(
        a, b, (((ca,), (cb,)), ((), ())), precision=highest, preferred_element_type=jnp.float32
    )


def call(kernel, shapes, operands, specs=None, scratch=()):
    return pl.pallas_call(
        kernel,
        out_shape=tuple(jax.ShapeDtypeStruct(s, jnp.float32) for s in shapes),
        in_specs=specs or [VMEM] * len(operands),
        out_specs=tuple(VMEM for _ in shapes),
        scratch_shapes=list(scratch),
        compiler_params=pltpu.CompilerParams(vmem_limit_bytes=48 << 20),
    )(*operands)


def exchange(array, bit):
    count = math.prod(lax.axis_size(a) for a in AXES)
    return lax.ppermute(array, AXES, [(i, i ^ bit) for i in range(count)])


def sum_over_devices(keep, send):
    count = math.prod(lax.axis_size(a) for a in AXES)
    total = keep + exchange(send, 1)
    bit = 2
    while bit < count:
        total = total + exchange(total, bit)
        bit *= 2
    return total, exchange(total, 1)


def shifted(array, axis, by):
    length = lax.axis_size(axis)
    pairs = [(i, i + by) for i in range(length) if 0 <= i + by < length]
    return lax.ppermute(array, axis, pairs)


def order_halves(odd, mine, other):
    return jnp.where(odd == 0, mine, other), jnp.where(odd == 0, other, mine)


def pack_one(gram):
    h, q = gram.shape[0] // 2, gram.shape[0] // 4
    g11, g12, g22 = gram[:h, :h], gram[:h, h:], gram[h:, h:]
    lane = lax.broadcasted_iota(jnp.int32, (q, h), 1)
    corner = jnp.where(lane < q, pltpu.roll(g11[q:], q, 1), g22[q:])
    return jnp.concatenate([g11[:q], g22[:q], corner, g12], axis=0)


def unpack_one(rows, h):
    q = h // 2
    lane = lax.broadcasted_iota(jnp.int32, (q, h), 1)
    corner = rows[2 * q : 3 * q]

    def block(top, low):
        square = jnp.concatenate([top, low], axis=0)
        flipped = square.T[q:]
        return jnp.concatenate([top, jnp.where(lane < q, flipped, low)], axis=0)

    g11 = block(rows[:q], pltpu.roll(corner, q, 1))
    g22 = block(rows[q : 2 * q], corner)
    return g11, rows[3 * q :], g22


def gram_kernel(odd_ref, s_ref, keep_ref, send_ref, top_ref):
    nodes = s_ref.shape[1]
    top_ref[...] = s_ref[:, nodes - SEC_NODES :, :]
    flat = s_ref[...].reshape(-1, s_ref.shape[2])
    packed = pack_one(dot(flat, flat, 0, 0))
    half = packed.shape[0] // 2
    keep_ref[...], send_ref[...] = order_halves(odd_ref[0], packed[:half], packed[half:])


def pieces_of(x):
    first = x.astype(jnp.bfloat16)
    rest = x - first.astype(jnp.float32)
    second = rest.astype(jnp.bfloat16)
    third = (rest - second.astype(jnp.float32)).astype(jnp.bfloat16)
    return first, second, third


def member_kernel(s_ref, below_ref, ends_ref, table_ref, own_ref, back_ref, parts_ref):
    nodes, width = s_ref.shape[1:]
    total = nodes + SEC_NODES
    for c in range(3):
        for i, piece in enumerate(pieces_of(s_ref[c])):
            parts_ref[i, c, :nodes, :] = piece
        for i, piece in enumerate(pieces_of(below_ref[c])):
            parts_ref[i, c, nodes:, :] = piece
    own_ref[...] = jnp.zeros_like(own_ref)
    back_ref[...] = jnp.zeros_like(back_ref)

    def chunk(start):
        rows = pl.ds(pl.multiple_of(start, CHUNK), CHUNK)
        table = table_ref[rows, :]
        node = lax.broadcasted_iota(jnp.int32, (CHUNK, total), 1).astype(jnp.float32)
        pick = (node == table[:, 0:1]).astype(jnp.float32) - (node == table[:, 1:2]).astype(jnp.float32)
        pick = pick.astype(jnp.bfloat16)
        ends = ends_ref[:, rows]
        node_t = lax.broadcasted_iota(jnp.int32, (total, CHUNK), 0)
        spread = (node_t == ends[0:1]).astype(jnp.float32) - (node_t == ends[1:2]).astype(jnp.float32)
        spread = spread.astype(jnp.bfloat16)
        elongation = jnp.zeros((CHUNK, width), jnp.float32)
        for c in range(3):
            difference = jnp.zeros((CHUNK, width), jnp.float32)
            for i in range(3):
                difference = difference + jnp.dot(pick, parts_ref[i, c], preferred_element_type=jnp.float32)
            elongation = elongation + table[:, 2 + c : 3 + c] * difference
        axial = elongation * table[:, 5:6]
        for c in range(3):
            push = table[:, 2 + c : 3 + c] * axial
            force = jnp.zeros((total, width), jnp.float32)
            for piece in pieces_of(push):
                force = force + jnp.dot(spread, piece, preferred_element_type=jnp.float32)
            own_ref[c] += force[:nodes]
            back_ref[c] += force[nodes:]

    def step(i, carry):
        chunk(i * CHUNK)
        return carry

    lax.fori_loop(0, table_ref.shape[0] // CHUNK, step, 0)


def factor_block(x_ref, u_ref, m_ref):
    n = x_ref.shape[0]
    tiles = [x_ref[8 * i : 8 * i + 8, :] for i in range(n // 8)]
    lane = lax.broadcasted_iota(jnp.int32, (8, n), 1)
    sub = lax.broadcasted_iota(jnp.int32, (8, n), 0)

    def column(tile, c):
        return jnp.broadcast_to(tile[:, c : c + 1], (8, n))

    for p in range(n // 8):
        c0 = 8 * p
        rows = [jnp.broadcast_to(tiles[p][r : r + 1, :], (8, n)) for r in range(8)]
        a = [[column(rows[r], c0 + c) if c >= r else None for c in range(8)] for r in range(8)]
        cols = {i: [column(tiles[i], c0 + k) for k in range(8)] for i in range(p + 1, n // 8)}
        m = [[None] * 8 for _ in range(8)]
        inverse = [None] * 8
        for k in range(8):
            inverse[k] = pltpu.reciprocal(a[k][k])
            for i in range(k + 1, 8):
                f = a[k][i] * inverse[k]
                for j in range(i, 8):
                    a[i][j] = a[i][j] - f * a[k][j]
                for j in range(k):
                    m[i][j] = m[i][j] - f * m[k][j]
                m[i][k] = -f
        panel = (lane >= c0) & (lane < c0 + 8)
        v = [jnp.where(panel, jnp.where(lane == c0 + k, 1.0, 0.0), rows[k]) for k in range(8)]
        y, u = [], []
        for i in range(8):
            yi, ui = v[i], rows[i]
            for k in range(i):
                yi = yi + m[i][k] * v[k]
                ui = ui + m[i][k] * rows[k]
            y.append(yi)
            u.append(ui)
        scaled = [y[i] * inverse[i] for i in range(8)]
        for i in range(p + 1, n // 8):
            xi = jnp.where(panel, 0.0, tiles[i])
            for k in range(8):
                ck = cols[i][k]
                for j in range(k):
                    ck = ck + m[k][j] * cols[i][j]
                xi = xi - ck * scaled[k]
            tiles[i] = xi
        yt, ut = y[0], u[0]
        for i in range(1, 8):
            yt = jnp.where(sub == i, y[i], yt)
            ut = jnp.where(sub == i, u[i], ut)
        u_ref[c0 : c0 + 8, :] = ut
        m_ref[c0 : c0 + 8, :] = yt


def factor_and_inverse(g11, g12, g22, w_ref, r_ref, x, u, m):
    h = g11.shape[0]
    rowi = lax.broadcasted_iota(jnp.int32, (h, h), 0)
    coli = lax.broadcasted_iota(jnp.int32, (h, h), 1)

    def finish():
        upper = u[...]
        d = jnp.sum(jnp.where(rowi == coli, upper, 0.0), axis=1, keepdims=True)
        s = lax.rsqrt(d)
        return jnp.where(rowi <= coli, upper, 0.0) * s, jnp.where(rowi >= coli, m[...], 0.0) * s

    x[...] = g11
    factor_block(x, u, m)
    r11, m1 = finish()
    r12 = dot(m1, g12)
    x[...] = g22 - dot(r12, r12, 0, 0)
    factor_block(x, u, m)
    r22, m2 = finish()
    zero = jnp.zeros((h, h), jnp.float32)
    r_ref[:h, :h], r_ref[:h, h:], r_ref[h:, :h], r_ref[h:, h:] = r11, r12, zero, r22
    w_ref[:h, :h], w_ref[h:, h:], w_ref[h:, :h] = m1.T, m2.T, zero
    w_ref[:h, h:] = -dot(m1, dot(r12, m2, 1, 1), 0, 0)


def first_factor_kernel(odd_ref, mine_ref, other_ref, w_ref, r_ref, diag_ref, x, u, m):
    h = x.shape[0]
    lo, hi = order_halves(odd_ref[0], mine_ref[...], other_ref[...])
    g11, g12, g22 = unpack_one(jnp.concatenate([lo, hi], axis=0), h)
    eye = lax.broadcasted_iota(jnp.int32, (h, h), 0) == lax.broadcasted_iota(jnp.int32, (h, h), 1)
    diag_ref[:, :h] = jnp.sum(jnp.where(eye, g11, 0.0), axis=0, keepdims=True)
    diag_ref[:, h:] = jnp.sum(jnp.where(eye, g22, 0.0), axis=0, keepdims=True)
    factor_and_inverse(g11, g12, g22, w_ref, r_ref, x, u, m)


def middle_kernel(odd_ref, s_ref, own_ref, back_ref, w_ref, q_ref, f_ref, keep_ref, send_ref):
    parts, nodes, width = s_ref.shape
    h = width // 2
    w = w_ref[...]
    q = dot(s_ref[...].reshape(-1, width), w)
    q_ref[...] = q
    f_ref[...] = own_ref[...]
    f_ref[:, nodes - SEC_NODES :, :] += back_ref[...]
    f = dot(f_ref[...].reshape(-1, width), w)
    f_ref[...] = f.reshape(parts, nodes, width)
    gram = dot(q, q, 0, 0)
    energy = dot(q, f, 0, 0)
    rowi = lax.broadcasted_iota(jnp.int32, (width, width), 0)
    coli = lax.broadcasted_iota(jnp.int32, (width, width), 1)
    both = jnp.where(rowi < coli, gram, energy)
    diag = jnp.sum(jnp.where(rowi == coli, gram, 0.0), axis=0, keepdims=True)
    lo = jnp.concatenate([both[:, :h], jnp.broadcast_to(diag[:, :h], (8, h))], axis=0)
    hi = jnp.concatenate([both[:, h:], jnp.broadcast_to(diag[:, h:], (8, h))], axis=0)
    keep_ref[...], send_ref[...] = order_halves(odd_ref[0], lo, hi)


def final_kernel(
    rows_all, odd_ref, mine_ref, other_ref, q_ref, f_ref, w1_ref, r1_ref,
    basis_ref, forces_ref, reduced_ref, coef_ref, w2, r2, x, u, m,
):
    parts, nodes, width = f_ref.shape
    h = width // 2
    root = math.sqrt(rows_all)
    lo, hi = order_halves(odd_ref[0], mine_ref[...], other_ref[...])
    both = jnp.concatenate([lo[:width], hi[:width]], axis=1)
    diag = jnp.concatenate([lo[width : width + 1], hi[width : width + 1]], axis=1)
    rowi = lax.broadcasted_iota(jnp.int32, (width, width), 0)
    coli = lax.broadcasted_iota(jnp.int32, (width, width), 1)
    flipped = both.T
    gram = jnp.where(rowi < coli, both, jnp.where(rowi > coli, flipped, diag))
    energy = jnp.where(rowi < coli, flipped, both)
    eye = jnp.where(rowi == coli, 1.0, 0.0)

    def upper_half(e):
        return jnp.where(rowi < coli, e, jnp.where(rowi == coli, 0.5 * e, 0.0))

    def largest(e):
        return jnp.max(jnp.abs(e))

    e0 = gram - eye
    size = jnp.sum(e0 * e0)

    @pl.when(size < 0.04)
    def _():
        w2[...] = eye - upper_half(e0)

        def residual():
            w = w2[...]
            return dot(w, dot(gram, w), 0, 0) - eye

        def more(state):
            return (state[0] > 1e-6) & (state[1] < 6)

        def improve(state):
            e = residual()
            w2[...] = w2[...] - dot(w2[...], upper_half(e))
            return largest(e) ** 2, state[1] + 1

        lax.while_loop(more, improve, (jnp.float32(1.0), jnp.int32(0)))
        r2[...] = jnp.where(rowi <= coli, dot(w2[...], gram, 0, 0), 0.0)

    @pl.when(jnp.logical_not(size < 0.04))
    def _():
        factor_and_inverse(gram[:h, :h], gram[:h, h:], gram[h:, h:], w2, r2, x, u, m)

    w = w2[...]
    basis_ref[...] = dot(q_ref[...], w * root).reshape(parts, nodes, width)
    forces_ref[...] = dot(f_ref[...].reshape(-1, width), w * root).reshape(parts, nodes, width)
    reduced_ref[...] = dot(w, dot(energy, w), 0, 0)
    r1 = r1_ref[...]
    r1 = r1 + dot(eye - dot(r1, w1_ref[...]), r1)
    coef_ref[...] = jnp.where(rowi <= coli, dot(r2[...], r1), 0.0) * (1.0 / root)


def local(snapshots, member_ends, member_dir, member_stiff):
    parts, nodes, width = snapshots.shape
    h = width // 2
    count = math.prod(lax.axis_size(a) for a in AXES)
    rows_all = parts * nodes * count
    odd = (lax.axis_index(AXES) % 2).astype(jnp.int32).reshape(1)
    square = (width, width)
    field = (parts, nodes, width)
    level = (parts, SEC_NODES, width)
    scratch = [pltpu.VMEM((h, h), jnp.float32)] * 3
    quarter = (5 * width // 8, h)

    keep, send, top = call(gram_kernel, [quarter, quarter, level], (odd, snapshots), [SMEM, VMEM])
    below = shifted(top, "span", 1)
    mine, other = sum_over_devices(keep, send)

    ends = member_ends.astype(jnp.float32)
    table = jnp.concatenate([ends, member_dir, member_stiff[None], jnp.zeros_like(ends)], axis=0).T
    own, back = call(
        member_kernel,
        [field, level],
        (snapshots, below, member_ends, table),
        scratch=[pltpu.VMEM((3, parts, nodes + SEC_NODES, width), jnp.bfloat16)],
    )
    returned = shifted(back, "span", -1)

    w1, r1, diag = call(
        first_factor_kernel, [square, square, (1, width)], (odd, mine, other), [SMEM, VMEM, VMEM], scratch
    )
    column_energy = jnp.log(diag[0] / rows_all)

    half = (width + 8, h)
    q, f, keep, send = call(
        middle_kernel,
        [(parts * nodes, width), field, half, half],
        (odd, snapshots, own, returned, w1),
        [SMEM] + [VMEM] * 4,
    )
    mine, other = sum_over_devices(keep, send)
    basis, forces, reduced, coef = call(
        lambda *refs: final_kernel(rows_all, *refs),
        [field, field, square, square],
        (odd, mine, other, q, f, w1, r1),
        [SMEM] + [VMEM] * 6,
        [pltpu.VMEM(square, jnp.float32)] * 2 + scratch,
    )
    return (basis, forces, reduced, coef, column_energy)


def solution(mesh):
    placed = (
        P(None, AXES, None),
        P(None, AXES),
        P(None, AXES),
        P(AXES),
    )
    return jax.shard_map(
        local,
        mesh=mesh,
        in_specs=placed,
        out_specs=(P(None, AXES, None), P(None, AXES, None), P(), P(), P()),
        check_vma=False,
    )
```

profile of v0, /device:TPU:0, one launch (start us, length us, event | category | flops | bytes accessed | tf_op | source)
XLA Modules:
  0.0 93.3 jit_solution(10376208616241929220)
XLA Ops:
  0.6 0.0 copy-start.2
  0.7 0.0 copy-start
  0.7 1.1 %copy-done = f32[3,256,256]{2,1,0:T(8,128)S(1)} copy-done((f32[3,256,256]{2,1,0:T(8,128)S(1)}, f32[3,256,256]{2,1,0:T(8,128)}, u32[]{:S(2)}) %copy-start) | copy-done | bytes 786456
  1.8 0.0 copy-start.1
  1.8 1.0 %shard_map.83 = (f32[160,128]{1,0:T(8,128)S(1)}, f32[160,128]{1,0:T(8,128)S(1)}, f32[3,128,256]{2,1,0:T(8,128)S(1)}) custom-call(s32[1]{0:T(128)} %bitcast.odd_ref.refs_0_, f32[3,256,256]{2,1,0:T(8,128)S(1)} %copy-done), custom_call_target="tpu_custom_call" | custom-call | tf_op jit(solution)/shard_map/pallas_call | solution.py:25
  2.8 5.0 %collective-permute-start = (f32[3,128,256]{2,1,0:T(8,128)S(1)}, f32[3,128,256]{2,1,0:T(8,128)S(1)}, u32[]{:S(2)}, u32[]{:S(2)}) collective-permute-start(f32[3,128,256]{2,1,0:T(8,128)S(1)} %get-tuple-element.21), channel_id=1, source_target_pairs={{0,8},{8,16},{16,24},{1,9},{9,17},{17,25},{2,10},{10,18},{18,26},{... | collective-permute-start | bytes 1179656 | tf_op jit(solution)/shard_map/ppermute | solution.py:53
  7.7 0.1 collective-permute-start.2
  7.8 0.0 copy-done.2
  7.9 0.1 pad.3.clone
  7.9 1.2 %collective-permute-done.2 = f32[160,128]{1,0:T(8,128)S(1)} collective-permute-done((f32[160,128]{1,0:T(8,128)S(1)}, f32[160,128]{1,0:T(8,128)S(1)}, u32[]{:S(2)}, u32[]{:S(2)}) %collective-permute-start.2) | collective-permute-done | bytes 81952 | tf_op jit(solution)/shard_map/ppermute | solution.py:37
  9.1 0.0 copy-start.3
  9.1 0.0 copy-start.4
  9.1 1.6 %collective-permute-start.3 = (f32[160,128]{1,0:T(8,128)S(1)}, f32[160,128]{1,0:T(8,128)S(1)}, u32[]{:S(2)}, u32[]{:S(2)}) collective-permute-start(f32[160,128]{1,0:T(8,128)S(1)} %add.43), channel_id=1, source_target_pairs={{0,2},{1,3},{2,0},{3,1},{4,6},{5,7},{6,4},{7,5},{8,10},{9,11},{10,... | collective-permute-start | bytes 245768 | tf_op jit(solution)/shard_map/ppermute | solution.py:37
  10.7 0.0 copy-done.3
  10.7 0.0 copy-done.4
  10.7 0.1 maximum_maximum_fusion
  10.8 0.2 copy.14
  11.0 5.1 %collective-permute-done.below_ref = f32[3,128,256]{2,1,0:T(8,128)S(1)} collective-permute-done((f32[3,128,256]{2,1,0:T(8,128)S(1)}, f32[3,128,256]{2,1,0:T(8,128)S(1)}, u32[]{:S(2)}, u32[]{:S(2)}) %collective-permute-start) | collective-permute-done | bytes 393248 | tf_op jit(solution)/shard_map/ppermute | solution.py:53
  16.1 0.0 copy-done.1
  16.1 7.5 %shard_map.84 = (f32[3,256,256]{2,1,0:T(8,128)S(1)}, f32[3,128,256]{2,1,0:T(8,128)S(1)}) custom-call(f32[3,256,256]{2,1,0:T(8,128)S(1)} %copy-done.1, f32[3,128,256]{2,1,0:T(8,128)S(1)} %collective-permute-done.below_ref, s32[2,1024]{1,0:T(2,128)S(1)} %copy-done.2, f32[1024,8]{1,0:T(8,128)S(1)} %bitcast.4), custom_call_target="tpu_custom_call" | custom-call | tf_op jit(solution)/shard_map/pallas_call | solution.py:25
  23.6 1.5 %collective-permute-start.1 = (f32[3,128,256]{2,1,0:T(8,128)S(1)}, f32[3,128,256]{2,1,0:T(8,128)S(1)}, u32[]{:S(2)}, u32[]{:S(2)}) collective-permute-start(f32[3,128,256]{2,1,0:T(8,128)S(1)} %get-tuple-element.23), channel_id=1, source_target_pairs={{8,0},{16,8},{24,16},{9,1},{17,9},{25,17},{10,2},{18,10},{26,18},{... | collective-permute-start | bytes 1179656 | tf_op jit(solution)/shard_map/ppermute | solution.py:53
  25.1 0.0 collective-permute-done.3
  25.1 1.6 %collective-permute-start.4 = (f32[160,128]{1,0:T(8,128)S(1)}, f32[160,128]{1,0:T(8,128)S(1)}, u32[]{:S(2)}, u32[]{:S(2)}) collective-permute-start(f32[160,128]{1,0:T(8,128)S(1)} %add.44), channel_id=1, source_target_pairs={{0,4},{1,5},{2,6},{3,7},{4,0},{5,1},{6,2},{7,3},{8,12},{9,13},{10,... | collective-permute-start | bytes 245768 | tf_op jit(solution)/shard_map/ppermute | solution.py:37
  26.6 3.0 %collective-permute-done.4 = f32[160,128]{1,0:T(8,128)S(1)} collective-permute-done((f32[160,128]{1,0:T(8,128)S(1)}, f32[160,128]{1,0:T(8,128)S(1)}, u32[]{:S(2)}, u32[]{:S(2)}) %collective-permute-start.4) | collective-permute-done | bytes 81952 | tf_op jit(solution)/shard_map/ppermute | solution.py:37
  29.6 3.2 %collective-permute-start.5 = (f32[160,128]{1,0:T(8,128)S(1)}, f32[160,128]{1,0:T(8,128)S(1)}, u32[]{:S(2)}, u32[]{:S(2)}) collective-permute-start(f32[160,128]{1,0:T(8,128)S(1)} %add.45), channel_id=1, source_target_pairs={{0,8},{1,9},{2,10},{3,11},{4,12},{5,13},{6,14},{7,15},{8,0},{9,1},... | collective-permute-start | bytes 245768 | tf_op jit(solution)/shard_map/ppermute | solution.py:37
  32.8 5.2 %collective-permute-done.5 = f32[160,128]{1,0:T(8,128)S(1)} collective-permute-done((f32[160,128]{1,0:T(8,128)S(1)}, f32[160,128]{1,0:T(8,128)S(1)}, u32[]{:S(2)}, u32[]{:S(2)}) %collective-permute-start.5) | collective-permute-done | bytes 81952 | tf_op jit(solution)/shard_map/ppermute | solution.py:37
  38.0 3.7 %collective-permute-start.6 = (f32[160,128]{1,0:T(8,128)S(1)}, f32[160,128]{1,0:T(8,128)S(1)}, u32[]{:S(2)}, u32[]{:S(2)}) collective-permute-start(f32[160,128]{1,0:T(8,128)S(1)} %add.46), channel_id=1, source_target_pairs={{0,16},{1,17},{2,18},{3,19},{4,20},{5,21},{6,22},{7,23},{8,24},{9,... | collective-permute-start | bytes 245768 | tf_op jit(solution)/shard_map/ppermute | solution.py:37
  41.7 2.4 %collective-permute-done.6 = f32[160,128]{1,0:T(8,128)S(1)} collective-permute-done((f32[160,128]{1,0:T(8,128)S(1)}, f32[160,128]{1,0:T(8,128)S(1)}, u32[]{:S(2)}, u32[]{:S(2)}) %collective-permute-start.6) | collective-permute-done | bytes 81952 | tf_op jit(solution)/shard_map/ppermute | solution.py:37
  44.1 0.1 collective-permute-start.7
  44.2 1.3 %collective-permute-done.7.other_ref = f32[160,128]{1,0:T(8,128)S(1)} collective-permute-done((f32[160,128]{1,0:T(8,128)S(1)}, f32[160,128]{1,0:T(8,128)S(1)}, u32[]{:S(2)}, u32[]{:S(2)}) %collective-permute-start.7) | collective-permute-done | bytes 81952 | tf_op jit(solution)/shard_map/ppermute | solution.py:37
  45.4 11.8 %shard_map.85 = (f32[256,256]{1,0:T(8,128)S(1)}, f32[256,256]{1,0:T(8,128)S(1)}, f32[1,256]{1,0:T(1,128)S(1)}) custom-call(s32[1]{0:T(128)} %bitcast.odd_ref.refs_0_, f32[160,128]{1,0:T(8,128)S(1)} %add.47.mine_ref, f32[160,128]{1,0:T(8,128)S(1)} %collective-permute-done.7.other_ref), custom_call_target="tpu_custom_call" | custom-call | tf_op jit(solution)/shard_map/pallas_call | solution.py:25
  57.2 0.0 collective-permute-done.1.back_ref
  57.2 3.0 %shard_map.86 = (f32[768,256]{1,0:T(8,128)S(1)}, f32[3,256,256]{2,1,0:T(8,128)S(1)}, f32[264,128]{1,0:T(8,128)S(1)}, f32[264,128]{1,0:T(8,128)S(1)}) custom-call(s32[1]{0:T(128)} %bitcast.odd_ref.refs_0_, f32[3,256,256]{2,1,0:T(8,128)S(1)} %copy-done.1, f32[3,256,256]{2,1,0:T(8,128)S(1)} %get-tuple-element.22.own_ref, ...), custom_call_target="tpu_custom_call" | custom-call | tf_op jit(solution)/shard_map/pallas_call | solution.py:25
  60.2 0.2 collective-permute-start.8
  60.4 1.2 %collective-permute-done.8 = f32[264,128]{1,0:T(8,128)S(1)} collective-permute-done((f32[264,128]{1,0:T(8,128)S(1)}, f32[264,128]{1,0:T(8,128)S(1)}, u32[]{:S(2)}, u32[]{:S(2)}) %collective-permute-start.8) | collective-permute-done | bytes 135200 | tf_op jit(solution)/shard_map/ppermute | solution.py:37
  61.6 1.6 %collective-permute-start.9 = (f32[264,128]{1,0:T(8,128)S(1)}, f32[264,128]{1,0:T(8,128)S(1)}, u32[]{:S(2)}, u32[]{:S(2)}) collective-permute-start(f32[264,128]{1,0:T(8,128)S(1)} %add.48), channel_id=1, source_target_pairs={{0,2},{1,3},{2,0},{3,1},{4,6},{5,7},{6,4},{7,5},{8,10},{9,11},{10,... | collective-permute-start | bytes 405512 | tf_op jit(solution)/shard_map/ppermute | solution.py:37
  63.2 4.1 %collective-permute-done.9 = f32[264,128]{1,0:T(8,128)S(1)} collective-permute-done((f32[264,128]{1,0:T(8,128)S(1)}, f32[264,128]{1,0:T(8,128)S(1)}, u32[]{:S(2)}, u32[]{:S(2)}) %collective-permute-start.9) | collective-permute-done | bytes 135200 | tf_op jit(solution)/shard_map/ppermute | solution.py:37
  67.4 1.6 %collective-permute-start.10 = (f32[264,128]{1,0:T(8,128)S(1)}, f32[264,128]{1,0:T(8,128)S(1)}, u32[]{:S(2)}, u32[]{:S(2)}) collective-permute-start(f32[264,128]{1,0:T(8,128)S(1)} %add.49), channel_id=1, source_target_pairs={{0,4},{1,5},{2,6},{3,7},{4,0},{5,1},{6,2},{7,3},{8,12},{9,13},{10,... | collective-permute-start | bytes 405512 | tf_op jit(solution)/shard_map/ppermute | solution.py:37
  68.9 3.5 %collective-permute-done.10 = f32[264,128]{1,0:T(8,128)S(1)} collective-permute-done((f32[264,128]{1,0:T(8,128)S(1)}, f32[264,128]{1,0:T(8,128)S(1)}, u32[]{:S(2)}, u32[]{:S(2)}) %collective-permute-start.10) | collective-permute-done | bytes 135200 | tf_op jit(solution)/shard_map/ppermute | solution.py:37
  72.5 0.1 collective-permute-start.11
  72.6 5.0 %collective-permute-done.11 = f32[264,128]{1,0:T(8,128)S(1)} collective-permute-done((f32[264,128]{1,0:T(8,128)S(1)}, f32[264,128]{1,0:T(8,128)S(1)}, u32[]{:S(2)}, u32[]{:S(2)}) %collective-permute-start.11) | collective-permute-done | bytes 135200 | tf_op jit(solution)/shard_map/ppermute | solution.py:37
  77.6 4.6 %collective-permute-start.12 = (f32[264,128]{1,0:T(8,128)S(1)}, f32[264,128]{1,0:T(8,128)S(1)}, u32[]{:S(2)}, u32[]{:S(2)}) collective-permute-start(f32[264,128]{1,0:T(8,128)S(1)} %add.51), channel_id=1, source_target_pairs={{0,16},{1,17},{2,18},{3,19},{4,20},{5,21},{6,22},{7,23},{8,24},{9,... | collective-permute-start | bytes 405512 | tf_op jit(solution)/shard_map/ppermute | solution.py:37
  82.1 3.4 %collective-permute-done.12 = f32[264,128]{1,0:T(8,128)S(1)} collective-permute-done((f32[264,128]{1,0:T(8,128)S(1)}, f32[264,128]{1,0:T(8,128)S(1)}, u32[]{:S(2)}, u32[]{:S(2)}) %collective-permute-start.12) | collective-permute-done | bytes 135200 | tf_op jit(solution)/shard_map/ppermute | solution.py:37
  85.6 0.1 collective-permute-start.13
  85.7 0.6 multiply_log_fusion
  86.2 0.8 collective-permute-done.13.refs_2_
  87.0 6.3 %shard_map.87 = (f32[3,256,256]{2,1,0:T(8,128)}, f32[3,256,256]{2,1,0:T(8,128)}, f32[256,256]{1,0:T(8,128)}, f32[256,256]{1,0:T(8,128)}) custom-call(s32[1]{0:T(128)} %bitcast.odd_ref.refs_0_, f32[264,128]{1,0:T(8,128)S(1)} %add.52.refs_1_, f32[264,128]{1,0:T(8,128)S(1)} %collective-permute-done.13.refs_2_, f32[768,256]{1,0:T(8,128)S(1)} %get-tuple-element.29.refs_3_, ...), custom_call_target="tpu_custom_call" | custom-call | tf_op jit(solution)/shard_map/pallas_call | solution.py:25
  (12 shorter events, 0.2 us)
Async XLA Ops:
  0.6 7.2 %copy-start.2 = (s32[2,1024]{1,0:T(2,128)S(1)}, s32[2,1024]{1,0:T(2,128)}, u32[]{:S(2)}) copy-start(s32[2,1024]{1,0:T(2,128)} %ends_ref.1) | copy-start | bytes 24580
  0.7 1.1 %copy-start = (f32[3,256,256]{2,1,0:T(8,128)S(1)}, f32[3,256,256]{2,1,0:T(8,128)}, u32[]{:S(2)}) copy-start(f32[3,256,256]{2,1,0:T(8,128)} %s_ref.5) | copy-start | bytes 2359300
  1.8 14.3 %copy-start.1 = (f32[3,256,256]{2,1,0:T(8,128)S(1)}, f32[3,256,256]{2,1,0:T(8,128)}, u32[]{:S(2)}) copy-start(f32[3,256,256]{2,1,0:T(8,128)} %s_ref.5) | copy-start | bytes 2359300
  2.8 13.3 %collective-permute-start = (f32[3,128,256]{2,1,0:T(8,128)S(1)}, f32[3,128,256]{2,1,0:T(8,128)S(1)}, u32[]{:S(2)}, u32[]{:S(2)}) collective-permute-start(f32[3,128,256]{2,1,0:T(8,128)S(1)} %get-tuple-element.21), channel_id=1, source_target_pairs={{0,8},{8,16},{16,24},{1,9},{9,17},{17,25},{2,10},{10,18},{18,26},{... | collective-permute-start | bytes 1179656 | tf_op jit(solution)/shard_map/ppermute | solution.py:53
  7.7 1.3 %collective-permute-start.2 = (f32[160,128]{1,0:T(8,128)S(1)}, f32[160,128]{1,0:T(8,128)S(1)}, u32[]{:S(2)}, u32[]{:S(2)}) collective-permute-start(f32[160,128]{1,0:T(8,128)S(1)} %get-tuple-element.25), channel_id=1, source_target_pairs={{0,1},{1,0},{2,3},{3,2},{4,5},{5,4},{6,7},{7,6},{8,9},{9,8},{10,11... | collective-permute-start | bytes 245768 | tf_op jit(solution)/shard_map/ppermute | solution.py:37
  9.1 1.6 %copy-start.3 = (f32[3,1024]{1,0:T(4,128)S(1)}, f32[3,1024]{1,0:T(4,128)}, u32[]{:S(2)}) copy-start(f32[3,1024]{1,0:T(4,128)} %param.6) | copy-start | bytes 36868
  9.1 1.6 %copy-start.4 = (f32[1024]{0:T(1024)S(1)}, f32[1024]{0:T(1024)}, u32[]{:S(2)}) copy-start(f32[1024]{0:T(1024)} %param.7) | copy-start | bytes 12292
  9.1 16.0 %collective-permute-start.3 = (f32[160,128]{1,0:T(8,128)S(1)}, f32[160,128]{1,0:T(8,128)S(1)}, u32[]{:S(2)}, u32[]{:S(2)}) collective-permute-start(f32[160,128]{1,0:T(8,128)S(1)} %add.43), channel_id=1, source_target_pairs={{0,2},{1,3},{2,0},{3,1},{4,6},{5,7},{6,4},{7,5},{8,10},{9,11},{10,... | collective-permute-start | bytes 245768 | tf_op jit(solution)/shard_map/ppermute | solution.py:37
  23.6 33.7 %collective-permute-start.1 = (f32[3,128,256]{2,1,0:T(8,128)S(1)}, f32[3,128,256]{2,1,0:T(8,128)S(1)}, u32[]{:S(2)}, u32[]{:S(2)}) collective-permute-start(f32[3,128,256]{2,1,0:T(8,128)S(1)} %get-tuple-element.23), channel_id=1, source_target_pairs={{8,0},{16,8},{24,16},{9,1},{17,9},{25,17},{10,2},{18,10},{26,18},{... | collective-permute-start | bytes 1179656 | tf_op jit(solution)/shard_map/ppermute | solution.py:53
  25.1 4.5 %collective-permute-start.4 = (f32[160,128]{1,0:T(8,128)S(1)}, f32[160,128]{1,0:T(8,128)S(1)}, u32[]{:S(2)}, u32[]{:S(2)}) collective-permute-start(f32[160,128]{1,0:T(8,128)S(1)} %add.44), channel_id=1, source_target_pairs={{0,4},{1,5},{2,6},{3,7},{4,0},{5,1},{6,2},{7,3},{8,12},{9,13},{10,... | collective-permute-start | bytes 245768 | tf_op jit(solution)/shard_map/ppermute | solution.py:37
  29.6 8.3 %collective-permute-start.5 = (f32[160,128]{1,0:T(8,128)S(1)}, f32[160,128]{1,0:T(8,128)S(1)}, u32[]{:S(2)}, u32[]{:S(2)}) collective-permute-start(f32[160,128]{1,0:T(8,128)S(1)} %add.45), channel_id=1, source_target_pairs={{0,8},{1,9},{2,10},{3,11},{4,12},{5,13},{6,14},{7,15},{8,0},{9,1},... | collective-permute-start | bytes 245768 | tf_op jit(solution)/shard_map/ppermute | solution.py:37
  38.0 6.1 %collective-permute-start.6 = (f32[160,128]{1,0:T(8,128)S(1)}, f32[160,128]{1,0:T(8,128)S(1)}, u32[]{:S(2)}, u32[]{:S(2)}) collective-permute-start(f32[160,128]{1,0:T(8,128)S(1)} %add.46), channel_id=1, source_target_pairs={{0,16},{1,17},{2,18},{3,19},{4,20},{5,21},{6,22},{7,23},{8,24},{9,... | collective-permute-start | bytes 245768 | tf_op jit(solution)/shard_map/ppermute | solution.py:37
  44.1 1.3 %collective-permute-start.7 = (f32[160,128]{1,0:T(8,128)S(1)}, f32[160,128]{1,0:T(8,128)S(1)}, u32[]{:S(2)}, u32[]{:S(2)}) collective-permute-start(f32[160,128]{1,0:T(8,128)S(1)} %add.47.mine_ref), channel_id=1, source_target_pairs={{0,1},{1,0},{2,3},{3,2},{4,5},{5,4},{6,7},{7,6},{8,9},{9,8},{10,11... | collective-permute-start | bytes 245768 | tf_op jit(solution)/shard_map/ppermute | solution.py:37
  60.2 1.4 %collective-permute-start.8 = (f32[264,128]{1,0:T(8,128)S(1)}, f32[264,128]{1,0:T(8,128)S(1)}, u32[]{:S(2)}, u32[]{:S(2)}) collective-permute-start(f32[264,128]{1,0:T(8,128)S(1)} %get-tuple-element.28), channel_id=1, source_target_pairs={{0,1},{1,0},{2,3},{3,2},{4,5},{5,4},{6,7},{7,6},{8,9},{9,8},{10,11... | collective-permute-start | bytes 405512 | tf_op jit(solution)/shard_map/ppermute | solution.py:37
  61.6 5.7 %collective-permute-start.9 = (f32[264,128]{1,0:T(8,128)S(1)}, f32[264,128]{1,0:T(8,128)S(1)}, u32[]{:S(2)}, u32[]{:S(2)}) collective-permute-start(f32[264,128]{1,0:T(8,128)S(1)} %add.48), channel_id=1, source_target_pairs={{0,2},{1,3},{2,0},{3,1},{4,6},{5,7},{6,4},{7,5},{8,10},{9,11},{10,... | collective-permute-start | bytes 405512 | tf_op jit(solution)/shard_map/ppermute | solution.py:37
  67.4 5.1 %collective-permute-start.10 = (f32[264,128]{1,0:T(8,128)S(1)}, f32[264,128]{1,0:T(8,128)S(1)}, u32[]{:S(2)}, u32[]{:S(2)}) collective-permute-start(f32[264,128]{1,0:T(8,128)S(1)} %add.49), channel_id=1, source_target_pairs={{0,4},{1,5},{2,6},{3,7},{4,0},{5,1},{6,2},{7,3},{8,12},{9,13},{10,... | collective-permute-start | bytes 405512 | tf_op jit(solution)/shard_map/ppermute | solution.py:37
  72.5 5.1 %collective-permute-start.11 = (f32[264,128]{1,0:T(8,128)S(1)}, f32[264,128]{1,0:T(8,128)S(1)}, u32[]{:S(2)}, u32[]{:S(2)}) collective-permute-start(f32[264,128]{1,0:T(8,128)S(1)} %add.50), channel_id=1, source_target_pairs={{0,8},{1,9},{2,10},{3,11},{4,12},{5,13},{6,14},{7,15},{8,0},{9,1},... | collective-permute-start | bytes 405512 | tf_op jit(solution)/shard_map/ppermute | solution.py:37
  77.6 8.0 %collective-permute-start.12 = (f32[264,128]{1,0:T(8,128)S(1)}, f32[264,128]{1,0:T(8,128)S(1)}, u32[]{:S(2)}, u32[]{:S(2)}) collective-permute-start(f32[264,128]{1,0:T(8,128)S(1)} %add.51), channel_id=1, source_target_pairs={{0,16},{1,17},{2,18},{3,19},{4,20},{5,21},{6,22},{7,23},{8,24},{9,... | collective-permute-start | bytes 405512 | tf_op jit(solution)/shard_map/ppermute | solution.py:37
  85.6 1.4 %collective-permute-start.13 = (f32[264,128]{1,0:T(8,128)S(1)}, f32[264,128]{1,0:T(8,128)S(1)}, u32[]{:S(2)}, u32[]{:S(2)}) collective-permute-start(f32[264,128]{1,0:T(8,128)S(1)} %add.52.refs_1_), channel_id=1, source_target_pairs={{0,1},{1,0},{2,3},{3,2},{4,5},{5,4},{6,7},{7,6},{8,9},{9,8},{10,11... | collective-permute-start | bytes 405512 | tf_op jit(solution)/shard_map/ppermute | solution.py:37
where the time goes:
time: 93.6 us; the launch traced here: 93.3 us
  waiting for transfers between devices  36.1 us (39%)
  Pallas kernels  29.5 us (32%)
  starting transfers between devices  24.6 us (26%)
  local copies, waits for them, and re-layouts  1.42 us (2%)
    ppermute x12, waiting for transfers between devices, exchange(): return lax.ppermute(array, AXES, [(i, i ^ bit) for i in range(count)])  31 us
    pallas_call x5, Pallas kernels, call(): pl.pallas_call(kernel, out_shape=tuple((jax.ShapeDtypeStruct(s, jnp.float...  29.5 us
    ppermute x12, starting transfers between devices, exchange(): return lax.ppermute(array, AXES, [(i, i ^ bit) for i in range(count)])  18.2 us
    ppermute x2, starting transfers between devices, shifted(): return lax.ppermute(array, axis, pairs)  6.43 us
    ppermute x2, waiting for transfers between devices, shifted(): return lax.ppermute(array, axis, pairs)  5.1 us
  transfers between devices with their start and end apart: 14, of which 12 were waited for; matrix products, arithmetic and copies ran while one was open for 1% of the time, Pallas kernels for 21%

commit v1 on v0

--- a/solution.py
+++ b/solution.py
@@ -13,6 +13,7 @@
 highest = lax.Precision.HIGHEST
 VMEM = pl.BlockSpec(memory_space=pltpu.VMEM)
 SMEM = pl.BlockSpec(memory_space=pltpu.SMEM)
+ANY = pl.BlockSpec(memory_space=pl.ANY)
 
 
 def dot(a, b, ca=1, cb=0):
@@ -37,13 +38,35 @@
     return lax.ppermute(array, AXES, [(i, i ^ bit) for i in range(count)])
 
 
-def sum_over_devices(keep, send):
+def add_kernel(a_ref, b_ref, *rest):
+    rest[-1][...] = a_ref[...] + b_ref[...]
+
+
+def add(a, b, beside):
+    return call(add_kernel, [a.shape], (a, b, *beside), [VMEM, VMEM] + [ANY] * len(beside))[0]
+
+
+def after(array, tie):
+    return pl.pallas_call(
+        lambda *refs: None,
+        out_shape=jax.ShapeDtypeStruct(array.shape, array.dtype),
+        in_specs=[ANY, ANY],
+        out_specs=ANY,
+        input_output_aliases={0: 0},
+    )(array, tie)
+
+
+def sum_over_devices(keep, send, beside=()):
     count = math.prod(lax.axis_size(a) for a in AXES)
-    total = keep + exchange(send, 1)
-    bit = 2
+    total = add(keep, exchange(send, 1), ())
+    bit, waiting = 2, list(beside)
     while bit < count:
-        total = total + exchange(total, bit)
+        received = exchange(total, bit)
+        done = waiting.pop(0)(total) if waiting else ()
+        total = add(total, received, done)
         bit *= 2
+    for work in waiting:
+        work(total)
     return total, exchange(total, 1)
 
 
@@ -97,47 +120,48 @@
     return first, second, third
 
 
-def member_kernel(s_ref, below_ref, ends_ref, table_ref, own_ref, back_ref, parts_ref):
-    nodes, width = s_ref.shape[1:]
-    total = nodes + SEC_NODES
-    for c in range(3):
-        for i, piece in enumerate(pieces_of(s_ref[c])):
-            parts_ref[i, c, :nodes, :] = piece
-        for i, piece in enumerate(pieces_of(below_ref[c])):
-            parts_ref[i, c, nodes:, :] = piece
-    own_ref[...] = jnp.zeros_like(own_ref)
-    back_ref[...] = jnp.zeros_like(back_ref)
-
-    def chunk(start):
-        rows = pl.ds(pl.multiple_of(start, CHUNK), CHUNK)
-        table = table_ref[rows, :]
-        node = lax.broadcasted_iota(jnp.int32, (CHUNK, total), 1).astype(jnp.float32)
-        pick = (node == table[:, 0:1]).astype(jnp.float32) - (node == table[:, 1:2]).astype(jnp.float32)
-        pick = pick.astype(jnp.bfloat16)
-        ends = ends_ref[:, rows]
-        node_t = lax.broadcasted_iota(jnp.int32, (total, CHUNK), 0)
-        spread = (node_t == ends[0:1]).astype(jnp.float32) - (node_t == ends[1:2]).astype(jnp.float32)
+def picks(node_count, first, second):
+    node = lax.broadcasted_iota(jnp.int32, (first.shape[0], node_count), 1).astype(jnp.float32)
+    pick = (node == first).astype(jnp.float32) - (node == second).astype(jnp.float32)
+    return pick.astype(jnp.bfloat16)
+
+
+def picked(pick, pieces):
+    return sum(jnp.dot(pick, piece, preferred_element_type=jnp.float32) for piece in pieces)
+
+
+def own_elongation_kernel(table_ref, s_ref, tie_ref, long_ref):
+    del tie_ref
+    nodes = s_ref.shape[1]
+    pieces = [pieces_of(s_ref[c]) for c in range(3)]
+    for start in range(0, table_ref.shape[0], CHUNK):
+        table = table_ref[start : start + CHUNK, :]
+        pick = picks(nodes, table[:, 0:1], table[:, 1:2])
+        long_ref[start : start + CHUNK, :] = sum(table[:, 2 + c : 3 + c] * picked(pick, pieces[c]) for c in range(3))
+
+
+def member_kernel(table_ref, ends_ref, long_ref, below_ref, *rest):
+    own_ref, back_ref = rest[-2:]
+    nodes = own_ref.shape[1]
+    if len(rest) > 3:
+        own_ref[...], back_ref[...] = rest[0][...], rest[1][...]
+    else:
+        own_ref[...], back_ref[...] = jnp.zeros_like(own_ref), jnp.zeros_like(back_ref)
+    pieces = [pieces_of(below_ref[c]) for c in range(3)]
+    for start in range(0, table_ref.shape[0], CHUNK):
+        table = table_ref[start : start + CHUNK, :]
+        pick = picks(SEC_NODES, table[:, 0:1] - nodes, table[:, 1:2] - nodes)
+        elongation = long_ref[start : start + CHUNK, :]
+        elongation += sum(table[:, 2 + c : 3 + c] * picked(pick, pieces[c]) for c in range(3))
+        axial = elongation * table[:, 5:6]
+        ends = ends_ref[:, start : start + CHUNK]
+        node = lax.broadcasted_iota(jnp.int32, (nodes + SEC_NODES, CHUNK), 0)
+        spread = (node == ends[0:1]).astype(jnp.float32) - (node == ends[1:2]).astype(jnp.float32)
         spread = spread.astype(jnp.bfloat16)
-        elongation = jnp.zeros((CHUNK, width), jnp.float32)
         for c in range(3):
-            difference = jnp.zeros((CHUNK, width), jnp.float32)
-            for i in range(3):
-                difference = difference + jnp.dot(pick, parts_ref[i, c], preferred_element_type=jnp.float32)
-            elongation = elongation + table[:, 2 + c : 3 + c] * difference
-        axial = elongation * table[:, 5:6]
-        for c in range(3):
-            push = table[:, 2 + c : 3 + c] * axial
-            force = jnp.zeros((total, width), jnp.float32)
-            for piece in pieces_of(push):
-                force = force + jnp.dot(spread, piece, preferred_element_type=jnp.float32)
+            force = picked(spread, pieces_of(table[:, 2 + c : 3 + c] * axial))
             own_ref[c] += force[:nodes]
             back_ref[c] += force[nodes:]
-
-    def step(i, carry):
-        chunk(i * CHUNK)
-        return carry
-
-    lax.fori_loop(0, table_ref.shape[0] // CHUNK, step, 0)
 
 
 def factor_block(x_ref, u_ref, m_ref):
@@ -247,8 +271,16 @@
     keep_ref[...], send_ref[...] = order_halves(odd_ref[0], lo, hi)
 
 
+def refine_kernel(w_ref, r_ref, tie_ref, out_ref):
+    del tie_ref
+    r = r_ref[...]
+    size = r.shape[0]
+    eye = lax.broadcasted_iota(jnp.int32, (size, size), 0) == lax.broadcasted_iota(jnp.int32, (size, size), 1)
+    out_ref[...] = r + dot(jnp.where(eye, 1.0, 0.0) - dot(r, w_ref[...]), r)
+
+
 def final_kernel(
-    rows_all, odd_ref, mine_ref, other_ref, q_ref, f_ref, w1_ref, r1_ref,
+    rows_all, odd_ref, mine_ref, other_ref, q_ref, f_ref, r1_ref,
     basis_ref, forces_ref, reduced_ref, coef_ref, w2, r2, x, u, m,
 ):
     parts, nodes, width = f_ref.shape
@@ -300,9 +332,7 @@
     basis_ref[...] = dot(q_ref[...], w * root).reshape(parts, nodes, width)
     forces_ref[...] = dot(f_ref[...].reshape(-1, width), w * root).reshape(parts, nodes, width)
     reduced_ref[...] = dot(w, dot(energy, w), 0, 0)
-    r1 = r1_ref[...]
-    r1 = r1 + dot(eye - dot(r1, w1_ref[...]), r1)
-    coef_ref[...] = jnp.where(rowi <= coli, dot(r2[...], r1), 0.0) * (1.0 / root)
+    coef_ref[...] = jnp.where(rowi <= coli, dot(r2[...], r1_ref[...]), 0.0) * (1.0 / root)
 
 
 def local(snapshots, member_ends, member_dir, member_stiff):
@@ -319,17 +349,42 @@
 
     keep, send, top = call(gram_kernel, [quarter, quarter, level], (odd, snapshots), [SMEM, VMEM])
     below = shifted(top, "span", 1)
-    mine, other = sum_over_devices(keep, send)
-
     ends = member_ends.astype(jnp.float32)
     table = jnp.concatenate([ends, member_dir, member_stiff[None], jnp.zeros_like(ends)], axis=0).T
-    own, back = call(
-        member_kernel,
-        [field, level],
-        (snapshots, below, member_ends, table),
-        scratch=[pltpu.VMEM((3, parts, nodes + SEC_NODES, width), jnp.bfloat16)],
-    )
-    returned = shifted(back, "span", -1)
+    split = table.shape[0] // 2
+    lows, highs = table[:split], table[split:]
+    held = {}
+
+    def own_part(name, rows):
+        def work(tie):
+            held[name] = call(own_elongation_kernel, [(split, width)], (rows, snapshots, tie), [VMEM, VMEM, ANY])
+            return held[name]
+
+        return work
+
+    def member_part(name, rows, ends_of, before):
+        def work(tie):
+            given = held.get(before, ())
+            operands = (rows, ends_of, held[name][0], below, *given, tie)
+            held["forces" + name] = call(
+                member_kernel, [field, level], operands, [VMEM] * (len(operands) - 1) + [ANY]
+            )
+            return held["forces" + name]
+
+        return work
+
+    mine, other = sum_over_devices(
+        keep,
+        send,
+        [
+            own_part("a", lows),
+            own_part("b", highs),
+            member_part("a", lows, member_ends[:, :split], None),
+            member_part("b", highs, member_ends[:, split:], "forcesa"),
+        ],
+    )
+    own, back = held["forcesb"]
+    returned = shifted(after(back, mine), "span", -1)
 
     w1, r1, diag = call(
         first_factor_kernel, [square, square, (1, width)], (odd, mine, other), [SMEM, VMEM, VMEM], scratch
@@ -343,12 +398,18 @@
         (odd, snapshots, own, returned, w1),
         [SMEM] + [VMEM] * 4,
     )
-    mine, other = sum_over_devices(keep, send)
+    refined = []
+
+    def refine(tie):
+        refined.extend(call(refine_kernel, [square], (w1, r1, tie), [VMEM, VMEM, ANY]))
+        return refined
+
+    mine, other = sum_over_devices(keep, send, [refine])
     basis, forces, reduced, coef = call(
         lambda *refs: final_kernel(rows_all, *refs),
         [field, field, square, square],
-        (odd, mine, other, q, f, w1, r1),
-        [SMEM] + [VMEM] * 6,
+        (odd, mine, other, q, f, refined[0]),
+        [SMEM] + [VMEM] * 5,
         [pltpu.VMEM(square, jnp.float32)] * 2 + scratch,
     )
     return (basis, forces, reduced, coef, column_energy)

time: 93.6 us -> 78.7 us (0.84)
  waiting for transfers between devices: 36.1 us -> 21 us
  local copies, waits for them, and re-layouts: 1.42 us -> 4.06 us
  starting transfers between devices: 24.6 us -> 22.7 us
    ppermute x12, waiting for transfers between devices: 31 us -> 21 us  [exchange(): return lax.ppermute(array, AXES, [(i, i ^ bit) for i in range(count)])]
    ppermute x2, waiting for transfers between devices: 5.1 us -> 0.01 us  [shifted(): return lax.ppermute(array, axis, pairs)]
    unnamed x10 -> x16, local copies, waits for them, and re-layouts: 1.14 us -> 3.75 us
    ppermute x12, starting transfers between devices: 18.2 us -> 16.7 us  [exchange(): return lax.ppermute(array, AXES, [(i, i ^ bit) for i in range(count)])]
    pallas_call x5 -> x19, Pallas kernels: 29.5 us -> 28.9 us  [call(): pl.pallas_call(kernel, out_shape=tuple((jax.ShapeDtypeStruct(s, jnp.float...]
  transfers between devices with their start and end apart: 14 -> 14, of which waited for: 12 -> 11; matrix products, arithmetic and copies ran while one was open for 1% -> 1% of each run, Pallas kernels for 21% -> 25%
where the time goes in v1:
time: 78.7 us; the launch traced here: 78.2 us
  Pallas kernels  28.9 us (37%)
  starting transfers between devices  22.7 us (29%)
  waiting for transfers between devices  21 us (27%)
  local copies, waits for them, and re-layouts  4.06 us (5%)
  between operations  0.89 us (1%)
    pallas_call x19, Pallas kernels, call(): pl.pallas_call(kernel, out_shape=tuple((jax.ShapeDtypeStruct(s, jnp.float...  28.9 us
    ppermute x12, waiting for transfers between devices, exchange(): return lax.ppermute(array, AXES, [(i, i ^ bit) for i in range(count)])  21 us
    ppermute x12, starting transfers between devices, exchange(): return lax.ppermute(array, AXES, [(i, i ^ bit) for i in range(count)])  16.7 us
    ppermute x2, starting transfers between devices, shifted(): return lax.ppermute(array, axis, pairs)  5.97 us
    unnamed x16, local copies, waits for them, and re-layouts  3.75 us
  transfers between devices with their start and end apart: 14, of which 11 were waited for; matrix products, arithmetic and copies ran while one was open for 1% of the time, Pallas kernels for 25%

profile of v1, /device:TPU:0, one launch (start us, length us, event | category | flops | bytes accessed | tf_op | source)
XLA Modules:
  0.0 78.2 jit_solution(837682637353078716)
XLA Ops:
  0.6 0.0 copy-start
  0.7 1.1 %copy-done = f32[3,256,256]{2,1,0:T(8,128)S(1)} copy-done((f32[3,256,256]{2,1,0:T(8,128)S(1)}, f32[3,256,256]{2,1,0:T(8,128)}, u32[]{:S(2)}) %copy-start) | copy-done | bytes 786456
  1.8 0.0 copy-start.5
  1.8 1.0 %shard_map.83 = (f32[160,128]{1,0:T(8,128)S(1)}, f32[160,128]{1,0:T(8,128)S(1)}, f32[3,128,256]{2,1,0:T(8,128)S(1)}) custom-call(s32[1]{0:T(128)} %bitcast.odd_ref.refs_0_, f32[3,256,256]{2,1,0:T(8,128)S(1)} %copy-done), custom_call_target="tpu_custom_call" | custom-call | tf_op jit(solution)/shard_map/pallas_call | solution.py:26
  2.8 0.0 copy-start.6
  2.8 0.5 collective-permute-start
  3.3 4.5 %collective-permute-start.2 = (f32[3,128,256]{2,1,0:T(8,128)S(1)}, f32[3,128,256]{2,1,0:T(8,128)S(1)}, u32[]{:S(2)}, u32[]{:S(2)}) collective-permute-start(f32[3,128,256]{2,1,0:T(8,128)S(1)} %get-tuple-element.25), channel_id=1, source_target_pairs={{0,8},{8,16},{16,24},{1,9},{9,17},{17,25},{2,10},{10,18},{18,26},{... | collective-permute-start | bytes 1179656 | tf_op jit(solution)/shard_map/ppermute | solution.py:76
  7.8 0.0 copy-done.5
  7.8 0.0 copy-start.7
  7.8 0.1 pad.3.clone
  7.9 0.0 copy-done.6
  7.9 0.6 copy-done.7
  8.5 0.1 maximum_maximum_fusion
  8.6 0.2 copy.15
  8.8 0.0 copy-start.1
  8.8 0.0 collective-permute-done.b_ref
  8.8 1.6 %collective-permute-start.1 = (f32[160,128]{1,0:T(8,128)S(1)}, f32[160,128]{1,0:T(8,128)S(1)}, u32[]{:S(2)}, u32[]{:S(2)}) collective-permute-start(f32[160,128]{1,0:T(8,128)S(1)} %shard_map.84.tie_ref.a_ref), channel_id=1, source_target_pairs={{0,2},{1,3},{2,0},{3,1},{4,6},{5,7},{6,4},{7,5},{8,10},{9,11},{10,... | collective-permute-start | bytes 245768 | tf_op jit(solution)/shard_map/ppermute | solution.py:38
  10.5 0.0 copy-done.1
  10.5 0.9 %shard_map.85.rest_0_.long_ref = f32[512,256]{1,0:T(8,128)S(1)} custom-call(f32[512,8]{1,0:T(8,128)S(1)} %get-tuple-element.41.table_ref, f32[3,256,256]{2,1,0:T(8,128)S(1)} %copy-done.1, f32[160,128]{1,0:T(8,128)S(1)} %shard_map.84.tie_ref.a_ref), custom_call_target="tpu_custom_call" | custom-call | tf_op jit(solution)/shard_map/pallas_call | solution.py:26
  11.3 2.1 %collective-permute-done.1.b_ref = f32[160,128]{1,0:T(8,128)S(1)} collective-permute-done((f32[160,128]{1,0:T(8,128)S(1)}, f32[160,128]{1,0:T(8,128)S(1)}, u32[]{:S(2)}, u32[]{:S(2)}) %collective-permute-start.1) | collective-permute-done | bytes 81952 | tf_op jit(solution)/shard_map/ppermute | solution.py:38
  13.5 1.6 %collective-permute-start.3 = (f32[160,128]{1,0:T(8,128)S(1)}, f32[160,128]{1,0:T(8,128)S(1)}, u32[]{:S(2)}, u32[]{:S(2)}) collective-permute-start(f32[160,128]{1,0:T(8,128)S(1)} %shard_map.86.tie_ref.a_ref), channel_id=1, source_target_pairs={{0,4},{1,5},{2,6},{3,7},{4,0},{5,1},{6,2},{7,3},{8,12},{9,13},{10,... | collective-permute-start | bytes 245768 | tf_op jit(solution)/shard_map/ppermute | solution.py:38
  15.0 0.9 %shard_map.87.rest_0_.long_ref = f32[512,256]{1,0:T(8,128)S(1)} custom-call(f32[512,8]{1,0:T(8,128)S(1)} %get-tuple-element.42.table_ref, f32[3,256,256]{2,1,0:T(8,128)S(1)} %copy-done.1, f32[160,128]{1,0:T(8,128)S(1)} %shard_map.86.tie_ref.a_ref), custom_call_target="tpu_custom_call" | custom-call | tf_op jit(solution)/shard_map/pallas_call | solution.py:26
  15.9 2.1 %collective-permute-done.3.b_ref = f32[160,128]{1,0:T(8,128)S(1)} collective-permute-done((f32[160,128]{1,0:T(8,128)S(1)}, f32[160,128]{1,0:T(8,128)S(1)}, u32[]{:S(2)}, u32[]{:S(2)}) %collective-permute-start.3) | collective-permute-done | bytes 81952 | tf_op jit(solution)/shard_map/ppermute | solution.py:38
  18.0 1.6 %collective-permute-start.4 = (f32[160,128]{1,0:T(8,128)S(1)}, f32[160,128]{1,0:T(8,128)S(1)}, u32[]{:S(2)}, u32[]{:S(2)}) collective-permute-start(f32[160,128]{1,0:T(8,128)S(1)} %shard_map.88.rest_0_.a_ref), channel_id=1, source_target_pairs={{0,8},{1,9},{2,10},{3,11},{4,12},{5,13},{6,14},{7,15},{8,0},{9,1},... | collective-permute-start | bytes 245768 | tf_op jit(solution)/shard_map/ppermute | solution.py:38
  19.6 0.0 collective-permute-done.2.below_ref
  19.6 2.5 %shard_map.89 = (f32[3,256,256]{2,1,0:T(8,128)S(1)}, f32[3,128,256]{2,1,0:T(8,128)S(1)}) custom-call(f32[512,8]{1,0:T(8,128)S(1)} %get-tuple-element.41.table_ref, s32[2,512]{1,0:T(2,128)S(1)} %get-tuple-element.43.ends_ref, f32[512,256]{1,0:T(8,128)S(1)} %shard_map.85.rest_0_.long_ref, f32[3,128,256]{2,1,0:T(8,128)S(1)} %collective-permute-done.2.below_ref, ...), custom_call_target="tpu_custom_call" | custom-call | tf_op jit(solution)/shard_map/pallas_call | solution.py:26
  22.1 0.4 collective-permute-done.4.b_ref
  22.5 2.6 %collective-permute-start.5 = (f32[160,128]{1,0:T(8,128)S(1)}, f32[160,128]{1,0:T(8,128)S(1)}, u32[]{:S(2)}, u32[]{:S(2)}) collective-permute-start(f32[160,128]{1,0:T(8,128)S(1)} %shard_map.90.rest_2_.a_ref), channel_id=1, source_target_pairs={{0,16},{1,17},{2,18},{3,19},{4,20},{5,21},{6,22},{7,23},{8,24},{9,... | collective-permute-start | bytes 245768 | tf_op jit(solution)/shard_map/ppermute | solution.py:38
  25.1 2.5 %shard_map.91 = (f32[3,256,256]{2,1,0:T(8,128)S(1)}, f32[3,128,256]{2,1,0:T(8,128)S(1)}) custom-call(f32[512,8]{1,0:T(8,128)S(1)} %get-tuple-element.42.table_ref, s32[2,512]{1,0:T(2,128)S(1)} %get-tuple-element.44.ends_ref, f32[512,256]{1,0:T(8,128)S(1)} %shard_map.87.rest_0_.long_ref, f32[3,128,256]{2,1,0:T(8,128)S(1)} %collective-permute-done.2.below_ref, ...), custom_call_target="tpu_custom_call" | custom-call | tf_op jit(solution)/shard_map/pallas_call | solution.py:26
  27.7 0.0 copy-start.2
  27.7 0.2 collective-permute-done.5.b_ref
  27.9 0.5 copy-done.2
  28.4 0.0 copy-start.3
  28.4 0.6 copy-done.3
  29.1 1.5 %collective-permute-start.6 = (f32[3,128,256]{2,1,0:T(8,128)}, f32[3,128,256]{2,1,0:T(8,128)S(1)}, u32[]{:S(2)}, u32[]{:S(2)}) collective-permute-start(f32[3,128,256]{2,1,0:T(8,128)} %shard_map.93), channel_id=1, source_target_pairs={{8,0},{16,8},{24,16},{9,1},{17,9},{25,17},{10,2},{18,10},{26,18},{... | collective-permute-start | bytes 1179656 | tf_op jit(solution)/shard_map/ppermute | solution.py:76
  30.5 0.1 collective-permute-start.7
  30.6 1.5 %collective-permute-done.7.other_ref = f32[160,128]{1,0:T(8,128)S(1)} collective-permute-done((f32[160,128]{1,0:T(8,128)}, f32[160,128]{1,0:T(8,128)S(1)}, u32[]{:S(2)}, u32[]{:S(2)}) %collective-permute-start.7) | collective-permute-done | bytes 81952 | tf_op jit(solution)/shard_map/ppermute | solution.py:38
  32.1 0.0 copy-start.4
  32.1 0.9 %copy-done.4 = f32[160,128]{1,0:T(8,128)S(1)} copy-done((f32[160,128]{1,0:T(8,128)S(1)}, f32[160,128]{1,0:T(8,128)}, u32[]{:S(2)}) %copy-start.4) | copy-done | bytes 81944
  33.0 11.8 %shard_map.94 = (f32[256,256]{1,0:T(8,128)S(1)}, f32[256,256]{1,0:T(8,128)S(1)}, f32[1,256]{1,0:T(1,128)S(1)}) custom-call(s32[1]{0:T(128)} %bitcast.odd_ref.refs_0_, f32[160,128]{1,0:T(8,128)S(1)} %copy-done.4, f32[160,128]{1,0:T(8,128)S(1)} %collective-permute-done.7.other_ref), custom_call_target="tpu_custom_call" | custom-call | tf_op jit(solution)/shard_map/pallas_call | solution.py:26
  44.8 0.0 collective-permute-done.6.back_ref
  44.8 2.9 %shard_map.95 = (f32[768,256]{1,0:T(8,128)S(1)}, f32[3,256,256]{2,1,0:T(8,128)S(1)}, f32[264,128]{1,0:T(8,128)S(1)}, f32[264,128]{1,0:T(8,128)S(1)}) custom-call(s32[1]{0:T(128)} %bitcast.odd_ref.refs_0_, f32[3,256,256]{2,1,0:T(8,128)S(1)} %copy-done.1, f32[3,256,256]{2,1,0:T(8,128)S(1)} %get-tuple-element.28.rest_0_.own_ref, ...), custom_call_target="tpu_custom_call" | custom-call | tf_op jit(solution)/shard_map/pallas_call | solution.py:26
  47.7 0.2 collective-permute-start.8
  47.9 1.2 %collective-permute-done.8.b_ref = f32[264,128]{1,0:T(8,128)S(1)} collective-permute-done((f32[264,128]{1,0:T(8,128)S(1)}, f32[264,128]{1,0:T(8,128)S(1)}, u32[]{:S(2)}, u32[]{:S(2)}) %collective-permute-start.8) | collective-permute-done | bytes 135200 | tf_op jit(solution)/shard_map/ppermute | solution.py:38
  49.2 1.6 %collective-permute-start.9 = (f32[264,128]{1,0:T(8,128)S(1)}, f32[264,128]{1,0:T(8,128)S(1)}, u32[]{:S(2)}, u32[]{:S(2)}) collective-permute-start(f32[264,128]{1,0:T(8,128)S(1)} %shard_map.96.tie_ref.a_ref), channel_id=1, source_target_pairs={{0,2},{1,3},{2,0},{3,1},{4,6},{5,7},{6,4},{7,5},{8,10},{9,11},{10,... | collective-permute-start | bytes 405512 | tf_op jit(solution)/shard_map/ppermute | solution.py:38
  50.7 1.2 %shard_map.97.rest_0_.refs_5_ = f32[256,256]{1,0:T(8,128)S(1)} custom-call(f32[256,256]{1,0:T(8,128)S(1)} %get-tuple-element.30.w_ref, f32[256,256]{1,0:T(8,128)S(1)} %get-tuple-element.33.r_ref, f32[264,128]{1,0:T(8,128)S(1)} %shard_map.96.tie_ref.a_ref), custom_call_target="tpu_custom_call" | custom-call | tf_op jit(solution)/shard_map/pallas_call | solution.py:26
  52.0 2.9 %collective-permute-done.9.b_ref = f32[264,128]{1,0:T(8,128)S(1)} collective-permute-done((f32[264,128]{1,0:T(8,128)S(1)}, f32[264,128]{1,0:T(8,128)S(1)}, u32[]{:S(2)}, u32[]{:S(2)}) %collective-permute-start.9) | collective-permute-done | bytes 135200 | tf_op jit(solution)/shard_map/ppermute | solution.py:38
  54.9 1.6 %collective-permute-start.10 = (f32[264,128]{1,0:T(8,128)S(1)}, f32[264,128]{1,0:T(8,128)S(1)}, u32[]{:S(2)}, u32[]{:S(2)}) collective-permute-start(f32[264,128]{1,0:T(8,128)S(1)} %shard_map.98.a_ref), channel_id=1, source_target_pairs={{0,4},{1,5},{2,6},{3,7},{4,0},{5,1},{6,2},{7,3},{8,12},{9,13},{10,... | collective-permute-start | bytes 405512 | tf_op jit(solution)/shard_map/ppermute | solution.py:38
  56.4 3.5 %collective-permute-done.10.b_ref = f32[264,128]{1,0:T(8,128)S(1)} collective-permute-done((f32[264,128]{1,0:T(8,128)S(1)}, f32[264,128]{1,0:T(8,128)S(1)}, u32[]{:S(2)}, u32[]{:S(2)}) %collective-permute-start.10) | collective-permute-done | bytes 135200 | tf_op jit(solution)/shard_map/ppermute | solution.py:38
  60.0 2.7 %collective-permute-start.11 = (f32[264,128]{1,0:T(8,128)S(1)}, f32[264,128]{1,0:T(8,128)S(1)}, u32[]{:S(2)}, u32[]{:S(2)}) collective-permute-start(f32[264,128]{1,0:T(8,128)S(1)} %shard_map.99.a_ref), channel_id=1, source_target_pairs={{0,8},{1,9},{2,10},{3,11},{4,12},{5,13},{6,14},{7,15},{8,0},{9,1},... | collective-permute-start | bytes 405512 | tf_op jit(solution)/shard_map/ppermute | solution.py:38
  62.7 3.0 %collective-permute-done.11.b_ref = f32[264,128]{1,0:T(8,128)S(1)} collective-permute-done((f32[264,128]{1,0:T(8,128)S(1)}, f32[264,128]{1,0:T(8,128)S(1)}, u32[]{:S(2)}, u32[]{:S(2)}) %collective-permute-start.11) | collective-permute-done | bytes 135200 | tf_op jit(solution)/shard_map/ppermute | solution.py:38
  65.7 2.6 %collective-permute-start.12 = (f32[264,128]{1,0:T(8,128)S(1)}, f32[264,128]{1,0:T(8,128)S(1)}, u32[]{:S(2)}, u32[]{:S(2)}) collective-permute-start(f32[264,128]{1,0:T(8,128)S(1)} %shard_map.100.a_ref), channel_id=1, source_target_pairs={{0,16},{1,17},{2,18},{3,19},{4,20},{5,21},{6,22},{7,23},{8,24},{9,... | collective-permute-start | bytes 405512 | tf_op jit(solution)/shard_map/ppermute | solution.py:38
  68.3 3.4 %collective-permute-done.12.b_ref = f32[264,128]{1,0:T(8,128)S(1)} collective-permute-done((f32[264,128]{1,0:T(8,128)S(1)}, f32[264,128]{1,0:T(8,128)S(1)}, u32[]{:S(2)}, u32[]{:S(2)}) %collective-permute-start.12) | collective-permute-done | bytes 135200 | tf_op jit(solution)/shard_map/ppermute | solution.py:38
  71.7 0.1 collective-permute-start.13
  71.8 0.6 multiply_log_fusion
  72.3 0.8 collective-permute-done.13.refs_2_
  73.1 5.1 %shard_map.102 = (f32[3,256,256]{2,1,0:T(8,128)}, f32[3,256,256]{2,1,0:T(8,128)}, f32[256,256]{1,0:T(8,128)}, f32[256,256]{1,0:T(8,128)}) custom-call(s32[1]{0:T(128)} %bitcast.odd_ref.refs_0_, f32[264,128]{1,0:T(8,128)S(1)} %shard_map.101.refs_1_, f32[264,128]{1,0:T(8,128)S(1)} %collective-permute-done.13.refs_2_, ...), custom_call_target="tpu_custom_call" | custom-call | tf_op jit(solution)/shard_map/pallas_call | solution.py:26
  (15 shorter events, 0.2 us)
Async XLA Ops:
  0.6 1.1 %copy-start = (f32[3,256,256]{2,1,0:T(8,128)S(1)}, f32[3,256,256]{2,1,0:T(8,128)}, u32[]{:S(2)}) copy-start(f32[3,256,256]{2,1,0:T(8,128)} %s_ref.7) | copy-start | bytes 2359300
  1.8 6.0 %copy-start.5 = (s32[2,1024]{1,0:T(2,128)S(1)}, s32[2,1024]{1,0:T(2,128)}, u32[]{:S(2)}) copy-start(s32[2,1024]{1,0:T(2,128)} %param.5) | copy-start | bytes 24580
  2.8 5.2 %copy-start.6 = (f32[3,1024]{1,0:T(4,128)S(1)}, f32[3,1024]{1,0:T(4,128)}, u32[]{:S(2)}) copy-start(f32[3,1024]{1,0:T(4,128)} %param.6) | copy-start | bytes 36868
  2.8 6.0 %collective-permute-start = (f32[160,128]{1,0:T(8,128)S(1)}, f32[160,128]{1,0:T(8,128)S(1)}, u32[]{:S(2)}, u32[]{:S(2)}) collective-permute-start(f32[160,128]{1,0:T(8,128)S(1)} %get-tuple-element.24), channel_id=1, source_target_pairs={{0,1},{1,0},{2,3},{3,2},{4,5},{5,4},{6,7},{7,6},{8,9},{9,8},{10,11... | collective-permute-start | bytes 245768 | tf_op jit(solution)/shard_map/ppermute | solution.py:38
  3.3 16.3 %collective-permute-start.2 = (f32[3,128,256]{2,1,0:T(8,128)S(1)}, f32[3,128,256]{2,1,0:T(8,128)S(1)}, u32[]{:S(2)}, u32[]{:S(2)}) collective-permute-start(f32[3,128,256]{2,1,0:T(8,128)S(1)} %get-tuple-element.25), channel_id=1, source_target_pairs={{0,8},{8,16},{16,24},{1,9},{9,17},{17,25},{2,10},{10,18},{18,26},{... | collective-permute-start | bytes 1179656 | tf_op jit(solution)/shard_map/ppermute | solution.py:76
  7.8 0.7 copy-start.7
  8.8 1.7 %copy-start.1 = (f32[3,256,256]{2,1,0:T(8,128)S(1)}, f32[3,256,256]{2,1,0:T(8,128)}, u32[]{:S(2)}) copy-start(f32[3,256,256]{2,1,0:T(8,128)} %s_ref.7) | copy-start | bytes 2359300
  8.8 4.6 %collective-permute-start.1 = (f32[160,128]{1,0:T(8,128)S(1)}, f32[160,128]{1,0:T(8,128)S(1)}, u32[]{:S(2)}, u32[]{:S(2)}) collective-permute-start(f32[160,128]{1,0:T(8,128)S(1)} %shard_map.84.tie_ref.a_ref), channel_id=1, source_target_pairs={{0,2},{1,3},{2,0},{3,1},{4,6},{5,7},{6,4},{7,5},{8,10},{9,11},{10,... | collective-permute-start | bytes 245768 | tf_op jit(solution)/shard_map/ppermute | solution.py:38
  13.5 4.5 %collective-permute-start.3 = (f32[160,128]{1,0:T(8,128)S(1)}, f32[160,128]{1,0:T(8,128)S(1)}, u32[]{:S(2)}, u32[]{:S(2)}) collective-permute-start(f32[160,128]{1,0:T(8,128)S(1)} %shard_map.86.tie_ref.a_ref), channel_id=1, source_target_pairs={{0,4},{1,5},{2,6},{3,7},{4,0},{5,1},{6,2},{7,3},{8,12},{9,13},{10,... | collective-permute-start | bytes 245768 | tf_op jit(solution)/shard_map/ppermute | solution.py:38
  18.0 4.5 %collective-permute-start.4 = (f32[160,128]{1,0:T(8,128)S(1)}, f32[160,128]{1,0:T(8,128)S(1)}, u32[]{:S(2)}, u32[]{:S(2)}) collective-permute-start(f32[160,128]{1,0:T(8,128)S(1)} %shard_map.88.rest_0_.a_ref), channel_id=1, source_target_pairs={{0,8},{1,9},{2,10},{3,11},{4,12},{5,13},{6,14},{7,15},{8,0},{9,1},... | collective-permute-start | bytes 245768 | tf_op jit(solution)/shard_map/ppermute | solution.py:38
  22.5 5.4 %collective-permute-start.5 = (f32[160,128]{1,0:T(8,128)S(1)}, f32[160,128]{1,0:T(8,128)S(1)}, u32[]{:S(2)}, u32[]{:S(2)}) collective-permute-start(f32[160,128]{1,0:T(8,128)S(1)} %shard_map.90.rest_2_.a_ref), channel_id=1, source_target_pairs={{0,16},{1,17},{2,18},{3,19},{4,20},{5,21},{6,22},{7,23},{8,24},{9,... | collective-permute-start | bytes 245768 | tf_op jit(solution)/shard_map/ppermute | solution.py:38
  27.7 0.7 copy-start.2
  28.4 0.6 copy-start.3
  29.1 15.7 %collective-permute-start.6 = (f32[3,128,256]{2,1,0:T(8,128)}, f32[3,128,256]{2,1,0:T(8,128)S(1)}, u32[]{:S(2)}, u32[]{:S(2)}) collective-permute-start(f32[3,128,256]{2,1,0:T(8,128)} %shard_map.93), channel_id=1, source_target_pairs={{8,0},{16,8},{24,16},{9,1},{17,9},{25,17},{10,2},{18,10},{26,18},{... | collective-permute-start | bytes 1179656 | tf_op jit(solution)/shard_map/ppermute | solution.py:76
  30.5 1.6 %collective-permute-start.7 = (f32[160,128]{1,0:T(8,128)}, f32[160,128]{1,0:T(8,128)S(1)}, u32[]{:S(2)}, u32[]{:S(2)}) collective-permute-start(f32[160,128]{1,0:T(8,128)} %copy-done.3), channel_id=1, source_target_pairs={{0,1},{1,0},{2,3},{3,2},{4,5},{5,4},{6,7},{7,6},{8,9},{9,8},{10,11... | collective-permute-start | bytes 245768 | tf_op jit(solution)/shard_map/ppermute | solution.py:38
  32.1 0.9 %copy-start.4 = (f32[160,128]{1,0:T(8,128)S(1)}, f32[160,128]{1,0:T(8,128)}, u32[]{:S(2)}) copy-start(f32[160,128]{1,0:T(8,128)} %copy-done.3) | copy-start | bytes 245764
  47.7 1.4 %collective-permute-start.8 = (f32[264,128]{1,0:T(8,128)S(1)}, f32[264,128]{1,0:T(8,128)S(1)}, u32[]{:S(2)}, u32[]{:S(2)}) collective-permute-start(f32[264,128]{1,0:T(8,128)S(1)} %get-tuple-element.32), channel_id=1, source_target_pairs={{0,1},{1,0},{2,3},{3,2},{4,5},{5,4},{6,7},{7,6},{8,9},{9,8},{10,11... | collective-permute-start | bytes 405512 | tf_op jit(solution)/shard_map/ppermute | solution.py:38
  49.2 5.7 %collective-permute-start.9 = (f32[264,128]{1,0:T(8,128)S(1)}, f32[264,128]{1,0:T(8,128)S(1)}, u32[]{:S(2)}, u32[]{:S(2)}) collective-permute-start(f32[264,128]{1,0:T(8,128)S(1)} %shard_map.96.tie_ref.a_ref), channel_id=1, source_target_pairs={{0,2},{1,3},{2,0},{3,1},{4,6},{5,7},{6,4},{7,5},{8,10},{9,11},{10,... | collective-permute-start | bytes 405512 | tf_op jit(solution)/shard_map/ppermute | solution.py:38
  54.9 5.1 %collective-permute-start.10 = (f32[264,128]{1,0:T(8,128)S(1)}, f32[264,128]{1,0:T(8,128)S(1)}, u32[]{:S(2)}, u32[]{:S(2)}) collective-permute-start(f32[264,128]{1,0:T(8,128)S(1)} %shard_map.98.a_ref), channel_id=1, source_target_pairs={{0,4},{1,5},{2,6},{3,7},{4,0},{5,1},{6,2},{7,3},{8,12},{9,13},{10,... | collective-permute-start | bytes 405512 | tf_op jit(solution)/shard_map/ppermute | solution.py:38
  60.0 5.7 %collective-permute-start.11 = (f32[264,128]{1,0:T(8,128)S(1)}, f32[264,128]{1,0:T(8,128)S(1)}, u32[]{:S(2)}, u32[]{:S(2)}) collective-permute-start(f32[264,128]{1,0:T(8,128)S(1)} %shard_map.99.a_ref), channel_id=1, source_target_pairs={{0,8},{1,9},{2,10},{3,11},{4,12},{5,13},{6,14},{7,15},{8,0},{9,1},... | collective-permute-start | bytes 405512 | tf_op jit(solution)/shard_map/ppermute | solution.py:38
  65.7 6.0 %collective-permute-start.12 = (f32[264,128]{1,0:T(8,128)S(1)}, f32[264,128]{1,0:T(8,128)S(1)}, u32[]{:S(2)}, u32[]{:S(2)}) collective-permute-start(f32[264,128]{1,0:T(8,128)S(1)} %shard_map.100.a_ref), channel_id=1, source_target_pairs={{0,16},{1,17},{2,18},{3,19},{4,20},{5,21},{6,22},{7,23},{8,24},{9,... | collective-permute-start | bytes 405512 | tf_op jit(solution)/shard_map/ppermute | solution.py:38
  71.7 1.4 %collective-permute-start.13 = (f32[264,128]{1,0:T(8,128)S(1)}, f32[264,128]{1,0:T(8,128)S(1)}, u32[]{:S(2)}, u32[]{:S(2)}) collective-permute-start(f32[264,128]{1,0:T(8,128)S(1)} %shard_map.101.refs_1_), channel_id=1, source_target_pairs={{0,1},{1,0},{2,3},{3,2},{4,5},{5,4},{6,7},{7,6},{8,9},{9,8},{10,11... | collective-permute-start | bytes 405512 | tf_op jit(solution)/shard_map/ppermute | solution.py:38

commit v2 on v1

v2 whole, which is shorter than its diff:
```python
import functools
import math

import jax
import jax.numpy as jnp
from jax import lax
from jax.experimental import pallas as pl
from jax.experimental.pallas import tpu as pltpu
from jax.sharding import PartitionSpec as P

AXES = ("span", "xsec", "leaf")
SEC_NODES = 128
CHUNK = 256
highest = lax.Precision.HIGHEST
VMEM = pl.BlockSpec(memory_space=pltpu.VMEM)
ANY = pl.BlockSpec(memory_space=pl.ANY)
HBM = pl.BlockSpec(memory_space=pltpu.HBM)


def dot(a, b, ca=1, cb=0):
    return lax.dot_general(
        a, b, (((ca,), (cb,)), ((), ())), precision=highest, preferred_element_type=jnp.float32
    )


def halves(x):
    high = x.astype(jnp.bfloat16)
    return high, (x - high.astype(jnp.float32)).astype(jnp.bfloat16)


def dot3(a, b, ca=1, cb=0):
    def one(x, y):
        return lax.dot_general(x, y, (((ca,), (cb,)), ((), ())), preferred_element_type=jnp.float32)

    return one(a[0], b[0]) + (one(a[0], b[1]) + one(a[1], b[0]))


def call(kernel, shapes, operands, specs=None, scratch=()):
    return pl.pallas_call(
        kernel,
        out_shape=tuple(s if isinstance(s, jax.ShapeDtypeStruct) else jax.ShapeDtypeStruct(s, jnp.float32) for s in shapes),
        in_specs=specs or [VMEM] * len(operands),
        out_specs=tuple(VMEM for _ in shapes),
        scratch_shapes=list(scratch),
        compiler_params=pltpu.CompilerParams(vmem_limit_bytes=48 << 20),
    )(*operands)


def exchange(array, bit):
    count = math.prod(lax.axis_size(a) for a in AXES)
    return lax.ppermute(array, AXES, [(i, i ^ bit) for i in range(count)])


def add_kernel(terms, handed, *refs):
    outs = refs[len(refs) - 1 - handed :]
    parts = [ref[...] for ref in refs[:terms]]
    while len(parts) > 1:
        parts = [sum(parts[i : i + 2]) for i in range(0, len(parts), 2)]
    outs[0][...] = parts[0]
    for given, out in zip(refs[terms : terms + handed], outs[1:], strict=True):
        out[...] = given[...]


def add(parts, beside=(), through=()):
    operands = (*parts, *through, *beside)
    specs = [VMEM] * (len(parts) + len(through)) + [ANY] * len(beside)
    kernel = functools.partial(add_kernel, len(parts), len(through))
    outs = call(kernel, [parts[0].shape, *(t.shape for t in through)], operands, specs)
    return outs if through else outs[0]


def sum_steps():
    count = math.prod(lax.axis_size(a) for a in AXES)
    bits = [1 << i for i in range(1, count.bit_length() - 1)]
    assert 1 << (len(bits) + 1) == count and len(bits) > 1
    return [(bits[0], bits[1], bits[0] | bits[1])] + [(bit,) for bit in bits[2:]]


def scatter_kernel(keep_ref, received_ref, mine_ref, *send_refs):
    place = lax.axis_index(AXES) // 2 % 4
    for i, ref in enumerate((mine_ref, *send_refs)):
        part = place ^ i
        ref[...] = (keep_ref[pl.ds(part, 1)] + received_ref[pl.ds(part, 1)])[0]


def gather_kernel(mine_ref, *rest):
    out_ref = rest[-1]
    place = lax.axis_index(AXES) // 2 % 4
    for i, ref in enumerate((mine_ref, *rest[:-1])):
        out_ref[pl.ds(place ^ i, 1)] = ref[...][None]


def sum_by_quarters(keep, send, work):
    first, *others = sum_steps()
    block = keep.shape[1:]
    mine, *parts = call(scatter_kernel, [block] * 4, (keep, exchange(send, 1)), [VMEM, VMEM])
    received = [exchange(part, bit) for part, bit in zip(parts, first, strict=True)]
    done = work(mine)
    mine = add((mine, *received), done[:1])
    for (bit,) in others:
        mine = add((mine, exchange(mine, bit)))
    received = [exchange(mine, bit) for bit in first]
    (total,) = call(gather_kernel, [keep.shape], (mine, *received), [VMEM] * 4)
    return total, exchange(total, 1), done


def shifted(array, axis, by):
    length = lax.axis_size(axis)
    pairs = [(i, i + by) for i in range(length) if 0 <= i + by < length]
    return lax.ppermute(array, axis, pairs)


def order_halves(mine, other):
    odd = lax.axis_index(AXES) % 2
    return jnp.where(odd == 0, mine, other), jnp.where(odd == 0, other, mine)


def pack_one(gram):
    h, q = gram.shape[0] // 2, gram.shape[0] // 4
    g11, g12, g22 = gram[:h, :h], gram[:h, h:], gram[h:, h:]
    lane = lax.broadcasted_iota(jnp.int32, (q, h), 1)
    corner = jnp.where(lane < q, pltpu.roll(g11[q:], q, 1), g22[q:])
    return jnp.concatenate([g11[:q], g22[:q], corner, g12], axis=0)


def unpack_one(rows, h):
    q = h // 2
    lane = lax.broadcasted_iota(jnp.int32, (q, h), 1)
    corner = rows[2 * q : 3 * q]

    def block(top, low):
        square = jnp.concatenate([top, low], axis=0)
        flipped = square.T[q:]
        return jnp.concatenate([top, jnp.where(lane < q, flipped, low)], axis=0)

    g11 = block(rows[:q], pltpu.roll(corner, q, 1))
    g22 = block(rows[q : 2 * q], corner)
    return g11, rows[3 * q :], g22


def gram_kernel(s_ref, keep_ref, send_ref, top_ref):
    nodes, width = s_ref.shape[1:]
    flat = s_ref[...].reshape(-1, width)
    packed = pack_one(dot(flat, flat, 0, 0))
    half = packed.shape[0] // 2
    keep_ref[...], send_ref[...] = order_halves(packed[:half], packed[half:])
    top_ref[...] = s_ref[:, nodes - SEC_NODES :, :]


def pieces_of(x):
    first = x.astype(jnp.bfloat16)
    rest = x - first.astype(jnp.float32)
    second = rest.astype(jnp.bfloat16)
    third = (rest - second.astype(jnp.float32)).astype(jnp.bfloat16)
    return first, second, third


def picks(node_count, first, second):
    node = lax.broadcasted_iota(jnp.int32, (first.shape[0], node_count), 1).astype(jnp.float32)
    pick = (node == first).astype(jnp.float32) - (node == second).astype(jnp.float32)
    return pick.astype(jnp.bfloat16)


def picked(pick, pieces):
    return sum(jnp.dot(pick, piece, preferred_element_type=jnp.float32) for piece in pieces)


def own_elongation(first, table, s_ref, long_ref):
    nodes = s_ref.shape[1]
    pieces = [pieces_of(s_ref[c]) for c in range(3)]
    for start in range(0, long_ref.shape[0], CHUNK):
        rows = table[first + start : first + start + CHUNK, :]
        pick = picks(nodes, rows[:, 0:1], rows[:, 1:2])
        long_ref[start : start + CHUNK, :] = sum(rows[:, 2 + c : 3 + c] * picked(pick, pieces[c]) for c in range(3))


def first_elongation_kernel(ends_ref, dir_ref, stiff_ref, s_ref, tie_ref, long_ref, table_ref):
    del tie_ref
    ends = ends_ref[...].astype(jnp.float32)
    table_ref[...] = jnp.concatenate([ends, dir_ref[...], stiff_ref[...], jnp.zeros_like(ends)], axis=0).T
    own_elongation(0, table_ref, s_ref, long_ref)


def second_elongation_kernel(table_ref, s_ref, tie_ref, long_ref):
    del tie_ref
    own_elongation(long_ref.shape[0], table_ref, s_ref, long_ref)


def member_kernel(first, table_ref, ends_ref, long_ref, below_ref, *rest):
    own_ref, back_ref = rest[-2:]
    nodes = own_ref.shape[1]
    if len(rest) > 3:
        own_ref[...], back_ref[...] = rest[0][...], rest[1][...]
    else:
        own_ref[...], back_ref[...] = jnp.zeros_like(own_ref), jnp.zeros_like(back_ref)
    pieces = [pieces_of(below_ref[c]) for c in range(3)]
    for start in range(0, long_ref.shape[0], CHUNK):
        table = table_ref[first + start : first + start + CHUNK, :]
        pick = picks(SEC_NODES, table[:, 0:1] - nodes, table[:, 1:2] - nodes)
        elongation = long_ref[start : start + CHUNK, :]
        elongation += sum(table[:, 2 + c : 3 + c] * picked(pick, pieces[c]) for c in range(3))
        axial = elongation * table[:, 5:6]
        ends = ends_ref[:, first + start : first + start + CHUNK]
        node = lax.broadcasted_iota(jnp.int32, (nodes + SEC_NODES, CHUNK), 0)
        spread = (node == ends[0:1]).astype(jnp.float32) - (node == ends[1:2]).astype(jnp.float32)
        spread = spread.astype(jnp.bfloat16)
        for c in range(3):
            force = picked(spread, pieces_of(table[:, 2 + c : 3 + c] * axial))
            own_ref[c] += force[:nodes]
            back_ref[c] += force[nodes:]


def factor_block(x_ref, u_ref, m_ref, rows_ref):
    n = x_ref.shape[0]
    count = n // 8
    tiles = [x_ref[8 * i : 8 * i + 8, :] for i in range(count)]
    lane = lax.broadcasted_iota(jnp.int32, (8, n), 1)
    sub = lax.broadcasted_iota(jnp.int32, (8, n), 0)

    def column(tile, c):
        return jnp.broadcast_to(tile[:, c : c + 1], (8, n))

    for p in range(count):
        c0 = 8 * p
        rows_ref[c0 : c0 + 8, :] = tiles[p]
        u = [rows_ref[pl.ds(c0 + r, 8, stride=0), :] for r in range(8)]
        a = [[column(u[r], c0 + c) if c >= r else None for c in range(8)] for r in range(8)]
        panel = (lane >= c0) & (lane < c0 + 8)
        v = [jnp.where(panel, jnp.where(lane == c0 + k, 1.0, 0.0), u[k]) for k in range(8)]
        cols = {t: [column(tiles[t], c0 + k) for k in range(8)] for t in range(p + 1, count)}
        for t in cols:
            tiles[t] = jnp.where(panel, 0.0, tiles[t])
        for k in range(8):
            inverse = pltpu.reciprocal(a[k][k])
            scaled = v[k] * inverse
            for i in range(k + 1, 8):
                f = a[k][i] * inverse
                for j in range(i, 8):
                    a[i][j] = a[i][j] - f * a[k][j]
                v[i] = v[i] - f * v[k]
                u[i] = u[i] - f * u[k]
                for t in cols:
                    cols[t][i] = cols[t][i] - f * cols[t][k]
            for t in cols:
                tiles[t] = tiles[t] - cols[t][k] * scaled
        yt, ut = v[0], u[0]
        for i in range(1, 8):
            yt = jnp.where(sub == i, v[i], yt)
            ut = jnp.where(sub == i, u[i], ut)
        u_ref[c0 : c0 + 8, :] = ut
        m_ref[c0 : c0 + 8, :] = yt


def factor_and_inverse(g11, g12, g22, w_ref, r_ref, x, u, m, rows):
    h = g11.shape[0]
    rowi = lax.broadcasted_iota(jnp.int32, (h, h), 0)
    coli = lax.broadcasted_iota(jnp.int32, (h, h), 1)

    def finish():
        upper = u[...]
        d = jnp.sum(jnp.where(rowi == coli, upper, 0.0), axis=1, keepdims=True)
        s = lax.rsqrt(d)
        return jnp.where(rowi <= coli, upper, 0.0) * s, jnp.where(rowi >= coli, m[...], 0.0) * s

    x[...] = g11
    factor_block(x, u, m, rows)
    r11, m1 = finish()
    r12 = dot(m1, g12)
    x[...] = g22 - dot(r12, r12, 0, 0)
    factor_block(x, u, m, rows)
    r22, m2 = finish()
    zero = jnp.zeros((h, h), jnp.float32)
    r_ref[:h, :h], r_ref[:h, h:], r_ref[h:, :h], r_ref[h:, h:] = r11, r12, zero, r22
    w_ref[:h, :h], w_ref[h:, h:], w_ref[h:, :h] = m1.T, m2.T, zero
    w_ref[:h, h:] = -dot(m1, dot(r12, m2, 1, 1), 0, 0)


def first_factor_kernel(mine_ref, other_ref, w_ref, r_ref, diag_ref, *scratch):
    h = scratch[0].shape[0]
    lo, hi = order_halves(mine_ref[...], other_ref[...])
    g11, g12, g22 = unpack_one(jnp.concatenate([lo, hi], axis=0), h)
    eye = lax.broadcasted_iota(jnp.int32, (h, h), 0) == lax.broadcasted_iota(jnp.int32, (h, h), 1)
    diag_ref[:, :h] = jnp.sum(jnp.where(eye, g11, 0.0), axis=0, keepdims=True)
    diag_ref[:, h:] = jnp.sum(jnp.where(eye, g22, 0.0), axis=0, keepdims=True)
    factor_and_inverse(g11, g12, g22, w_ref, r_ref, *scratch)


def middle_kernel(
    s_ref, own_ref, back_ref, w_ref, q_ref, f_ref, q_halves, f_halves, keep_ref, send_ref
):
    parts, nodes, width = s_ref.shape
    h = width // 2
    w = w_ref[...]
    q = dot(s_ref[...].reshape(-1, width), w)
    q_ref[...] = q.reshape(parts, nodes, width)
    f_ref[...] = own_ref[...]
    f_ref[:, nodes - SEC_NODES :, :] += back_ref[...]
    f = dot(f_ref[...].reshape(-1, width), w)
    f_ref[...] = f.reshape(parts, nodes, width)
    q, f = halves(q), halves(f)
    for i in range(2):
        q_halves[i] = q[i].reshape(parts, nodes, width)
        f_halves[i] = f[i].reshape(parts, nodes, width)
    gram = dot3(q, q, 0, 0)
    energy = dot3(q, f, 0, 0)
    rowi = lax.broadcasted_iota(jnp.int32, (width, width), 0)
    coli = lax.broadcasted_iota(jnp.int32, (width, width), 1)
    both = jnp.where(rowi < coli, gram, energy)
    diag = jnp.sum(jnp.where(rowi == coli, gram, 0.0), axis=0, keepdims=True)
    quarter = width // 4
    keep, send = order_halves(both[:, :h], both[:, h:])
    keep_diag, send_diag = order_halves(diag[:, :h], diag[:, h:])
    for i in range(4):
        keep_ref[i, :quarter], send_ref[i, :quarter] = (x[quarter * i : quarter * (i + 1)] for x in (keep, send))
        keep_ref[i, quarter:], send_ref[i, quarter:] = (jnp.broadcast_to(x, (8, h)) for x in (keep_diag, send_diag))


def refine_kernel(rows_all, w_ref, r_ref, diag_ref, tie_ref, out_ref, log_ref):
    del tie_ref
    r = r_ref[...]
    size = r.shape[0]
    eye = lax.broadcasted_iota(jnp.int32, (size, size), 0) == lax.broadcasted_iota(jnp.int32, (size, size), 1)
    log_ref[...] = jnp.log(diag_ref[...] / rows_all)
    out_ref[...] = r + dot(jnp.where(eye, 1.0, 0.0) - dot(r, w_ref[...]), r)


def final_kernel(
    rows_all, mine_ref, other_ref, q_ref, f_ref, q_halves, f_halves, r1_ref,
    basis_ref, forces_ref, reduced_ref, coef_ref, v_ref, e_ref, w2, r2, held, sems, *scratch,
):
    parts, _, width = f_ref.shape
    h = width // 2
    root = math.sqrt(rows_all)
    lo, hi = order_halves(mine_ref[...], other_ref[...])
    quarter = width // 4
    both = jnp.concatenate([x[:, :quarter].reshape(width, h) for x in (lo, hi)], axis=1)
    diag = jnp.concatenate([x[0, quarter : quarter + 1] for x in (lo, hi)], axis=1)
    rowi = lax.broadcasted_iota(jnp.int32, (width, width), 0)
    coli = lax.broadcasted_iota(jnp.int32, (width, width), 1)
    flipped = both.T
    energy = jnp.where(rowi < coli, flipped, both)
    eye = jnp.where(rowi == coli, 1.0, 0.0)
    start = jnp.where(rowi < coli, both, jnp.where(rowi > coli, flipped, diag - 1.0))

    def upper_half(e):
        return jnp.where(rowi < coli, e, jnp.where(rowi == coli, 0.5 * e, 0.0))

    e_ref[...] = start
    size = jnp.sum(start * start)

    @pl.when(size < 0.01)
    def _():
        first = upper_half(start)
        low = first.astype(jnp.bfloat16)
        p = jnp.dot(start.astype(jnp.bfloat16), low, preferred_element_type=jnp.float32)
        e = lax.dot_general(
            low, (first + p).astype(jnp.bfloat16), (((0,), (0,)), ((), ())), preferred_element_type=jnp.float32
        )
        upper = upper_half(e - (p + p.T))
        both = jnp.dot(low, upper.astype(jnp.bfloat16), preferred_element_type=jnp.float32)
        v_ref[...] = both - (first + upper)

    @pl.when((size >= 0.01) & (size < 0.04))
    def _():
        v_ref[...] = -upper_half(start)

        def improve(i, carry):
            e = e_ref[...]
            upper = upper_half(e)
            split = halves(upper)
            p = dot3(halves(e), split)
            e = dot3(split, halves(upper + p), 0, 0) - (p + p.T)
            e_ref[...] = e
            upper = upper_half(e)
            v = v_ref[...]
            v_ref[...] = v - (upper + dot3(halves(v), halves(upper)))
            return carry

        lax.fori_loop(0, 2, improve, 0)

    @pl.when(jnp.logical_not(size < 0.04))
    def _():
        square = start + eye
        factor_and_inverse(square[:h, :h], square[:h, h:], square[h:, h:], w2, r2, *scratch)
        v_ref[...] = w2[...] - eye

    v = v_ref[...]
    v_split = halves(v)
    copies = []
    for i, (source, split, target) in enumerate(((q_ref, q_halves, basis_ref), (f_ref, f_halves, forces_ref))):
        for c in range(parts):
            k = parts * i + c
            held[k] = (source[c] + dot3((split[0, c], split[1, c]), v_split)) * root
            copies.append(pltpu.make_async_copy(held.at[k], target.at[c], sems.at[k]))
            copies[-1].start()
    right = energy + dot3(halves(energy), v_split)
    reduced_ref[...] = right + dot3(v_split, halves(right), 0, 0)
    change = jnp.where(rowi <= coli, v.T + start + dot3(v_split, halves(start), 0, 0), 0.0)
    r1 = r1_ref[...]
    coef_ref[...] = (r1 + dot3(halves(change), halves(r1))) * (1.0 / root)
    for copy in copies:
        copy.wait()


def local(snapshots, member_ends, member_dir, member_stiff):
    parts, nodes, width = snapshots.shape
    h = width // 2
    count = math.prod(lax.axis_size(a) for a in AXES)
    rows_all = parts * nodes * count
    steps = sum_steps()
    square = (width, width)
    field = (parts, nodes, width)
    level = (parts, SEC_NODES, width)
    packed = (5 * width // 8, h)
    scratch = [pltpu.VMEM((h, h), jnp.float32)] * 4

    keep, send, top = call(gram_kernel, [packed, packed, level], (snapshots,), [VMEM])
    below = shifted(top, "span", 1)
    members = member_dir.shape[1]
    split = members // 2
    forces = []

    def member_part(i, tie):
        operands = (table, member_ends, long[i], below, *forces, tie)
        kernel = functools.partial(member_kernel, split * i)
        forces[:] = call(kernel, [field, level], operands, [VMEM] * (len(operands) - 1) + [ANY])

    total = add((keep, exchange(send, 1)))
    for i, bits in enumerate(steps):
        received = [exchange(total, bit) for bit in bits]
        if i == 0:
            first, table = call(
                first_elongation_kernel,
                [(split, width), (members, 8)],
                (member_ends, member_dir, member_stiff[None], snapshots, total),
                [VMEM] * 4 + [ANY],
            )
            second = call(second_elongation_kernel, [(split, width)], (table, snapshots, total), [VMEM, VMEM, ANY])
            long = [first, *second]
            total = add((total, *received), long)
        elif i < len(steps) - 1:
            if i == 1:
                member_part(0, total)
            total = add((total, *received), forces)
        else:
            if i == 1:
                member_part(0, total)
            member_part(1, total)
            total, back = add((total, *received), forces[:1], forces[1:])
    other = exchange(total, 1)
    returned = shifted(back, "span", -1)

    w1, r1, diag = call(
        first_factor_kernel, [square, square, (1, width)], (total, other), [VMEM, VMEM], scratch
    )

    half = (4, width // 4 + 8, h)
    two = jax.ShapeDtypeStruct((2, *field), jnp.bfloat16)
    q, f, q_halves, f_halves, keep, send = call(
        middle_kernel,
        [field, field, two, two, half, half],
        (snapshots, forces[0], returned, w1),
        [VMEM] * 4,
    )
    refine = functools.partial(refine_kernel, rows_all)
    total, other, (r1, column_energy) = sum_by_quarters(
        keep,
        send,
        lambda tie: call(refine, [square, (1, width)], (w1, r1, diag, tie), [VMEM] * 3 + [ANY]),
    )

    basis, forces, reduced, coef = pl.pallas_call(
        functools.partial(final_kernel, rows_all),
        out_shape=tuple(jax.ShapeDtypeStruct(s, jnp.float32) for s in (field, field, square, square)),
        in_specs=[VMEM] * 7,
        out_specs=(HBM, HBM, VMEM, VMEM),
        scratch_shapes=[pltpu.VMEM(square, jnp.float32)] * 4
        + [pltpu.VMEM((2 * parts, nodes, width), jnp.float32), pltpu.SemaphoreType.DMA((2 * parts,))]
        + scratch,
        compiler_params=pltpu.CompilerParams(vmem_limit_bytes=48 << 20),
    )(total, other, q, f, q_halves, f_halves, r1)
    return (basis, forces, reduced, coef, column_energy[0])


def solution(mesh):
    placed = (
        P(None, AXES, None),
        P(None, AXES),
        P(None, AXES),
        P(AXES),
    )
    return jax.shard_map(
        local,
        mesh=mesh,
        in_specs=placed,
        out_specs=(P(None, AXES, None), P(None, AXES, None), P(), P(), P()),
        check_vma=False,
    )
```

time: 78.7 us -> 70.3 us (0.89)
  Pallas kernels: 28.9 us -> 23.6 us
  starting transfers between devices: 22.7 us -> 26.9 us
  waiting for transfers between devices: 21 us -> 17.5 us
  local copies, waits for them, and re-layouts: 4.06 us -> 1.14 us
    pallas_call x20 -> x18, Pallas kernels: 28.9 us -> 23.6 us  [the longest x17 20.1 us: call(): pl.pallas_call(kernel, out_shape=tuple((s if isinstance(s, jax.ShapeDtype...]
    ppermute x12 -> x17, waiting for transfers between devices: 21 us -> 17.2 us  [exchange(): return lax.ppermute(array, AXES, [(i, i ^ bit) for i in range(count)])]
    ppermute x12 -> x17, starting transfers between devices: 16.7 us -> 20.4 us  [exchange(): return lax.ppermute(array, AXES, [(i, i ^ bit) for i in range(count)])]
    unnamed x16 -> x10, local copies, waits for them, and re-layouts: 3.75 us -> 1.14 us
  transfers between devices with their start and end apart: 14 -> 19, of which waited for: 11 -> 16; matrix products, arithmetic and copies ran while one was open for 1% -> 0% of each run, Pallas kernels for 25% -> 24%
where the time goes in v2:
time: 70.3 us; the launch traced here: 70.1 us
  starting transfers between devices  26.9 us (38%)
  Pallas kernels  23.6 us (34%)
  waiting for transfers between devices  17.5 us (25%)
  local copies, waits for them, and re-layouts  1.14 us (2%)
  between operations  0.96 us (1%)
    ppermute x17, starting transfers between devices, exchange(): return lax.ppermute(array, AXES, [(i, i ^ bit) for i in range(count)])  20.4 us
    pallas_call x17, Pallas kernels, call(): pl.pallas_call(kernel, out_shape=tuple((s if isinstance(s, jax.ShapeDtype...  20.1 us
    ppermute x17, waiting for transfers between devices, exchange(): return lax.ppermute(array, AXES, [(i, i ^ bit) for i in range(count)])  17.2 us
    ppermute x2, starting transfers between devices, shifted(): return lax.ppermute(array, axis, pairs)  6.43 us
    pallas_call x1, Pallas kernels, local(): pl.pallas_call(functools.partial(final_kernel, rows_all), out_shape=tuple...  3.52 us
  transfers between devices with their start and end apart: 19, of which 16 were waited for; matrix products, arithmetic and copies ran while one was open for 0% of the time, Pallas kernels for 24%

profile of v2, /device:TPU:0, one launch (start us, length us, event | category | flops | bytes accessed | tf_op | source)
XLA Modules:
  0.0 70.1 jit_solution(16976322980345902527)
XLA Ops:
  0.6 0.0 copy-start
  0.6 1.1 %copy-done = f32[3,256,256]{2,1,0:T(8,128)S(1)} copy-done((f32[3,256,256]{2,1,0:T(8,128)S(1)}, f32[3,256,256]{2,1,0:T(8,128)}, u32[]{:S(2)}) %copy-start) | copy-done | bytes 786456
  1.8 0.0 copy-start.1
  1.8 0.9 %shard_map.83 = (f32[160,128]{1,0:T(8,128)S(1)}, f32[160,128]{1,0:T(8,128)S(1)}, f32[3,128,256]{2,1,0:T(8,128)S(1)}) custom-call(f32[3,256,256]{2,1,0:T(8,128)S(1)} %copy-done), custom_call_target="tpu_custom_call" | custom-call | tf_op jit(solution)/shard_map/pallas_call | solution.py:39
  2.7 5.0 %collective-permute-start.1 = (f32[3,128,256]{2,1,0:T(8,128)S(1)}, f32[3,128,256]{2,1,0:T(8,128)S(1)}, u32[]{:S(2)}, u32[]{:S(2)}) collective-permute-start(f32[3,128,256]{2,1,0:T(8,128)S(1)} %get-tuple-element.38), channel_id=1, source_target_pairs={{0,8},{8,16},{16,24},{1,9},{9,17},{17,25},{2,10},{10,18},{18,26},{... | collective-permute-start | bytes 1179656 | tf_op jit(solution)/shard_map/ppermute | solution.py:110
  7.7 0.1 collective-permute-start
  7.8 1.3 %collective-permute-done.refs_1_ = f32[160,128]{1,0:T(8,128)S(1)} collective-permute-done((f32[160,128]{1,0:T(8,128)S(1)}, f32[160,128]{1,0:T(8,128)S(1)}, u32[]{:S(2)}, u32[]{:S(2)}) %collective-permute-start) | collective-permute-done | bytes 81952 | tf_op jit(solution)/shard_map/ppermute | solution.py:51
  9.0 0.0 copy-start.2
  9.0 0.0 copy-start.3
  9.0 0.0 copy-start.4
  9.0 2.5 %collective-permute-start.4 = (f32[160,128]{1,0:T(8,128)S(1)}, f32[160,128]{1,0:T(8,128)S(1)}, u32[]{:S(2)}, u32[]{:S(2)}) collective-permute-start(f32[160,128]{1,0:T(8,128)S(1)} %shard_map.84.tie_ref.refs_0_), channel_id=1, source_target_pairs={{0,6},{1,7},{2,4},{3,5},{4,2},{5,3},{6,0},{7,1},{8,14},{9,15},{10,... | collective-permute-start | bytes 245768 | tf_op jit(solution)/shard_map/ppermute | solution.py:51
  11.5 0.5 collective-permute-start.3
  12.1 0.5 collective-permute-start.2
  12.6 0.0 copy-done.1
  12.6 0.0 copy-done.2
  12.6 0.0 copy-done.3
  12.6 0.0 copy-done.4
  12.6 1.2 %shard_map.85 = (f32[512,256]{1,0:T(8,128)S(1)}, f32[1024,8]{1,0:T(8,128)S(1)}) custom-call(s32[2,1024]{1,0:T(2,128)S(1)} %copy-done.2, f32[3,1024]{1,0:T(4,128)S(1)} %copy-done.3, f32[1,1024]{1,0:T(1,128)S(1)} %bitcast.2, f32[3,256,256]{2,1,0:T(8,128)S(1)} %copy-done.1, f32[160,128]{1,0:T(8,128)S(1)} %shard_map.84.tie_ref.refs_0_), custom_call_target="tpu_custom_call" | custom-call | tf_op jit(solution)/shard_map/pallas_call | solution.py:39
  13.8 0.9 %shard_map.86.refs_5_.long_ref = f32[512,256]{1,0:T(8,128)S(1)} custom-call(f32[1024,8]{1,0:T(8,128)S(1)} %get-tuple-element.37.table_ref, f32[3,256,256]{2,1,0:T(8,128)S(1)} %copy-done.1, f32[160,128]{1,0:T(8,128)S(1)} %shard_map.84.tie_ref.refs_0_), custom_call_target="tpu_custom_call" | custom-call | tf_op jit(solution)/shard_map/pallas_call | solution.py:39
  14.7 0.4 collective-permute-done.4.refs_3_
  15.1 1.3 %collective-permute-done.3.refs_2_ = f32[160,128]{1,0:T(8,128)S(1)} collective-permute-done((f32[160,128]{1,0:T(8,128)S(1)}, f32[160,128]{1,0:T(8,128)S(1)}, u32[]{:S(2)}, u32[]{:S(2)}) %collective-permute-start.3) | collective-permute-done | bytes 81952 | tf_op jit(solution)/shard_map/ppermute | solution.py:51
  16.3 0.2 collective-permute-done.2.refs_1_
  16.6 1.6 %collective-permute-start.5 = (f32[160,128]{1,0:T(8,128)S(1)}, f32[160,128]{1,0:T(8,128)S(1)}, u32[]{:S(2)}, u32[]{:S(2)}) collective-permute-start(f32[160,128]{1,0:T(8,128)S(1)} %shard_map.87.rest_0_.refs_0_), channel_id=1, source_target_pairs={{0,8},{1,9},{2,10},{3,11},{4,12},{5,13},{6,14},{7,15},{8,0},{9,1},... | collective-permute-start | bytes 245768 | tf_op jit(solution)/shard_map/ppermute | solution.py:51
  18.2 0.0 collective-permute-done.1.below_ref
  18.2 2.5 %shard_map.88 = (f32[3,256,256]{2,1,0:T(8,128)S(1)}, f32[3,128,256]{2,1,0:T(8,128)S(1)}) custom-call(f32[1024,8]{1,0:T(8,128)S(1)} %get-tuple-element.37.table_ref, s32[2,1024]{1,0:T(2,128)S(1)} %copy-done.2, f32[512,256]{1,0:T(8,128)S(1)} %get-tuple-element.39.refs_4_.long_ref, f32[3,128,256]{2,1,0:T(8,128)S(1)} %collective-permute-done.1.below_ref, ...), custom_call_target="tpu_custom_call" | custom-call | tf_op jit(solution)/shard_map/pallas_call | solution.py:39
  20.7 0.3 collective-permute-done.5.refs_1_
  21.1 2.6 %collective-permute-start.6 = (f32[160,128]{1,0:T(8,128)S(1)}, f32[160,128]{1,0:T(8,128)S(1)}, u32[]{:S(2)}, u32[]{:S(2)}) collective-permute-start(f32[160,128]{1,0:T(8,128)S(1)} %shard_map.89.rest_2_.refs_0_), channel_id=1, source_target_pairs={{0,16},{1,17},{2,18},{3,19},{4,20},{5,21},{6,22},{7,23},{8,24},{9,... | collective-permute-start | bytes 245768 | tf_op jit(solution)/shard_map/ppermute | solution.py:51
  23.7 2.5 %shard_map.90 = (f32[3,256,256]{2,1,0:T(8,128)S(1)}, f32[3,128,256]{2,1,0:T(8,128)S(1)}) custom-call(f32[1024,8]{1,0:T(8,128)S(1)} %get-tuple-element.37.table_ref, s32[2,1024]{1,0:T(2,128)S(1)} %copy-done.2, f32[512,256]{1,0:T(8,128)S(1)} %shard_map.86.refs_5_.long_ref, f32[3,128,256]{2,1,0:T(8,128)S(1)} %collective-permute-done.1.below_ref, ...), custom_call_target="tpu_custom_call" | custom-call | tf_op jit(solution)/shard_map/pallas_call | solution.py:39
  26.3 0.2 collective-permute-done.6.refs_1_
  26.5 1.5 %collective-permute-start.7 = (f32[3,128,256]{2,1,0:T(8,128)S(1)}, f32[3,128,256]{2,1,0:T(8,128)S(1)}, u32[]{:S(2)}, u32[]{:S(2)}) collective-permute-start(f32[3,128,256]{2,1,0:T(8,128)S(1)} %get-tuple-element.44), channel_id=1, source_target_pairs={{8,0},{16,8},{24,16},{9,1},{17,9},{25,17},{10,2},{18,10},{26,18},{... | collective-permute-start | bytes 1179656 | tf_op jit(solution)/shard_map/ppermute | solution.py:110
  28.0 0.1 collective-permute-start.8
  28.1 1.3 %collective-permute-done.8.other_ref = f32[160,128]{1,0:T(8,128)S(1)} collective-permute-done((f32[160,128]{1,0:T(8,128)S(1)}, f32[160,128]{1,0:T(8,128)S(1)}, u32[]{:S(2)}, u32[]{:S(2)}) %collective-permute-start.8) | collective-permute-done | bytes 81952 | tf_op jit(solution)/shard_map/ppermute | solution.py:51
  29.3 8.2 %shard_map.92 = (f32[256,256]{1,0:T(8,128)S(1)}, f32[256,256]{1,0:T(8,128)S(1)}, f32[1,256]{1,0:T(1,128)S(1)}) custom-call(f32[160,128]{1,0:T(8,128)S(1)} %get-tuple-element.45.mine_ref, f32[160,128]{1,0:T(8,128)S(1)} %collective-permute-done.8.other_ref), custom_call_target="tpu_custom_call" | custom-call | tf_op jit(solution)/shard_map/pallas_call | solution.py:39
  37.5 0.4 collective-permute-done.7.back_ref
  37.9 2.3 %shard_map.93 = (f32[3,256,256]{2,1,0:T(8,128)S(1)}, f32[3,256,256]{2,1,0:T(8,128)S(1)}, bf16[2,3,256,256]{3,2,1,0:T(8,128)(2,1)S(1)}, bf16[2,3,256,256]{3,2,1,0...) custom-call(f32[3,256,256]{2,1,0:T(8,128)S(1)} %copy-done.1, ...), custom_call_target="tpu_custom_call" | custom-call | tf_op jit(solution)/shard_map/pallas_call | solution.py:39
  40.2 0.1 collective-permute-start.9
  40.3 1.4 %collective-permute-done.9.received_ref = f32[4,72,128]{2,1,0:T(8,128)S(1)} collective-permute-done((f32[4,72,128]{2,1,0:T(8,128)S(1)}, f32[4,72,128]{2,1,0:T(8,128)S(1)}, u32[]{:S(2)}, u32[]{:S(2)}) %collective-permute-start.9) | collective-permute-done | bytes 147488 | tf_op jit(solution)/shard_map/ppermute | solution.py:51
  41.7 1.7 %collective-permute-start.10 = (f32[72,128]{1,0:T(8,128)S(1)}, f32[72,128]{1,0:T(8,128)S(1)}, u32[]{:S(2)}, u32[]{:S(2)}) collective-permute-start(f32[72,128]{1,0:T(8,128)S(1)} %get-tuple-element.50), channel_id=1, source_target_pairs={{0,2},{1,3},{2,0},{3,1},{4,6},{5,7},{6,4},{7,5},{8,10},{9,11},{10,... | collective-permute-start | bytes 110600 | tf_op jit(solution)/shard_map/ppermute | solution.py:51
  43.4 1.3 %collective-permute-start.11 = (f32[72,128]{1,0:T(8,128)S(1)}, f32[72,128]{1,0:T(8,128)S(1)}, u32[]{:S(2)}, u32[]{:S(2)}) collective-permute-start(f32[72,128]{1,0:T(8,128)S(1)} %get-tuple-element.51), channel_id=1, source_target_pairs={{0,4},{1,5},{2,6},{3,7},{4,0},{5,1},{6,2},{7,3},{8,12},{9,13},{10,... | collective-permute-start | bytes 110600 | tf_op jit(solution)/shard_map/ppermute | solution.py:51
  44.7 0.5 collective-permute-start.12
  45.2 1.4 %shard_map.95 = (f32[256,256]{1,0:T(8,128)S(1)}, f32[1,256]{1,0:T(1,128)}) custom-call(f32[256,256]{1,0:T(8,128)S(1)} %get-tuple-element.46.w_ref, f32[256,256]{1,0:T(8,128)S(1)} %get-tuple-element.53.r_ref, f32[1,256]{1,0:T(1,128)S(1)} %get-tuple-element.54.diag_ref, f32[72,128]{1,0:T(8,128)S(1)} %get-tuple-element.49.tie_ref.refs_0_), custom_call_target="tpu_custom_call" | custom-call | tf_op jit(solution)/shard_map/pallas_call | solution.py:39
  46.6 0.0 collective-permute-done.10.refs_1_
  46.6 0.9 %collective-permute-done.11.refs_2_ = f32[72,128]{1,0:T(8,128)S(1)} collective-permute-done((f32[72,128]{1,0:T(8,128)S(1)}, f32[72,128]{1,0:T(8,128)S(1)}, u32[]{:S(2)}, u32[]{:S(2)}) %collective-permute-start.11) | collective-permute-done | bytes 36896 | tf_op jit(solution)/shard_map/ppermute | solution.py:51
  47.5 2.0 %collective-permute-done.12.refs_3_ = f32[72,128]{1,0:T(8,128)S(1)} collective-permute-done((f32[72,128]{1,0:T(8,128)S(1)}, f32[72,128]{1,0:T(8,128)S(1)}, u32[]{:S(2)}, u32[]{:S(2)}) %collective-permute-start.12) | collective-permute-done | bytes 36896 | tf_op jit(solution)/shard_map/ppermute | solution.py:51
  49.6 2.1 %collective-permute-start.13 = (f32[72,128]{1,0:T(8,128)S(1)}, f32[72,128]{1,0:T(8,128)S(1)}, u32[]{:S(2)}, u32[]{:S(2)}) collective-permute-start(f32[72,128]{1,0:T(8,128)S(1)} %shard_map.96.refs_0_), channel_id=1, source_target_pairs={{0,8},{1,9},{2,10},{3,11},{4,12},{5,13},{6,14},{7,15},{8,0},{9,1},... | collective-permute-start | bytes 110600 | tf_op jit(solution)/shard_map/ppermute | solution.py:51
  51.7 1.9 %collective-permute-done.13.refs_1_ = f32[72,128]{1,0:T(8,128)S(1)} collective-permute-done((f32[72,128]{1,0:T(8,128)S(1)}, f32[72,128]{1,0:T(8,128)S(1)}, u32[]{:S(2)}, u32[]{:S(2)}) %collective-permute-start.13) | collective-permute-done | bytes 36896 | tf_op jit(solution)/shard_map/ppermute | solution.py:51
  53.6 3.2 %collective-permute-start.14 = (f32[72,128]{1,0:T(8,128)S(1)}, f32[72,128]{1,0:T(8,128)S(1)}, u32[]{:S(2)}, u32[]{:S(2)}) collective-permute-start(f32[72,128]{1,0:T(8,128)S(1)} %shard_map.97.refs_0_), channel_id=1, source_target_pairs={{0,16},{1,17},{2,18},{3,19},{4,20},{5,21},{6,22},{7,23},{8,24},{9,... | collective-permute-start | bytes 110600 | tf_op jit(solution)/shard_map/ppermute | solution.py:51
  56.9 1.9 %collective-permute-done.14.refs_1_ = f32[72,128]{1,0:T(8,128)S(1)} collective-permute-done((f32[72,128]{1,0:T(8,128)S(1)}, f32[72,128]{1,0:T(8,128)S(1)}, u32[]{:S(2)}, u32[]{:S(2)}) %collective-permute-start.14) | collective-permute-done | bytes 36896 | tf_op jit(solution)/shard_map/ppermute | solution.py:51
  58.8 0.7 %collective-permute-start.17 = (f32[72,128]{1,0:T(8,128)S(1)}, f32[72,128]{1,0:T(8,128)S(1)}, u32[]{:S(2)}, u32[]{:S(2)}) collective-permute-start(f32[72,128]{1,0:T(8,128)S(1)} %shard_map.98.mine_ref), channel_id=1, source_target_pairs={{0,6},{1,7},{2,4},{3,5},{4,2},{5,3},{6,0},{7,1},{8,14},{9,15},{10,... | collective-permute-start | bytes 110600 | tf_op jit(solution)/shard_map/ppermute | solution.py:51
  59.5 1.5 %collective-permute-start.16 = (f32[72,128]{1,0:T(8,128)S(1)}, f32[72,128]{1,0:T(8,128)S(1)}, u32[]{:S(2)}, u32[]{:S(2)}) collective-permute-start(f32[72,128]{1,0:T(8,128)S(1)} %shard_map.98.mine_ref), channel_id=1, source_target_pairs={{0,4},{1,5},{2,6},{3,7},{4,0},{5,1},{6,2},{7,3},{8,12},{9,13},{10,... | collective-permute-start | bytes 110600 | tf_op jit(solution)/shard_map/ppermute | solution.py:51
  61.0 1.3 %collective-permute-start.15 = (f32[72,128]{1,0:T(8,128)S(1)}, f32[72,128]{1,0:T(8,128)S(1)}, u32[]{:S(2)}, u32[]{:S(2)}) collective-permute-start(f32[72,128]{1,0:T(8,128)S(1)} %shard_map.98.mine_ref), channel_id=1, source_target_pairs={{0,2},{1,3},{2,0},{3,1},{4,6},{5,7},{6,4},{7,5},{8,10},{9,11},{10,... | collective-permute-start | bytes 110600 | tf_op jit(solution)/shard_map/ppermute | solution.py:51
  62.3 1.4 %collective-permute-done.17.rest_2_ = f32[72,128]{1,0:T(8,128)S(1)} collective-permute-done((f32[72,128]{1,0:T(8,128)S(1)}, f32[72,128]{1,0:T(8,128)S(1)}, u32[]{:S(2)}, u32[]{:S(2)}) %collective-permute-start.17) | collective-permute-done | bytes 36896 | tf_op jit(solution)/shard_map/ppermute | solution.py:51
  63.7 0.0 collective-permute-done.16.rest_1_
  63.7 1.3 %collective-permute-done.15.rest_0_ = f32[72,128]{1,0:T(8,128)S(1)} collective-permute-done((f32[72,128]{1,0:T(8,128)S(1)}, f32[72,128]{1,0:T(8,128)S(1)}, u32[]{:S(2)}, u32[]{:S(2)}) %collective-permute-start.15) | collective-permute-done | bytes 36896 | tf_op jit(solution)/shard_map/ppermute | solution.py:51
  65.0 0.1 collective-permute-start.18
  65.0 1.4 %collective-permute-done.18.other_ref = f32[4,72,128]{2,1,0:T(8,128)S(1)} collective-permute-done((f32[4,72,128]{2,1,0:T(8,128)S(1)}, f32[4,72,128]{2,1,0:T(8,128)S(1)}, u32[]{:S(2)}, u32[]{:S(2)}) %collective-permute-start.18) | collective-permute-done | bytes 147488 | tf_op jit(solution)/shard_map/ppermute | solution.py:51
  66.4 3.5 %shard_map.100 = (f32[3,256,256]{2,1,0:T(8,128)}, f32[3,256,256]{2,1,0:T(8,128)}, f32[256,256]{1,0:T(8,128)}, f32[256,256]{1,0:T(8,128)}) custom-call(f32[4,72,128]{2,1,0:T(8,128)S(1)} %shard_map.99.mine_ref, f32[4,72,128]{2,1,0:T(8,128)S(1)} %collective-permute-done.18.other_ref, f32[3,256,256]{2,1,0:T(8,128)S(1)} %get-tuple-element.56.q_ref, ...), custom_call_target="tpu_custom_call" | custom-call | tf_op jit(solution)/shard_map/pallas_call | solution.py:472
  (9 shorter events, 0.1 us)
Async XLA Ops:
  0.6 1.1 %copy-start = (f32[3,256,256]{2,1,0:T(8,128)S(1)}, f32[3,256,256]{2,1,0:T(8,128)}, u32[]{:S(2)}) copy-start(f32[3,256,256]{2,1,0:T(8,128)} %s_ref.7) | copy-start | bytes 2359300
  1.8 10.8 %copy-start.1 = (f32[3,256,256]{2,1,0:T(8,128)S(1)}, f32[3,256,256]{2,1,0:T(8,128)}, u32[]{:S(2)}) copy-start(f32[3,256,256]{2,1,0:T(8,128)} %s_ref.7) | copy-start | bytes 2359300
  2.7 15.5 %collective-permute-start.1 = (f32[3,128,256]{2,1,0:T(8,128)S(1)}, f32[3,128,256]{2,1,0:T(8,128)S(1)}, u32[]{:S(2)}, u32[]{:S(2)}) collective-permute-start(f32[3,128,256]{2,1,0:T(8,128)S(1)} %get-tuple-element.38), channel_id=1, source_target_pairs={{0,8},{8,16},{16,24},{1,9},{9,17},{17,25},{2,10},{10,18},{18,26},{... | collective-permute-start | bytes 1179656 | tf_op jit(solution)/shard_map/ppermute | solution.py:110
  7.7 1.3 %collective-permute-start = (f32[160,128]{1,0:T(8,128)S(1)}, f32[160,128]{1,0:T(8,128)S(1)}, u32[]{:S(2)}, u32[]{:S(2)}) collective-permute-start(f32[160,128]{1,0:T(8,128)S(1)} %get-tuple-element.36), channel_id=1, source_target_pairs={{0,1},{1,0},{2,3},{3,2},{4,5},{5,4},{6,7},{7,6},{8,9},{9,8},{10,11... | collective-permute-start | bytes 245768 | tf_op jit(solution)/shard_map/ppermute | solution.py:51
  9.0 3.6 %copy-start.2 = (s32[2,1024]{1,0:T(2,128)S(1)}, s32[2,1024]{1,0:T(2,128)}, u32[]{:S(2)}) copy-start(s32[2,1024]{1,0:T(2,128)} %ends_ref.5) | copy-start | bytes 24580
  9.0 3.6 %copy-start.3 = (f32[3,1024]{1,0:T(4,128)S(1)}, f32[3,1024]{1,0:T(4,128)}, u32[]{:S(2)}) copy-start(f32[3,1024]{1,0:T(4,128)} %dir_ref.1) | copy-start | bytes 36868
  9.0 3.6 %copy-start.4 = (f32[1024]{0:T(1024)S(1)}, f32[1024]{0:T(1024)}, u32[]{:S(2)}) copy-start(f32[1024]{0:T(1024)} %param.7) | copy-start | bytes 12292
  9.0 6.0 %collective-permute-start.4 = (f32[160,128]{1,0:T(8,128)S(1)}, f32[160,128]{1,0:T(8,128)S(1)}, u32[]{:S(2)}, u32[]{:S(2)}) collective-permute-start(f32[160,128]{1,0:T(8,128)S(1)} %shard_map.84.tie_ref.refs_0_), channel_id=1, source_target_pairs={{0,6},{1,7},{2,4},{3,5},{4,2},{5,3},{6,0},{7,1},{8,14},{9,15},{10,... | collective-permute-start | bytes 245768 | tf_op jit(solution)/shard_map/ppermute | solution.py:51
  11.5 4.8 %collective-permute-start.3 = (f32[160,128]{1,0:T(8,128)S(1)}, f32[160,128]{1,0:T(8,128)S(1)}, u32[]{:S(2)}, u32[]{:S(2)}) collective-permute-start(f32[160,128]{1,0:T(8,128)S(1)} %shard_map.84.tie_ref.refs_0_), channel_id=1, source_target_pairs={{0,4},{1,5},{2,6},{3,7},{4,0},{5,1},{6,2},{7,3},{8,12},{9,13},{10,... | collective-permute-start | bytes 245768 | tf_op jit(solution)/shard_map/ppermute | solution.py:51
  12.1 4.4 %collective-permute-start.2 = (f32[160,128]{1,0:T(8,128)S(1)}, f32[160,128]{1,0:T(8,128)S(1)}, u32[]{:S(2)}, u32[]{:S(2)}) collective-permute-start(f32[160,128]{1,0:T(8,128)S(1)} %shard_map.84.tie_ref.refs_0_), channel_id=1, source_target_pairs={{0,2},{1,3},{2,0},{3,1},{4,6},{5,7},{6,4},{7,5},{8,10},{9,11},{10,... | collective-permute-start | bytes 245768 | tf_op jit(solution)/shard_map/ppermute | solution.py:51
  16.6 4.5 %collective-permute-start.5 = (f32[160,128]{1,0:T(8,128)S(1)}, f32[160,128]{1,0:T(8,128)S(1)}, u32[]{:S(2)}, u32[]{:S(2)}) collective-permute-start(f32[160,128]{1,0:T(8,128)S(1)} %shard_map.87.rest_0_.refs_0_), channel_id=1, source_target_pairs={{0,8},{1,9},{2,10},{3,11},{4,12},{5,13},{6,14},{7,15},{8,0},{9,1},... | collective-permute-start | bytes 245768 | tf_op jit(solution)/shard_map/ppermute | solution.py:51
  21.1 5.4 %collective-permute-start.6 = (f32[160,128]{1,0:T(8,128)S(1)}, f32[160,128]{1,0:T(8,128)S(1)}, u32[]{:S(2)}, u32[]{:S(2)}) collective-permute-start(f32[160,128]{1,0:T(8,128)S(1)} %shard_map.89.rest_2_.refs_0_), channel_id=1, source_target_pairs={{0,16},{1,17},{2,18},{3,19},{4,20},{5,21},{6,22},{7,23},{8,24},{9,... | collective-permute-start | bytes 245768 | tf_op jit(solution)/shard_map/ppermute | solution.py:51
  26.5 11.4 %collective-permute-start.7 = (f32[3,128,256]{2,1,0:T(8,128)S(1)}, f32[3,128,256]{2,1,0:T(8,128)S(1)}, u32[]{:S(2)}, u32[]{:S(2)}) collective-permute-start(f32[3,128,256]{2,1,0:T(8,128)S(1)} %get-tuple-element.44), channel_id=1, source_target_pairs={{8,0},{16,8},{24,16},{9,1},{17,9},{25,17},{10,2},{18,10},{26,18},{... | collective-permute-start | bytes 1179656 | tf_op jit(solution)/shard_map/ppermute | solution.py:110
  28.0 1.3 %collective-permute-start.8 = (f32[160,128]{1,0:T(8,128)S(1)}, f32[160,128]{1,0:T(8,128)S(1)}, u32[]{:S(2)}, u32[]{:S(2)}) collective-permute-start(f32[160,128]{1,0:T(8,128)S(1)} %get-tuple-element.45.mine_ref), channel_id=1, source_target_pairs={{0,1},{1,0},{2,3},{3,2},{4,5},{5,4},{6,7},{7,6},{8,9},{9,8},{10,11... | collective-permute-start | bytes 245768 | tf_op jit(solution)/shard_map/ppermute | solution.py:51
  40.2 1.4 %collective-permute-start.9 = (f32[4,72,128]{2,1,0:T(8,128)S(1)}, f32[4,72,128]{2,1,0:T(8,128)S(1)}, u32[]{:S(2)}, u32[]{:S(2)}) collective-permute-start(f32[4,72,128]{2,1,0:T(8,128)S(1)} %get-tuple-element.48), channel_id=1, source_target_pairs={{0,1},{1,0},{2,3},{3,2},{4,5},{5,4},{6,7},{7,6},{8,9},{9,8},{10,11... | collective-permute-start | bytes 442376 | tf_op jit(solution)/shard_map/ppermute | solution.py:51
  41.7 5.0 %collective-permute-start.10 = (f32[72,128]{1,0:T(8,128)S(1)}, f32[72,128]{1,0:T(8,128)S(1)}, u32[]{:S(2)}, u32[]{:S(2)}) collective-permute-start(f32[72,128]{1,0:T(8,128)S(1)} %get-tuple-element.50), channel_id=1, source_target_pairs={{0,2},{1,3},{2,0},{3,1},{4,6},{5,7},{6,4},{7,5},{8,10},{9,11},{10,... | collective-permute-start | bytes 110600 | tf_op jit(solution)/shard_map/ppermute | solution.py:51
  43.4 4.1 %collective-permute-start.11 = (f32[72,128]{1,0:T(8,128)S(1)}, f32[72,128]{1,0:T(8,128)S(1)}, u32[]{:S(2)}, u32[]{:S(2)}) collective-permute-start(f32[72,128]{1,0:T(8,128)S(1)} %get-tuple-element.51), channel_id=1, source_target_pairs={{0,4},{1,5},{2,6},{3,7},{4,0},{5,1},{6,2},{7,3},{8,12},{9,13},{10,... | collective-permute-start | bytes 110600 | tf_op jit(solution)/shard_map/ppermute | solution.py:51
  44.7 4.9 %collective-permute-start.12 = (f32[72,128]{1,0:T(8,128)S(1)}, f32[72,128]{1,0:T(8,128)S(1)}, u32[]{:S(2)}, u32[]{:S(2)}) collective-permute-start(f32[72,128]{1,0:T(8,128)S(1)} %get-tuple-element.52), channel_id=1, source_target_pairs={{0,6},{1,7},{2,4},{3,5},{4,2},{5,3},{6,0},{7,1},{8,14},{9,15},{10,... | collective-permute-start | bytes 110600 | tf_op jit(solution)/shard_map/ppermute | solution.py:51
  49.6 4.0 %collective-permute-start.13 = (f32[72,128]{1,0:T(8,128)S(1)}, f32[72,128]{1,0:T(8,128)S(1)}, u32[]{:S(2)}, u32[]{:S(2)}) collective-permute-start(f32[72,128]{1,0:T(8,128)S(1)} %shard_map.96.refs_0_), channel_id=1, source_target_pairs={{0,8},{1,9},{2,10},{3,11},{4,12},{5,13},{6,14},{7,15},{8,0},{9,1},... | collective-permute-start | bytes 110600 | tf_op jit(solution)/shard_map/ppermute | solution.py:51
  53.6 5.2 %collective-permute-start.14 = (f32[72,128]{1,0:T(8,128)S(1)}, f32[72,128]{1,0:T(8,128)S(1)}, u32[]{:S(2)}, u32[]{:S(2)}) collective-permute-start(f32[72,128]{1,0:T(8,128)S(1)} %shard_map.97.refs_0_), channel_id=1, source_target_pairs={{0,16},{1,17},{2,18},{3,19},{4,20},{5,21},{6,22},{7,23},{8,24},{9,... | collective-permute-start | bytes 110600 | tf_op jit(solution)/shard_map/ppermute | solution.py:51
  58.8 4.9 %collective-permute-start.17 = (f32[72,128]{1,0:T(8,128)S(1)}, f32[72,128]{1,0:T(8,128)S(1)}, u32[]{:S(2)}, u32[]{:S(2)}) collective-permute-start(f32[72,128]{1,0:T(8,128)S(1)} %shard_map.98.mine_ref), channel_id=1, source_target_pairs={{0,6},{1,7},{2,4},{3,5},{4,2},{5,3},{6,0},{7,1},{8,14},{9,15},{10,... | collective-permute-start | bytes 110600 | tf_op jit(solution)/shard_map/ppermute | solution.py:51
  59.5 4.1 %collective-permute-start.16 = (f32[72,128]{1,0:T(8,128)S(1)}, f32[72,128]{1,0:T(8,128)S(1)}, u32[]{:S(2)}, u32[]{:S(2)}) collective-permute-start(f32[72,128]{1,0:T(8,128)S(1)} %shard_map.98.mine_ref), channel_id=1, source_target_pairs={{0,4},{1,5},{2,6},{3,7},{4,0},{5,1},{6,2},{7,3},{8,12},{9,13},{10,... | collective-permute-start | bytes 110600 | tf_op jit(solution)/shard_map/ppermute | solution.py:51
  61.0 4.0 %collective-permute-start.15 = (f32[72,128]{1,0:T(8,128)S(1)}, f32[72,128]{1,0:T(8,128)S(1)}, u32[]{:S(2)}, u32[]{:S(2)}) collective-permute-start(f32[72,128]{1,0:T(8,128)S(1)} %shard_map.98.mine_ref), channel_id=1, source_target_pairs={{0,2},{1,3},{2,0},{3,1},{4,6},{5,7},{6,4},{7,5},{8,10},{9,11},{10,... | collective-permute-start | bytes 110600 | tf_op jit(solution)/shard_map/ppermute | solution.py:51
  65.0 1.4 %collective-permute-start.18 = (f32[4,72,128]{2,1,0:T(8,128)S(1)}, f32[4,72,128]{2,1,0:T(8,128)S(1)}, u32[]{:S(2)}, u32[]{:S(2)}) collective-permute-start(f32[4,72,128]{2,1,0:T(8,128)S(1)} %shard_map.99.mine_ref), channel_id=1, source_target_pairs={{0,1},{1,0},{2,3},{3,2},{4,5},{5,4},{6,7},{7,6},{8,9},{9,8},{10,11... | collective-permute-start | bytes 442376 | tf_op jit(solution)/shard_map/ppermute | solution.py:51

commit v3 on v2

--- a/solution.py
+++ b/solution.py
@@ -10,6 +10,7 @@
 
 AXES = ("span", "xsec", "leaf")
 SEC_NODES = 128
+NODES = 256
 CHUNK = 256
 highest = lax.Precision.HIGHEST
 VMEM = pl.BlockSpec(memory_space=pltpu.VMEM)
@@ -76,7 +77,8 @@
     return [(bits[0], bits[1], bits[0] | bits[1])] + [(bit,) for bit in bits[2:]]
 
 
-def scatter_kernel(keep_ref, received_ref, mine_ref, *send_refs):
+def scatter_kernel(keep_ref, received_ref, tie_ref, mine_ref, *send_refs):
+    del tie_ref
     place = lax.axis_index(AXES) // 2 % 4
     for i, ref in enumerate((mine_ref, *send_refs)):
         part = place ^ i
@@ -90,23 +92,32 @@
         out_ref[pl.ds(place ^ i, 1)] = ref[...][None]
 
 
-def sum_by_quarters(keep, send, work):
+def sum_by_quarters(keep, send, works):
     first, *others = sum_steps()
+    others = [bit for (bit,) in others]
+    others = [(*pair, sum(pair))[: 2 * len(pair) - 1] for pair in (others[i : i + 2] for i in range(0, len(others), 2))]
     block = keep.shape[1:]
-    mine, *parts = call(scatter_kernel, [block] * 4, (keep, exchange(send, 1)), [VMEM, VMEM])
+    received = exchange(send, 1)
+    tie = works[0](keep)
+    mine, *parts = call(scatter_kernel, [block] * 4, (keep, received, tie), [VMEM, VMEM, ANY])
     received = [exchange(part, bit) for part, bit in zip(parts, first, strict=True)]
-    done = work(mine)
-    mine = add((mine, *received), done[:1])
-    for (bit,) in others:
-        mine = add((mine, exchange(mine, bit)))
+    handed = works[1](mine)
+    mine = add((mine, *received), (handed,))
+    for i, bits in enumerate(others):
+        received = [exchange(mine, bit) for bit in bits]
+        tie = works[2](mine) if i == 0 else ()
+        if i < len(others) - 1:
+            mine = add((mine, *received), tie)
+        else:
+            mine, handed = add((mine, *received), tie, (handed,))
     received = [exchange(mine, bit) for bit in first]
-    (total,) = call(gather_kernel, [keep.shape], (mine, *received), [VMEM] * 4)
-    return total, exchange(total, 1), done
-
-
-def shifted(array, axis, by):
+    (total,) = call(gather_kernel, [keep.shape], (mine, *received))
+    return total, exchange(total, 1), handed
+
+
+def shifted(array, axis, by, round_off=False):
     length = lax.axis_size(axis)
-    pairs = [(i, i + by) for i in range(length) if 0 <= i + by < length]
+    pairs = [(i, (i + by) % length) for i in range(length) if round_off or 0 <= i + by < length]
     return lax.ppermute(array, axis, pairs)
 
 
@@ -186,28 +197,41 @@
     own_elongation(long_ref.shape[0], table_ref, s_ref, long_ref)
 
 
-def member_kernel(first, table_ref, ends_ref, long_ref, below_ref, *rest):
+def below_elongation_kernel(table_ref, below_ref, first_ref, second_ref, tie_ref, long_ref):
+    del tie_ref
+    stands = lax.axis_index("span") == 0
+    pieces = [pieces_of(jnp.where(stands, 0.0, below_ref[c])) for c in range(3)]
+    split = first_ref.shape[0]
+    for half, given in enumerate((first_ref, second_ref)):
+        for start in range(0, split, CHUNK):
+            at = split * half + start
+            rows = table_ref[at : at + CHUNK, :]
+            pick = picks(SEC_NODES, rows[:, 0:1] - NODES, rows[:, 1:2] - NODES)
+            added = sum(rows[:, 2 + c : 3 + c] * picked(pick, pieces[c]) for c in range(3))
+            long_ref[at : at + CHUNK, :] = given[start : start + CHUNK, :] + added
+
+
+def force_kernel(first, count, table_ref, ends_ref, long_ref, tie_ref, *rest):
+    del tie_ref
     own_ref, back_ref = rest[-2:]
     nodes = own_ref.shape[1]
-    if len(rest) > 3:
-        own_ref[...], back_ref[...] = rest[0][...], rest[1][...]
-    else:
-        own_ref[...], back_ref[...] = jnp.zeros_like(own_ref), jnp.zeros_like(back_ref)
-    pieces = [pieces_of(below_ref[c]) for c in range(3)]
-    for start in range(0, long_ref.shape[0], CHUNK):
-        table = table_ref[first + start : first + start + CHUNK, :]
-        pick = picks(SEC_NODES, table[:, 0:1] - nodes, table[:, 1:2] - nodes)
-        elongation = long_ref[start : start + CHUNK, :]
-        elongation += sum(table[:, 2 + c : 3 + c] * picked(pick, pieces[c]) for c in range(3))
-        axial = elongation * table[:, 5:6]
-        ends = ends_ref[:, first + start : first + start + CHUNK]
+    for start in range(first, first + count, CHUNK):
+        rows = table_ref[start : start + CHUNK, :]
+        axial = long_ref[start : start + CHUNK, :] * rows[:, 5:6]
+        ends = ends_ref[:, start : start + CHUNK]
         node = lax.broadcasted_iota(jnp.int32, (nodes + SEC_NODES, CHUNK), 0)
         spread = (node == ends[0:1]).astype(jnp.float32) - (node == ends[1:2]).astype(jnp.float32)
         spread = spread.astype(jnp.bfloat16)
         for c in range(3):
-            force = picked(spread, pieces_of(table[:, 2 + c : 3 + c] * axial))
-            own_ref[c] += force[:nodes]
-            back_ref[c] += force[nodes:]
+            force = picked(spread, halves(rows[:, 2 + c : 3 + c] * axial))
+            if start > first:
+                given = own_ref[c], back_ref[c]
+            elif len(rest) > 2:
+                given = rest[0][c], rest[1][c]
+            else:
+                given = 0.0, 0.0
+            own_ref[c] = given[0] + force[:nodes]
+            back_ref[c] = given[1] + force[nodes:]
 
 
 def factor_block(x_ref, u_ref, m_ref, rows_ref):
@@ -285,24 +309,19 @@
     factor_and_inverse(g11, g12, g22, w_ref, r_ref, *scratch)
 
 
-def middle_kernel(
-    s_ref, own_ref, back_ref, w_ref, q_ref, f_ref, q_halves, f_halves, keep_ref, send_ref
-):
+def middle_kernel(s_ref, long_ref, table_ref, w_ref, q_ref, q_halves, long_out, keep_ref, send_ref):
     parts, nodes, width = s_ref.shape
     h = width // 2
     w = w_ref[...]
     q = dot(s_ref[...].reshape(-1, width), w)
     q_ref[...] = q.reshape(parts, nodes, width)
-    f_ref[...] = own_ref[...]
-    f_ref[:, nodes - SEC_NODES :, :] += back_ref[...]
-    f = dot(f_ref[...].reshape(-1, width), w)
-    f_ref[...] = f.reshape(parts, nodes, width)
-    q, f = halves(q), halves(f)
+    long = dot(long_ref[...], w)
+    long_out[...] = long
+    q = halves(q)
     for i in range(2):
         q_halves[i] = q[i].reshape(parts, nodes, width)
-        f_halves[i] = f[i].reshape(parts, nodes, width)
     gram = dot3(q, q, 0, 0)
-    energy = dot3(q, f, 0, 0)
+    energy = dot3(halves(long), halves(long * table_ref[:, 5:6]), 0, 0)
     rowi = lax.broadcasted_iota(jnp.int32, (width, width), 0)
     coli = lax.broadcasted_iota(jnp.int32, (width, width), 1)
     both = jnp.where(rowi < coli, gram, energy)
@@ -325,10 +344,10 @@
 
 
 def final_kernel(
-    rows_all, mine_ref, other_ref, q_ref, f_ref, q_halves, f_halves, r1_ref,
+    rows_all, mine_ref, other_ref, q_ref, q_halves, own_ref, back_ref, r1_ref,
     basis_ref, forces_ref, reduced_ref, coef_ref, v_ref, e_ref, w2, r2, held, sems, *scratch,
 ):
-    parts, _, width = f_ref.shape
+    parts, nodes, width = q_ref.shape
     h = width // 2
     root = math.sqrt(rows_all)
     lo, hi = order_halves(mine_ref[...], other_ref[...])
@@ -348,7 +367,7 @@
     e_ref[...] = start
     size = jnp.sum(start * start)
 
-    @pl.when(size < 0.01)
+    @pl.when(size < 0.02)
     def _():
         first = upper_half(start)
         low = first.astype(jnp.bfloat16)
@@ -360,7 +379,7 @@
         both = jnp.dot(low, upper.astype(jnp.bfloat16), preferred_element_type=jnp.float32)
         v_ref[...] = both - (first + upper)
 
-    @pl.when((size >= 0.01) & (size < 0.04))
+    @pl.when((size >= 0.02) & (size < 0.06))
     def _():
         v_ref[...] = -upper_half(start)
 
@@ -378,7 +397,7 @@
 
         lax.fori_loop(0, 2, improve, 0)
 
-    @pl.when(jnp.logical_not(size < 0.04))
+    @pl.when(jnp.logical_not(size < 0.06))
     def _():
         square = start + eye
         factor_and_inverse(square[:h, :h], square[:h, h:], square[h:, h:], w2, r2, *scratch)
@@ -387,12 +406,20 @@
     v = v_ref[...]
     v_split = halves(v)
     copies = []
-    for i, (source, split, target) in enumerate(((q_ref, q_halves, basis_ref), (f_ref, f_halves, forces_ref))):
-        for c in range(parts):
-            k = parts * i + c
-            held[k] = (source[c] + dot3((split[0, c], split[1, c]), v_split)) * root
-            copies.append(pltpu.make_async_copy(held.at[k], target.at[c], sems.at[k]))
-            copies[-1].start()
+    top = lax.axis_index("span") == lax.axis_size("span") - 1
+    for k in range(2 * parts):
+        c = k % parts
+        if k < parts:
+            source, split, target = q_ref[c], (q_halves[0, c], q_halves[1, c]), basis_ref
+        else:
+            returned = jnp.where(top, 0.0, back_ref[c])
+            source = jnp.concatenate(
+                [own_ref[c, : nodes - SEC_NODES], own_ref[c, nodes - SEC_NODES :] + returned], axis=0
+            )
+            split, target = halves(source), forces_ref
+        held[k] = (source + dot3(split, v_split)) * root
+        copies.append(pltpu.make_async_copy(held.at[k], target.at[c], sems.at[k]))
+        copies[-1].start()
     right = energy + dot3(halves(energy), v_split)
     reduced_ref[...] = right + dot3(v_split, halves(right), 0, 0)
     change = jnp.where(rowi <= coli, v.T + start + dot3(v_split, halves(start), 0, 0), 0.0)
@@ -415,16 +442,9 @@
     scratch = [pltpu.VMEM((h, h), jnp.float32)] * 4
 
     keep, send, top = call(gram_kernel, [packed, packed, level], (snapshots,), [VMEM])
-    below = shifted(top, "span", 1)
+    below = shifted(top, "span", 1, True)
     members = member_dir.shape[1]
     split = members // 2
-    forces = []
-
-    def member_part(i, tie):
-        operands = (table, member_ends, long[i], below, *forces, tie)
-        kernel = functools.partial(member_kernel, split * i)
-        forces[:] = call(kernel, [field, level], operands, [VMEM] * (len(operands) - 1) + [ANY])
-
     total = add((keep, exchange(send, 1)))
     for i, bits in enumerate(steps):
         received = [exchange(total, bit) for bit in bits]
@@ -439,35 +459,42 @@
             long = [first, *second]
             total = add((total, *received), long)
         elif i < len(steps) - 1:
-            if i == 1:
-                member_part(0, total)
-            total = add((total, *received), forces)
+            total = add((total, *received))
         else:
-            if i == 1:
-                member_part(0, total)
-            member_part(1, total)
-            total, back = add((total, *received), forces[:1], forces[1:])
+            operands = (table, below, *long, total)
+            (stretch,) = call(below_elongation_kernel, [(members, width)], operands, [VMEM] * 4 + [ANY])
+            total = add((total, *received), (stretch,))
     other = exchange(total, 1)
-    returned = shifted(back, "span", -1)
 
     w1, r1, diag = call(
         first_factor_kernel, [square, square, (1, width)], (total, other), [VMEM, VMEM], scratch
     )
 
     half = (4, width // 4 + 8, h)
-    two = jax.ShapeDtypeStruct((2, *field), jnp.bfloat16)
-    q, f, q_halves, f_halves, keep, send = call(
+    q, q_halves, stretch, keep, send = call(
         middle_kernel,
-        [field, field, two, two, half, half],
-        (snapshots, forces[0], returned, w1),
-        [VMEM] * 4,
+        [field, jax.ShapeDtypeStruct((2, *field), jnp.bfloat16), (members, width), half, half],
+        (snapshots, stretch, table, w1),
     )
-    refine = functools.partial(refine_kernel, rows_all)
-    total, other, (r1, column_energy) = sum_by_quarters(
-        keep,
-        send,
-        lambda tie: call(refine, [square, (1, width)], (w1, r1, diag, tie), [VMEM] * 3 + [ANY]),
-    )
+    held = []
+
+    def members_forces(tie):
+        operands = (table, member_ends, stretch, tie, *held)
+        first = split if held else 0
+        kernel = functools.partial(force_kernel, first, split)
+        held[:] = call(kernel, [field, level], operands, [VMEM] * 3 + [ANY] + [VMEM] * len(held))
+        return held[1]
+
+    def refined(tie):
+        refine = functools.partial(refine_kernel, rows_all)
+        r1_and_log.extend(call(refine, [square, (1, width)], (w1, r1, diag, tie), [VMEM] * 3 + [ANY]))
+        return r1_and_log[:1]
+
+    r1_and_log = []
+    total, other, back = sum_by_quarters(keep, send, [members_forces, members_forces, refined])
+    own = held[0]
+    returned = shifted(back, "span", -1)
+    r1, column_energy = r1_and_log
 
     basis, forces, reduced, coef = pl.pallas_call(
         functools.partial(final_kernel, rows_all),
@@ -478,7 +505,7 @@
         + [pltpu.VMEM((2 * parts, nodes, width), jnp.float32), pltpu.SemaphoreType.DMA((2 * parts,))]
         + scratch,
         compiler_params=pltpu.CompilerParams(vmem_limit_bytes=48 << 20),
-    )(total, other, q, f, q_halves, f_halves, r1)
+    )(total, other, q, q_halves, own, returned, r1)
     return (basis, forces, reduced, coef, column_energy[0])
 
 

time: 70.3 us -> 67 us (0.953)
  starting transfers between devices: 26.9 us -> 24.1 us
  Pallas kernels: 23.6 us -> 22.4 us
    ppermute x2, starting transfers between devices: 6.43 us -> 4.37 us  [shifted(): return lax.ppermute(array, axis, pairs)]
    pallas_call x17, Pallas kernels: 20.1 us -> 19.1 us  [call(): pl.pallas_call(kernel, out_shape=tuple((s if isinstance(s, jax.ShapeDtype...]
    ppermute x17 -> x18, starting transfers between devices: 20.4 us -> 19.8 us  [exchange(): return lax.ppermute(array, AXES, [(i, i ^ bit) for i in range(count)])]
    ppermute x17 -> x18, waiting for transfers between devices: 17.2 us -> 17.5 us  [exchange(): return lax.ppermute(array, AXES, [(i, i ^ bit) for i in range(count)])]
  transfers between devices with their start and end apart: 19 -> 20, of which waited for: 16 -> 17; matrix products, arithmetic and copies ran while one was open for 0% -> 0% of each run, Pallas kernels for 24% -> 10%
where the time goes in v3:
time: 67 us; the launch traced here: 66.8 us
  starting transfers between devices  24.1 us (36%)
  Pallas kernels  22.4 us (33%)
  waiting for transfers between devices  18.2 us (27%)
  local copies, waits for them, and re-layouts  1.14 us (2%)
  between operations  0.94 us (1%)
    ppermute x18, starting transfers between devices, exchange(): return lax.ppermute(array, AXES, [(i, i ^ bit) for i in range(count)])  19.8 us
    pallas_call x17, Pallas kernels, call(): pl.pallas_call(kernel, out_shape=tuple((s if isinstance(s, jax.ShapeDtype...  19.1 us
    ppermute x18, waiting for transfers between devices, exchange(): return lax.ppermute(array, AXES, [(i, i ^ bit) for i in range(count)])  17.5 us
    ppermute x2, starting transfers between devices, shifted(): return lax.ppermute(array, axis, pairs)  4.37 us
    pallas_call x1, Pallas kernels, local(): pl.pallas_call(functools.partial(final_kernel, rows_all), out_shape=tuple...  3.31 us
  transfers between devices with their start and end apart: 20, of which 17 were waited for; matrix products, arithmetic and copies ran while one was open for 0% of the time, Pallas kernels for 10%

profile of v3, /device:TPU:0, one launch (start us, length us, event | category | flops | bytes accessed | tf_op | source)
XLA Modules:
  0.0 66.8 jit_solution(16916887194711431601)
XLA Ops:
  0.6 0.0 copy-start
  0.6 1.1 %copy-done = f32[3,256,256]{2,1,0:T(8,128)S(1)} copy-done((f32[3,256,256]{2,1,0:T(8,128)S(1)}, f32[3,256,256]{2,1,0:T(8,128)}, u32[]{:S(2)}) %copy-start) | copy-done | bytes 786456
  1.8 0.0 copy-start.1
  1.8 0.9 %shard_map.83 = (f32[160,128]{1,0:T(8,128)S(1)}, f32[160,128]{1,0:T(8,128)S(1)}, f32[3,128,256]{2,1,0:T(8,128)S(1)}) custom-call(f32[3,256,256]{2,1,0:T(8,128)S(1)} %copy-done), custom_call_target="tpu_custom_call" | custom-call | tf_op jit(solution)/shard_map/pallas_call | solution.py:40
  2.7 3.1 %collective-permute-start.1 = (f32[3,128,256]{2,1,0:T(8,128)S(1)}, f32[3,128,256]{2,1,0:T(8,128)S(1)}, u32[]{:S(2)}, u32[]{:S(2)}) collective-permute-start(f32[3,128,256]{2,1,0:T(8,128)S(1)} %get-tuple-element.37), channel_id=1, source_target_pairs={{0,8},{8,16},{16,24},{24,0},{1,9},{9,17},{17,25},{25,1},{2,10},{10... | collective-permute-start | bytes 1179656 | tf_op jit(solution)/shard_map/ppermute | solution.py:121
  5.8 0.0 collective-permute-start
  5.8 1.3 %collective-permute-done.refs_1_ = f32[160,128]{1,0:T(8,128)S(1)} collective-permute-done((f32[160,128]{1,0:T(8,128)S(1)}, f32[160,128]{1,0:T(8,128)S(1)}, u32[]{:S(2)}, u32[]{:S(2)}) %collective-permute-start) | collective-permute-done | bytes 81952 | tf_op jit(solution)/shard_map/ppermute | solution.py:52
  7.1 0.0 copy-start.2
  7.1 0.0 copy-start.3
  7.1 0.0 copy-start.4
  7.1 2.5 %collective-permute-start.4 = (f32[160,128]{1,0:T(8,128)S(1)}, f32[160,128]{1,0:T(8,128)S(1)}, u32[]{:S(2)}, u32[]{:S(2)}) collective-permute-start(f32[160,128]{1,0:T(8,128)S(1)} %shard_map.84.tie_ref.refs_0_), channel_id=1, source_target_pairs={{0,6},{1,7},{2,4},{3,5},{4,2},{5,3},{6,0},{7,1},{8,14},{9,15},{10,... | collective-permute-start | bytes 245768 | tf_op jit(solution)/shard_map/ppermute | solution.py:52
  9.6 0.5 collective-permute-start.3
  10.1 0.5 collective-permute-start.2
  10.6 0.0 copy-done.1
  10.6 0.0 copy-done.2
  10.6 0.0 copy-done.3
  10.7 0.0 copy-done.4
  10.7 1.1 %shard_map.85 = (f32[512,256]{1,0:T(8,128)S(1)}, f32[1024,8]{1,0:T(8,128)S(1)}) custom-call(s32[2,1024]{1,0:T(2,128)S(1)} %copy-done.2, f32[3,1024]{1,0:T(4,128)S(1)} %copy-done.3, f32[1,1024]{1,0:T(1,128)S(1)} %bitcast.2, f32[3,256,256]{2,1,0:T(8,128)S(1)} %copy-done.1, f32[160,128]{1,0:T(8,128)S(1)} %shard_map.84.tie_ref.refs_0_), custom_call_target="tpu_custom_call" | custom-call | tf_op jit(solution)/shard_map/pallas_call | solution.py:40
  11.8 0.9 %shard_map.86.refs_5_.second_ref = f32[512,256]{1,0:T(8,128)S(1)} custom-call(f32[1024,8]{1,0:T(8,128)S(1)} %get-tuple-element.36.table_ref, f32[3,256,256]{2,1,0:T(8,128)S(1)} %copy-done.1, f32[160,128]{1,0:T(8,128)S(1)} %shard_map.84.tie_ref.refs_0_), custom_call_target="tpu_custom_call" | custom-call | tf_op jit(solution)/shard_map/pallas_call | solution.py:40
  12.7 0.4 collective-permute-done.4.refs_3_
  13.1 1.3 %collective-permute-done.3.refs_2_ = f32[160,128]{1,0:T(8,128)S(1)} collective-permute-done((f32[160,128]{1,0:T(8,128)S(1)}, f32[160,128]{1,0:T(8,128)S(1)}, u32[]{:S(2)}, u32[]{:S(2)}) %collective-permute-start.3) | collective-permute-done | bytes 81952 | tf_op jit(solution)/shard_map/ppermute | solution.py:52
  14.4 0.2 collective-permute-done.2.refs_1_
  14.6 1.6 %collective-permute-start.5 = (f32[160,128]{1,0:T(8,128)S(1)}, f32[160,128]{1,0:T(8,128)S(1)}, u32[]{:S(2)}, u32[]{:S(2)}) collective-permute-start(f32[160,128]{1,0:T(8,128)S(1)} %shard_map.87.refs_0_), channel_id=1, source_target_pairs={{0,8},{1,9},{2,10},{3,11},{4,12},{5,13},{6,14},{7,15},{8,0},{9,1},... | collective-permute-start | bytes 245768 | tf_op jit(solution)/shard_map/ppermute | solution.py:52
  16.2 2.9 %collective-permute-done.5.refs_1_ = f32[160,128]{1,0:T(8,128)S(1)} collective-permute-done((f32[160,128]{1,0:T(8,128)S(1)}, f32[160,128]{1,0:T(8,128)S(1)}, u32[]{:S(2)}, u32[]{:S(2)}) %collective-permute-start.5) | collective-permute-done | bytes 81952 | tf_op jit(solution)/shard_map/ppermute | solution.py:52
  19.1 2.7 %collective-permute-start.6 = (f32[160,128]{1,0:T(8,128)S(1)}, f32[160,128]{1,0:T(8,128)S(1)}, u32[]{:S(2)}, u32[]{:S(2)}) collective-permute-start(f32[160,128]{1,0:T(8,128)S(1)} %shard_map.88.tie_ref.refs_0_), channel_id=1, source_target_pairs={{0,16},{1,17},{2,18},{3,19},{4,20},{5,21},{6,22},{7,23},{8,24},{9,... | collective-permute-start | bytes 245768 | tf_op jit(solution)/shard_map/ppermute | solution.py:52
  21.8 0.0 collective-permute-done.1.below_ref
  21.8 1.5 %shard_map.89.refs_2_.long_ref = f32[1024,256]{1,0:T(8,128)S(1)} custom-call(f32[1024,8]{1,0:T(8,128)S(1)} %get-tuple-element.36.table_ref, f32[3,128,256]{2,1,0:T(8,128)S(1)} %collective-permute-done.1.below_ref, f32[512,256]{1,0:T(8,128)S(1)} %get-tuple-element.38.refs_4_.first_ref, f32[512,256]{1,0:T(8,128)S(1)} %shard_map.86.refs_5_.second_ref, ...), custom_call_target="tpu_custom_call" | custom-call | tf_op jit(solution)/shard_map/pallas_call | solution.py:40
  23.3 1.3 %collective-permute-done.6.refs_1_ = f32[160,128]{1,0:T(8,128)S(1)} collective-permute-done((f32[160,128]{1,0:T(8,128)S(1)}, f32[160,128]{1,0:T(8,128)S(1)}, u32[]{:S(2)}, u32[]{:S(2)}) %collective-permute-start.6) | collective-permute-done | bytes 81952 | tf_op jit(solution)/shard_map/ppermute | solution.py:52
  24.5 0.1 collective-permute-start.7
  24.6 1.3 %collective-permute-done.7.other_ref = f32[160,128]{1,0:T(8,128)S(1)} collective-permute-done((f32[160,128]{1,0:T(8,128)S(1)}, f32[160,128]{1,0:T(8,128)S(1)}, u32[]{:S(2)}, u32[]{:S(2)}) %collective-permute-start.7) | collective-permute-done | bytes 81952 | tf_op jit(solution)/shard_map/ppermute | solution.py:52
  25.9 8.2 %shard_map.91 = (f32[256,256]{1,0:T(8,128)S(1)}, f32[256,256]{1,0:T(8,128)S(1)}, f32[1,256]{1,0:T(1,128)S(1)}) custom-call(f32[160,128]{1,0:T(8,128)S(1)} %shard_map.90.mine_ref, f32[160,128]{1,0:T(8,128)S(1)} %collective-permute-done.7.other_ref), custom_call_target="tpu_custom_call" | custom-call | tf_op jit(solution)/shard_map/pallas_call | solution.py:40
  34.1 2.9 %shard_map.92 = (f32[3,256,256]{2,1,0:T(8,128)S(1)}, bf16[2,3,256,256]{3,2,1,0:T(8,128)(2,1)S(1)}, f32[1024,256]{1,0:T(8,128)S(1)}, f32[4,72,128]{2,1,0:T(8,128)S(1)}, f32[4,72,128]{2,1,0:T(8,128)S(1)}) custom-call(f32[3,256,256]{2,1,0:T(8,128)S(1)} %copy-done.1, f32[1024,256]{1,0:T(8,128)S(1)} %shard_map.89.refs_2_.long_ref, ...), custom_call_target="tpu_custom_call" | custom-call | tf_op jit(solution)/shard_map/pallas_call | solution.py:40
  37.0 0.2 collective-permute-start.8
  37.2 1.0 %shard_map.93 = (f32[3,256,256]{2,1,0:T(8,128)S(1)}, f32[3,128,256]{2,1,0:T(8,128)S(1)}) custom-call(f32[1024,8]{1,0:T(8,128)S(1)} %get-tuple-element.36.table_ref, s32[2,1024]{1,0:T(2,128)S(1)} %copy-done.2, f32[1024,256]{1,0:T(8,128)S(1)} %get-tuple-element.42.long_ref, f32[4,72,128]{2,1,0:T(8,128)S(1)} %get-tuple-element.40.tie_ref.keep_ref), custom_call_target="tpu_custom_call" | custom-call | tf_op jit(solution)/shard_map/pallas_call | solution.py:40
  38.2 0.2 collective-permute-done.8.received_ref
  38.5 1.3 %collective-permute-start.9 = (f32[72,128]{1,0:T(8,128)S(1)}, f32[72,128]{1,0:T(8,128)S(1)}, u32[]{:S(2)}, u32[]{:S(2)}) collective-permute-start(f32[72,128]{1,0:T(8,128)S(1)} %get-tuple-element.45), channel_id=1, source_target_pairs={{0,2},{1,3},{2,0},{3,1},{4,6},{5,7},{6,4},{7,5},{8,10},{9,11},{10,... | collective-permute-start | bytes 110600 | tf_op jit(solution)/shard_map/ppermute | solution.py:52
  39.8 1.5 %collective-permute-start.10 = (f32[72,128]{1,0:T(8,128)S(1)}, f32[72,128]{1,0:T(8,128)S(1)}, u32[]{:S(2)}, u32[]{:S(2)}) collective-permute-start(f32[72,128]{1,0:T(8,128)S(1)} %get-tuple-element.46), channel_id=1, source_target_pairs={{0,4},{1,5},{2,6},{3,7},{4,0},{5,1},{6,2},{7,3},{8,12},{9,13},{10,... | collective-permute-start | bytes 110600 | tf_op jit(solution)/shard_map/ppermute | solution.py:52
  41.3 0.7 %collective-permute-start.11 = (f32[72,128]{1,0:T(8,128)S(1)}, f32[72,128]{1,0:T(8,128)S(1)}, u32[]{:S(2)}, u32[]{:S(2)}) collective-permute-start(f32[72,128]{1,0:T(8,128)S(1)} %get-tuple-element.47), channel_id=1, source_target_pairs={{0,6},{1,7},{2,4},{3,5},{4,2},{5,3},{6,0},{7,1},{8,14},{9,15},{10,... | collective-permute-start | bytes 110600 | tf_op jit(solution)/shard_map/ppermute | solution.py:52
  42.0 1.0 %shard_map.95 = (f32[3,256,256]{2,1,0:T(8,128)S(1)}, f32[3,128,256]{2,1,0:T(8,128)S(1)}) custom-call(f32[1024,8]{1,0:T(8,128)S(1)} %get-tuple-element.36.table_ref, s32[2,1024]{1,0:T(2,128)S(1)} %copy-done.2, f32[1024,256]{1,0:T(8,128)S(1)} %get-tuple-element.42.long_ref, f32[72,128]{1,0:T(8,128)S(1)} %get-tuple-element.44.tie_ref.refs_0_, ...), custom_call_target="tpu_custom_call" | custom-call | tf_op jit(solution)/shard_map/pallas_call | solution.py:40
  43.0 0.0 collective-permute-done.9.refs_1_
  43.1 0.8 %collective-permute-done.10.refs_2_ = f32[72,128]{1,0:T(8,128)S(1)} collective-permute-done((f32[72,128]{1,0:T(8,128)S(1)}, f32[72,128]{1,0:T(8,128)S(1)}, u32[]{:S(2)}, u32[]{:S(2)}) %collective-permute-start.10) | collective-permute-done | bytes 36896 | tf_op jit(solution)/shard_map/ppermute | solution.py:52
  43.8 2.3 %collective-permute-done.11.refs_3_ = f32[72,128]{1,0:T(8,128)S(1)} collective-permute-done((f32[72,128]{1,0:T(8,128)S(1)}, f32[72,128]{1,0:T(8,128)S(1)}, u32[]{:S(2)}, u32[]{:S(2)}) %collective-permute-start.11) | collective-permute-done | bytes 36896 | tf_op jit(solution)/shard_map/ppermute | solution.py:52
  46.1 2.3 %collective-permute-start.14 = (f32[72,128]{1,0:T(8,128)S(1)}, f32[72,128]{1,0:T(8,128)S(1)}, u32[]{:S(2)}, u32[]{:S(2)}) collective-permute-start(f32[72,128]{1,0:T(8,128)S(1)} %shard_map.96.tie_ref.refs_0_), channel_id=1, source_target_pairs={{0,24},{1,25},{2,26},{3,27},{4,28},{5,29},{6,30},{7,31},{8,16},{9,... | collective-permute-start | bytes 110600 | tf_op jit(solution)/shard_map/ppermute | solution.py:52
  48.5 0.8 %collective-permute-start.13 = (f32[72,128]{1,0:T(8,128)S(1)}, f32[72,128]{1,0:T(8,128)S(1)}, u32[]{:S(2)}, u32[]{:S(2)}) collective-permute-start(f32[72,128]{1,0:T(8,128)S(1)} %shard_map.96.tie_ref.refs_0_), channel_id=1, source_target_pairs={{0,16},{1,17},{2,18},{3,19},{4,20},{5,21},{6,22},{7,23},{8,24},{9,... | collective-permute-start | bytes 110600 | tf_op jit(solution)/shard_map/ppermute | solution.py:52
  49.2 1.3 %collective-permute-start.12 = (f32[72,128]{1,0:T(8,128)S(1)}, f32[72,128]{1,0:T(8,128)S(1)}, u32[]{:S(2)}, u32[]{:S(2)}) collective-permute-start(f32[72,128]{1,0:T(8,128)S(1)} %shard_map.96.tie_ref.refs_0_), channel_id=1, source_target_pairs={{0,8},{1,9},{2,10},{3,11},{4,12},{5,13},{6,14},{7,15},{8,0},{9,1},... | collective-permute-start | bytes 110600 | tf_op jit(solution)/shard_map/ppermute | solution.py:52
  50.6 1.4 %shard_map.97 = (f32[256,256]{1,0:T(8,128)S(1)}, f32[1,256]{1,0:T(1,128)}) custom-call(f32[256,256]{1,0:T(8,128)S(1)} %get-tuple-element.39.w_ref, f32[256,256]{1,0:T(8,128)S(1)} %get-tuple-element.50.r_ref, f32[1,256]{1,0:T(1,128)S(1)} %get-tuple-element.51.diag_ref, f32[72,128]{1,0:T(8,128)S(1)} %shard_map.96.tie_ref.refs_0_), custom_call_target="tpu_custom_call" | custom-call | tf_op jit(solution)/shard_map/pallas_call | solution.py:40
  52.0 0.1 collective-permute-done.14.refs_3_
  52.1 1.3 %collective-permute-done.13.refs_2_ = f32[72,128]{1,0:T(8,128)S(1)} collective-permute-done((f32[72,128]{1,0:T(8,128)S(1)}, f32[72,128]{1,0:T(8,128)S(1)}, u32[]{:S(2)}, u32[]{:S(2)}) %collective-permute-start.13) | collective-permute-done | bytes 36896 | tf_op jit(solution)/shard_map/ppermute | solution.py:52
  53.4 0.2 collective-permute-done.12.refs_1_
  53.6 1.3 %collective-permute-start.19 = (f32[3,128,256]{2,1,0:T(8,128)S(1)}, f32[3,128,256]{2,1,0:T(8,128)S(1)}, u32[]{:S(2)}, u32[]{:S(2)}) collective-permute-start(f32[3,128,256]{2,1,0:T(8,128)S(1)} %get-tuple-element.57), channel_id=1, source_target_pairs={{8,0},{16,8},{24,16},{9,1},{17,9},{25,17},{10,2},{18,10},{26,18},{... | collective-permute-start | bytes 1179656 | tf_op jit(solution)/shard_map/ppermute | solution.py:121
  54.9 0.8 %collective-permute-start.17 = (f32[72,128]{1,0:T(8,128)S(1)}, f32[72,128]{1,0:T(8,128)S(1)}, u32[]{:S(2)}, u32[]{:S(2)}) collective-permute-start(f32[72,128]{1,0:T(8,128)S(1)} %get-tuple-element.53.mine_ref), channel_id=1, source_target_pairs={{0,6},{1,7},{2,4},{3,5},{4,2},{5,3},{6,0},{7,1},{8,14},{9,15},{10,... | collective-permute-start | bytes 110600 | tf_op jit(solution)/shard_map/ppermute | solution.py:52
  55.7 1.5 %collective-permute-start.16 = (f32[72,128]{1,0:T(8,128)S(1)}, f32[72,128]{1,0:T(8,128)S(1)}, u32[]{:S(2)}, u32[]{:S(2)}) collective-permute-start(f32[72,128]{1,0:T(8,128)S(1)} %get-tuple-element.53.mine_ref), channel_id=1, source_target_pairs={{0,4},{1,5},{2,6},{3,7},{4,0},{5,1},{6,2},{7,3},{8,12},{9,13},{10,... | collective-permute-start | bytes 110600 | tf_op jit(solution)/shard_map/ppermute | solution.py:52
  57.2 1.2 %collective-permute-start.15 = (f32[72,128]{1,0:T(8,128)S(1)}, f32[72,128]{1,0:T(8,128)S(1)}, u32[]{:S(2)}, u32[]{:S(2)}) collective-permute-start(f32[72,128]{1,0:T(8,128)S(1)} %get-tuple-element.53.mine_ref), channel_id=1, source_target_pairs={{0,2},{1,3},{2,0},{3,1},{4,6},{5,7},{6,4},{7,5},{8,10},{9,11},{10,... | collective-permute-start | bytes 110600 | tf_op jit(solution)/shard_map/ppermute | solution.py:52
  58.5 1.4 %collective-permute-done.17.rest_2_ = f32[72,128]{1,0:T(8,128)S(1)} collective-permute-done((f32[72,128]{1,0:T(8,128)S(1)}, f32[72,128]{1,0:T(8,128)S(1)}, u32[]{:S(2)}, u32[]{:S(2)}) %collective-permute-start.17) | collective-permute-done | bytes 36896 | tf_op jit(solution)/shard_map/ppermute | solution.py:52
  59.9 0.0 collective-permute-done.16.rest_1_
  59.9 1.3 %collective-permute-done.15.rest_0_ = f32[72,128]{1,0:T(8,128)S(1)} collective-permute-done((f32[72,128]{1,0:T(8,128)S(1)}, f32[72,128]{1,0:T(8,128)S(1)}, u32[]{:S(2)}, u32[]{:S(2)}) %collective-permute-start.15) | collective-permute-done | bytes 36896 | tf_op jit(solution)/shard_map/ppermute | solution.py:52
  61.2 0.1 collective-permute-start.18
  61.3 1.4 %collective-permute-done.18.other_ref = f32[4,72,128]{2,1,0:T(8,128)S(1)} collective-permute-done((f32[4,72,128]{2,1,0:T(8,128)S(1)}, f32[4,72,128]{2,1,0:T(8,128)S(1)}, u32[]{:S(2)}, u32[]{:S(2)}) %collective-permute-start.18) | collective-permute-done | bytes 147488 | tf_op jit(solution)/shard_map/ppermute | solution.py:52
  62.7 0.7 collective-permute-done.19.back_ref
  63.3 3.3 %shard_map.100 = (f32[3,256,256]{2,1,0:T(8,128)}, f32[3,256,256]{2,1,0:T(8,128)}, f32[256,256]{1,0:T(8,128)}, f32[256,256]{1,0:T(8,128)}) custom-call(f32[4,72,128]{2,1,0:T(8,128)S(1)} %shard_map.99.mine_ref, f32[4,72,128]{2,1,0:T(8,128)S(1)} %collective-permute-done.18.other_ref, f32[3,256,256]{2,1,0:T(8,128)S(1)} %get-tuple-element.54.q_ref, ...), custom_call_target="tpu_custom_call" | custom-call | tf_op jit(solution)/shard_map/pallas_call | solution.py:499
  (8 shorter events, 0.1 us)
Async XLA Ops:
  0.6 1.1 %copy-start = (f32[3,256,256]{2,1,0:T(8,128)S(1)}, f32[3,256,256]{2,1,0:T(8,128)}, u32[]{:S(2)}) copy-start(f32[3,256,256]{2,1,0:T(8,128)} %s_ref.7) | copy-start | bytes 2359300
  1.8 8.9 %copy-start.1 = (f32[3,256,256]{2,1,0:T(8,128)S(1)}, f32[3,256,256]{2,1,0:T(8,128)}, u32[]{:S(2)}) copy-start(f32[3,256,256]{2,1,0:T(8,128)} %s_ref.7) | copy-start | bytes 2359300
  2.7 19.1 %collective-permute-start.1 = (f32[3,128,256]{2,1,0:T(8,128)S(1)}, f32[3,128,256]{2,1,0:T(8,128)S(1)}, u32[]{:S(2)}, u32[]{:S(2)}) collective-permute-start(f32[3,128,256]{2,1,0:T(8,128)S(1)} %get-tuple-element.37), channel_id=1, source_target_pairs={{0,8},{8,16},{16,24},{24,0},{1,9},{9,17},{17,25},{25,1},{2,10},{10... | collective-permute-start | bytes 1179656 | tf_op jit(solution)/shard_map/ppermute | solution.py:121
  5.8 1.3 %collective-permute-start = (f32[160,128]{1,0:T(8,128)S(1)}, f32[160,128]{1,0:T(8,128)S(1)}, u32[]{:S(2)}, u32[]{:S(2)}) collective-permute-start(f32[160,128]{1,0:T(8,128)S(1)} %get-tuple-element.35), channel_id=1, source_target_pairs={{0,1},{1,0},{2,3},{3,2},{4,5},{5,4},{6,7},{7,6},{8,9},{9,8},{10,11... | collective-permute-start | bytes 245768 | tf_op jit(solution)/shard_map/ppermute | solution.py:52
  7.1 3.6 %copy-start.2 = (s32[2,1024]{1,0:T(2,128)S(1)}, s32[2,1024]{1,0:T(2,128)}, u32[]{:S(2)}) copy-start(s32[2,1024]{1,0:T(2,128)} %ends_ref.5) | copy-start | bytes 24580
  7.1 3.6 %copy-start.3 = (f32[3,1024]{1,0:T(4,128)S(1)}, f32[3,1024]{1,0:T(4,128)}, u32[]{:S(2)}) copy-start(f32[3,1024]{1,0:T(4,128)} %dir_ref.1) | copy-start | bytes 36868
  7.1 3.6 %copy-start.4 = (f32[1024]{0:T(1024)S(1)}, f32[1024]{0:T(1024)}, u32[]{:S(2)}) copy-start(f32[1024]{0:T(1024)} %param.7) | copy-start | bytes 12292
  7.1 6.0 %collective-permute-start.4 = (f32[160,128]{1,0:T(8,128)S(1)}, f32[160,128]{1,0:T(8,128)S(1)}, u32[]{:S(2)}, u32[]{:S(2)}) collective-permute-start(f32[160,128]{1,0:T(8,128)S(1)} %shard_map.84.tie_ref.refs_0_), channel_id=1, source_target_pairs={{0,6},{1,7},{2,4},{3,5},{4,2},{5,3},{6,0},{7,1},{8,14},{9,15},{10,... | collective-permute-start | bytes 245768 | tf_op jit(solution)/shard_map/ppermute | solution.py:52
  9.6 4.8 %collective-permute-start.3 = (f32[160,128]{1,0:T(8,128)S(1)}, f32[160,128]{1,0:T(8,128)S(1)}, u32[]{:S(2)}, u32[]{:S(2)}) collective-permute-start(f32[160,128]{1,0:T(8,128)S(1)} %shard_map.84.tie_ref.refs_0_), channel_id=1, source_target_pairs={{0,4},{1,5},{2,6},{3,7},{4,0},{5,1},{6,2},{7,3},{8,12},{9,13},{10,... | collective-permute-start | bytes 245768 | tf_op jit(solution)/shard_map/ppermute | solution.py:52
  10.1 4.4 %collective-permute-start.2 = (f32[160,128]{1,0:T(8,128)S(1)}, f32[160,128]{1,0:T(8,128)S(1)}, u32[]{:S(2)}, u32[]{:S(2)}) collective-permute-start(f32[160,128]{1,0:T(8,128)S(1)} %shard_map.84.tie_ref.refs_0_), channel_id=1, source_target_pairs={{0,2},{1,3},{2,0},{3,1},{4,6},{5,7},{6,4},{7,5},{8,10},{9,11},{10,... | collective-permute-start | bytes 245768 | tf_op jit(solution)/shard_map/ppermute | solution.py:52
  14.6 4.5 %collective-permute-start.5 = (f32[160,128]{1,0:T(8,128)S(1)}, f32[160,128]{1,0:T(8,128)S(1)}, u32[]{:S(2)}, u32[]{:S(2)}) collective-permute-start(f32[160,128]{1,0:T(8,128)S(1)} %shard_map.87.refs_0_), channel_id=1, source_target_pairs={{0,8},{1,9},{2,10},{3,11},{4,12},{5,13},{6,14},{7,15},{8,0},{9,1},... | collective-permute-start | bytes 245768 | tf_op jit(solution)/shard_map/ppermute | solution.py:52
  19.1 5.4 %collective-permute-start.6 = (f32[160,128]{1,0:T(8,128)S(1)}, f32[160,128]{1,0:T(8,128)S(1)}, u32[]{:S(2)}, u32[]{:S(2)}) collective-permute-start(f32[160,128]{1,0:T(8,128)S(1)} %shard_map.88.tie_ref.refs_0_), channel_id=1, source_target_pairs={{0,16},{1,17},{2,18},{3,19},{4,20},{5,21},{6,22},{7,23},{8,24},{9,... | collective-permute-start | bytes 245768 | tf_op jit(solution)/shard_map/ppermute | solution.py:52
  24.5 1.3 %collective-permute-start.7 = (f32[160,128]{1,0:T(8,128)S(1)}, f32[160,128]{1,0:T(8,128)S(1)}, u32[]{:S(2)}, u32[]{:S(2)}) collective-permute-start(f32[160,128]{1,0:T(8,128)S(1)} %shard_map.90.mine_ref), channel_id=1, source_target_pairs={{0,1},{1,0},{2,3},{3,2},{4,5},{5,4},{6,7},{7,6},{8,9},{9,8},{10,11... | collective-permute-start | bytes 245768 | tf_op jit(solution)/shard_map/ppermute | solution.py:52
  37.0 1.4 %collective-permute-start.8 = (f32[4,72,128]{2,1,0:T(8,128)S(1)}, f32[4,72,128]{2,1,0:T(8,128)S(1)}, u32[]{:S(2)}, u32[]{:S(2)}) collective-permute-start(f32[4,72,128]{2,1,0:T(8,128)S(1)} %get-tuple-element.41), channel_id=1, source_target_pairs={{0,1},{1,0},{2,3},{3,2},{4,5},{5,4},{6,7},{7,6},{8,9},{9,8},{10,11... | collective-permute-start | bytes 442376 | tf_op jit(solution)/shard_map/ppermute | solution.py:52
  38.5 4.6 %collective-permute-start.9 = (f32[72,128]{1,0:T(8,128)S(1)}, f32[72,128]{1,0:T(8,128)S(1)}, u32[]{:S(2)}, u32[]{:S(2)}) collective-permute-start(f32[72,128]{1,0:T(8,128)S(1)} %get-tuple-element.45), channel_id=1, source_target_pairs={{0,2},{1,3},{2,0},{3,1},{4,6},{5,7},{6,4},{7,5},{8,10},{9,11},{10,... | collective-permute-start | bytes 110600 | tf_op jit(solution)/shard_map/ppermute | solution.py:52
  39.8 4.1 %collective-permute-start.10 = (f32[72,128]{1,0:T(8,128)S(1)}, f32[72,128]{1,0:T(8,128)S(1)}, u32[]{:S(2)}, u32[]{:S(2)}) collective-permute-start(f32[72,128]{1,0:T(8,128)S(1)} %get-tuple-element.46), channel_id=1, source_target_pairs={{0,4},{1,5},{2,6},{3,7},{4,0},{5,1},{6,2},{7,3},{8,12},{9,13},{10,... | collective-permute-start | bytes 110600 | tf_op jit(solution)/shard_map/ppermute | solution.py:52
  41.3 4.9 %collective-permute-start.11 = (f32[72,128]{1,0:T(8,128)S(1)}, f32[72,128]{1,0:T(8,128)S(1)}, u32[]{:S(2)}, u32[]{:S(2)}) collective-permute-start(f32[72,128]{1,0:T(8,128)S(1)} %get-tuple-element.47), channel_id=1, source_target_pairs={{0,6},{1,7},{2,4},{3,5},{4,2},{5,3},{6,0},{7,1},{8,14},{9,15},{10,... | collective-permute-start | bytes 110600 | tf_op jit(solution)/shard_map/ppermute | solution.py:52
  46.1 6.0 %collective-permute-start.14 = (f32[72,128]{1,0:T(8,128)S(1)}, f32[72,128]{1,0:T(8,128)S(1)}, u32[]{:S(2)}, u32[]{:S(2)}) collective-permute-start(f32[72,128]{1,0:T(8,128)S(1)} %shard_map.96.tie_ref.refs_0_), channel_id=1, source_target_pairs={{0,24},{1,25},{2,26},{3,27},{4,28},{5,29},{6,30},{7,31},{8,16},{9,... | collective-permute-start | bytes 110600 | tf_op jit(solution)/shard_map/ppermute | solution.py:52
  48.5 5.0 %collective-permute-start.13 = (f32[72,128]{1,0:T(8,128)S(1)}, f32[72,128]{1,0:T(8,128)S(1)}, u32[]{:S(2)}, u32[]{:S(2)}) collective-permute-start(f32[72,128]{1,0:T(8,128)S(1)} %shard_map.96.tie_ref.refs_0_), channel_id=1, source_target_pairs={{0,16},{1,17},{2,18},{3,19},{4,20},{5,21},{6,22},{7,23},{8,24},{9,... | collective-permute-start | bytes 110600 | tf_op jit(solution)/shard_map/ppermute | solution.py:52
  49.2 4.4 %collective-permute-start.12 = (f32[72,128]{1,0:T(8,128)S(1)}, f32[72,128]{1,0:T(8,128)S(1)}, u32[]{:S(2)}, u32[]{:S(2)}) collective-permute-start(f32[72,128]{1,0:T(8,128)S(1)} %shard_map.96.tie_ref.refs_0_), channel_id=1, source_target_pairs={{0,8},{1,9},{2,10},{3,11},{4,12},{5,13},{6,14},{7,15},{8,0},{9,1},... | collective-permute-start | bytes 110600 | tf_op jit(solution)/shard_map/ppermute | solution.py:52
  53.6 9.7 %collective-permute-start.19 = (f32[3,128,256]{2,1,0:T(8,128)S(1)}, f32[3,128,256]{2,1,0:T(8,128)S(1)}, u32[]{:S(2)}, u32[]{:S(2)}) collective-permute-start(f32[3,128,256]{2,1,0:T(8,128)S(1)} %get-tuple-element.57), channel_id=1, source_target_pairs={{8,0},{16,8},{24,16},{9,1},{17,9},{25,17},{10,2},{18,10},{26,18},{... | collective-permute-start | bytes 1179656 | tf_op jit(solution)/shard_map/ppermute | solution.py:121
  54.9 4.9 %collective-permute-start.17 = (f32[72,128]{1,0:T(8,128)S(1)}, f32[72,128]{1,0:T(8,128)S(1)}, u32[]{:S(2)}, u32[]{:S(2)}) collective-permute-start(f32[72,128]{1,0:T(8,128)S(1)} %get-tuple-element.53.mine_ref), channel_id=1, source_target_pairs={{0,6},{1,7},{2,4},{3,5},{4,2},{5,3},{6,0},{7,1},{8,14},{9,15},{10,... | collective-permute-start | bytes 110600 | tf_op jit(solution)/shard_map/ppermute | solution.py:52
  55.7 4.1 %collective-permute-start.16 = (f32[72,128]{1,0:T(8,128)S(1)}, f32[72,128]{1,0:T(8,128)S(1)}, u32[]{:S(2)}, u32[]{:S(2)}) collective-permute-start(f32[72,128]{1,0:T(8,128)S(1)} %get-tuple-element.53.mine_ref), channel_id=1, source_target_pairs={{0,4},{1,5},{2,6},{3,7},{4,0},{5,1},{6,2},{7,3},{8,12},{9,13},{10,... | collective-permute-start | bytes 110600 | tf_op jit(solution)/shard_map/ppermute | solution.py:52
  57.2 4.0 %collective-permute-start.15 = (f32[72,128]{1,0:T(8,128)S(1)}, f32[72,128]{1,0:T(8,128)S(1)}, u32[]{:S(2)}, u32[]{:S(2)}) collective-permute-start(f32[72,128]{1,0:T(8,128)S(1)} %get-tuple-element.53.mine_ref), channel_id=1, source_target_pairs={{0,2},{1,3},{2,0},{3,1},{4,6},{5,7},{6,4},{7,5},{8,10},{9,11},{10,... | collective-permute-start | bytes 110600 | tf_op jit(solution)/shard_map/ppermute | solution.py:52
  61.2 1.4 %collective-permute-start.18 = (f32[4,72,128]{2,1,0:T(8,128)S(1)}, f32[4,72,128]{2,1,0:T(8,128)S(1)}, u32[]{:S(2)}, u32[]{:S(2)}) collective-permute-start(f32[4,72,128]{2,1,0:T(8,128)S(1)} %shard_map.99.mine_ref), channel_id=1, source_target_pairs={{0,1},{1,0},{2,3},{3,2},{4,5},{5,4},{6,7},{7,6},{8,9},{9,8},{10,11... | collective-permute-start | bytes 442376 | tf_op jit(solution)/shard_map/ppermute | solution.py:52

commit v4 on v3

--- a/solution.py
+++ b/solution.py
@@ -36,12 +36,12 @@
     return one(a[0], b[0]) + (one(a[0], b[1]) + one(a[1], b[0]))
 
 
-def call(kernel, shapes, operands, specs=None, scratch=()):
+def call(kernel, shapes, operands, specs=None, scratch=(), outs=None):
     return pl.pallas_call(
         kernel,
         out_shape=tuple(s if isinstance(s, jax.ShapeDtypeStruct) else jax.ShapeDtypeStruct(s, jnp.float32) for s in shapes),
         in_specs=specs or [VMEM] * len(operands),
-        out_specs=tuple(VMEM for _ in shapes),
+        out_specs=outs or tuple(VMEM for _ in shapes),
         scratch_shapes=list(scratch),
         compiler_params=pltpu.CompilerParams(vmem_limit_bytes=48 << 20),
     )(*operands)
@@ -112,7 +112,7 @@
             mine, handed = add((mine, *received), tie, (handed,))
     received = [exchange(mine, bit) for bit in first]
     (total,) = call(gather_kernel, [keep.shape], (mine, *received))
-    return total, exchange(total, 1), handed
+    return total, handed
 
 
 def shifted(array, axis, by, round_off=False):
@@ -126,36 +126,44 @@
     return jnp.where(odd == 0, mine, other), jnp.where(odd == 0, other, mine)
 
 
-def pack_one(gram):
-    h, q = gram.shape[0] // 2, gram.shape[0] // 4
-    g11, g12, g22 = gram[:h, :h], gram[:h, h:], gram[h:, h:]
-    lane = lax.broadcasted_iota(jnp.int32, (q, h), 1)
-    corner = jnp.where(lane < q, pltpu.roll(g11[q:], q, 1), g22[q:])
-    return jnp.concatenate([g11[:q], g22[:q], corner, g12], axis=0)
-
-
-def unpack_one(rows, h):
+def pack_block(block):
+    h, q = block.shape[0], block.shape[0] // 2
+    e = q // 2
+    lane = lax.broadcasted_iota(jnp.int32, (e, h), 1)
+    corner = jnp.where(lane < q, pltpu.roll(block[q : q + e], q, 1), block[q + e :])
+    return jnp.concatenate([block[:q], corner], axis=0)
+
+
+def unpack_block(rows):
+    h = rows.shape[1]
     q = h // 2
     lane = lax.broadcasted_iota(jnp.int32, (q, h), 1)
-    corner = rows[2 * q : 3 * q]
-
-    def block(top, low):
-        square = jnp.concatenate([top, low], axis=0)
-        flipped = square.T[q:]
-        return jnp.concatenate([top, jnp.where(lane < q, flipped, low)], axis=0)
-
-    g11 = block(rows[:q], pltpu.roll(corner, q, 1))
-    g22 = block(rows[q : 2 * q], corner)
-    return g11, rows[3 * q :], g22
-
-
-def gram_kernel(s_ref, keep_ref, send_ref, top_ref):
-    nodes, width = s_ref.shape[1:]
+    low = jnp.concatenate([pltpu.roll(rows[q:], q, 1), rows[q:]], axis=0)
+    square = jnp.concatenate([rows[:q], low], axis=0)
+    return jnp.concatenate([rows[:q], jnp.where(lane < q, square.T[q:], low)], axis=0)
+
+
+def pack(square):
+    h = square.shape[0] // 2
+    return jnp.concatenate([pack_block(square[:h, :h]), pack_block(square[h:, h:]), square[:h, h:]], axis=0)
+
+
+def unpack(rows):
+    h = rows.shape[1]
+    p = 3 * h // 4
+    corner = rows[2 * p :]
+    upper = jnp.concatenate([unpack_block(rows[:p]), corner], axis=1)
+    return jnp.concatenate([upper, jnp.concatenate([corner.T, unpack_block(rows[p : 2 * p])], axis=1)], axis=0)
+
+
+def gram_kernel(s_ref, keep_ref, send_ref):
+    width = s_ref.shape[2]
     flat = s_ref[...].reshape(-1, width)
-    packed = pack_one(dot(flat, flat, 0, 0))
-    half = packed.shape[0] // 2
-    keep_ref[...], send_ref[...] = order_halves(packed[:half], packed[half:])
-    top_ref[...] = s_ref[:, nodes - SEC_NODES :, :]
+    gram = dot(flat, flat, 0, 0)
+    h, q = width // 2, width // 4
+    even = jnp.concatenate([pack_block(gram[h:, h:]), gram[:q, h:]], axis=0)
+    odd = jnp.concatenate([pack_block(gram[:h, :h]), gram[q:h, h:]], axis=0)
+    keep_ref[...], send_ref[...] = order_halves(even, odd)
 
 
 def pieces_of(x):
@@ -275,43 +283,71 @@
         m_ref[c0 : c0 + 8, :] = yt
 
 
-def factor_and_inverse(g11, g12, g22, w_ref, r_ref, x, u, m, rows):
-    h = g11.shape[0]
+def factored(block, x, u, m, rows):
+    h = block.shape[0]
     rowi = lax.broadcasted_iota(jnp.int32, (h, h), 0)
     coli = lax.broadcasted_iota(jnp.int32, (h, h), 1)
-
-    def finish():
-        upper = u[...]
-        d = jnp.sum(jnp.where(rowi == coli, upper, 0.0), axis=1, keepdims=True)
-        s = lax.rsqrt(d)
-        return jnp.where(rowi <= coli, upper, 0.0) * s, jnp.where(rowi >= coli, m[...], 0.0) * s
-
-    x[...] = g11
+    x[...] = block
     factor_block(x, u, m, rows)
-    r11, m1 = finish()
+    upper = u[...]
+    s = lax.rsqrt(jnp.sum(jnp.where(rowi == coli, upper, 0.0), axis=1, keepdims=True))
+    return jnp.where(rowi <= coli, upper, 0.0) * s, jnp.where(rowi >= coli, m[...], 0.0) * s
+
+
+def finish_factor(r11, m1, g12, g22, w_ref, r_ref, scratch):
+    h = r11.shape[0]
     r12 = dot(m1, g12)
-    x[...] = g22 - dot(r12, r12, 0, 0)
-    factor_block(x, u, m, rows)
-    r22, m2 = finish()
+    r22, m2 = factored(g22 - dot(r12, r12, 0, 0), *scratch)
     zero = jnp.zeros((h, h), jnp.float32)
     r_ref[:h, :h], r_ref[:h, h:], r_ref[h:, :h], r_ref[h:, h:] = r11, r12, zero, r22
     w_ref[:h, :h], w_ref[h:, h:], w_ref[h:, :h] = m1.T, m2.T, zero
     w_ref[:h, h:] = -dot(m1, dot(r12, m2, 1, 1), 0, 0)
 
 
-def first_factor_kernel(mine_ref, other_ref, w_ref, r_ref, diag_ref, *scratch):
-    h = scratch[0].shape[0]
-    lo, hi = order_halves(mine_ref[...], other_ref[...])
-    g11, g12, g22 = unpack_one(jnp.concatenate([lo, hi], axis=0), h)
-    eye = lax.broadcasted_iota(jnp.int32, (h, h), 0) == lax.broadcasted_iota(jnp.int32, (h, h), 1)
-    diag_ref[:, :h] = jnp.sum(jnp.where(eye, g11, 0.0), axis=0, keepdims=True)
-    diag_ref[:, h:] = jnp.sum(jnp.where(eye, g22, 0.0), axis=0, keepdims=True)
-    factor_and_inverse(g11, g12, g22, w_ref, r_ref, *scratch)
+def on_diagonal(block):
+    shape = block.shape
+    eye = lax.broadcasted_iota(jnp.int32, shape, 0) == lax.broadcasted_iota(jnp.int32, shape, 1)
+    return jnp.sum(jnp.where(eye, block, 0.0), axis=0, keepdims=True)
+
+
+def first_block_kernel(sum_ref, message_ref, *scratch):
+    odd = lax.axis_index(AXES) % 2 == 1
+    h = sum_ref.shape[1]
+    p = 3 * h // 4
+
+    @pl.when(odd)
+    def _():
+        g11 = unpack_block(sum_ref[:p])
+        r11, m1 = factored(g11, *scratch)
+        rowi = lax.broadcasted_iota(jnp.int32, (h, h), 0)
+        coli = lax.broadcasted_iota(jnp.int32, (h, h), 1)
+        message_ref[:h] = jnp.where(rowi < coli, r11, m1)
+        message_ref[h : h + h // 2] = sum_ref[p:]
+        message_ref[h + h // 2 :] = jnp.broadcast_to(on_diagonal(g11), (8, h))
+
+    @pl.when(jnp.logical_not(odd))
+    def _():
+        message_ref[: sum_ref.shape[0]] = sum_ref[...]
+        message_ref[sum_ref.shape[0] :] = jnp.zeros_like(message_ref[sum_ref.shape[0] :])
+
+
+def second_block_kernel(mine_ref, other_ref, w_ref, r_ref, diag_ref, *scratch):
+    h = mine_ref.shape[1]
+    p, q = 3 * h // 4, h // 2
+    even, odd = order_halves(mine_ref[...], other_ref[...])
+    rowi = lax.broadcasted_iota(jnp.int32, (h, h), 0)
+    coli = lax.broadcasted_iota(jnp.int32, (h, h), 1)
+    m1 = jnp.where(rowi >= coli, odd[:h], 0.0)
+    r11 = jnp.where(rowi < coli, odd[:h], jnp.where(rowi == coli, pltpu.reciprocal(odd[:h]), 0.0))
+    g12 = jnp.concatenate([even[p : p + q], odd[h : h + q]], axis=0)
+    g22 = unpack_block(even[:p])
+    diag_ref[:, :h] = odd[h + q : h + q + 1]
+    diag_ref[:, h:] = on_diagonal(g22)
+    finish_factor(r11, m1, g12, g22, w_ref, r_ref, scratch)
 
 
 def middle_kernel(s_ref, long_ref, table_ref, w_ref, q_ref, q_halves, long_out, keep_ref, send_ref):
     parts, nodes, width = s_ref.shape
-    h = width // 2
     w = w_ref[...]
     q = dot(s_ref[...].reshape(-1, width), w)
     q_ref[...] = q.reshape(parts, nodes, width)
@@ -322,16 +358,9 @@
         q_halves[i] = q[i].reshape(parts, nodes, width)
     gram = dot3(q, q, 0, 0)
     energy = dot3(halves(long), halves(long * table_ref[:, 5:6]), 0, 0)
-    rowi = lax.broadcasted_iota(jnp.int32, (width, width), 0)
-    coli = lax.broadcasted_iota(jnp.int32, (width, width), 1)
-    both = jnp.where(rowi < coli, gram, energy)
-    diag = jnp.sum(jnp.where(rowi == coli, gram, 0.0), axis=0, keepdims=True)
-    quarter = width // 4
-    keep, send = order_halves(both[:, :h], both[:, h:])
-    keep_diag, send_diag = order_halves(diag[:, :h], diag[:, h:])
-    for i in range(4):
-        keep_ref[i, :quarter], send_ref[i, :quarter] = (x[quarter * i : quarter * (i + 1)] for x in (keep, send))
-        keep_ref[i, quarter:], send_ref[i, quarter:] = (jnp.broadcast_to(x, (8, h)) for x in (keep_diag, send_diag))
+    keep, send = order_halves(pack(energy), pack(gram))
+    keep_ref[...] = keep.reshape(keep_ref.shape)
+    send_ref[...] = send.reshape(send_ref.shape)
 
 
 def refine_kernel(rows_all, w_ref, r_ref, diag_ref, tie_ref, out_ref, log_ref):
@@ -343,23 +372,30 @@
     out_ref[...] = r + dot(jnp.where(eye, 1.0, 0.0) - dot(r, w_ref[...]), r)
 
 
-def final_kernel(
-    rows_all, mine_ref, other_ref, q_ref, q_halves, own_ref, back_ref, r1_ref,
-    basis_ref, forces_ref, reduced_ref, coef_ref, v_ref, e_ref, w2, r2, held, sems, *scratch,
-):
-    parts, nodes, width = q_ref.shape
+def second_factor_kernel(rows_all, sum_ref, r1_ref, message_ref, *scratch):
+    odd = lax.axis_index(AXES) % 2 == 1
+    width = message_ref.shape[1]
     h = width // 2
-    root = math.sqrt(rows_all)
-    lo, hi = order_halves(mine_ref[...], other_ref[...])
-    quarter = width // 4
-    both = jnp.concatenate([x[:, :quarter].reshape(width, h) for x in (lo, hi)], axis=1)
-    diag = jnp.concatenate([x[0, quarter : quarter + 1] for x in (lo, hi)], axis=1)
+    packed = sum_ref[...].reshape(-1, h)
+    half = packed.shape[0] // 2
+
+    @pl.when(odd)
+    def _():
+        second_factor(rows_all, unpack(packed), r1_ref, message_ref, *scratch)
+
+    @pl.when(jnp.logical_not(odd))
+    def _():
+        message_ref[:half] = jnp.concatenate([packed[:half], packed[half:]], axis=1)
+        message_ref[half:] = jnp.zeros_like(message_ref[half:])
+
+
+def second_factor(rows_all, gram, r1_ref, message_ref, v_ref, e_ref, w2, r2, *scratch):
+    width = gram.shape[0]
+    h = width // 2
     rowi = lax.broadcasted_iota(jnp.int32, (width, width), 0)
     coli = lax.broadcasted_iota(jnp.int32, (width, width), 1)
-    flipped = both.T
-    energy = jnp.where(rowi < coli, flipped, both)
     eye = jnp.where(rowi == coli, 1.0, 0.0)
-    start = jnp.where(rowi < coli, both, jnp.where(rowi > coli, flipped, diag - 1.0))
+    start = gram - eye
 
     def upper_half(e):
         return jnp.where(rowi < coli, e, jnp.where(rowi == coli, 0.5 * e, 0.0))
@@ -399,32 +435,63 @@
 
     @pl.when(jnp.logical_not(size < 0.06))
     def _():
-        square = start + eye
-        factor_and_inverse(square[:h, :h], square[:h, h:], square[h:, h:], w2, r2, *scratch)
+        r11, m1 = factored(gram[:h, :h], *scratch)
+        finish_factor(r11, m1, gram[:h, h:], gram[h:, h:], w2, r2, scratch)
         v_ref[...] = w2[...] - eye
 
     v = v_ref[...]
-    v_split = halves(v)
+    change = jnp.where(rowi <= coli, v.T + start + dot3(halves(v), halves(start), 0, 0), 0.0)
+    r1 = r1_ref[...]
+    coef = (r1 + dot3(halves(change), halves(r1))) * (1.0 / math.sqrt(rows_all))
+    message_ref[:width] = jnp.where(rowi < coli, v, coef.T)
+    message_ref[width:] = jnp.broadcast_to(on_diagonal(v), (8, width))
+
+
+def copied(held, target, sems, blocks):
     copies = []
+    for k, block in enumerate(blocks):
+        held[k] = block
+        copies.append(pltpu.make_async_copy(held.at[k], target.at[k], sems.at[k]))
+        copies[-1].start()
+    return copies
+
+
+def basis_kernel(
+    rows_all, mine_ref, other_ref, q_ref, q_halves, basis_ref, reduced_ref, coef_ref, v_ref, held, sems
+):
+    width = v_ref.shape[0]
+    h = width // 2
+    even, odd = order_halves(mine_ref[...], other_ref[...])
+    rowi = lax.broadcasted_iota(jnp.int32, (width, width), 0)
+    coli = lax.broadcasted_iota(jnp.int32, (width, width), 1)
+    diag = jnp.where(rowi == coli, odd[width : width + 1], 0.0)
+    v = jnp.where(rowi < coli, odd[:width], diag)
+    v_ref[...] = v
+    v = halves(v)
+    root = math.sqrt(rows_all)
+    blocks = ((q_ref[c] + dot3((q_halves[0, c], q_halves[1, c]), v)) * root for c in range(q_ref.shape[0]))
+    copies = copied(held, basis_ref, sems, blocks)
+    coef_ref[...] = jnp.where(rowi <= coli, odd[:width].T, 0.0)
+    half = 5 * h // 4
+    energy = unpack(jnp.concatenate([even[:half, :h], even[:half, h:]], axis=0))
+    right = energy + dot3(halves(energy), v)
+    reduced_ref[...] = right + dot3(v, halves(right), 0, 0)
+    for copy in copies:
+        copy.wait()
+
+
+def forces_kernel(rows_all, own_ref, back_ref, v_ref, forces_ref, held, sems):
+    parts, nodes, _ = own_ref.shape
     top = lax.axis_index("span") == lax.axis_size("span") - 1
-    for k in range(2 * parts):
-        c = k % parts
-        if k < parts:
-            source, split, target = q_ref[c], (q_halves[0, c], q_halves[1, c]), basis_ref
-        else:
-            returned = jnp.where(top, 0.0, back_ref[c])
-            source = jnp.concatenate(
-                [own_ref[c, : nodes - SEC_NODES], own_ref[c, nodes - SEC_NODES :] + returned], axis=0
-            )
-            split, target = halves(source), forces_ref
-        held[k] = (source + dot3(split, v_split)) * root
-        copies.append(pltpu.make_async_copy(held.at[k], target.at[c], sems.at[k]))
-        copies[-1].start()
-    right = energy + dot3(halves(energy), v_split)
-    reduced_ref[...] = right + dot3(v_split, halves(right), 0, 0)
-    change = jnp.where(rowi <= coli, v.T + start + dot3(v_split, halves(start), 0, 0), 0.0)
-    r1 = r1_ref[...]
-    coef_ref[...] = (r1 + dot3(halves(change), halves(r1))) * (1.0 / root)
+    v = halves(v_ref[...])
+
+    def block(c):
+        returned = jnp.where(top, 0.0, back_ref[c])
+        low, high = own_ref[c, : nodes - SEC_NODES], own_ref[c, nodes - SEC_NODES :]
+        forces = jnp.concatenate([low, high + returned], axis=0)
+        return (forces + dot3(halves(forces), v)) * math.sqrt(rows_all)
+
+    copies = copied(held, forces_ref, sems, (block(c) for c in range(parts)))
     for copy in copies:
         copy.wait()
 
@@ -441,8 +508,8 @@
     packed = (5 * width // 8, h)
     scratch = [pltpu.VMEM((h, h), jnp.float32)] * 4
 
-    keep, send, top = call(gram_kernel, [packed, packed, level], (snapshots,), [VMEM])
-    below = shifted(top, "span", 1, True)
+    below = shifted(snapshots[:, nodes - SEC_NODES :, :], "span", 1, True)
+    keep, send = call(gram_kernel, [packed, packed], (snapshots,))
     members = member_dir.shape[1]
     split = members // 2
     total = add((keep, exchange(send, 1)))
@@ -464,16 +531,15 @@
             operands = (table, below, *long, total)
             (stretch,) = call(below_elongation_kernel, [(members, width)], operands, [VMEM] * 4 + [ANY])
             total = add((total, *received), (stretch,))
-    other = exchange(total, 1)
-
+    (message,) = call(first_block_kernel, [(h + h // 2 + 8, h)], (total,), scratch=scratch)
     w1, r1, diag = call(
-        first_factor_kernel, [square, square, (1, width)], (total, other), [VMEM, VMEM], scratch
-    )
-
-    half = (4, width // 4 + 8, h)
+        second_block_kernel, [square, square, (1, width)], (message, exchange(message, 1)), scratch=scratch
+    )
+
+    quarters = (4, 5 * width // 16, h)
     q, q_halves, stretch, keep, send = call(
         middle_kernel,
-        [field, jax.ShapeDtypeStruct((2, *field), jnp.bfloat16), (members, width), half, half],
+        [field, jax.ShapeDtypeStruct((2, *field), jnp.bfloat16), (members, width), quarters, quarters],
         (snapshots, stretch, table, w1),
     )
     held = []
@@ -491,21 +557,28 @@
         return r1_and_log[:1]
 
     r1_and_log = []
-    total, other, back = sum_by_quarters(keep, send, [members_forces, members_forces, refined])
+    total, back = sum_by_quarters(keep, send, [members_forces, members_forces, refined])
     own = held[0]
     returned = shifted(back, "span", -1)
     r1, column_energy = r1_and_log
 
-    basis, forces, reduced, coef = pl.pallas_call(
-        functools.partial(final_kernel, rows_all),
-        out_shape=tuple(jax.ShapeDtypeStruct(s, jnp.float32) for s in (field, field, square, square)),
-        in_specs=[VMEM] * 7,
-        out_specs=(HBM, HBM, VMEM, VMEM),
-        scratch_shapes=[pltpu.VMEM(square, jnp.float32)] * 4
-        + [pltpu.VMEM((2 * parts, nodes, width), jnp.float32), pltpu.SemaphoreType.DMA((2 * parts,))]
-        + scratch,
-        compiler_params=pltpu.CompilerParams(vmem_limit_bytes=48 << 20),
-    )(total, other, q, q_halves, own, returned, r1)
+    (message,) = call(
+        functools.partial(second_factor_kernel, rows_all),
+        [(width + 8, width)],
+        (total, r1),
+        scratch=[pltpu.VMEM(square, jnp.float32)] * 4 + scratch,
+    )
+    staged = [pltpu.VMEM(field, jnp.float32), pltpu.SemaphoreType.DMA((parts,))]
+    basis, reduced, coef, v = call(
+        functools.partial(basis_kernel, rows_all),
+        [field, square, square, square],
+        (message, exchange(message, 1), q, q_halves),
+        scratch=staged,
+        outs=(HBM, VMEM, VMEM, VMEM),
+    )
+    (forces,) = call(
+        functools.partial(forces_kernel, rows_all), [field], (own, returned, v), scratch=staged, outs=(HBM,)
+    )
     return (basis, forces, reduced, coef, column_energy[0])
 
 

time: 67 us -> 64.1 us (0.957)
  Pallas kernels: 22.4 us -> 19.7 us
  waiting for transfers between devices: 18.2 us -> 17.5 us
    pallas_call x1 -> x0, Pallas kernels: 3.31 us -> none  [local(): pl.pallas_call(functools.partial(final_kernel, rows_all), out_shape=tuple...]
    unnamed x10 -> x8, local copies, waits for them, and re-layouts: 1.14 us -> 0.02 us
    slice x0 -> x1, local copies, waits for them, and re-layouts: none -> 1.1 us  [local(): below = shifted(snapshots[:, nodes - SEC_NODES:, :], 'span', 1, True)]
    pallas_call x17 -> x21, Pallas kernels: 19.1 us -> 19.7 us  [call(): pl.pallas_call(kernel, out_shape=tuple((s if isinstance(s, jax.ShapeDtype...]
  transfers between devices with their start and end apart: 20 -> 20, of which waited for: 17 -> 15; matrix products, arithmetic and copies ran while one was open for 0% -> 0% of each run, Pallas kernels for 10% -> 16%
where the time goes in v4:
time: 64.1 us; the launch traced here: 63.9 us
  starting transfers between devices  24.6 us (38%)
  Pallas kernels  19.7 us (31%)
  waiting for transfers between devices  17.5 us (27%)
  local copies, waits for them, and re-layouts  1.11 us (2%)
  between operations  0.97 us (2%)
    ppermute x18, starting transfers between devices, exchange(): return lax.ppermute(array, AXES, [(i, i ^ bit) for i in range(count)])  20.2 us
    pallas_call x21, Pallas kernels, call(): pl.pallas_call(kernel, out_shape=tuple((s if isinstance(s, jax.ShapeDtype...  19.7 us
    ppermute x18, waiting for transfers between devices, exchange(): return lax.ppermute(array, AXES, [(i, i ^ bit) for i in range(count)])  17.5 us
    ppermute x2, starting transfers between devices, shifted(): return lax.ppermute(array, axis, pairs)  4.37 us
  transfers between devices with their start and end apart: 20, of which 15 were waited for; matrix products, arithmetic and copies ran while one was open for 0% of the time, Pallas kernels for 16%

profile of v4, /device:TPU:0, one launch (start us, length us, event | category | flops | bytes accessed | tf_op | source)
XLA Modules:
  0.0 63.9 jit_solution(3011517544612024145)
XLA Ops:
  0.6 0.0 copy-start
  0.6 1.1 %slice.3 = f32[3,128,256]{2,1,0:T(8,128)S(1)} slice(f32[3,256,256]{2,1,0:T(8,128)} %s_ref.7), slice={[0:3], [128:256], [0:256]} | slice | bytes 786432 | tf_op jit(solution)/shard_map/slice | solution.py:511
  1.7 3.1 %collective-permute-start.1 = (f32[3,128,256]{2,1,0:T(8,128)S(1)}, f32[3,128,256]{2,1,0:T(8,128)S(1)}, u32[]{:S(2)}, u32[]{:S(2)}) collective-permute-start(f32[3,128,256]{2,1,0:T(8,128)S(1)} %slice.3), channel_id=1, source_target_pairs={{0,8},{8,16},{16,24},{24,0},{1,9},{9,17},{17,25},{25,1},{2,10},{10... | collective-permute-start | bytes 1179656 | tf_op jit(solution)/shard_map/ppermute | solution.py:121
  4.8 0.0 copy-done
  4.8 1.0 %shard_map.83 = (f32[160,128]{1,0:T(8,128)S(1)}, f32[160,128]{1,0:T(8,128)S(1)}) custom-call(f32[3,256,256]{2,1,0:T(8,128)S(1)} %copy-done), custom_call_target="tpu_custom_call" | custom-call | tf_op jit(solution)/shard_map/pallas_call | solution.py:40
  5.8 0.1 collective-permute-start
  5.9 1.3 %collective-permute-done.refs_1_ = f32[160,128]{1,0:T(8,128)S(1)} collective-permute-done((f32[160,128]{1,0:T(8,128)S(1)}, f32[160,128]{1,0:T(8,128)S(1)}, u32[]{:S(2)}, u32[]{:S(2)}) %collective-permute-start) | collective-permute-done | bytes 81952 | tf_op jit(solution)/shard_map/ppermute | solution.py:52
  7.1 0.0 copy-start.1
  7.1 0.0 copy-start.2
  7.1 0.0 copy-start.3
  7.2 2.5 %collective-permute-start.4 = (f32[160,128]{1,0:T(8,128)S(1)}, f32[160,128]{1,0:T(8,128)S(1)}, u32[]{:S(2)}, u32[]{:S(2)}) collective-permute-start(f32[160,128]{1,0:T(8,128)S(1)} %shard_map.84.tie_ref.refs_0_), channel_id=1, source_target_pairs={{0,6},{1,7},{2,4},{3,5},{4,2},{5,3},{6,0},{7,1},{8,14},{9,15},{10,... | collective-permute-start | bytes 245768 | tf_op jit(solution)/shard_map/ppermute | solution.py:52
  9.7 0.5 collective-permute-start.3
  10.2 0.5 collective-permute-start.2
  10.7 0.0 copy-done.1
  10.7 0.0 copy-done.2
  10.7 0.0 copy-done.3
  10.7 1.1 %shard_map.85 = (f32[512,256]{1,0:T(8,128)S(1)}, f32[1024,8]{1,0:T(8,128)S(1)}) custom-call(s32[2,1024]{1,0:T(2,128)S(1)} %copy-done.1, f32[3,1024]{1,0:T(4,128)S(1)} %copy-done.2, f32[1,1024]{1,0:T(1,128)S(1)} %bitcast.2, f32[3,256,256]{2,1,0:T(8,128)S(1)} %copy-done, f32[160,128]{1,0:T(8,128)S(1)} %shard_map.84.tie_ref.refs_0_), custom_call_target="tpu_custom_call" | custom-call | tf_op jit(solution)/shard_map/pallas_call | solution.py:40
  11.9 0.9 %shard_map.86.refs_5_.second_ref = f32[512,256]{1,0:T(8,128)S(1)} custom-call(f32[1024,8]{1,0:T(8,128)S(1)} %get-tuple-element.35.table_ref, f32[3,256,256]{2,1,0:T(8,128)S(1)} %copy-done, f32[160,128]{1,0:T(8,128)S(1)} %shard_map.84.tie_ref.refs_0_), custom_call_target="tpu_custom_call" | custom-call | tf_op jit(solution)/shard_map/pallas_call | solution.py:40
  12.7 0.4 collective-permute-done.4.refs_3_
  13.2 1.3 %collective-permute-done.3.refs_2_ = f32[160,128]{1,0:T(8,128)S(1)} collective-permute-done((f32[160,128]{1,0:T(8,128)S(1)}, f32[160,128]{1,0:T(8,128)S(1)}, u32[]{:S(2)}, u32[]{:S(2)}) %collective-permute-start.3) | collective-permute-done | bytes 81952 | tf_op jit(solution)/shard_map/ppermute | solution.py:52
  14.4 0.2 collective-permute-done.2.refs_1_
  14.7 1.6 %collective-permute-start.5 = (f32[160,128]{1,0:T(8,128)S(1)}, f32[160,128]{1,0:T(8,128)S(1)}, u32[]{:S(2)}, u32[]{:S(2)}) collective-permute-start(f32[160,128]{1,0:T(8,128)S(1)} %shard_map.87.refs_0_), channel_id=1, source_target_pairs={{0,8},{1,9},{2,10},{3,11},{4,12},{5,13},{6,14},{7,15},{8,0},{9,1},... | collective-permute-start | bytes 245768 | tf_op jit(solution)/shard_map/ppermute | solution.py:52
  16.3 2.9 %collective-permute-done.5.refs_1_ = f32[160,128]{1,0:T(8,128)S(1)} collective-permute-done((f32[160,128]{1,0:T(8,128)S(1)}, f32[160,128]{1,0:T(8,128)S(1)}, u32[]{:S(2)}, u32[]{:S(2)}) %collective-permute-start.5) | collective-permute-done | bytes 81952 | tf_op jit(solution)/shard_map/ppermute | solution.py:52
  19.2 2.7 %collective-permute-start.6 = (f32[160,128]{1,0:T(8,128)S(1)}, f32[160,128]{1,0:T(8,128)S(1)}, u32[]{:S(2)}, u32[]{:S(2)}) collective-permute-start(f32[160,128]{1,0:T(8,128)S(1)} %shard_map.88.tie_ref.refs_0_), channel_id=1, source_target_pairs={{0,16},{1,17},{2,18},{3,19},{4,20},{5,21},{6,22},{7,23},{8,24},{9,... | collective-permute-start | bytes 245768 | tf_op jit(solution)/shard_map/ppermute | solution.py:52
  21.8 0.0 collective-permute-done.1.below_ref
  21.8 1.5 %shard_map.89.refs_2_.long_ref = f32[1024,256]{1,0:T(8,128)S(1)} custom-call(f32[1024,8]{1,0:T(8,128)S(1)} %get-tuple-element.35.table_ref, f32[3,128,256]{2,1,0:T(8,128)S(1)} %collective-permute-done.1.below_ref, f32[512,256]{1,0:T(8,128)S(1)} %get-tuple-element.36.refs_4_.first_ref, f32[512,256]{1,0:T(8,128)S(1)} %shard_map.86.refs_5_.second_ref, ...), custom_call_target="tpu_custom_call" | custom-call | tf_op jit(solution)/shard_map/pallas_call | solution.py:40
  23.3 1.3 %collective-permute-done.6.refs_1_ = f32[160,128]{1,0:T(8,128)S(1)} collective-permute-done((f32[160,128]{1,0:T(8,128)S(1)}, f32[160,128]{1,0:T(8,128)S(1)}, u32[]{:S(2)}, u32[]{:S(2)}) %collective-permute-start.6) | collective-permute-done | bytes 81952 | tf_op jit(solution)/shard_map/ppermute | solution.py:52
  24.6 0.2 shard_map.91.mine_ref
  24.8 0.3 collective-permute-start.7
  25.2 1.0 %collective-permute-done.7.other_ref = f32[200,128]{1,0:T(8,128)S(1)} collective-permute-done((f32[200,128]{1,0:T(8,128)S(1)}, f32[200,128]{1,0:T(8,128)S(1)}, u32[]{:S(2)}, u32[]{:S(2)}) %collective-permute-start.7) | collective-permute-done | bytes 102432 | tf_op jit(solution)/shard_map/ppermute | solution.py:52
  26.2 4.9 %shard_map.92 = (f32[256,256]{1,0:T(8,128)S(1)}, f32[256,256]{1,0:T(8,128)S(1)}, f32[1,256]{1,0:T(1,128)S(1)}) custom-call(f32[200,128]{1,0:T(8,128)S(1)} %shard_map.91.mine_ref, f32[200,128]{1,0:T(8,128)S(1)} %collective-permute-done.7.other_ref), custom_call_target="tpu_custom_call" | custom-call | tf_op jit(solution)/shard_map/pallas_call | solution.py:40
  31.1 2.8 %shard_map.93 = (f32[3,256,256]{2,1,0:T(8,128)S(1)}, bf16[2,3,256,256]{3,2,1,0:T(8,128)(2,1)S(1)}, f32[1024,256]{1,0:T(8,128)S(1)}, f32[4,80,128]{2,1,0:T(8,128)S(1)}, f32[4,80,128]{2,1,0:T(8,128)S(1)}) custom-call(f32[3,256,256]{2,1,0:T(8,128)S(1)} %copy-done, f32[1024,256]{1,0:T(8,128)S(1)} %shard_map.89.refs_2_.long_ref, ...), custom_call_target="tpu_custom_call" | custom-call | tf_op jit(solution)/shard_map/pallas_call | solution.py:40
  33.9 0.3 collective-permute-start.8
  34.2 1.0 %shard_map.94 = (f32[3,256,256]{2,1,0:T(8,128)S(1)}, f32[3,128,256]{2,1,0:T(8,128)S(1)}) custom-call(f32[1024,8]{1,0:T(8,128)S(1)} %get-tuple-element.35.table_ref, s32[2,1024]{1,0:T(2,128)S(1)} %copy-done.1, f32[1024,256]{1,0:T(8,128)S(1)} %get-tuple-element.40.long_ref, f32[4,80,128]{2,1,0:T(8,128)S(1)} %get-tuple-element.38.tie_ref.keep_ref), custom_call_target="tpu_custom_call" | custom-call | tf_op jit(solution)/shard_map/pallas_call | solution.py:40
  35.2 0.1 collective-permute-done.8.received_ref
  35.4 1.7 %collective-permute-start.9 = (f32[80,128]{1,0:T(8,128)S(1)}, f32[80,128]{1,0:T(8,128)S(1)}, u32[]{:S(2)}, u32[]{:S(2)}) collective-permute-start(f32[80,128]{1,0:T(8,128)S(1)} %get-tuple-element.43), channel_id=1, source_target_pairs={{0,2},{1,3},{2,0},{3,1},{4,6},{5,7},{6,4},{7,5},{8,10},{9,11},{10,... | collective-permute-start | bytes 122888 | tf_op jit(solution)/shard_map/ppermute | solution.py:52
  37.1 1.3 %collective-permute-start.10 = (f32[80,128]{1,0:T(8,128)S(1)}, f32[80,128]{1,0:T(8,128)S(1)}, u32[]{:S(2)}, u32[]{:S(2)}) collective-permute-start(f32[80,128]{1,0:T(8,128)S(1)} %get-tuple-element.44), channel_id=1, source_target_pairs={{0,4},{1,5},{2,6},{3,7},{4,0},{5,1},{6,2},{7,3},{8,12},{9,13},{10,... | collective-permute-start | bytes 122888 | tf_op jit(solution)/shard_map/ppermute | solution.py:52
  38.4 0.6 collective-permute-start.11
  38.9 1.0 %shard_map.96 = (f32[3,256,256]{2,1,0:T(8,128)S(1)}, f32[3,128,256]{2,1,0:T(8,128)S(1)}) custom-call(f32[1024,8]{1,0:T(8,128)S(1)} %get-tuple-element.35.table_ref, s32[2,1024]{1,0:T(2,128)S(1)} %copy-done.1, f32[1024,256]{1,0:T(8,128)S(1)} %get-tuple-element.40.long_ref, f32[80,128]{1,0:T(8,128)S(1)} %get-tuple-element.42.tie_ref.refs_0_, ...), custom_call_target="tpu_custom_call" | custom-call | tf_op jit(solution)/shard_map/pallas_call | solution.py:40
  40.0 0.0 collective-permute-done.9.refs_1_
  40.0 1.5 %collective-permute-done.10.refs_2_ = f32[80,128]{1,0:T(8,128)S(1)} collective-permute-done((f32[80,128]{1,0:T(8,128)S(1)}, f32[80,128]{1,0:T(8,128)S(1)}, u32[]{:S(2)}, u32[]{:S(2)}) %collective-permute-start.10) | collective-permute-done | bytes 40992 | tf_op jit(solution)/shard_map/ppermute | solution.py:52
  41.5 1.8 %collective-permute-done.11.refs_3_ = f32[80,128]{1,0:T(8,128)S(1)} collective-permute-done((f32[80,128]{1,0:T(8,128)S(1)}, f32[80,128]{1,0:T(8,128)S(1)}, u32[]{:S(2)}, u32[]{:S(2)}) %collective-permute-start.11) | collective-permute-done | bytes 40992 | tf_op jit(solution)/shard_map/ppermute | solution.py:52
  43.3 2.4 %collective-permute-start.14 = (f32[80,128]{1,0:T(8,128)S(1)}, f32[80,128]{1,0:T(8,128)S(1)}, u32[]{:S(2)}, u32[]{:S(2)}) collective-permute-start(f32[80,128]{1,0:T(8,128)S(1)} %shard_map.97.tie_ref.refs_0_), channel_id=1, source_target_pairs={{0,24},{1,25},{2,26},{3,27},{4,28},{5,29},{6,30},{7,31},{8,16},{9,... | collective-permute-start | bytes 122888 | tf_op jit(solution)/shard_map/ppermute | solution.py:52
  45.7 0.7 %collective-permute-start.13 = (f32[80,128]{1,0:T(8,128)S(1)}, f32[80,128]{1,0:T(8,128)S(1)}, u32[]{:S(2)}, u32[]{:S(2)}) collective-permute-start(f32[80,128]{1,0:T(8,128)S(1)} %shard_map.97.tie_ref.refs_0_), channel_id=1, source_target_pairs={{0,16},{1,17},{2,18},{3,19},{4,20},{5,21},{6,22},{7,23},{8,24},{9,... | collective-permute-start | bytes 122888 | tf_op jit(solution)/shard_map/ppermute | solution.py:52
  46.4 1.3 %collective-permute-start.12 = (f32[80,128]{1,0:T(8,128)S(1)}, f32[80,128]{1,0:T(8,128)S(1)}, u32[]{:S(2)}, u32[]{:S(2)}) collective-permute-start(f32[80,128]{1,0:T(8,128)S(1)} %shard_map.97.tie_ref.refs_0_), channel_id=1, source_target_pairs={{0,8},{1,9},{2,10},{3,11},{4,12},{5,13},{6,14},{7,15},{8,0},{9,1},... | collective-permute-start | bytes 122888 | tf_op jit(solution)/shard_map/ppermute | solution.py:52
  47.7 1.4 %shard_map.98 = (f32[256,256]{1,0:T(8,128)S(1)}, f32[1,256]{1,0:T(1,128)}) custom-call(f32[256,256]{1,0:T(8,128)S(1)} %get-tuple-element.37.w_ref, f32[256,256]{1,0:T(8,128)S(1)} %get-tuple-element.48.r_ref, f32[1,256]{1,0:T(1,128)S(1)} %get-tuple-element.49.diag_ref, f32[80,128]{1,0:T(8,128)S(1)} %shard_map.97.tie_ref.refs_0_), custom_call_target="tpu_custom_call" | custom-call | tf_op jit(solution)/shard_map/pallas_call | solution.py:40
  49.2 0.4 collective-permute-done.14.refs_3_
  49.6 1.4 %collective-permute-done.13.refs_2_ = f32[80,128]{1,0:T(8,128)S(1)} collective-permute-done((f32[80,128]{1,0:T(8,128)S(1)}, f32[80,128]{1,0:T(8,128)S(1)}, u32[]{:S(2)}, u32[]{:S(2)}) %collective-permute-start.13) | collective-permute-done | bytes 40992 | tf_op jit(solution)/shard_map/ppermute | solution.py:52
  51.0 0.0 collective-permute-done.12.refs_1_
  51.1 1.3 %collective-permute-start.19 = (f32[3,128,256]{2,1,0:T(8,128)S(1)}, f32[3,128,256]{2,1,0:T(8,128)S(1)}, u32[]{:S(2)}, u32[]{:S(2)}) collective-permute-start(f32[3,128,256]{2,1,0:T(8,128)S(1)} %get-tuple-element.56), channel_id=1, source_target_pairs={{8,0},{16,8},{24,16},{9,1},{17,9},{25,17},{10,2},{18,10},{26,18},{... | collective-permute-start | bytes 1179656 | tf_op jit(solution)/shard_map/ppermute | solution.py:121
  52.4 0.4 collective-permute-start.17
  52.8 1.5 %collective-permute-start.16 = (f32[80,128]{1,0:T(8,128)S(1)}, f32[80,128]{1,0:T(8,128)S(1)}, u32[]{:S(2)}, u32[]{:S(2)}) collective-permute-start(f32[80,128]{1,0:T(8,128)S(1)} %get-tuple-element.51.mine_ref), channel_id=1, source_target_pairs={{0,4},{1,5},{2,6},{3,7},{4,0},{5,1},{6,2},{7,3},{8,12},{9,13},{10,... | collective-permute-start | bytes 122888 | tf_op jit(solution)/shard_map/ppermute | solution.py:52
  54.3 1.6 %collective-permute-start.15 = (f32[80,128]{1,0:T(8,128)S(1)}, f32[80,128]{1,0:T(8,128)S(1)}, u32[]{:S(2)}, u32[]{:S(2)}) collective-permute-start(f32[80,128]{1,0:T(8,128)S(1)} %get-tuple-element.51.mine_ref), channel_id=1, source_target_pairs={{0,2},{1,3},{2,0},{3,1},{4,6},{5,7},{6,4},{7,5},{8,10},{9,11},{10,... | collective-permute-start | bytes 122888 | tf_op jit(solution)/shard_map/ppermute | solution.py:52
  55.9 1.4 %collective-permute-done.17.rest_2_ = f32[80,128]{1,0:T(8,128)S(1)} collective-permute-done((f32[80,128]{1,0:T(8,128)S(1)}, f32[80,128]{1,0:T(8,128)S(1)}, u32[]{:S(2)}, u32[]{:S(2)}) %collective-permute-start.17) | collective-permute-done | bytes 40992 | tf_op jit(solution)/shard_map/ppermute | solution.py:52
  57.3 0.0 collective-permute-done.16.rest_1_
  57.3 1.0 %collective-permute-done.15.rest_0_ = f32[80,128]{1,0:T(8,128)S(1)} collective-permute-done((f32[80,128]{1,0:T(8,128)S(1)}, f32[80,128]{1,0:T(8,128)S(1)}, u32[]{:S(2)}, u32[]{:S(2)}) %collective-permute-start.15) | collective-permute-done | bytes 40992 | tf_op jit(solution)/shard_map/ppermute | solution.py:52
  58.4 0.1 collective-permute-start.18
  58.5 1.5 %collective-permute-done.18.other_ref = f32[264,256]{1,0:T(8,128)S(1)} collective-permute-done((f32[264,256]{1,0:T(8,128)S(1)}, f32[264,256]{1,0:T(8,128)S(1)}, u32[]{:S(2)}, u32[]{:S(2)}) %collective-permute-start.18) | collective-permute-done | bytes 270368 | tf_op jit(solution)/shard_map/ppermute | solution.py:52
  60.0 2.4 %shard_map.102 = (f32[3,256,256]{2,1,0:T(8,128)}, f32[256,256]{1,0:T(8,128)}, f32[256,256]{1,0:T(8,128)}, f32[256,256]{1,0:T(8,128)S(1)}) custom-call(f32[264,256]{1,0:T(8,128)S(1)} %shard_map.101.mine_ref, f32[264,256]{1,0:T(8,128)S(1)} %collective-permute-done.18.other_ref, f32[3,256,256]{2,1,0:T(8,128)S(1)} %get-tuple-element.52.q_ref, ...), custom_call_target="tpu_custom_call" | custom-call | tf_op jit(solution)/shard_map/pallas_call | solution.py:40
  62.4 0.0 collective-permute-done.19.back_ref
  62.4 1.3 %shard_map.103 = f32[3,256,256]{2,1,0:T(8,128)} custom-call(f32[3,256,256]{2,1,0:T(8,128)S(1)} %get-tuple-element.55.own_ref, f32[3,128,256]{2,1,0:T(8,128)S(1)} %collective-permute-done.19.back_ref, f32[256,256]{1,0:T(8,128)S(1)} %get-tuple-element.57.v_ref), custom_call_target="tpu_custom_call" | custom-call | tf_op jit(solution)/shard_map/pallas_call | solution.py:40
  (9 shorter events, 0.2 us)
Async XLA Ops:
  0.6 4.2 %copy-start = (f32[3,256,256]{2,1,0:T(8,128)S(1)}, f32[3,256,256]{2,1,0:T(8,128)}, u32[]{:S(2)}) copy-start(f32[3,256,256]{2,1,0:T(8,128)} %s_ref.7) | copy-start | bytes 2359300
  1.7 20.1 %collective-permute-start.1 = (f32[3,128,256]{2,1,0:T(8,128)S(1)}, f32[3,128,256]{2,1,0:T(8,128)S(1)}, u32[]{:S(2)}, u32[]{:S(2)}) collective-permute-start(f32[3,128,256]{2,1,0:T(8,128)S(1)} %slice.3), channel_id=1, source_target_pairs={{0,8},{8,16},{16,24},{24,0},{1,9},{9,17},{17,25},{25,1},{2,10},{10... | collective-permute-start | bytes 1179656 | tf_op jit(solution)/shard_map/ppermute | solution.py:121
  5.8 1.3 %collective-permute-start = (f32[160,128]{1,0:T(8,128)S(1)}, f32[160,128]{1,0:T(8,128)S(1)}, u32[]{:S(2)}, u32[]{:S(2)}) collective-permute-start(f32[160,128]{1,0:T(8,128)S(1)} %get-tuple-element.34), channel_id=1, source_target_pairs={{0,1},{1,0},{2,3},{3,2},{4,5},{5,4},{6,7},{7,6},{8,9},{9,8},{10,11... | collective-permute-start | bytes 245768 | tf_op jit(solution)/shard_map/ppermute | solution.py:52
  7.1 3.6 %copy-start.1 = (s32[2,1024]{1,0:T(2,128)S(1)}, s32[2,1024]{1,0:T(2,128)}, u32[]{:S(2)}) copy-start(s32[2,1024]{1,0:T(2,128)} %ends_ref.5) | copy-start | bytes 24580
  7.1 3.6 %copy-start.2 = (f32[3,1024]{1,0:T(4,128)S(1)}, f32[3,1024]{1,0:T(4,128)}, u32[]{:S(2)}) copy-start(f32[3,1024]{1,0:T(4,128)} %dir_ref.1) | copy-start | bytes 36868
  7.1 3.6 %copy-start.3 = (f32[1024]{0:T(1024)S(1)}, f32[1024]{0:T(1024)}, u32[]{:S(2)}) copy-start(f32[1024]{0:T(1024)} %param.7) | copy-start | bytes 12292
  7.2 6.0 %collective-permute-start.4 = (f32[160,128]{1,0:T(8,128)S(1)}, f32[160,128]{1,0:T(8,128)S(1)}, u32[]{:S(2)}, u32[]{:S(2)}) collective-permute-start(f32[160,128]{1,0:T(8,128)S(1)} %shard_map.84.tie_ref.refs_0_), channel_id=1, source_target_pairs={{0,6},{1,7},{2,4},{3,5},{4,2},{5,3},{6,0},{7,1},{8,14},{9,15},{10,... | collective-permute-start | bytes 245768 | tf_op jit(solution)/shard_map/ppermute | solution.py:52
  9.7 4.8 %collective-permute-start.3 = (f32[160,128]{1,0:T(8,128)S(1)}, f32[160,128]{1,0:T(8,128)S(1)}, u32[]{:S(2)}, u32[]{:S(2)}) collective-permute-start(f32[160,128]{1,0:T(8,128)S(1)} %shard_map.84.tie_ref.refs_0_), channel_id=1, source_target_pairs={{0,4},{1,5},{2,6},{3,7},{4,0},{5,1},{6,2},{7,3},{8,12},{9,13},{10,... | collective-permute-start | bytes 245768 | tf_op jit(solution)/shard_map/ppermute | solution.py:52
  10.2 4.4 %collective-permute-start.2 = (f32[160,128]{1,0:T(8,128)S(1)}, f32[160,128]{1,0:T(8,128)S(1)}, u32[]{:S(2)}, u32[]{:S(2)}) collective-permute-start(f32[160,128]{1,0:T(8,128)S(1)} %shard_map.84.tie_ref.refs_0_), channel_id=1, source_target_pairs={{0,2},{1,3},{2,0},{3,1},{4,6},{5,7},{6,4},{7,5},{8,10},{9,11},{10,... | collective-permute-start | bytes 245768 | tf_op jit(solution)/shard_map/ppermute | solution.py:52
  14.7 4.5 %collective-permute-start.5 = (f32[160,128]{1,0:T(8,128)S(1)}, f32[160,128]{1,0:T(8,128)S(1)}, u32[]{:S(2)}, u32[]{:S(2)}) collective-permute-start(f32[160,128]{1,0:T(8,128)S(1)} %shard_map.87.refs_0_), channel_id=1, source_target_pairs={{0,8},{1,9},{2,10},{3,11},{4,12},{5,13},{6,14},{7,15},{8,0},{9,1},... | collective-permute-start | bytes 245768 | tf_op jit(solution)/shard_map/ppermute | solution.py:52
  19.2 5.4 %collective-permute-start.6 = (f32[160,128]{1,0:T(8,128)S(1)}, f32[160,128]{1,0:T(8,128)S(1)}, u32[]{:S(2)}, u32[]{:S(2)}) collective-permute-start(f32[160,128]{1,0:T(8,128)S(1)} %shard_map.88.tie_ref.refs_0_), channel_id=1, source_target_pairs={{0,16},{1,17},{2,18},{3,19},{4,20},{5,21},{6,22},{7,23},{8,24},{9,... | collective-permute-start | bytes 245768 | tf_op jit(solution)/shard_map/ppermute | solution.py:52
  24.8 1.4 %collective-permute-start.7 = (f32[200,128]{1,0:T(8,128)S(1)}, f32[200,128]{1,0:T(8,128)S(1)}, u32[]{:S(2)}, u32[]{:S(2)}) collective-permute-start(f32[200,128]{1,0:T(8,128)S(1)} %shard_map.91.mine_ref), channel_id=1, source_target_pairs={{0,1},{1,0},{2,3},{3,2},{4,5},{5,4},{6,7},{7,6},{8,9},{9,8},{10,11... | collective-permute-start | bytes 307208 | tf_op jit(solution)/shard_map/ppermute | solution.py:52
  33.9 1.5 %collective-permute-start.8 = (f32[4,80,128]{2,1,0:T(8,128)S(1)}, f32[4,80,128]{2,1,0:T(8,128)S(1)}, u32[]{:S(2)}, u32[]{:S(2)}) collective-permute-start(f32[4,80,128]{2,1,0:T(8,128)S(1)} %get-tuple-element.39), channel_id=1, source_target_pairs={{0,1},{1,0},{2,3},{3,2},{4,5},{5,4},{6,7},{7,6},{8,9},{9,8},{10,11... | collective-permute-start | bytes 491528 | tf_op jit(solution)/shard_map/ppermute | solution.py:52
  35.4 4.6 %collective-permute-start.9 = (f32[80,128]{1,0:T(8,128)S(1)}, f32[80,128]{1,0:T(8,128)S(1)}, u32[]{:S(2)}, u32[]{:S(2)}) collective-permute-start(f32[80,128]{1,0:T(8,128)S(1)} %get-tuple-element.43), channel_id=1, source_target_pairs={{0,2},{1,3},{2,0},{3,1},{4,6},{5,7},{6,4},{7,5},{8,10},{9,11},{10,... | collective-permute-start | bytes 122888 | tf_op jit(solution)/shard_map/ppermute | solution.py:52
  37.1 4.4 %collective-permute-start.10 = (f32[80,128]{1,0:T(8,128)S(1)}, f32[80,128]{1,0:T(8,128)S(1)}, u32[]{:S(2)}, u32[]{:S(2)}) collective-permute-start(f32[80,128]{1,0:T(8,128)S(1)} %get-tuple-element.44), channel_id=1, source_target_pairs={{0,4},{1,5},{2,6},{3,7},{4,0},{5,1},{6,2},{7,3},{8,12},{9,13},{10,... | collective-permute-start | bytes 122888 | tf_op jit(solution)/shard_map/ppermute | solution.py:52
  38.4 4.9 %collective-permute-start.11 = (f32[80,128]{1,0:T(8,128)S(1)}, f32[80,128]{1,0:T(8,128)S(1)}, u32[]{:S(2)}, u32[]{:S(2)}) collective-permute-start(f32[80,128]{1,0:T(8,128)S(1)} %get-tuple-element.45), channel_id=1, source_target_pairs={{0,6},{1,7},{2,4},{3,5},{4,2},{5,3},{6,0},{7,1},{8,14},{9,15},{10,... | collective-permute-start | bytes 122888 | tf_op jit(solution)/shard_map/ppermute | solution.py:52
  43.3 6.3 %collective-permute-start.14 = (f32[80,128]{1,0:T(8,128)S(1)}, f32[80,128]{1,0:T(8,128)S(1)}, u32[]{:S(2)}, u32[]{:S(2)}) collective-permute-start(f32[80,128]{1,0:T(8,128)S(1)} %shard_map.97.tie_ref.refs_0_), channel_id=1, source_target_pairs={{0,24},{1,25},{2,26},{3,27},{4,28},{5,29},{6,30},{7,31},{8,16},{9,... | collective-permute-start | bytes 122888 | tf_op jit(solution)/shard_map/ppermute | solution.py:52
  45.7 5.3 %collective-permute-start.13 = (f32[80,128]{1,0:T(8,128)S(1)}, f32[80,128]{1,0:T(8,128)S(1)}, u32[]{:S(2)}, u32[]{:S(2)}) collective-permute-start(f32[80,128]{1,0:T(8,128)S(1)} %shard_map.97.tie_ref.refs_0_), channel_id=1, source_target_pairs={{0,16},{1,17},{2,18},{3,19},{4,20},{5,21},{6,22},{7,23},{8,24},{9,... | collective-permute-start | bytes 122888 | tf_op jit(solution)/shard_map/ppermute | solution.py:52
  46.4 4.6 %collective-permute-start.12 = (f32[80,128]{1,0:T(8,128)S(1)}, f32[80,128]{1,0:T(8,128)S(1)}, u32[]{:S(2)}, u32[]{:S(2)}) collective-permute-start(f32[80,128]{1,0:T(8,128)S(1)} %shard_map.97.tie_ref.refs_0_), channel_id=1, source_target_pairs={{0,8},{1,9},{2,10},{3,11},{4,12},{5,13},{6,14},{7,15},{8,0},{9,1},... | collective-permute-start | bytes 122888 | tf_op jit(solution)/shard_map/ppermute | solution.py:52
  51.1 11.4 %collective-permute-start.19 = (f32[3,128,256]{2,1,0:T(8,128)S(1)}, f32[3,128,256]{2,1,0:T(8,128)S(1)}, u32[]{:S(2)}, u32[]{:S(2)}) collective-permute-start(f32[3,128,256]{2,1,0:T(8,128)S(1)} %get-tuple-element.56), channel_id=1, source_target_pairs={{8,0},{16,8},{24,16},{9,1},{17,9},{25,17},{10,2},{18,10},{26,18},{... | collective-permute-start | bytes 1179656 | tf_op jit(solution)/shard_map/ppermute | solution.py:121
  52.4 5.0 %collective-permute-start.17 = (f32[80,128]{1,0:T(8,128)S(1)}, f32[80,128]{1,0:T(8,128)S(1)}, u32[]{:S(2)}, u32[]{:S(2)}) collective-permute-start(f32[80,128]{1,0:T(8,128)S(1)} %get-tuple-element.51.mine_ref), channel_id=1, source_target_pairs={{0,6},{1,7},{2,4},{3,5},{4,2},{5,3},{6,0},{7,1},{8,14},{9,15},{10,... | collective-permute-start | bytes 122888 | tf_op jit(solution)/shard_map/ppermute | solution.py:52
  52.8 4.5 %collective-permute-start.16 = (f32[80,128]{1,0:T(8,128)S(1)}, f32[80,128]{1,0:T(8,128)S(1)}, u32[]{:S(2)}, u32[]{:S(2)}) collective-permute-start(f32[80,128]{1,0:T(8,128)S(1)} %get-tuple-element.51.mine_ref), channel_id=1, source_target_pairs={{0,4},{1,5},{2,6},{3,7},{4,0},{5,1},{6,2},{7,3},{8,12},{9,13},{10,... | collective-permute-start | bytes 122888 | tf_op jit(solution)/shard_map/ppermute | solution.py:52
  54.3 4.0 %collective-permute-start.15 = (f32[80,128]{1,0:T(8,128)S(1)}, f32[80,128]{1,0:T(8,128)S(1)}, u32[]{:S(2)}, u32[]{:S(2)}) collective-permute-start(f32[80,128]{1,0:T(8,128)S(1)} %get-tuple-element.51.mine_ref), channel_id=1, source_target_pairs={{0,2},{1,3},{2,0},{3,1},{4,6},{5,7},{6,4},{7,5},{8,10},{9,11},{10,... | collective-permute-start | bytes 122888 | tf_op jit(solution)/shard_map/ppermute | solution.py:52
  58.4 1.6 %collective-permute-start.18 = (f32[264,256]{1,0:T(8,128)S(1)}, f32[264,256]{1,0:T(8,128)S(1)}, u32[]{:S(2)}, u32[]{:S(2)}) collective-permute-start(f32[264,256]{1,0:T(8,128)S(1)} %shard_map.101.mine_ref), channel_id=1, source_target_pairs={{0,1},{1,0},{2,3},{3,2},{4,5},{5,4},{6,7},{7,6},{8,9},{9,8},{10,11... | collective-permute-start | bytes 811016 | tf_op jit(solution)/shard_map/ppermute | solution.py:52

commit v5 on v4

--- a/solution.py
+++ b/solution.py
@@ -36,7 +36,7 @@
     return one(a[0], b[0]) + (one(a[0], b[1]) + one(a[1], b[0]))
 
 
-def call(kernel, shapes, operands, specs=None, scratch=(), outs=None):
+def call(kernel, shapes, operands, specs=None, scratch=(), outs=None, us=0.1):
     return pl.pallas_call(
         kernel,
         out_shape=tuple(s if isinstance(s, jax.ShapeDtypeStruct) else jax.ShapeDtypeStruct(s, jnp.float32) for s in shapes),
@@ -44,6 +44,7 @@
         out_specs=outs or tuple(VMEM for _ in shapes),
         scratch_shapes=list(scratch),
         compiler_params=pltpu.CompilerParams(vmem_limit_bytes=48 << 20),
+        cost_estimate=pl.CostEstimate(flops=0, bytes_accessed=int(us * 3.69e6), transcendentals=0),
     )(*operands)
 
 
@@ -88,7 +89,7 @@
 def gather_kernel(mine_ref, *rest):
     out_ref = rest[-1]
     place = lax.axis_index(AXES) // 2 % 4
-    for i, ref in enumerate((mine_ref, *rest[:-1])):
+    for i, ref in enumerate((mine_ref, *rest[:-2])):
         out_ref[pl.ds(place ^ i, 1)] = ref[...][None]
 
 
@@ -97,22 +98,17 @@
     others = [bit for (bit,) in others]
     others = [(*pair, sum(pair))[: 2 * len(pair) - 1] for pair in (others[i : i + 2] for i in range(0, len(others), 2))]
     block = keep.shape[1:]
-    received = exchange(send, 1)
-    tie = works[0](keep)
-    mine, *parts = call(scatter_kernel, [block] * 4, (keep, received, tie), [VMEM, VMEM, ANY])
+    operands = (keep, exchange(send, 1), works[0](keep))
+    mine, *parts = call(scatter_kernel, [block] * 4, operands, [VMEM, VMEM, ANY])
     received = [exchange(part, bit) for part, bit in zip(parts, first, strict=True)]
-    handed = works[1](mine)
-    mine = add((mine, *received), (handed,))
+    mine = add((mine, *received), works[1](mine))
     for i, bits in enumerate(others):
         received = [exchange(mine, bit) for bit in bits]
-        tie = works[2](mine) if i == 0 else ()
-        if i < len(others) - 1:
-            mine = add((mine, *received), tie)
-        else:
-            mine, handed = add((mine, *received), tie, (handed,))
+        mine = add((mine, *received), works[2](mine) if i == len(others) - 1 else ())
     received = [exchange(mine, bit) for bit in first]
-    (total,) = call(gather_kernel, [keep.shape], (mine, *received))
-    return total, handed
+    operands = (mine, *received, works[3](mine))
+    (total,) = call(gather_kernel, [keep.shape], operands, [VMEM] * 4 + [ANY])
+    return total
 
 
 def shifted(array, axis, by, round_off=False):
@@ -219,27 +215,59 @@
             long_ref[at : at + CHUNK, :] = given[start : start + CHUNK, :] + added
 
 
-def force_kernel(first, count, table_ref, ends_ref, long_ref, tie_ref, *rest):
-    del tie_ref
-    own_ref, back_ref = rest[-2:]
+def force_kernel(table_ref, ends_ref, long_ref, top_ref, tie_ref, own_ref):
+    del tie_ref
     nodes = own_ref.shape[1]
-    for start in range(first, first + count, CHUNK):
-        rows = table_ref[start : start + CHUNK, :]
-        axial = long_ref[start : start + CHUNK, :] * rows[:, 5:6]
-        ends = ends_ref[:, start : start + CHUNK]
-        node = lax.broadcasted_iota(jnp.int32, (nodes + SEC_NODES, CHUNK), 0)
-        spread = (node == ends[0:1]).astype(jnp.float32) - (node == ends[1:2]).astype(jnp.float32)
-        spread = spread.astype(jnp.bfloat16)
-        for c in range(3):
-            force = picked(spread, halves(rows[:, 2 + c : 3 + c] * axial))
-            if start > first:
-                given = own_ref[c], back_ref[c]
-            elif len(rest) > 2:
-                given = rest[0][c], rest[1][c]
-            else:
-                given = 0.0, 0.0
-            own_ref[c] = given[0] + force[:nodes]
-            back_ref[c] = given[1] + force[nodes:]
+    members = long_ref.shape[0]
+    axial = long_ref[...] * table_ref[:, 5:6]
+    node = lax.broadcasted_iota(jnp.int32, (nodes, members), 0)
+    ends = ends_ref[...]
+    spread = (node == ends[0:1]).astype(jnp.float32) - (node == ends[1:2]).astype(jnp.float32)
+    spread = spread.astype(jnp.bfloat16)
+    for c in range(3):
+        force = picked(spread, halves(table_ref[:, 2 + c : 3 + c] * axial))
+        own_ref[c, : nodes - SEC_NODES] = force[: nodes - SEC_NODES]
+        own_ref[c, nodes - SEC_NODES :] = force[nodes - SEC_NODES :] - top_ref[c]
+
+
+def downward_kernel(s_ref, ends_ref, dir_ref, stiff_ref, tie_ref, out_ref):
+    del tie_ref
+    width = out_ref.shape[1]
+    rows = 3 * SEC_NODES
+    out_ref[:rows] = s_ref[:, :SEC_NODES].reshape(rows, width)
+    table = jnp.concatenate([ends_ref[...].astype(jnp.float32), dir_ref[...], stiff_ref[...]], axis=0)
+    out_ref[rows:] = jnp.concatenate([table[:, at : at + width] for at in range(0, table.shape[1], width)], axis=0)
+
+
+def above_elongation_kernel(above_ref, s_ref, tie_ref, long_ref, table_ref, seconds_ref):
+    del tie_ref
+    nodes, width = s_ref.shape[1:]
+    rows = 3 * SEC_NODES
+    held = above_ref[rows:]
+    table = jnp.concatenate([held[at : at + 6] for at in range(0, held.shape[0], 6)], axis=1)
+    table = jnp.concatenate([table, jnp.zeros_like(table[:2])], axis=0)
+    seconds_ref[...] = table
+    table_ref[...] = table.T
+    top = lax.axis_index("span") == lax.axis_size("span") - 1
+    pieces = []
+    for c in range(3):
+        both = jnp.concatenate([above_ref[SEC_NODES * c : SEC_NODES * (c + 1)], s_ref[c, nodes - SEC_NODES :]], axis=0)
+        pieces.append(pieces_of(jnp.where(top, 0.0, both)))
+    for start in range(0, long_ref.shape[0], CHUNK):
+        members = table_ref[start : start + CHUNK, :]
+        second = members[:, 1:2] - nodes
+        first = jnp.where(second >= 0.0, members[:, 0:1], -1.0)
+        pick = picks(2 * SEC_NODES, first, second + jnp.where(second >= 0.0, 1.0 * SEC_NODES, -1.0 * nodes))
+        long_ref[start : start + CHUNK, :] = sum(members[:, 2 + c : 3 + c] * picked(pick, pieces[c]) for c in range(3))
+
+
+def above_force_kernel(nodes, table_ref, seconds_ref, long_ref, w_ref, tie_ref, top_ref):
+    del tie_ref
+    axial = dot(long_ref[...], w_ref[...]) * table_ref[:, 5:6]
+    node = lax.broadcasted_iota(jnp.int32, (SEC_NODES, long_ref.shape[0]), 0).astype(jnp.float32)
+    spread = (node == seconds_ref[1:2] - nodes).astype(jnp.float32).astype(jnp.bfloat16)
+    for c in range(3):
+        top_ref[c] = picked(spread, halves(table_ref[:, 2 + c : 3 + c] * axial))
 
 
 def factor_block(x_ref, u_ref, m_ref, rows_ref):
@@ -447,51 +475,34 @@
     message_ref[width:] = jnp.broadcast_to(on_diagonal(v), (8, width))
 
 
-def copied(held, target, sems, blocks):
-    copies = []
-    for k, block in enumerate(blocks):
-        held[k] = block
-        copies.append(pltpu.make_async_copy(held.at[k], target.at[k], sems.at[k]))
-        copies[-1].start()
-    return copies
-
-
-def basis_kernel(
-    rows_all, mine_ref, other_ref, q_ref, q_halves, basis_ref, reduced_ref, coef_ref, v_ref, held, sems
+def final_kernel(
+    rows_all, mine_ref, other_ref, q_ref, q_halves, own_ref,
+    basis_ref, forces_ref, reduced_ref, coef_ref, held, sems,
 ):
-    width = v_ref.shape[0]
+    parts, nodes, width = q_ref.shape
     h = width // 2
     even, odd = order_halves(mine_ref[...], other_ref[...])
     rowi = lax.broadcasted_iota(jnp.int32, (width, width), 0)
     coli = lax.broadcasted_iota(jnp.int32, (width, width), 1)
     diag = jnp.where(rowi == coli, odd[width : width + 1], 0.0)
-    v = jnp.where(rowi < coli, odd[:width], diag)
-    v_ref[...] = v
-    v = halves(v)
+    v = halves(jnp.where(rowi < coli, odd[:width], diag))
     root = math.sqrt(rows_all)
-    blocks = ((q_ref[c] + dot3((q_halves[0, c], q_halves[1, c]), v)) * root for c in range(q_ref.shape[0]))
-    copies = copied(held, basis_ref, sems, blocks)
+    copies = []
+    for k in range(2 * parts):
+        c = k % parts
+        if k < parts:
+            source, split, target = q_ref[c], (q_halves[0, c], q_halves[1, c]), basis_ref
+        else:
+            source, target = own_ref[c], forces_ref
+            split = halves(source)
+        held[k] = (source + dot3(split, v)) * root
+        copies.append(pltpu.make_async_copy(held.at[k], target.at[c], sems.at[k]))
+        copies[-1].start()
     coef_ref[...] = jnp.where(rowi <= coli, odd[:width].T, 0.0)
     half = 5 * h // 4
     energy = unpack(jnp.concatenate([even[:half, :h], even[:half, h:]], axis=0))
     right = energy + dot3(halves(energy), v)
     reduced_ref[...] = right + dot3(v, halves(right), 0, 0)
-    for copy in copies:
-        copy.wait()
-
-
-def forces_kernel(rows_all, own_ref, back_ref, v_ref, forces_ref, held, sems):
-    parts, nodes, _ = own_ref.shape
-    top = lax.axis_index("span") == lax.axis_size("span") - 1
-    v = halves(v_ref[...])
-
-    def block(c):
-        returned = jnp.where(top, 0.0, back_ref[c])
-        low, high = own_ref[c, : nodes - SEC_NODES], own_ref[c, nodes - SEC_NODES :]
-        forces = jnp.concatenate([low, high + returned], axis=0)
-        return (forces + dot3(halves(forces), v)) * math.sqrt(rows_all)
-
-    copies = copied(held, forces_ref, sems, (block(c) for c in range(parts)))
     for copy in copies:
         copy.wait()
 
@@ -504,9 +515,8 @@
     steps = sum_steps()
     square = (width, width)
     field = (parts, nodes, width)
-    level = (parts, SEC_NODES, width)
     packed = (5 * width // 8, h)
-    scratch = [pltpu.VMEM((h, h), jnp.float32)] * 4
+    scratch = [pltpu.VMEM((h, h), jnp.float32)] * 3 + [pltpu.VMEM((h + 8, h), jnp.float32)]
 
     below = shifted(snapshots[:, nodes - SEC_NODES :, :], "span", 1, True)
     keep, send = call(gram_kernel, [packed, packed], (snapshots,))
@@ -530,10 +540,17 @@
         else:
             operands = (table, below, *long, total)
             (stretch,) = call(below_elongation_kernel, [(members, width)], operands, [VMEM] * 4 + [ANY])
-            total = add((total, *received), (stretch,))
-    (message,) = call(first_block_kernel, [(h + h // 2 + 8, h)], (total,), scratch=scratch)
+            (downward,) = call(
+                downward_kernel,
+                [(3 * SEC_NODES + 6 * members // width, width)],
+                (snapshots, member_ends, member_dir, member_stiff[None], total),
+                [VMEM] * 4 + [ANY],
+            )
+            total, downward = add((total, *received), (stretch,), (downward,))
+    above = shifted(downward, "span", -1, True)
+    (message,) = call(first_block_kernel, [(h + h // 2 + 8, h)], (total,), scratch=scratch, us=2)
     w1, r1, diag = call(
-        second_block_kernel, [square, square, (1, width)], (message, exchange(message, 1)), scratch=scratch
+        second_block_kernel, [square, square, (1, width)], (message, exchange(message, 1)), scratch=scratch, us=5
     )
 
     quarters = (4, 5 * width // 16, h)
@@ -541,26 +558,33 @@
         middle_kernel,
         [field, jax.ShapeDtypeStruct((2, *field), jnp.bfloat16), (members, width), quarters, quarters],
         (snapshots, stretch, table, w1),
+        us=3,
     )
-    held = []
-
-    def members_forces(tie):
-        operands = (table, member_ends, stretch, tie, *held)
-        first = split if held else 0
-        kernel = functools.partial(force_kernel, first, split)
-        held[:] = call(kernel, [field, level], operands, [VMEM] * 3 + [ANY] + [VMEM] * len(held))
-        return held[1]
-
     def refined(tie):
         refine = functools.partial(refine_kernel, rows_all)
-        r1_and_log.extend(call(refine, [square, (1, width)], (w1, r1, diag, tie), [VMEM] * 3 + [ANY]))
-        return r1_and_log[:1]
-
-    r1_and_log = []
-    total, back = sum_by_quarters(keep, send, [members_forces, members_forces, refined])
-    own = held[0]
-    returned = shifted(back, "span", -1)
-    r1, column_energy = r1_and_log
+        made["r1"] = call(refine, [square, (1, width)], (w1, r1, diag, tie), [VMEM] * 3 + [ANY], us=1)
+        return made["r1"][0]
+
+    def above_elongation(tie):
+        shapes = [(members, width), (members, 8), (8, members)]
+        made["above"] = call(above_elongation_kernel, shapes, (above, snapshots, tie), [VMEM] * 2 + [ANY], us=2)
+        return made["above"][:1]
+
+    def above_forces(tie):
+        stretch_above, table_above, seconds = made["above"]
+        operands = (table_above, seconds, stretch_above, w1, tie)
+        kernel = functools.partial(above_force_kernel, nodes)
+        made["top"] = call(kernel, [(parts, SEC_NODES, width)], operands, [VMEM] * 4 + [ANY], us=2.5)
+        return made["top"]
+
+    def own_forces(tie):
+        operands = (table, member_ends, stretch, made["top"][0], tie)
+        (made["own"],) = call(force_kernel, [field], operands, [VMEM] * 4 + [ANY], us=1.5)
+        return made["own"]
+
+    made = {}
+    total = sum_by_quarters(keep, send, [refined, above_elongation, above_forces, own_forces])
+    r1, column_energy = made["r1"]
 
     (message,) = call(
         functools.partial(second_factor_kernel, rows_all),
@@ -568,16 +592,12 @@
         (total, r1),
         scratch=[pltpu.VMEM(square, jnp.float32)] * 4 + scratch,
     )
-    staged = [pltpu.VMEM(field, jnp.float32), pltpu.SemaphoreType.DMA((parts,))]
-    basis, reduced, coef, v = call(
-        functools.partial(basis_kernel, rows_all),
-        [field, square, square, square],
-        (message, exchange(message, 1), q, q_halves),
-        scratch=staged,
-        outs=(HBM, VMEM, VMEM, VMEM),
-    )
-    (forces,) = call(
-        functools.partial(forces_kernel, rows_all), [field], (own, returned, v), scratch=staged, outs=(HBM,)
+    basis, forces, reduced, coef = call(
+        functools.partial(final_kernel, rows_all),
+        [field, field, square, square],
+        (message, exchange(message, 1), q, q_halves, made["own"]),
+        scratch=[pltpu.VMEM((2 * parts, nodes, width), jnp.float32), pltpu.SemaphoreType.DMA((2 * parts,))],
+        outs=(HBM, HBM, VMEM, VMEM),
     )
     return (basis, forces, reduced, coef, column_energy[0])
 

time: 64.1 us -> 63.5 us (level)
  waiting for transfers between devices: 17.5 us -> 13.3 us
  Pallas kernels: 19.7 us -> 22.4 us
  starting transfers between devices: 24.6 us -> 25.5 us
    ppermute x18, waiting for transfers between devices: 17.5 us -> 13.3 us  [exchange(): return lax.ppermute(array, AXES, [(i, i ^ bit) for i in range(count)])]
    pallas_call x21 -> x22, Pallas kernels: 19.7 us -> 22.4 us  [call(): pl.pallas_call(kernel, out_shape=tuple((s if isinstance(s, jax.ShapeDtype...]
    ppermute x2, starting transfers between devices: 4.37 us -> 5.35 us  [shifted(): return lax.ppermute(array, axis, pairs)]
  transfers between devices with their start and end apart: 20 -> 20, of which waited for: 15 -> 11; matrix products, arithmetic and copies ran while one was open for 0% -> 0% of each run, Pallas kernels for 16% -> 31%
where the time goes in v5:
time: 63.5 us; the launch traced here: 63.4 us
  starting transfers between devices  25.5 us (40%)
  Pallas kernels  22.4 us (35%)
  waiting for transfers between devices  13.3 us (21%)
  local copies, waits for them, and re-layouts  1.11 us (2%)
  between operations  1.02 us (2%)
    pallas_call x22, Pallas kernels, call(): pl.pallas_call(kernel, out_shape=tuple((s if isinstance(s, jax.ShapeDtype...  22.4 us
    ppermute x18, starting transfers between devices, exchange(): return lax.ppermute(array, AXES, [(i, i ^ bit) for i in range(count)])  20.2 us
    ppermute x18, waiting for transfers between devices, exchange(): return lax.ppermute(array, AXES, [(i, i ^ bit) for i in range(count)])  13.3 us
    ppermute x2, starting transfers between devices, shifted(): return lax.ppermute(array, axis, pairs)  5.35 us
  transfers between devices with their start and end apart: 20, of which 11 were waited for; matrix products, arithmetic and copies ran while one was open for 0% of the time, Pallas kernels for 31%

profile of v5, /device:TPU:0, one launch (start us, length us, event | category | flops | bytes accessed | tf_op | source)
XLA Modules:
  0.0 63.4 jit_solution(11428268903008707431)
XLA Ops:
  0.6 0.0 copy-start
  0.6 1.1 %slice.3 = f32[3,128,256]{2,1,0:T(8,128)S(1)} slice(f32[3,256,256]{2,1,0:T(8,128)} %s_ref.11), slice={[0:3], [128:256], [0:256]} | slice | bytes 786432 | tf_op jit(solution)/shard_map/slice | solution.py:521
  1.7 3.1 %collective-permute-start.1 = (f32[3,128,256]{2,1,0:T(8,128)S(1)}, f32[3,128,256]{2,1,0:T(8,128)S(1)}, u32[]{:S(2)}, u32[]{:S(2)}) collective-permute-start(f32[3,128,256]{2,1,0:T(8,128)S(1)} %slice.3), channel_id=1, source_target_pairs={{0,8},{8,16},{16,24},{24,0},{1,9},{9,17},{17,25},{25,1},{2,10},{10... | collective-permute-start | bytes 1179656 | tf_op jit(solution)/shard_map/ppermute | solution.py:117
  4.8 0.0 copy-done
  4.8 1.0 %shard_map.83 = (f32[160,128]{1,0:T(8,128)S(1)}, f32[160,128]{1,0:T(8,128)S(1)}) custom-call(f32[3,256,256]{2,1,0:T(8,128)S(1)} %copy-done), custom_call_target="tpu_custom_call" | custom-call | bytes 369000 | tf_op jit(solution)/shard_map/pallas_call | solution.py:40
  5.8 0.1 collective-permute-start
  5.9 1.3 %collective-permute-done.refs_1_ = f32[160,128]{1,0:T(8,128)S(1)} collective-permute-done((f32[160,128]{1,0:T(8,128)S(1)}, f32[160,128]{1,0:T(8,128)S(1)}, u32[]{:S(2)}, u32[]{:S(2)}) %collective-permute-start) | collective-permute-done | bytes 81952 | tf_op jit(solution)/shard_map/ppermute | solution.py:53
  7.1 0.0 copy-start.1
  7.1 0.0 copy-start.2
  7.1 0.0 copy-start.3
  7.2 2.5 %collective-permute-start.4 = (f32[160,128]{1,0:T(8,128)S(1)}, f32[160,128]{1,0:T(8,128)S(1)}, u32[]{:S(2)}, u32[]{:S(2)}) collective-permute-start(f32[160,128]{1,0:T(8,128)S(1)} %shard_map.84.tie_ref.refs_0_), channel_id=1, source_target_pairs={{0,6},{1,7},{2,4},{3,5},{4,2},{5,3},{6,0},{7,1},{8,14},{9,15},{10,... | collective-permute-start | bytes 245768 | tf_op jit(solution)/shard_map/ppermute | solution.py:53
  9.7 0.5 collective-permute-start.3
  10.2 0.5 collective-permute-start.2
  10.7 0.0 copy-done.1
  10.7 0.0 copy-done.2
  10.7 0.0 copy-done.3
  10.7 1.1 %shard_map.85 = (f32[512,256]{1,0:T(8,128)S(1)}, f32[1024,8]{1,0:T(8,128)S(1)}) custom-call(s32[2,1024]{1,0:T(2,128)S(1)} %copy-done.1, f32[3,1024]{1,0:T(4,128)S(1)} %copy-done.2, f32[1,1024]{1,0:T(1,128)S(1)} %bitcast.2, f32[3,256,256]{2,1,0:T(8,128)S(1)} %copy-done, f32[160,128]{1,0:T(8,128)S(1)} %shard_map.84.tie_ref.refs_0_), custom_call_target="tpu_custom_call" | custom-call | bytes 369000 | tf_op jit(solution)/shard_map/pallas_call | solution.py:40
  11.9 0.9 %shard_map.86.refs_5_.second_ref = f32[512,256]{1,0:T(8,128)S(1)} custom-call(f32[1024,8]{1,0:T(8,128)S(1)} %get-tuple-element.34.table_ref, f32[3,256,256]{2,1,0:T(8,128)S(1)} %copy-done, f32[160,128]{1,0:T(8,128)S(1)} %shard_map.84.tie_ref.refs_0_), custom_call_target="tpu_custom_call" | custom-call | bytes 369000 | tf_op jit(solution)/shard_map/pallas_call | solution.py:40
  12.7 0.4 collective-permute-done.4.refs_3_
  13.2 1.3 %collective-permute-done.3.refs_2_ = f32[160,128]{1,0:T(8,128)S(1)} collective-permute-done((f32[160,128]{1,0:T(8,128)S(1)}, f32[160,128]{1,0:T(8,128)S(1)}, u32[]{:S(2)}, u32[]{:S(2)}) %collective-permute-start.3) | collective-permute-done | bytes 81952 | tf_op jit(solution)/shard_map/ppermute | solution.py:53
  14.4 0.2 collective-permute-done.2.refs_1_
  14.7 1.6 %collective-permute-start.5 = (f32[160,128]{1,0:T(8,128)S(1)}, f32[160,128]{1,0:T(8,128)S(1)}, u32[]{:S(2)}, u32[]{:S(2)}) collective-permute-start(f32[160,128]{1,0:T(8,128)S(1)} %shard_map.87.refs_0_), channel_id=1, source_target_pairs={{0,8},{1,9},{2,10},{3,11},{4,12},{5,13},{6,14},{7,15},{8,0},{9,1},... | collective-permute-start | bytes 245768 | tf_op jit(solution)/shard_map/ppermute | solution.py:53
  16.3 2.9 %collective-permute-done.5.refs_1_ = f32[160,128]{1,0:T(8,128)S(1)} collective-permute-done((f32[160,128]{1,0:T(8,128)S(1)}, f32[160,128]{1,0:T(8,128)S(1)}, u32[]{:S(2)}, u32[]{:S(2)}) %collective-permute-start.5) | collective-permute-done | bytes 81952 | tf_op jit(solution)/shard_map/ppermute | solution.py:53
  19.2 2.7 %collective-permute-start.6 = (f32[160,128]{1,0:T(8,128)S(1)}, f32[160,128]{1,0:T(8,128)S(1)}, u32[]{:S(2)}, u32[]{:S(2)}) collective-permute-start(f32[160,128]{1,0:T(8,128)S(1)} %shard_map.88.tie_ref.refs_0_), channel_id=1, source_target_pairs={{0,16},{1,17},{2,18},{3,19},{4,20},{5,21},{6,22},{7,23},{8,24},{9,... | collective-permute-start | bytes 245768 | tf_op jit(solution)/shard_map/ppermute | solution.py:53
  21.9 0.0 collective-permute-done.1.below_ref
  21.9 1.5 %shard_map.89.refs_3_.long_ref = f32[1024,256]{1,0:T(8,128)S(1)} custom-call(f32[1024,8]{1,0:T(8,128)S(1)} %get-tuple-element.34.table_ref, f32[3,128,256]{2,1,0:T(8,128)S(1)} %collective-permute-done.1.below_ref, f32[512,256]{1,0:T(8,128)S(1)} %get-tuple-element.35.refs_4_.first_ref, f32[512,256]{1,0:T(8,128)S(1)} %shard_map.86.refs_5_.second_ref, ...), custom_call_target="tpu_custom_call" | custom-call | bytes 369000 | tf_op jit(solution)/shard_map/pallas_call | solution.py:40
  23.4 1.2 %collective-permute-done.6.refs_1_ = f32[160,128]{1,0:T(8,128)S(1)} collective-permute-done((f32[160,128]{1,0:T(8,128)S(1)}, f32[160,128]{1,0:T(8,128)S(1)}, u32[]{:S(2)}, u32[]{:S(2)}) %collective-permute-start.6) | collective-permute-done | bytes 81952 | tf_op jit(solution)/shard_map/ppermute | solution.py:53
  24.7 2.3 %collective-permute-start.12 = (f32[408,256]{1,0:T(8,128)S(1)}, f32[408,256]{1,0:T(8,128)S(1)}, u32[]{:S(2)}, u32[]{:S(2)}) collective-permute-start(f32[408,256]{1,0:T(8,128)S(1)} %get-tuple-element.47), channel_id=1, source_target_pairs={{0,24},{8,0},{16,8},{24,16},{1,25},{9,1},{17,9},{25,17},{2,26},{10... | collective-permute-start | bytes 1253384 | tf_op jit(solution)/shard_map/ppermute | solution.py:117
  26.9 0.3 collective-permute-start.7
  27.3 1.1 %collective-permute-done.7.other_ref = f32[200,128]{1,0:T(8,128)S(1)} collective-permute-done((f32[200,128]{1,0:T(8,128)S(1)}, f32[200,128]{1,0:T(8,128)S(1)}, u32[]{:S(2)}, u32[]{:S(2)}) %collective-permute-start.7) | collective-permute-done | bytes 102432 | tf_op jit(solution)/shard_map/ppermute | solution.py:53
  28.3 4.9 %shard_map.93 = (f32[256,256]{1,0:T(8,128)S(1)}, f32[256,256]{1,0:T(8,128)S(1)}, f32[1,256]{1,0:T(1,128)S(1)}) custom-call(f32[200,128]{1,0:T(8,128)S(1)} %shard_map.92.mine_ref, f32[200,128]{1,0:T(8,128)S(1)} %collective-permute-done.7.other_ref), custom_call_target="tpu_custom_call" | custom-call | bytes 18450000 | tf_op jit(solution)/shard_map/pallas_call | solution.py:40
  33.2 2.8 %shard_map.94 = (f32[3,256,256]{2,1,0:T(8,128)S(1)}, bf16[2,3,256,256]{3,2,1,0:T(8,128)(2,1)S(1)}, f32[1024,256]{1,0:T(8,128)S(1)}, f32[4,80,128]{2,1,0:T(8,128)S(1)}, f32[4,80,128]{2,1,0:T(8,128)S(1)}) custom-call(f32[3,256,256]{2,1,0:T(8,128)S(1)} %copy-done, f32[1024,256]{1,0:T(8,128)S(1)} %shard_map.89.refs_3_.long_ref, ...), custom_call_target="tpu_custom_call" | custom-call | bytes 11070000 | tf_op jit(solution)/shard_map/pallas_call | solution.py:40
  36.0 0.3 collective-permute-start.8
  36.3 1.4 %shard_map.95 = (f32[256,256]{1,0:T(8,128)S(1)}, f32[1,256]{1,0:T(1,128)}) custom-call(f32[256,256]{1,0:T(8,128)S(1)} %get-tuple-element.37.w_ref, f32[256,256]{1,0:T(8,128)S(1)} %get-tuple-element.40.r_ref, f32[1,256]{1,0:T(1,128)S(1)} %get-tuple-element.41.diag_ref, f32[4,80,128]{2,1,0:T(8,128)S(1)} %get-tuple-element.38.tie_ref.keep_ref), custom_call_target="tpu_custom_call" | custom-call | bytes 3690000 | tf_op jit(solution)/shard_map/pallas_call | solution.py:40
  37.7 0.0 collective-permute-done.8.received_ref
  37.8 1.8 %collective-permute-start.9 = (f32[80,128]{1,0:T(8,128)S(1)}, f32[80,128]{1,0:T(8,128)S(1)}, u32[]{:S(2)}, u32[]{:S(2)}) collective-permute-start(f32[80,128]{1,0:T(8,128)S(1)} %get-tuple-element.44), channel_id=1, source_target_pairs={{0,2},{1,3},{2,0},{3,1},{4,6},{5,7},{6,4},{7,5},{8,10},{9,11},{10,... | collective-permute-start | bytes 122888 | tf_op jit(solution)/shard_map/ppermute | solution.py:53
  39.5 1.3 %collective-permute-start.10 = (f32[80,128]{1,0:T(8,128)S(1)}, f32[80,128]{1,0:T(8,128)S(1)}, u32[]{:S(2)}, u32[]{:S(2)}) collective-permute-start(f32[80,128]{1,0:T(8,128)S(1)} %get-tuple-element.45), channel_id=1, source_target_pairs={{0,4},{1,5},{2,6},{3,7},{4,0},{5,1},{6,2},{7,3},{8,12},{9,13},{10,... | collective-permute-start | bytes 122888 | tf_op jit(solution)/shard_map/ppermute | solution.py:53
  40.8 0.5 collective-permute-start.11
  41.3 0.0 collective-permute-done.12.above_ref
  41.3 1.8 %shard_map.97 = (f32[1024,256]{1,0:T(8,128)S(1)}, f32[1024,8]{1,0:T(8,128)S(1)}, f32[8,1024]{1,0:T(8,128)S(1)}) custom-call(f32[408,256]{1,0:T(8,128)S(1)} %collective-permute-done.12.above_ref, f32[3,256,256]{2,1,0:T(8,128)S(1)} %copy-done, f32[80,128]{1,0:T(8,128)S(1)} %get-tuple-element.43.tie_ref.refs_0_), custom_call_target="tpu_custom_call" | custom-call | bytes 7380000 | tf_op jit(solution)/shard_map/pallas_call | solution.py:40
  43.1 0.0 collective-permute-done.9.refs_1_
  43.1 0.8 %collective-permute-done.10.refs_2_ = f32[80,128]{1,0:T(8,128)S(1)} collective-permute-done((f32[80,128]{1,0:T(8,128)S(1)}, f32[80,128]{1,0:T(8,128)S(1)}, u32[]{:S(2)}, u32[]{:S(2)}) %collective-permute-start.10) | collective-permute-done | bytes 40992 | tf_op jit(solution)/shard_map/ppermute | solution.py:53
  44.0 1.8 %collective-permute-done.11.refs_3_ = f32[80,128]{1,0:T(8,128)S(1)} collective-permute-done((f32[80,128]{1,0:T(8,128)S(1)}, f32[80,128]{1,0:T(8,128)S(1)}, u32[]{:S(2)}, u32[]{:S(2)}) %collective-permute-start.11) | collective-permute-done | bytes 40992 | tf_op jit(solution)/shard_map/ppermute | solution.py:53
  45.7 1.8 %collective-permute-start.15 = (f32[80,128]{1,0:T(8,128)S(1)}, f32[80,128]{1,0:T(8,128)S(1)}, u32[]{:S(2)}, u32[]{:S(2)}) collective-permute-start(f32[80,128]{1,0:T(8,128)S(1)} %shard_map.98.tie_ref.refs_0_), channel_id=1, source_target_pairs={{0,24},{1,25},{2,26},{3,27},{4,28},{5,29},{6,30},{7,31},{8,16},{9,... | collective-permute-start | bytes 122888 | tf_op jit(solution)/shard_map/ppermute | solution.py:53
  47.6 0.0 collective-permute-start.14
  47.6 2.6 %collective-permute-start.13 = (f32[80,128]{1,0:T(8,128)S(1)}, f32[80,128]{1,0:T(8,128)S(1)}, u32[]{:S(2)}, u32[]{:S(2)}) collective-permute-start(f32[80,128]{1,0:T(8,128)S(1)} %shard_map.98.tie_ref.refs_0_), channel_id=1, source_target_pairs={{0,8},{1,9},{2,10},{3,11},{4,12},{5,13},{6,14},{7,15},{8,0},{9,1},... | collective-permute-start | bytes 122888 | tf_op jit(solution)/shard_map/ppermute | solution.py:53
  50.2 2.4 %shard_map.99.refs_4_.top_ref = f32[3,128,256]{2,1,0:T(8,128)S(1)} custom-call(f32[1024,8]{1,0:T(8,128)S(1)} %get-tuple-element.49.table_ref, f32[8,1024]{1,0:T(8,128)S(1)} %get-tuple-element.50.seconds_ref, f32[1024,256]{1,0:T(8,128)S(1)} %get-tuple-element.48.refs_4_.long_ref, f32[256,256]{1,0:T(8,128)S(1)} %get-tuple-element.37.w_ref, ...), custom_call_target="tpu_custom_call" | custom-call | bytes 9225000 | tf_op jit(solution)/shard_map/pallas_call | solution.py:40
  52.6 0.0 collective-permute-done.15.refs_3_
  52.6 0.0 collective-permute-done.14.refs_2_
  52.6 0.0 collective-permute-done.13.refs_1_
  52.7 0.5 collective-permute-start.18
  53.2 1.5 %collective-permute-start.17 = (f32[80,128]{1,0:T(8,128)S(1)}, f32[80,128]{1,0:T(8,128)S(1)}, u32[]{:S(2)}, u32[]{:S(2)}) collective-permute-start(f32[80,128]{1,0:T(8,128)S(1)} %shard_map.100.tie_ref.mine_ref), channel_id=1, source_target_pairs={{0,4},{1,5},{2,6},{3,7},{4,0},{5,1},{6,2},{7,3},{8,12},{9,13},{10,... | collective-permute-start | bytes 122888 | tf_op jit(solution)/shard_map/ppermute | solution.py:53
  54.7 1.5 %collective-permute-start.16 = (f32[80,128]{1,0:T(8,128)S(1)}, f32[80,128]{1,0:T(8,128)S(1)}, u32[]{:S(2)}, u32[]{:S(2)}) collective-permute-start(f32[80,128]{1,0:T(8,128)S(1)} %shard_map.100.tie_ref.mine_ref), channel_id=1, source_target_pairs={{0,2},{1,3},{2,0},{3,1},{4,6},{5,7},{6,4},{7,5},{8,10},{9,11},{10,... | collective-permute-start | bytes 122888 | tf_op jit(solution)/shard_map/ppermute | solution.py:53
  56.2 1.7 %shard_map.101.rest_3_.own_ref = f32[3,256,256]{2,1,0:T(8,128)S(1)} custom-call(f32[1024,8]{1,0:T(8,128)S(1)} %get-tuple-element.34.table_ref, s32[2,1024]{1,0:T(2,128)S(1)} %copy-done.1, f32[1024,256]{1,0:T(8,128)S(1)} %get-tuple-element.51.long_ref, f32[3,128,256]{2,1,0:T(8,128)S(1)} %shard_map.99.refs_4_.top_ref, f32[80,128]{1,0:T(8,128)S(1)} %shard_map.100.tie_ref.mine_ref), custom_call_target="tpu_custom_call" | custom-call | bytes 5535000 | tf_op jit(solution)/shard_map/pallas_call | solution.py:40
  57.9 0.0 collective-permute-done.18.rest_2_
  57.9 0.0 collective-permute-done.17.rest_1_
  57.9 0.8 %collective-permute-done.16.rest_0_ = f32[80,128]{1,0:T(8,128)S(1)} collective-permute-done((f32[80,128]{1,0:T(8,128)S(1)}, f32[80,128]{1,0:T(8,128)S(1)}, u32[]{:S(2)}, u32[]{:S(2)}) %collective-permute-start.16) | collective-permute-done | bytes 40992 | tf_op jit(solution)/shard_map/ppermute | solution.py:53
  58.8 0.1 collective-permute-start.19
  58.9 1.5 %collective-permute-done.19.other_ref = f32[264,256]{1,0:T(8,128)S(1)} collective-permute-done((f32[264,256]{1,0:T(8,128)S(1)}, f32[264,256]{1,0:T(8,128)S(1)}, u32[]{:S(2)}, u32[]{:S(2)}) %collective-permute-start.19) | collective-permute-done | bytes 270368 | tf_op jit(solution)/shard_map/ppermute | solution.py:53
  60.4 2.7 %shard_map.104 = (f32[3,256,256]{2,1,0:T(8,128)}, f32[3,256,256]{2,1,0:T(8,128)}, f32[256,256]{1,0:T(8,128)}, f32[256,256]{1,0:T(8,128)}) custom-call(f32[264,256]{1,0:T(8,128)S(1)} %shard_map.103.mine_ref, f32[264,256]{1,0:T(8,128)S(1)} %collective-permute-done.19.other_ref, f32[3,256,256]{2,1,0:T(8,128)S(1)} %get-tuple-element.52.q_ref, ...), custom_call_target="tpu_custom_call" | custom-call | bytes 369000 | tf_op jit(solution)/shard_map/pallas_call | solution.py:40
  (11 shorter events, 0.2 us)
Async XLA Ops:
  0.6 4.2 %copy-start = (f32[3,256,256]{2,1,0:T(8,128)S(1)}, f32[3,256,256]{2,1,0:T(8,128)}, u32[]{:S(2)}) copy-start(f32[3,256,256]{2,1,0:T(8,128)} %s_ref.11) | copy-start | bytes 2359300
  1.7 20.1 %collective-permute-start.1 = (f32[3,128,256]{2,1,0:T(8,128)S(1)}, f32[3,128,256]{2,1,0:T(8,128)S(1)}, u32[]{:S(2)}, u32[]{:S(2)}) collective-permute-start(f32[3,128,256]{2,1,0:T(8,128)S(1)} %slice.3), channel_id=1, source_target_pairs={{0,8},{8,16},{16,24},{24,0},{1,9},{9,17},{17,25},{25,1},{2,10},{10... | collective-permute-start | bytes 1179656 | tf_op jit(solution)/shard_map/ppermute | solution.py:117
  5.8 1.3 %collective-permute-start = (f32[160,128]{1,0:T(8,128)S(1)}, f32[160,128]{1,0:T(8,128)S(1)}, u32[]{:S(2)}, u32[]{:S(2)}) collective-permute-start(f32[160,128]{1,0:T(8,128)S(1)} %get-tuple-element.33), channel_id=1, source_target_pairs={{0,1},{1,0},{2,3},{3,2},{4,5},{5,4},{6,7},{7,6},{8,9},{9,8},{10,11... | collective-permute-start | bytes 245768 | tf_op jit(solution)/shard_map/ppermute | solution.py:53
  7.1 3.6 %copy-start.1 = (s32[2,1024]{1,0:T(2,128)S(1)}, s32[2,1024]{1,0:T(2,128)}, u32[]{:S(2)}) copy-start(s32[2,1024]{1,0:T(2,128)} %ends_ref.5) | copy-start | bytes 24580
  7.1 3.6 %copy-start.2 = (f32[3,1024]{1,0:T(4,128)S(1)}, f32[3,1024]{1,0:T(4,128)}, u32[]{:S(2)}) copy-start(f32[3,1024]{1,0:T(4,128)} %dir_ref.3) | copy-start | bytes 36868
  7.1 3.6 %copy-start.3 = (f32[1024]{0:T(1024)S(1)}, f32[1024]{0:T(1024)}, u32[]{:S(2)}) copy-start(f32[1024]{0:T(1024)} %param.7) | copy-start | bytes 12292
  7.2 6.0 %collective-permute-start.4 = (f32[160,128]{1,0:T(8,128)S(1)}, f32[160,128]{1,0:T(8,128)S(1)}, u32[]{:S(2)}, u32[]{:S(2)}) collective-permute-start(f32[160,128]{1,0:T(8,128)S(1)} %shard_map.84.tie_ref.refs_0_), channel_id=1, source_target_pairs={{0,6},{1,7},{2,4},{3,5},{4,2},{5,3},{6,0},{7,1},{8,14},{9,15},{10,... | collective-permute-start | bytes 245768 | tf_op jit(solution)/shard_map/ppermute | solution.py:53
  9.7 4.8 %collective-permute-start.3 = (f32[160,128]{1,0:T(8,128)S(1)}, f32[160,128]{1,0:T(8,128)S(1)}, u32[]{:S(2)}, u32[]{:S(2)}) collective-permute-start(f32[160,128]{1,0:T(8,128)S(1)} %shard_map.84.tie_ref.refs_0_), channel_id=1, source_target_pairs={{0,4},{1,5},{2,6},{3,7},{4,0},{5,1},{6,2},{7,3},{8,12},{9,13},{10,... | collective-permute-start | bytes 245768 | tf_op jit(solution)/shard_map/ppermute | solution.py:53
  10.2 4.4 %collective-permute-start.2 = (f32[160,128]{1,0:T(8,128)S(1)}, f32[160,128]{1,0:T(8,128)S(1)}, u32[]{:S(2)}, u32[]{:S(2)}) collective-permute-start(f32[160,128]{1,0:T(8,128)S(1)} %shard_map.84.tie_ref.refs_0_), channel_id=1, source_target_pairs={{0,2},{1,3},{2,0},{3,1},{4,6},{5,7},{6,4},{7,5},{8,10},{9,11},{10,... | collective-permute-start | bytes 245768 | tf_op jit(solution)/shard_map/ppermute | solution.py:53
  14.7 4.5 %collective-permute-start.5 = (f32[160,128]{1,0:T(8,128)S(1)}, f32[160,128]{1,0:T(8,128)S(1)}, u32[]{:S(2)}, u32[]{:S(2)}) collective-permute-start(f32[160,128]{1,0:T(8,128)S(1)} %shard_map.87.refs_0_), channel_id=1, source_target_pairs={{0,8},{1,9},{2,10},{3,11},{4,12},{5,13},{6,14},{7,15},{8,0},{9,1},... | collective-permute-start | bytes 245768 | tf_op jit(solution)/shard_map/ppermute | solution.py:53
  19.2 5.4 %collective-permute-start.6 = (f32[160,128]{1,0:T(8,128)S(1)}, f32[160,128]{1,0:T(8,128)S(1)}, u32[]{:S(2)}, u32[]{:S(2)}) collective-permute-start(f32[160,128]{1,0:T(8,128)S(1)} %shard_map.88.tie_ref.refs_0_), channel_id=1, source_target_pairs={{0,16},{1,17},{2,18},{3,19},{4,20},{5,21},{6,22},{7,23},{8,24},{9,... | collective-permute-start | bytes 245768 | tf_op jit(solution)/shard_map/ppermute | solution.py:53
  24.7 16.6 %collective-permute-start.12 = (f32[408,256]{1,0:T(8,128)S(1)}, f32[408,256]{1,0:T(8,128)S(1)}, u32[]{:S(2)}, u32[]{:S(2)}) collective-permute-start(f32[408,256]{1,0:T(8,128)S(1)} %get-tuple-element.47), channel_id=1, source_target_pairs={{0,24},{8,0},{16,8},{24,16},{1,25},{9,1},{17,9},{25,17},{2,26},{10... | collective-permute-start | bytes 1253384 | tf_op jit(solution)/shard_map/ppermute | solution.py:117
  26.9 1.4 %collective-permute-start.7 = (f32[200,128]{1,0:T(8,128)S(1)}, f32[200,128]{1,0:T(8,128)S(1)}, u32[]{:S(2)}, u32[]{:S(2)}) collective-permute-start(f32[200,128]{1,0:T(8,128)S(1)} %shard_map.92.mine_ref), channel_id=1, source_target_pairs={{0,1},{1,0},{2,3},{3,2},{4,5},{5,4},{6,7},{7,6},{8,9},{9,8},{10,11... | collective-permute-start | bytes 307208 | tf_op jit(solution)/shard_map/ppermute | solution.py:53
  36.0 1.7 %collective-permute-start.8 = (f32[4,80,128]{2,1,0:T(8,128)S(1)}, f32[4,80,128]{2,1,0:T(8,128)S(1)}, u32[]{:S(2)}, u32[]{:S(2)}) collective-permute-start(f32[4,80,128]{2,1,0:T(8,128)S(1)} %get-tuple-element.39), channel_id=1, source_target_pairs={{0,1},{1,0},{2,3},{3,2},{4,5},{5,4},{6,7},{7,6},{8,9},{9,8},{10,11... | collective-permute-start | bytes 491528 | tf_op jit(solution)/shard_map/ppermute | solution.py:53
  37.8 5.4 %collective-permute-start.9 = (f32[80,128]{1,0:T(8,128)S(1)}, f32[80,128]{1,0:T(8,128)S(1)}, u32[]{:S(2)}, u32[]{:S(2)}) collective-permute-start(f32[80,128]{1,0:T(8,128)S(1)} %get-tuple-element.44), channel_id=1, source_target_pairs={{0,2},{1,3},{2,0},{3,1},{4,6},{5,7},{6,4},{7,5},{8,10},{9,11},{10,... | collective-permute-start | bytes 122888 | tf_op jit(solution)/shard_map/ppermute | solution.py:53
  39.5 4.4 %collective-permute-start.10 = (f32[80,128]{1,0:T(8,128)S(1)}, f32[80,128]{1,0:T(8,128)S(1)}, u32[]{:S(2)}, u32[]{:S(2)}) collective-permute-start(f32[80,128]{1,0:T(8,128)S(1)} %get-tuple-element.45), channel_id=1, source_target_pairs={{0,4},{1,5},{2,6},{3,7},{4,0},{5,1},{6,2},{7,3},{8,12},{9,13},{10,... | collective-permute-start | bytes 122888 | tf_op jit(solution)/shard_map/ppermute | solution.py:53
  40.8 4.9 %collective-permute-start.11 = (f32[80,128]{1,0:T(8,128)S(1)}, f32[80,128]{1,0:T(8,128)S(1)}, u32[]{:S(2)}, u32[]{:S(2)}) collective-permute-start(f32[80,128]{1,0:T(8,128)S(1)} %get-tuple-element.46), channel_id=1, source_target_pairs={{0,6},{1,7},{2,4},{3,5},{4,2},{5,3},{6,0},{7,1},{8,14},{9,15},{10,... | collective-permute-start | bytes 122888 | tf_op jit(solution)/shard_map/ppermute | solution.py:53
  45.7 6.9 %collective-permute-start.15 = (f32[80,128]{1,0:T(8,128)S(1)}, f32[80,128]{1,0:T(8,128)S(1)}, u32[]{:S(2)}, u32[]{:S(2)}) collective-permute-start(f32[80,128]{1,0:T(8,128)S(1)} %shard_map.98.tie_ref.refs_0_), channel_id=1, source_target_pairs={{0,24},{1,25},{2,26},{3,27},{4,28},{5,29},{6,30},{7,31},{8,16},{9,... | collective-permute-start | bytes 122888 | tf_op jit(solution)/shard_map/ppermute | solution.py:53
  47.6 5.1 %collective-permute-start.14 = (f32[80,128]{1,0:T(8,128)S(1)}, f32[80,128]{1,0:T(8,128)S(1)}, u32[]{:S(2)}, u32[]{:S(2)}) collective-permute-start(f32[80,128]{1,0:T(8,128)S(1)} %shard_map.98.tie_ref.refs_0_), channel_id=1, source_target_pairs={{0,16},{1,17},{2,18},{3,19},{4,20},{5,21},{6,22},{7,23},{8,24},{9,... | collective-permute-start | bytes 122888 | tf_op jit(solution)/shard_map/ppermute | solution.py:53
  47.6 5.1 %collective-permute-start.13 = (f32[80,128]{1,0:T(8,128)S(1)}, f32[80,128]{1,0:T(8,128)S(1)}, u32[]{:S(2)}, u32[]{:S(2)}) collective-permute-start(f32[80,128]{1,0:T(8,128)S(1)} %shard_map.98.tie_ref.refs_0_), channel_id=1, source_target_pairs={{0,8},{1,9},{2,10},{3,11},{4,12},{5,13},{6,14},{7,15},{8,0},{9,1},... | collective-permute-start | bytes 122888 | tf_op jit(solution)/shard_map/ppermute | solution.py:53
  52.7 5.2 %collective-permute-start.18 = (f32[80,128]{1,0:T(8,128)S(1)}, f32[80,128]{1,0:T(8,128)S(1)}, u32[]{:S(2)}, u32[]{:S(2)}) collective-permute-start(f32[80,128]{1,0:T(8,128)S(1)} %shard_map.100.tie_ref.mine_ref), channel_id=1, source_target_pairs={{0,6},{1,7},{2,4},{3,5},{4,2},{5,3},{6,0},{7,1},{8,14},{9,15},{10,... | collective-permute-start | bytes 122888 | tf_op jit(solution)/shard_map/ppermute | solution.py:53
  53.2 4.7 %collective-permute-start.17 = (f32[80,128]{1,0:T(8,128)S(1)}, f32[80,128]{1,0:T(8,128)S(1)}, u32[]{:S(2)}, u32[]{:S(2)}) collective-permute-start(f32[80,128]{1,0:T(8,128)S(1)} %shard_map.100.tie_ref.mine_ref), channel_id=1, source_target_pairs={{0,4},{1,5},{2,6},{3,7},{4,0},{5,1},{6,2},{7,3},{8,12},{9,13},{10,... | collective-permute-start | bytes 122888 | tf_op jit(solution)/shard_map/ppermute | solution.py:53
  54.7 4.0 %collective-permute-start.16 = (f32[80,128]{1,0:T(8,128)S(1)}, f32[80,128]{1,0:T(8,128)S(1)}, u32[]{:S(2)}, u32[]{:S(2)}) collective-permute-start(f32[80,128]{1,0:T(8,128)S(1)} %shard_map.100.tie_ref.mine_ref), channel_id=1, source_target_pairs={{0,2},{1,3},{2,0},{3,1},{4,6},{5,7},{6,4},{7,5},{8,10},{9,11},{10,... | collective-permute-start | bytes 122888 | tf_op jit(solution)/shard_map/ppermute | solution.py:53
  58.8 1.6 %collective-permute-start.19 = (f32[264,256]{1,0:T(8,128)S(1)}, f32[264,256]{1,0:T(8,128)S(1)}, u32[]{:S(2)}, u32[]{:S(2)}) collective-permute-start(f32[264,256]{1,0:T(8,128)S(1)} %shard_map.103.mine_ref), channel_id=1, source_target_pairs={{0,1},{1,0},{2,3},{3,2},{4,5},{5,4},{6,7},{7,6},{8,9},{9,8},{10,11... | collective-permute-start | bytes 811016 | tf_op jit(solution)/shard_map/ppermute | solution.py:53

commit v6 on v5

--- a/solution.py
+++ b/solution.py
@@ -34,6 +34,21 @@
         return lax.dot_general(x, y, (((ca,), (cb,)), ((), ())), preferred_element_type=jnp.float32)
 
     return one(a[0], b[0]) + (one(a[0], b[1]) + one(a[1], b[0]))
+
+
+def pieces_of(x):
+    first = x.astype(jnp.bfloat16)
+    rest = x - first.astype(jnp.float32)
+    second = rest.astype(jnp.bfloat16)
+    third = (rest - second.astype(jnp.float32)).astype(jnp.bfloat16)
+    return first, second, third
+
+
+def dot6(a, b, ca=1, cb=0):
+    def one(i, j):
+        return lax.dot_general(a[i], b[j], (((ca,), (cb,)), ((), ())), preferred_element_type=jnp.float32)
+
+    return one(0, 0) + ((one(0, 1) + one(1, 0)) + ((one(0, 2) + one(2, 0)) + one(1, 1)))
 
 
 def call(kernel, shapes, operands, specs=None, scratch=(), outs=None, us=0.1):
@@ -155,19 +170,12 @@
 def gram_kernel(s_ref, keep_ref, send_ref):
     width = s_ref.shape[2]
     flat = s_ref[...].reshape(-1, width)
-    gram = dot(flat, flat, 0, 0)
+    flat = pieces_of(flat)
+    gram = dot6(flat, flat, 0, 0)
     h, q = width // 2, width // 4
     even = jnp.concatenate([pack_block(gram[h:, h:]), gram[:q, h:]], axis=0)
     odd = jnp.concatenate([pack_block(gram[:h, :h]), gram[q:h, h:]], axis=0)
     keep_ref[...], send_ref[...] = order_halves(even, odd)
-
-
-def pieces_of(x):
-    first = x.astype(jnp.bfloat16)
-    rest = x - first.astype(jnp.float32)
-    second = rest.astype(jnp.bfloat16)
-    third = (rest - second.astype(jnp.float32)).astype(jnp.bfloat16)
-    return first, second, third
 
 
 def picks(node_count, first, second):
@@ -263,7 +271,7 @@
 
 def above_force_kernel(nodes, table_ref, seconds_ref, long_ref, w_ref, tie_ref, top_ref):
     del tie_ref
-    axial = dot(long_ref[...], w_ref[...]) * table_ref[:, 5:6]
+    axial = dot6(pieces_of(long_ref[...]), pieces_of(w_ref[...])) * table_ref[:, 5:6]
     node = lax.broadcasted_iota(jnp.int32, (SEC_NODES, long_ref.shape[0]), 0).astype(jnp.float32)
     spread = (node == seconds_ref[1:2] - nodes).astype(jnp.float32).astype(jnp.bfloat16)
     for c in range(3):
@@ -377,9 +385,10 @@
 def middle_kernel(s_ref, long_ref, table_ref, w_ref, q_ref, q_halves, long_out, keep_ref, send_ref):
     parts, nodes, width = s_ref.shape
     w = w_ref[...]
-    q = dot(s_ref[...].reshape(-1, width), w)
+    w = pieces_of(w)
+    q = dot6(pieces_of(s_ref[...].reshape(-1, width)), w)
     q_ref[...] = q.reshape(parts, nodes, width)
-    long = dot(long_ref[...], w)
+    long = dot6(pieces_of(long_ref[...]), w)
     long_out[...] = long
     q = halves(q)
     for i in range(2):
@@ -393,11 +402,14 @@
 
 def refine_kernel(rows_all, w_ref, r_ref, diag_ref, tie_ref, out_ref, log_ref):
     del tie_ref
-    r = r_ref[...]
-    size = r.shape[0]
-    eye = lax.broadcasted_iota(jnp.int32, (size, size), 0) == lax.broadcasted_iota(jnp.int32, (size, size), 1)
     log_ref[...] = jnp.log(diag_ref[...] / rows_all)
-    out_ref[...] = r + dot(jnp.where(eye, 1.0, 0.0) - dot(r, w_ref[...]), r)
+
+    @pl.when(lax.axis_index(AXES) % 2 == 1)
+    def _():
+        r = r_ref[...]
+        size = r.shape[0]
+        eye = lax.broadcasted_iota(jnp.int32, (size, size), 0) == lax.broadcasted_iota(jnp.int32, (size, size), 1)
+        out_ref[...] = r + dot(jnp.where(eye, 1.0, 0.0) - dot(r, w_ref[...]), r)
 
 
 def second_factor_kernel(rows_all, sum_ref, r1_ref, message_ref, *scratch):
@@ -431,19 +443,7 @@
     e_ref[...] = start
     size = jnp.sum(start * start)
 
-    @pl.when(size < 0.02)
-    def _():
-        first = upper_half(start)
-        low = first.astype(jnp.bfloat16)
-        p = jnp.dot(start.astype(jnp.bfloat16), low, preferred_element_type=jnp.float32)
-        e = lax.dot_general(
-            low, (first + p).astype(jnp.bfloat16), (((0,), (0,)), ((), ())), preferred_element_type=jnp.float32
-        )
-        upper = upper_half(e - (p + p.T))
-        both = jnp.dot(low, upper.astype(jnp.bfloat16), preferred_element_type=jnp.float32)
-        v_ref[...] = both - (first + upper)
-
-    @pl.when((size >= 0.02) & (size < 0.06))
+    @pl.when(size < 0.06)
     def _():
         v_ref[...] = -upper_half(start)
 

time: 63.5 us -> 63.4 us (level)
  Pallas kernels: 22.4 us -> 21.2 us
  waiting for transfers between devices: 13.3 us -> 14.4 us
    pallas_call x22, Pallas kernels: 22.4 us -> 21.2 us  [call(): pl.pallas_call(kernel, out_shape=tuple((s if isinstance(s, jax.ShapeDtype...]
    ppermute x18, waiting for transfers between devices: 13.3 us -> 14.4 us  [exchange(): return lax.ppermute(array, AXES, [(i, i ^ bit) for i in range(count)])]
  transfers between devices with their start and end apart: 20 -> 20, of which waited for: 11 -> 13; matrix products, arithmetic and copies ran while one was open for 0% -> 0% of each run, Pallas kernels for 31% -> 29%
where the time goes in v6:
time: 63.4 us; the launch traced here: 63.2 us
  starting transfers between devices  25.5 us (40%)
  Pallas kernels  21.2 us (33%)
  waiting for transfers between devices  14.4 us (23%)
  local copies, waits for them, and re-layouts  1.11 us (2%)
  between operations  1 us (2%)
    pallas_call x22, Pallas kernels, call(): pl.pallas_call(kernel, out_shape=tuple((s if isinstance(s, jax.ShapeDtype...  21.2 us
    ppermute x18, starting transfers between devices, exchange(): return lax.ppermute(array, AXES, [(i, i ^ bit) for i in range(count)])  20.2 us
    ppermute x18, waiting for transfers between devices, exchange(): return lax.ppermute(array, AXES, [(i, i ^ bit) for i in range(count)])  14.4 us
    ppermute x2, starting transfers between devices, shifted(): return lax.ppermute(array, axis, pairs)  5.34 us
  transfers between devices with their start and end apart: 20, of which 13 were waited for; matrix products, arithmetic and copies ran while one was open for 0% of the time, Pallas kernels for 29%

profile of v6, /device:TPU:0, one launch (start us, length us, event | category | flops | bytes accessed | tf_op | source)
XLA Modules:
  0.0 63.2 jit_solution(10907248683264869342)
XLA Ops:
  0.6 0.0 copy-start
  0.6 1.1 %slice.3 = f32[3,128,256]{2,1,0:T(8,128)S(1)} slice(f32[3,256,256]{2,1,0:T(8,128)} %s_ref.11), slice={[0:3], [128:256], [0:256]} | slice | bytes 786432 | tf_op jit(solution)/shard_map/slice | solution.py:521
  1.7 3.1 %collective-permute-start.1 = (f32[3,128,256]{2,1,0:T(8,128)S(1)}, f32[3,128,256]{2,1,0:T(8,128)S(1)}, u32[]{:S(2)}, u32[]{:S(2)}) collective-permute-start(f32[3,128,256]{2,1,0:T(8,128)S(1)} %slice.3), channel_id=1, source_target_pairs={{0,8},{8,16},{16,24},{24,0},{1,9},{9,17},{17,25},{25,1},{2,10},{10... | collective-permute-start | bytes 1179656 | tf_op jit(solution)/shard_map/ppermute | solution.py:132
  4.8 0.0 copy-done
  4.8 0.9 %shard_map.83 = (f32[160,128]{1,0:T(8,128)S(1)}, f32[160,128]{1,0:T(8,128)S(1)}) custom-call(f32[3,256,256]{2,1,0:T(8,128)S(1)} %copy-done), custom_call_target="tpu_custom_call" | custom-call | bytes 369000 | tf_op jit(solution)/shard_map/pallas_call | solution.py:55
  5.7 0.1 collective-permute-start
  5.8 1.3 %collective-permute-done.refs_1_ = f32[160,128]{1,0:T(8,128)S(1)} collective-permute-done((f32[160,128]{1,0:T(8,128)S(1)}, f32[160,128]{1,0:T(8,128)S(1)}, u32[]{:S(2)}, u32[]{:S(2)}) %collective-permute-start) | collective-permute-done | bytes 81952 | tf_op jit(solution)/shard_map/ppermute | solution.py:68
  7.0 0.0 copy-start.1
  7.0 0.0 copy-start.2
  7.0 0.0 copy-start.3
  7.0 2.5 %collective-permute-start.4 = (f32[160,128]{1,0:T(8,128)S(1)}, f32[160,128]{1,0:T(8,128)S(1)}, u32[]{:S(2)}, u32[]{:S(2)}) collective-permute-start(f32[160,128]{1,0:T(8,128)S(1)} %shard_map.84.tie_ref.refs_0_), channel_id=1, source_target_pairs={{0,6},{1,7},{2,4},{3,5},{4,2},{5,3},{6,0},{7,1},{8,14},{9,15},{10,... | collective-permute-start | bytes 245768 | tf_op jit(solution)/shard_map/ppermute | solution.py:68
  9.6 0.5 collective-permute-start.3
  10.1 0.5 collective-permute-start.2
  10.6 0.0 copy-done.1
  10.6 0.0 copy-done.2
  10.6 0.0 copy-done.3
  10.6 1.1 %shard_map.85 = (f32[512,256]{1,0:T(8,128)S(1)}, f32[1024,8]{1,0:T(8,128)S(1)}) custom-call(s32[2,1024]{1,0:T(2,128)S(1)} %copy-done.1, f32[3,1024]{1,0:T(4,128)S(1)} %copy-done.2, f32[1,1024]{1,0:T(1,128)S(1)} %bitcast.2, f32[3,256,256]{2,1,0:T(8,128)S(1)} %copy-done, f32[160,128]{1,0:T(8,128)S(1)} %shard_map.84.tie_ref.refs_0_), custom_call_target="tpu_custom_call" | custom-call | bytes 369000 | tf_op jit(solution)/shard_map/pallas_call | solution.py:55
  11.8 0.9 %shard_map.86.refs_5_.second_ref = f32[512,256]{1,0:T(8,128)S(1)} custom-call(f32[1024,8]{1,0:T(8,128)S(1)} %get-tuple-element.34.table_ref, f32[3,256,256]{2,1,0:T(8,128)S(1)} %copy-done, f32[160,128]{1,0:T(8,128)S(1)} %shard_map.84.tie_ref.refs_0_), custom_call_target="tpu_custom_call" | custom-call | bytes 369000 | tf_op jit(solution)/shard_map/pallas_call | solution.py:55
  12.6 0.4 collective-permute-done.4.refs_3_
  13.1 1.3 %collective-permute-done.3.refs_2_ = f32[160,128]{1,0:T(8,128)S(1)} collective-permute-done((f32[160,128]{1,0:T(8,128)S(1)}, f32[160,128]{1,0:T(8,128)S(1)}, u32[]{:S(2)}, u32[]{:S(2)}) %collective-permute-start.3) | collective-permute-done | bytes 81952 | tf_op jit(solution)/shard_map/ppermute | solution.py:68
  14.3 0.2 collective-permute-done.2.refs_1_
  14.6 1.6 %collective-permute-start.5 = (f32[160,128]{1,0:T(8,128)S(1)}, f32[160,128]{1,0:T(8,128)S(1)}, u32[]{:S(2)}, u32[]{:S(2)}) collective-permute-start(f32[160,128]{1,0:T(8,128)S(1)} %shard_map.87.refs_0_), channel_id=1, source_target_pairs={{0,8},{1,9},{2,10},{3,11},{4,12},{5,13},{6,14},{7,15},{8,0},{9,1},... | collective-permute-start | bytes 245768 | tf_op jit(solution)/shard_map/ppermute | solution.py:68
  16.2 2.9 %collective-permute-done.5.refs_1_ = f32[160,128]{1,0:T(8,128)S(1)} collective-permute-done((f32[160,128]{1,0:T(8,128)S(1)}, f32[160,128]{1,0:T(8,128)S(1)}, u32[]{:S(2)}, u32[]{:S(2)}) %collective-permute-start.5) | collective-permute-done | bytes 81952 | tf_op jit(solution)/shard_map/ppermute | solution.py:68
  19.1 2.6 %collective-permute-start.6 = (f32[160,128]{1,0:T(8,128)S(1)}, f32[160,128]{1,0:T(8,128)S(1)}, u32[]{:S(2)}, u32[]{:S(2)}) collective-permute-start(f32[160,128]{1,0:T(8,128)S(1)} %shard_map.88.tie_ref.refs_0_), channel_id=1, source_target_pairs={{0,16},{1,17},{2,18},{3,19},{4,20},{5,21},{6,22},{7,23},{8,24},{9,... | collective-permute-start | bytes 245768 | tf_op jit(solution)/shard_map/ppermute | solution.py:68
  21.8 0.0 collective-permute-done.1.below_ref
  21.8 1.5 %shard_map.89.refs_3_.long_ref = f32[1024,256]{1,0:T(8,128)S(1)} custom-call(f32[1024,8]{1,0:T(8,128)S(1)} %get-tuple-element.34.table_ref, f32[3,128,256]{2,1,0:T(8,128)S(1)} %collective-permute-done.1.below_ref, f32[512,256]{1,0:T(8,128)S(1)} %get-tuple-element.35.refs_4_.first_ref, f32[512,256]{1,0:T(8,128)S(1)} %shard_map.86.refs_5_.second_ref, ...), custom_call_target="tpu_custom_call" | custom-call | bytes 369000 | tf_op jit(solution)/shard_map/pallas_call | solution.py:55
  23.3 1.2 %collective-permute-done.6.refs_1_ = f32[160,128]{1,0:T(8,128)S(1)} collective-permute-done((f32[160,128]{1,0:T(8,128)S(1)}, f32[160,128]{1,0:T(8,128)S(1)}, u32[]{:S(2)}, u32[]{:S(2)}) %collective-permute-start.6) | collective-permute-done | bytes 81952 | tf_op jit(solution)/shard_map/ppermute | solution.py:68
  24.6 2.3 %collective-permute-start.12 = (f32[408,256]{1,0:T(8,128)S(1)}, f32[408,256]{1,0:T(8,128)S(1)}, u32[]{:S(2)}, u32[]{:S(2)}) collective-permute-start(f32[408,256]{1,0:T(8,128)S(1)} %get-tuple-element.47), channel_id=1, source_target_pairs={{0,24},{8,0},{16,8},{24,16},{1,25},{9,1},{17,9},{25,17},{2,26},{10... | collective-permute-start | bytes 1253384 | tf_op jit(solution)/shard_map/ppermute | solution.py:132
  26.8 0.3 collective-permute-start.7
  27.2 1.1 %collective-permute-done.7.other_ref = f32[200,128]{1,0:T(8,128)S(1)} collective-permute-done((f32[200,128]{1,0:T(8,128)S(1)}, f32[200,128]{1,0:T(8,128)S(1)}, u32[]{:S(2)}, u32[]{:S(2)}) %collective-permute-start.7) | collective-permute-done | bytes 102432 | tf_op jit(solution)/shard_map/ppermute | solution.py:68
  28.2 4.9 %shard_map.93 = (f32[256,256]{1,0:T(8,128)S(1)}, f32[256,256]{1,0:T(8,128)S(1)}, f32[1,256]{1,0:T(1,128)S(1)}) custom-call(f32[200,128]{1,0:T(8,128)S(1)} %shard_map.92.mine_ref, f32[200,128]{1,0:T(8,128)S(1)} %collective-permute-done.7.other_ref), custom_call_target="tpu_custom_call" | custom-call | bytes 18450000 | tf_op jit(solution)/shard_map/pallas_call | solution.py:55
  33.1 2.8 %shard_map.94 = (f32[3,256,256]{2,1,0:T(8,128)S(1)}, bf16[2,3,256,256]{3,2,1,0:T(8,128)(2,1)S(1)}, f32[1024,256]{1,0:T(8,128)S(1)}, f32[4,80,128]{2,1,0:T(8,128)S(1)}, f32[4,80,128]{2,1,0:T(8,128)S(1)}) custom-call(f32[3,256,256]{2,1,0:T(8,128)S(1)} %copy-done, f32[1024,256]{1,0:T(8,128)S(1)} %shard_map.89.refs_3_.long_ref, ...), custom_call_target="tpu_custom_call" | custom-call | bytes 11070000 | tf_op jit(solution)/shard_map/pallas_call | solution.py:55
  35.9 0.3 collective-permute-start.8
  36.2 0.6 shard_map.95
  36.8 0.6 collective-permute-done.8.received_ref
  37.4 1.6 %collective-permute-start.9 = (f32[80,128]{1,0:T(8,128)S(1)}, f32[80,128]{1,0:T(8,128)S(1)}, u32[]{:S(2)}, u32[]{:S(2)}) collective-permute-start(f32[80,128]{1,0:T(8,128)S(1)} %get-tuple-element.44), channel_id=1, source_target_pairs={{0,2},{1,3},{2,0},{3,1},{4,6},{5,7},{6,4},{7,5},{8,10},{9,11},{10,... | collective-permute-start | bytes 122888 | tf_op jit(solution)/shard_map/ppermute | solution.py:68
  39.0 1.3 %collective-permute-start.10 = (f32[80,128]{1,0:T(8,128)S(1)}, f32[80,128]{1,0:T(8,128)S(1)}, u32[]{:S(2)}, u32[]{:S(2)}) collective-permute-start(f32[80,128]{1,0:T(8,128)S(1)} %get-tuple-element.45), channel_id=1, source_target_pairs={{0,4},{1,5},{2,6},{3,7},{4,0},{5,1},{6,2},{7,3},{8,12},{9,13},{10,... | collective-permute-start | bytes 122888 | tf_op jit(solution)/shard_map/ppermute | solution.py:68
  40.3 0.6 collective-permute-start.11
  40.9 0.0 collective-permute-done.12.above_ref
  40.9 1.8 %shard_map.97 = (f32[1024,256]{1,0:T(8,128)S(1)}, f32[1024,8]{1,0:T(8,128)S(1)}, f32[8,1024]{1,0:T(8,128)S(1)}) custom-call(f32[408,256]{1,0:T(8,128)S(1)} %collective-permute-done.12.above_ref, f32[3,256,256]{2,1,0:T(8,128)S(1)} %copy-done, f32[80,128]{1,0:T(8,128)S(1)} %get-tuple-element.43.tie_ref.refs_0_), custom_call_target="tpu_custom_call" | custom-call | bytes 7380000 | tf_op jit(solution)/shard_map/pallas_call | solution.py:55
  42.7 0.0 collective-permute-done.9.refs_1_
  42.8 0.4 collective-permute-done.10.refs_2_
  43.1 2.1 %collective-permute-done.11.refs_3_ = f32[80,128]{1,0:T(8,128)S(1)} collective-permute-done((f32[80,128]{1,0:T(8,128)S(1)}, f32[80,128]{1,0:T(8,128)S(1)}, u32[]{:S(2)}, u32[]{:S(2)}) %collective-permute-start.11) | collective-permute-done | bytes 40992 | tf_op jit(solution)/shard_map/ppermute | solution.py:68
  45.3 1.8 %collective-permute-start.15 = (f32[80,128]{1,0:T(8,128)S(1)}, f32[80,128]{1,0:T(8,128)S(1)}, u32[]{:S(2)}, u32[]{:S(2)}) collective-permute-start(f32[80,128]{1,0:T(8,128)S(1)} %shard_map.98.tie_ref.refs_0_), channel_id=1, source_target_pairs={{0,24},{1,25},{2,26},{3,27},{4,28},{5,29},{6,30},{7,31},{8,16},{9,... | collective-permute-start | bytes 122888 | tf_op jit(solution)/shard_map/ppermute | solution.py:68
  47.1 0.0 collective-permute-start.14
  47.1 2.6 %collective-permute-start.13 = (f32[80,128]{1,0:T(8,128)S(1)}, f32[80,128]{1,0:T(8,128)S(1)}, u32[]{:S(2)}, u32[]{:S(2)}) collective-permute-start(f32[80,128]{1,0:T(8,128)S(1)} %shard_map.98.tie_ref.refs_0_), channel_id=1, source_target_pairs={{0,8},{1,9},{2,10},{3,11},{4,12},{5,13},{6,14},{7,15},{8,0},{9,1},... | collective-permute-start | bytes 122888 | tf_op jit(solution)/shard_map/ppermute | solution.py:68
  49.7 2.4 %shard_map.99.refs_4_.top_ref = f32[3,128,256]{2,1,0:T(8,128)S(1)} custom-call(f32[1024,8]{1,0:T(8,128)S(1)} %get-tuple-element.49.table_ref, f32[8,1024]{1,0:T(8,128)S(1)} %get-tuple-element.50.seconds_ref, f32[1024,256]{1,0:T(8,128)S(1)} %get-tuple-element.48.refs_4_.long_ref, f32[256,256]{1,0:T(8,128)S(1)} %get-tuple-element.37.w_ref, ...), custom_call_target="tpu_custom_call" | custom-call | bytes 9225000 | tf_op jit(solution)/shard_map/pallas_call | solution.py:55
  52.1 0.0 collective-permute-done.15.refs_3_
  52.1 0.3 collective-permute-done.14.refs_2_
  52.4 0.0 collective-permute-done.13.refs_1_
  52.4 0.9 %collective-permute-start.18 = (f32[80,128]{1,0:T(8,128)S(1)}, f32[80,128]{1,0:T(8,128)S(1)}, u32[]{:S(2)}, u32[]{:S(2)}) collective-permute-start(f32[80,128]{1,0:T(8,128)S(1)} %shard_map.100.tie_ref.mine_ref), channel_id=1, source_target_pairs={{0,6},{1,7},{2,4},{3,5},{4,2},{5,3},{6,0},{7,1},{8,14},{9,15},{10,... | collective-permute-start | bytes 122888 | tf_op jit(solution)/shard_map/ppermute | solution.py:68
  53.3 1.3 %collective-permute-start.17 = (f32[80,128]{1,0:T(8,128)S(1)}, f32[80,128]{1,0:T(8,128)S(1)}, u32[]{:S(2)}, u32[]{:S(2)}) collective-permute-start(f32[80,128]{1,0:T(8,128)S(1)} %shard_map.100.tie_ref.mine_ref), channel_id=1, source_target_pairs={{0,4},{1,5},{2,6},{3,7},{4,0},{5,1},{6,2},{7,3},{8,12},{9,13},{10,... | collective-permute-start | bytes 122888 | tf_op jit(solution)/shard_map/ppermute | solution.py:68
  54.6 1.4 %collective-permute-start.16 = (f32[80,128]{1,0:T(8,128)S(1)}, f32[80,128]{1,0:T(8,128)S(1)}, u32[]{:S(2)}, u32[]{:S(2)}) collective-permute-start(f32[80,128]{1,0:T(8,128)S(1)} %shard_map.100.tie_ref.mine_ref), channel_id=1, source_target_pairs={{0,2},{1,3},{2,0},{3,1},{4,6},{5,7},{6,4},{7,5},{8,10},{9,11},{10,... | collective-permute-start | bytes 122888 | tf_op jit(solution)/shard_map/ppermute | solution.py:68
  56.0 1.5 %shard_map.101.rest_3_.own_ref = f32[3,256,256]{2,1,0:T(8,128)S(1)} custom-call(f32[1024,8]{1,0:T(8,128)S(1)} %get-tuple-element.34.table_ref, s32[2,1024]{1,0:T(2,128)S(1)} %copy-done.1, f32[1024,256]{1,0:T(8,128)S(1)} %get-tuple-element.51.long_ref, f32[3,128,256]{2,1,0:T(8,128)S(1)} %shard_map.99.refs_4_.top_ref, f32[80,128]{1,0:T(8,128)S(1)} %shard_map.100.tie_ref.mine_ref), custom_call_target="tpu_custom_call" | custom-call | bytes 5535000 | tf_op jit(solution)/shard_map/pallas_call | solution.py:55
  57.5 0.0 collective-permute-done.18.rest_2_
  57.5 0.0 collective-permute-done.17.rest_1_
  57.5 1.1 %collective-permute-done.16.rest_0_ = f32[80,128]{1,0:T(8,128)S(1)} collective-permute-done((f32[80,128]{1,0:T(8,128)S(1)}, f32[80,128]{1,0:T(8,128)S(1)}, u32[]{:S(2)}, u32[]{:S(2)}) %collective-permute-start.16) | collective-permute-done | bytes 40992 | tf_op jit(solution)/shard_map/ppermute | solution.py:68
  58.7 0.1 collective-permute-start.19
  58.8 1.5 %collective-permute-done.19.other_ref = f32[264,256]{1,0:T(8,128)S(1)} collective-permute-done((f32[264,256]{1,0:T(8,128)S(1)}, f32[264,256]{1,0:T(8,128)S(1)}, u32[]{:S(2)}, u32[]{:S(2)}) %collective-permute-start.19) | collective-permute-done | bytes 270368 | tf_op jit(solution)/shard_map/ppermute | solution.py:68
  60.3 2.7 %shard_map.104 = (f32[3,256,256]{2,1,0:T(8,128)}, f32[3,256,256]{2,1,0:T(8,128)}, f32[256,256]{1,0:T(8,128)}, f32[256,256]{1,0:T(8,128)}) custom-call(f32[264,256]{1,0:T(8,128)S(1)} %shard_map.103.mine_ref, f32[264,256]{1,0:T(8,128)S(1)} %collective-permute-done.19.other_ref, f32[3,256,256]{2,1,0:T(8,128)S(1)} %get-tuple-element.52.q_ref, ...), custom_call_target="tpu_custom_call" | custom-call | bytes 369000 | tf_op jit(solution)/shard_map/pallas_call | solution.py:55
  (11 shorter events, 0.2 us)
Async XLA Ops:
  0.6 4.2 %copy-start = (f32[3,256,256]{2,1,0:T(8,128)S(1)}, f32[3,256,256]{2,1,0:T(8,128)}, u32[]{:S(2)}) copy-start(f32[3,256,256]{2,1,0:T(8,128)} %s_ref.11) | copy-start | bytes 2359300
  1.7 20.0 %collective-permute-start.1 = (f32[3,128,256]{2,1,0:T(8,128)S(1)}, f32[3,128,256]{2,1,0:T(8,128)S(1)}, u32[]{:S(2)}, u32[]{:S(2)}) collective-permute-start(f32[3,128,256]{2,1,0:T(8,128)S(1)} %slice.3), channel_id=1, source_target_pairs={{0,8},{8,16},{16,24},{24,0},{1,9},{9,17},{17,25},{25,1},{2,10},{10... | collective-permute-start | bytes 1179656 | tf_op jit(solution)/shard_map/ppermute | solution.py:132
  5.7 1.3 %collective-permute-start = (f32[160,128]{1,0:T(8,128)S(1)}, f32[160,128]{1,0:T(8,128)S(1)}, u32[]{:S(2)}, u32[]{:S(2)}) collective-permute-start(f32[160,128]{1,0:T(8,128)S(1)} %get-tuple-element.33), channel_id=1, source_target_pairs={{0,1},{1,0},{2,3},{3,2},{4,5},{5,4},{6,7},{7,6},{8,9},{9,8},{10,11... | collective-permute-start | bytes 245768 | tf_op jit(solution)/shard_map/ppermute | solution.py:68
  7.0 3.6 %copy-start.1 = (s32[2,1024]{1,0:T(2,128)S(1)}, s32[2,1024]{1,0:T(2,128)}, u32[]{:S(2)}) copy-start(s32[2,1024]{1,0:T(2,128)} %ends_ref.5) | copy-start | bytes 24580
  7.0 3.6 %copy-start.2 = (f32[3,1024]{1,0:T(4,128)S(1)}, f32[3,1024]{1,0:T(4,128)}, u32[]{:S(2)}) copy-start(f32[3,1024]{1,0:T(4,128)} %dir_ref.3) | copy-start | bytes 36868
  7.0 3.6 %copy-start.3 = (f32[1024]{0:T(1024)S(1)}, f32[1024]{0:T(1024)}, u32[]{:S(2)}) copy-start(f32[1024]{0:T(1024)} %param.7) | copy-start | bytes 12292
  7.0 6.0 %collective-permute-start.4 = (f32[160,128]{1,0:T(8,128)S(1)}, f32[160,128]{1,0:T(8,128)S(1)}, u32[]{:S(2)}, u32[]{:S(2)}) collective-permute-start(f32[160,128]{1,0:T(8,128)S(1)} %shard_map.84.tie_ref.refs_0_), channel_id=1, source_target_pairs={{0,6},{1,7},{2,4},{3,5},{4,2},{5,3},{6,0},{7,1},{8,14},{9,15},{10,... | collective-permute-start | bytes 245768 | tf_op jit(solution)/shard_map/ppermute | solution.py:68
  9.6 4.8 %collective-permute-start.3 = (f32[160,128]{1,0:T(8,128)S(1)}, f32[160,128]{1,0:T(8,128)S(1)}, u32[]{:S(2)}, u32[]{:S(2)}) collective-permute-start(f32[160,128]{1,0:T(8,128)S(1)} %shard_map.84.tie_ref.refs_0_), channel_id=1, source_target_pairs={{0,4},{1,5},{2,6},{3,7},{4,0},{5,1},{6,2},{7,3},{8,12},{9,13},{10,... | collective-permute-start | bytes 245768 | tf_op jit(solution)/shard_map/ppermute | solution.py:68
  10.1 4.4 %collective-permute-start.2 = (f32[160,128]{1,0:T(8,128)S(1)}, f32[160,128]{1,0:T(8,128)S(1)}, u32[]{:S(2)}, u32[]{:S(2)}) collective-permute-start(f32[160,128]{1,0:T(8,128)S(1)} %shard_map.84.tie_ref.refs_0_), channel_id=1, source_target_pairs={{0,2},{1,3},{2,0},{3,1},{4,6},{5,7},{6,4},{7,5},{8,10},{9,11},{10,... | collective-permute-start | bytes 245768 | tf_op jit(solution)/shard_map/ppermute | solution.py:68
  14.6 4.5 %collective-permute-start.5 = (f32[160,128]{1,0:T(8,128)S(1)}, f32[160,128]{1,0:T(8,128)S(1)}, u32[]{:S(2)}, u32[]{:S(2)}) collective-permute-start(f32[160,128]{1,0:T(8,128)S(1)} %shard_map.87.refs_0_), channel_id=1, source_target_pairs={{0,8},{1,9},{2,10},{3,11},{4,12},{5,13},{6,14},{7,15},{8,0},{9,1},... | collective-permute-start | bytes 245768 | tf_op jit(solution)/shard_map/ppermute | solution.py:68
  19.1 5.4 %collective-permute-start.6 = (f32[160,128]{1,0:T(8,128)S(1)}, f32[160,128]{1,0:T(8,128)S(1)}, u32[]{:S(2)}, u32[]{:S(2)}) collective-permute-start(f32[160,128]{1,0:T(8,128)S(1)} %shard_map.88.tie_ref.refs_0_), channel_id=1, source_target_pairs={{0,16},{1,17},{2,18},{3,19},{4,20},{5,21},{6,22},{7,23},{8,24},{9,... | collective-permute-start | bytes 245768 | tf_op jit(solution)/shard_map/ppermute | solution.py:68
  24.6 16.4 %collective-permute-start.12 = (f32[408,256]{1,0:T(8,128)S(1)}, f32[408,256]{1,0:T(8,128)S(1)}, u32[]{:S(2)}, u32[]{:S(2)}) collective-permute-start(f32[408,256]{1,0:T(8,128)S(1)} %get-tuple-element.47), channel_id=1, source_target_pairs={{0,24},{8,0},{16,8},{24,16},{1,25},{9,1},{17,9},{25,17},{2,26},{10... | collective-permute-start | bytes 1253384 | tf_op jit(solution)/shard_map/ppermute | solution.py:132
  26.8 1.4 %collective-permute-start.7 = (f32[200,128]{1,0:T(8,128)S(1)}, f32[200,128]{1,0:T(8,128)S(1)}, u32[]{:S(2)}, u32[]{:S(2)}) collective-permute-start(f32[200,128]{1,0:T(8,128)S(1)} %shard_map.92.mine_ref), channel_id=1, source_target_pairs={{0,1},{1,0},{2,3},{3,2},{4,5},{5,4},{6,7},{7,6},{8,9},{9,8},{10,11... | collective-permute-start | bytes 307208 | tf_op jit(solution)/shard_map/ppermute | solution.py:68
  35.9 1.5 %collective-permute-start.8 = (f32[4,80,128]{2,1,0:T(8,128)S(1)}, f32[4,80,128]{2,1,0:T(8,128)S(1)}, u32[]{:S(2)}, u32[]{:S(2)}) collective-permute-start(f32[4,80,128]{2,1,0:T(8,128)S(1)} %get-tuple-element.39), channel_id=1, source_target_pairs={{0,1},{1,0},{2,3},{3,2},{4,5},{5,4},{6,7},{7,6},{8,9},{9,8},{10,11... | collective-permute-start | bytes 491528 | tf_op jit(solution)/shard_map/ppermute | solution.py:68
  37.4 5.4 %collective-permute-start.9 = (f32[80,128]{1,0:T(8,128)S(1)}, f32[80,128]{1,0:T(8,128)S(1)}, u32[]{:S(2)}, u32[]{:S(2)}) collective-permute-start(f32[80,128]{1,0:T(8,128)S(1)} %get-tuple-element.44), channel_id=1, source_target_pairs={{0,2},{1,3},{2,0},{3,1},{4,6},{5,7},{6,4},{7,5},{8,10},{9,11},{10,... | collective-permute-start | bytes 122888 | tf_op jit(solution)/shard_map/ppermute | solution.py:68
  39.0 4.1 %collective-permute-start.10 = (f32[80,128]{1,0:T(8,128)S(1)}, f32[80,128]{1,0:T(8,128)S(1)}, u32[]{:S(2)}, u32[]{:S(2)}) collective-permute-start(f32[80,128]{1,0:T(8,128)S(1)} %get-tuple-element.45), channel_id=1, source_target_pairs={{0,4},{1,5},{2,6},{3,7},{4,0},{5,1},{6,2},{7,3},{8,12},{9,13},{10,... | collective-permute-start | bytes 122888 | tf_op jit(solution)/shard_map/ppermute | solution.py:68
  40.3 4.9 %collective-permute-start.11 = (f32[80,128]{1,0:T(8,128)S(1)}, f32[80,128]{1,0:T(8,128)S(1)}, u32[]{:S(2)}, u32[]{:S(2)}) collective-permute-start(f32[80,128]{1,0:T(8,128)S(1)} %get-tuple-element.46), channel_id=1, source_target_pairs={{0,6},{1,7},{2,4},{3,5},{4,2},{5,3},{6,0},{7,1},{8,14},{9,15},{10,... | collective-permute-start | bytes 122888 | tf_op jit(solution)/shard_map/ppermute | solution.py:68
  45.3 6.8 %collective-permute-start.15 = (f32[80,128]{1,0:T(8,128)S(1)}, f32[80,128]{1,0:T(8,128)S(1)}, u32[]{:S(2)}, u32[]{:S(2)}) collective-permute-start(f32[80,128]{1,0:T(8,128)S(1)} %shard_map.98.tie_ref.refs_0_), channel_id=1, source_target_pairs={{0,24},{1,25},{2,26},{3,27},{4,28},{5,29},{6,30},{7,31},{8,16},{9,... | collective-permute-start | bytes 122888 | tf_op jit(solution)/shard_map/ppermute | solution.py:68
  47.1 5.4 %collective-permute-start.14 = (f32[80,128]{1,0:T(8,128)S(1)}, f32[80,128]{1,0:T(8,128)S(1)}, u32[]{:S(2)}, u32[]{:S(2)}) collective-permute-start(f32[80,128]{1,0:T(8,128)S(1)} %shard_map.98.tie_ref.refs_0_), channel_id=1, source_target_pairs={{0,16},{1,17},{2,18},{3,19},{4,20},{5,21},{6,22},{7,23},{8,24},{9,... | collective-permute-start | bytes 122888 | tf_op jit(solution)/shard_map/ppermute | solution.py:68
  47.1 5.4 %collective-permute-start.13 = (f32[80,128]{1,0:T(8,128)S(1)}, f32[80,128]{1,0:T(8,128)S(1)}, u32[]{:S(2)}, u32[]{:S(2)}) collective-permute-start(f32[80,128]{1,0:T(8,128)S(1)} %shard_map.98.tie_ref.refs_0_), channel_id=1, source_target_pairs={{0,8},{1,9},{2,10},{3,11},{4,12},{5,13},{6,14},{7,15},{8,0},{9,1},... | collective-permute-start | bytes 122888 | tf_op jit(solution)/shard_map/ppermute | solution.py:68
  52.4 5.0 %collective-permute-start.18 = (f32[80,128]{1,0:T(8,128)S(1)}, f32[80,128]{1,0:T(8,128)S(1)}, u32[]{:S(2)}, u32[]{:S(2)}) collective-permute-start(f32[80,128]{1,0:T(8,128)S(1)} %shard_map.100.tie_ref.mine_ref), channel_id=1, source_target_pairs={{0,6},{1,7},{2,4},{3,5},{4,2},{5,3},{6,0},{7,1},{8,14},{9,15},{10,... | collective-permute-start | bytes 122888 | tf_op jit(solution)/shard_map/ppermute | solution.py:68
  53.3 4.1 %collective-permute-start.17 = (f32[80,128]{1,0:T(8,128)S(1)}, f32[80,128]{1,0:T(8,128)S(1)}, u32[]{:S(2)}, u32[]{:S(2)}) collective-permute-start(f32[80,128]{1,0:T(8,128)S(1)} %shard_map.100.tie_ref.mine_ref), channel_id=1, source_target_pairs={{0,4},{1,5},{2,6},{3,7},{4,0},{5,1},{6,2},{7,3},{8,12},{9,13},{10,... | collective-permute-start | bytes 122888 | tf_op jit(solution)/shard_map/ppermute | solution.py:68
  54.6 4.0 %collective-permute-start.16 = (f32[80,128]{1,0:T(8,128)S(1)}, f32[80,128]{1,0:T(8,128)S(1)}, u32[]{:S(2)}, u32[]{:S(2)}) collective-permute-start(f32[80,128]{1,0:T(8,128)S(1)} %shard_map.100.tie_ref.mine_ref), channel_id=1, source_target_pairs={{0,2},{1,3},{2,0},{3,1},{4,6},{5,7},{6,4},{7,5},{8,10},{9,11},{10,... | collective-permute-start | bytes 122888 | tf_op jit(solution)/shard_map/ppermute | solution.py:68
  58.7 1.6 %collective-permute-start.19 = (f32[264,256]{1,0:T(8,128)S(1)}, f32[264,256]{1,0:T(8,128)S(1)}, u32[]{:S(2)}, u32[]{:S(2)}) collective-permute-start(f32[264,256]{1,0:T(8,128)S(1)} %shard_map.103.mine_ref), channel_id=1, source_target_pairs={{0,1},{1,0},{2,3},{3,2},{4,5},{5,4},{6,7},{7,6},{8,9},{9,8},{10,11... | collective-permute-start | bytes 811016 | tf_op jit(solution)/shard_map/ppermute | solution.py:68

commit v7 on v6

--- a/solution.py
+++ b/solution.py
@@ -49,6 +49,15 @@
         return lax.dot_general(a[i], b[j], (((ca,), (cb,)), ((), ())), preferred_element_type=jnp.float32)
 
     return one(0, 0) + ((one(0, 1) + one(1, 0)) + ((one(0, 2) + one(2, 0)) + one(1, 1)))
+
+
+def gram_of(parts):
+    def one(i, j):
+        return lax.dot_general(parts[i], parts[j], (((0,), (0,)), ((), ())), preferred_element_type=jnp.float32)
+
+    mixed = one(0, 1) if len(parts) == 2 else one(0, 1) + one(0, 2)
+    mixed = mixed + mixed.T
+    return one(0, 0) + (mixed if len(parts) == 2 else mixed + one(1, 1))
 
 
 def call(kernel, shapes, operands, specs=None, scratch=(), outs=None, us=0.1):
@@ -171,7 +180,7 @@
     width = s_ref.shape[2]
     flat = s_ref[...].reshape(-1, width)
     flat = pieces_of(flat)
-    gram = dot6(flat, flat, 0, 0)
+    gram = gram_of(flat)
     h, q = width // 2, width // 4
     even = jnp.concatenate([pack_block(gram[h:, h:]), gram[:q, h:]], axis=0)
     odd = jnp.concatenate([pack_block(gram[:h, :h]), gram[q:h, h:]], axis=0)
@@ -393,8 +402,8 @@
     q = halves(q)
     for i in range(2):
         q_halves[i] = q[i].reshape(parts, nodes, width)
-    gram = dot3(q, q, 0, 0)
-    energy = dot3(halves(long), halves(long * table_ref[:, 5:6]), 0, 0)
+    gram = gram_of(q)
+    energy = gram_of(halves(long * jnp.sqrt(table_ref[:, 5:6])))
     keep, send = order_halves(pack(energy), pack(gram))
     keep_ref[...] = keep.reshape(keep_ref.shape)
     send_ref[...] = send.reshape(send_ref.shape)

time: 63.4 us -> 62.7 us (0.989)
  Pallas kernels: 21.2 us -> 20.5 us
    pallas_call x22, Pallas kernels: 21.2 us -> 20.5 us  [call(): pl.pallas_call(kernel, out_shape=tuple((s if isinstance(s, jax.ShapeDtype...]
  transfers between devices with their start and end apart: 20 -> 20, of which waited for: 13 -> 13; matrix products, arithmetic and copies ran while one was open for 0% -> 0% of each run, Pallas kernels for 29% -> 28%
where the time goes in v7:
time: 62.7 us; the launch traced here: 62.6 us
  starting transfers between devices  25.5 us (41%)
  Pallas kernels  20.5 us (33%)
  waiting for transfers between devices  14.4 us (23%)
  local copies, waits for them, and re-layouts  1.11 us (2%)
  between operations  1 us (2%)
    pallas_call x22, Pallas kernels, call(): pl.pallas_call(kernel, out_shape=tuple((s if isinstance(s, jax.ShapeDtype...  20.5 us
    ppermute x18, starting transfers between devices, exchange(): return lax.ppermute(array, AXES, [(i, i ^ bit) for i in range(count)])  20.2 us
    ppermute x18, waiting for transfers between devices, exchange(): return lax.ppermute(array, AXES, [(i, i ^ bit) for i in range(count)])  14.4 us
    ppermute x2, starting transfers between devices, shifted(): return lax.ppermute(array, axis, pairs)  5.34 us
  transfers between devices with their start and end apart: 20, of which 13 were waited for; matrix products, arithmetic and copies ran while one was open for 0% of the time, Pallas kernels for 28%

profile of v7, /device:TPU:0, one launch (start us, length us, event | category | flops | bytes accessed | tf_op | source)
XLA Modules:
  0.0 62.6 jit_solution(13650333481101345048)
XLA Ops:
  0.6 0.0 copy-start
  0.6 1.1 %slice.3 = f32[3,128,256]{2,1,0:T(8,128)S(1)} slice(f32[3,256,256]{2,1,0:T(8,128)} %s_ref.11), slice={[0:3], [128:256], [0:256]} | slice | bytes 786432 | tf_op jit(solution)/shard_map/slice | solution.py:530
  1.7 3.1 %collective-permute-start.1 = (f32[3,128,256]{2,1,0:T(8,128)S(1)}, f32[3,128,256]{2,1,0:T(8,128)S(1)}, u32[]{:S(2)}, u32[]{:S(2)}) collective-permute-start(f32[3,128,256]{2,1,0:T(8,128)S(1)} %slice.3), channel_id=1, source_target_pairs={{0,8},{8,16},{16,24},{24,0},{1,9},{9,17},{17,25},{25,1},{2,10},{10... | collective-permute-start | bytes 1179656 | tf_op jit(solution)/shard_map/ppermute | solution.py:141
  4.8 0.0 copy-done
  4.8 0.7 %shard_map.83 = (f32[160,128]{1,0:T(8,128)S(1)}, f32[160,128]{1,0:T(8,128)S(1)}) custom-call(f32[3,256,256]{2,1,0:T(8,128)S(1)} %copy-done), custom_call_target="tpu_custom_call" | custom-call | bytes 369000 | tf_op jit(solution)/shard_map/pallas_call | solution.py:64
  5.5 0.1 collective-permute-start
  5.6 1.3 %collective-permute-done.refs_1_ = f32[160,128]{1,0:T(8,128)S(1)} collective-permute-done((f32[160,128]{1,0:T(8,128)S(1)}, f32[160,128]{1,0:T(8,128)S(1)}, u32[]{:S(2)}, u32[]{:S(2)}) %collective-permute-start) | collective-permute-done | bytes 81952 | tf_op jit(solution)/shard_map/ppermute | solution.py:77
  6.9 0.0 copy-start.1
  6.9 0.0 copy-start.2
  6.9 0.0 copy-start.3
  6.9 2.5 %collective-permute-start.4 = (f32[160,128]{1,0:T(8,128)S(1)}, f32[160,128]{1,0:T(8,128)S(1)}, u32[]{:S(2)}, u32[]{:S(2)}) collective-permute-start(f32[160,128]{1,0:T(8,128)S(1)} %shard_map.84.tie_ref.refs_0_), channel_id=1, source_target_pairs={{0,6},{1,7},{2,4},{3,5},{4,2},{5,3},{6,0},{7,1},{8,14},{9,15},{10,... | collective-permute-start | bytes 245768 | tf_op jit(solution)/shard_map/ppermute | solution.py:77
  9.4 0.5 collective-permute-start.3
  10.0 0.5 collective-permute-start.2
  10.5 0.0 copy-done.1
  10.5 0.0 copy-done.2
  10.5 0.0 copy-done.3
  10.5 1.1 %shard_map.85 = (f32[512,256]{1,0:T(8,128)S(1)}, f32[1024,8]{1,0:T(8,128)S(1)}) custom-call(s32[2,1024]{1,0:T(2,128)S(1)} %copy-done.1, f32[3,1024]{1,0:T(4,128)S(1)} %copy-done.2, f32[1,1024]{1,0:T(1,128)S(1)} %bitcast.2, f32[3,256,256]{2,1,0:T(8,128)S(1)} %copy-done, f32[160,128]{1,0:T(8,128)S(1)} %shard_map.84.tie_ref.refs_0_), custom_call_target="tpu_custom_call" | custom-call | bytes 369000 | tf_op jit(solution)/shard_map/pallas_call | solution.py:64
  11.6 0.9 %shard_map.86.refs_5_.second_ref = f32[512,256]{1,0:T(8,128)S(1)} custom-call(f32[1024,8]{1,0:T(8,128)S(1)} %get-tuple-element.34.table_ref, f32[3,256,256]{2,1,0:T(8,128)S(1)} %copy-done, f32[160,128]{1,0:T(8,128)S(1)} %shard_map.84.tie_ref.refs_0_), custom_call_target="tpu_custom_call" | custom-call | bytes 369000 | tf_op jit(solution)/shard_map/pallas_call | solution.py:64
  12.5 0.4 collective-permute-done.4.refs_3_
  12.9 1.3 %collective-permute-done.3.refs_2_ = f32[160,128]{1,0:T(8,128)S(1)} collective-permute-done((f32[160,128]{1,0:T(8,128)S(1)}, f32[160,128]{1,0:T(8,128)S(1)}, u32[]{:S(2)}, u32[]{:S(2)}) %collective-permute-start.3) | collective-permute-done | bytes 81952 | tf_op jit(solution)/shard_map/ppermute | solution.py:77
  14.2 0.2 collective-permute-done.2.refs_1_
  14.4 1.6 %collective-permute-start.5 = (f32[160,128]{1,0:T(8,128)S(1)}, f32[160,128]{1,0:T(8,128)S(1)}, u32[]{:S(2)}, u32[]{:S(2)}) collective-permute-start(f32[160,128]{1,0:T(8,128)S(1)} %shard_map.87.refs_0_), channel_id=1, source_target_pairs={{0,8},{1,9},{2,10},{3,11},{4,12},{5,13},{6,14},{7,15},{8,0},{9,1},... | collective-permute-start | bytes 245768 | tf_op jit(solution)/shard_map/ppermute | solution.py:77
  16.1 2.9 %collective-permute-done.5.refs_1_ = f32[160,128]{1,0:T(8,128)S(1)} collective-permute-done((f32[160,128]{1,0:T(8,128)S(1)}, f32[160,128]{1,0:T(8,128)S(1)}, u32[]{:S(2)}, u32[]{:S(2)}) %collective-permute-start.5) | collective-permute-done | bytes 81952 | tf_op jit(solution)/shard_map/ppermute | solution.py:77
  18.9 2.6 %collective-permute-start.6 = (f32[160,128]{1,0:T(8,128)S(1)}, f32[160,128]{1,0:T(8,128)S(1)}, u32[]{:S(2)}, u32[]{:S(2)}) collective-permute-start(f32[160,128]{1,0:T(8,128)S(1)} %shard_map.88.tie_ref.refs_0_), channel_id=1, source_target_pairs={{0,16},{1,17},{2,18},{3,19},{4,20},{5,21},{6,22},{7,23},{8,24},{9,... | collective-permute-start | bytes 245768 | tf_op jit(solution)/shard_map/ppermute | solution.py:77
  21.6 0.0 collective-permute-done.1.below_ref
  21.6 1.5 %shard_map.89.refs_3_.long_ref = f32[1024,256]{1,0:T(8,128)S(1)} custom-call(f32[1024,8]{1,0:T(8,128)S(1)} %get-tuple-element.34.table_ref, f32[3,128,256]{2,1,0:T(8,128)S(1)} %collective-permute-done.1.below_ref, f32[512,256]{1,0:T(8,128)S(1)} %get-tuple-element.35.refs_4_.first_ref, f32[512,256]{1,0:T(8,128)S(1)} %shard_map.86.refs_5_.second_ref, ...), custom_call_target="tpu_custom_call" | custom-call | bytes 369000 | tf_op jit(solution)/shard_map/pallas_call | solution.py:64
  23.1 1.2 %collective-permute-done.6.refs_1_ = f32[160,128]{1,0:T(8,128)S(1)} collective-permute-done((f32[160,128]{1,0:T(8,128)S(1)}, f32[160,128]{1,0:T(8,128)S(1)}, u32[]{:S(2)}, u32[]{:S(2)}) %collective-permute-start.6) | collective-permute-done | bytes 81952 | tf_op jit(solution)/shard_map/ppermute | solution.py:77
  24.4 2.3 %collective-permute-start.12 = (f32[408,256]{1,0:T(8,128)S(1)}, f32[408,256]{1,0:T(8,128)S(1)}, u32[]{:S(2)}, u32[]{:S(2)}) collective-permute-start(f32[408,256]{1,0:T(8,128)S(1)} %get-tuple-element.47), channel_id=1, source_target_pairs={{0,24},{8,0},{16,8},{24,16},{1,25},{9,1},{17,9},{25,17},{2,26},{10... | collective-permute-start | bytes 1253384 | tf_op jit(solution)/shard_map/ppermute | solution.py:141
  26.7 0.3 collective-permute-start.7
  27.0 1.1 %collective-permute-done.7.other_ref = f32[200,128]{1,0:T(8,128)S(1)} collective-permute-done((f32[200,128]{1,0:T(8,128)S(1)}, f32[200,128]{1,0:T(8,128)S(1)}, u32[]{:S(2)}, u32[]{:S(2)}) %collective-permute-start.7) | collective-permute-done | bytes 102432 | tf_op jit(solution)/shard_map/ppermute | solution.py:77
  28.1 4.9 %shard_map.93 = (f32[256,256]{1,0:T(8,128)S(1)}, f32[256,256]{1,0:T(8,128)S(1)}, f32[1,256]{1,0:T(1,128)S(1)}) custom-call(f32[200,128]{1,0:T(8,128)S(1)} %shard_map.92.mine_ref, f32[200,128]{1,0:T(8,128)S(1)} %collective-permute-done.7.other_ref), custom_call_target="tpu_custom_call" | custom-call | bytes 18450000 | tf_op jit(solution)/shard_map/pallas_call | solution.py:64
  33.0 2.3 %shard_map.94 = (f32[3,256,256]{2,1,0:T(8,128)S(1)}, bf16[2,3,256,256]{3,2,1,0:T(8,128)(2,1)S(1)}, f32[1024,256]{1,0:T(8,128)S(1)}, f32[4,80,128]{2,1,0:T(8,128)S(1)}, f32[4,80,128]{2,1,0:T(8,128)S(1)}) custom-call(f32[3,256,256]{2,1,0:T(8,128)S(1)} %copy-done, f32[1024,256]{1,0:T(8,128)S(1)} %shard_map.89.refs_3_.long_ref, ...), custom_call_target="tpu_custom_call" | custom-call | bytes 11070000 | tf_op jit(solution)/shard_map/pallas_call | solution.py:64
  35.2 0.3 collective-permute-start.8
  35.5 0.6 shard_map.95
  36.1 0.6 collective-permute-done.8.received_ref
  36.7 1.6 %collective-permute-start.9 = (f32[80,128]{1,0:T(8,128)S(1)}, f32[80,128]{1,0:T(8,128)S(1)}, u32[]{:S(2)}, u32[]{:S(2)}) collective-permute-start(f32[80,128]{1,0:T(8,128)S(1)} %get-tuple-element.44), channel_id=1, source_target_pairs={{0,2},{1,3},{2,0},{3,1},{4,6},{5,7},{6,4},{7,5},{8,10},{9,11},{10,... | collective-permute-start | bytes 122888 | tf_op jit(solution)/shard_map/ppermute | solution.py:77
  38.4 1.3 %collective-permute-start.10 = (f32[80,128]{1,0:T(8,128)S(1)}, f32[80,128]{1,0:T(8,128)S(1)}, u32[]{:S(2)}, u32[]{:S(2)}) collective-permute-start(f32[80,128]{1,0:T(8,128)S(1)} %get-tuple-element.45), channel_id=1, source_target_pairs={{0,4},{1,5},{2,6},{3,7},{4,0},{5,1},{6,2},{7,3},{8,12},{9,13},{10,... | collective-permute-start | bytes 122888 | tf_op jit(solution)/shard_map/ppermute | solution.py:77
  39.7 0.6 collective-permute-start.11
  40.3 0.0 collective-permute-done.12.above_ref
  40.3 1.8 %shard_map.97 = (f32[1024,256]{1,0:T(8,128)S(1)}, f32[1024,8]{1,0:T(8,128)S(1)}, f32[8,1024]{1,0:T(8,128)S(1)}) custom-call(f32[408,256]{1,0:T(8,128)S(1)} %collective-permute-done.12.above_ref, f32[3,256,256]{2,1,0:T(8,128)S(1)} %copy-done, f32[80,128]{1,0:T(8,128)S(1)} %get-tuple-element.43.tie_ref.refs_0_), custom_call_target="tpu_custom_call" | custom-call | bytes 7380000 | tf_op jit(solution)/shard_map/pallas_call | solution.py:64
  42.1 0.0 collective-permute-done.9.refs_1_
  42.1 0.4 collective-permute-done.10.refs_2_
  42.5 2.1 %collective-permute-done.11.refs_3_ = f32[80,128]{1,0:T(8,128)S(1)} collective-permute-done((f32[80,128]{1,0:T(8,128)S(1)}, f32[80,128]{1,0:T(8,128)S(1)}, u32[]{:S(2)}, u32[]{:S(2)}) %collective-permute-start.11) | collective-permute-done | bytes 40992 | tf_op jit(solution)/shard_map/ppermute | solution.py:77
  44.6 1.8 %collective-permute-start.15 = (f32[80,128]{1,0:T(8,128)S(1)}, f32[80,128]{1,0:T(8,128)S(1)}, u32[]{:S(2)}, u32[]{:S(2)}) collective-permute-start(f32[80,128]{1,0:T(8,128)S(1)} %shard_map.98.tie_ref.refs_0_), channel_id=1, source_target_pairs={{0,24},{1,25},{2,26},{3,27},{4,28},{5,29},{6,30},{7,31},{8,16},{9,... | collective-permute-start | bytes 122888 | tf_op jit(solution)/shard_map/ppermute | solution.py:77
  46.4 0.0 collective-permute-start.14
  46.4 2.6 %collective-permute-start.13 = (f32[80,128]{1,0:T(8,128)S(1)}, f32[80,128]{1,0:T(8,128)S(1)}, u32[]{:S(2)}, u32[]{:S(2)}) collective-permute-start(f32[80,128]{1,0:T(8,128)S(1)} %shard_map.98.tie_ref.refs_0_), channel_id=1, source_target_pairs={{0,8},{1,9},{2,10},{3,11},{4,12},{5,13},{6,14},{7,15},{8,0},{9,1},... | collective-permute-start | bytes 122888 | tf_op jit(solution)/shard_map/ppermute | solution.py:77
  49.1 2.4 %shard_map.99.refs_4_.top_ref = f32[3,128,256]{2,1,0:T(8,128)S(1)} custom-call(f32[1024,8]{1,0:T(8,128)S(1)} %get-tuple-element.49.table_ref, f32[8,1024]{1,0:T(8,128)S(1)} %get-tuple-element.50.seconds_ref, f32[1024,256]{1,0:T(8,128)S(1)} %get-tuple-element.48.refs_4_.long_ref, f32[256,256]{1,0:T(8,128)S(1)} %get-tuple-element.37.w_ref, ...), custom_call_target="tpu_custom_call" | custom-call | bytes 9225000 | tf_op jit(solution)/shard_map/pallas_call | solution.py:64
  51.4 0.0 collective-permute-done.15.refs_3_
  51.4 0.3 collective-permute-done.14.refs_2_
  51.8 0.0 collective-permute-done.13.refs_1_
  51.8 0.9 %collective-permute-start.18 = (f32[80,128]{1,0:T(8,128)S(1)}, f32[80,128]{1,0:T(8,128)S(1)}, u32[]{:S(2)}, u32[]{:S(2)}) collective-permute-start(f32[80,128]{1,0:T(8,128)S(1)} %shard_map.100.tie_ref.mine_ref), channel_id=1, source_target_pairs={{0,6},{1,7},{2,4},{3,5},{4,2},{5,3},{6,0},{7,1},{8,14},{9,15},{10,... | collective-permute-start | bytes 122888 | tf_op jit(solution)/shard_map/ppermute | solution.py:77
  52.7 1.3 %collective-permute-start.17 = (f32[80,128]{1,0:T(8,128)S(1)}, f32[80,128]{1,0:T(8,128)S(1)}, u32[]{:S(2)}, u32[]{:S(2)}) collective-permute-start(f32[80,128]{1,0:T(8,128)S(1)} %shard_map.100.tie_ref.mine_ref), channel_id=1, source_target_pairs={{0,4},{1,5},{2,6},{3,7},{4,0},{5,1},{6,2},{7,3},{8,12},{9,13},{10,... | collective-permute-start | bytes 122888 | tf_op jit(solution)/shard_map/ppermute | solution.py:77
  54.0 1.4 %collective-permute-start.16 = (f32[80,128]{1,0:T(8,128)S(1)}, f32[80,128]{1,0:T(8,128)S(1)}, u32[]{:S(2)}, u32[]{:S(2)}) collective-permute-start(f32[80,128]{1,0:T(8,128)S(1)} %shard_map.100.tie_ref.mine_ref), channel_id=1, source_target_pairs={{0,2},{1,3},{2,0},{3,1},{4,6},{5,7},{6,4},{7,5},{8,10},{9,11},{10,... | collective-permute-start | bytes 122888 | tf_op jit(solution)/shard_map/ppermute | solution.py:77
  55.3 1.5 %shard_map.101.rest_3_.own_ref = f32[3,256,256]{2,1,0:T(8,128)S(1)} custom-call(f32[1024,8]{1,0:T(8,128)S(1)} %get-tuple-element.34.table_ref, s32[2,1024]{1,0:T(2,128)S(1)} %copy-done.1, f32[1024,256]{1,0:T(8,128)S(1)} %get-tuple-element.51.long_ref, f32[3,128,256]{2,1,0:T(8,128)S(1)} %shard_map.99.refs_4_.top_ref, f32[80,128]{1,0:T(8,128)S(1)} %shard_map.100.tie_ref.mine_ref), custom_call_target="tpu_custom_call" | custom-call | bytes 5535000 | tf_op jit(solution)/shard_map/pallas_call | solution.py:64
  56.8 0.0 collective-permute-done.18.rest_2_
  56.8 0.0 collective-permute-done.17.rest_1_
  56.8 1.1 %collective-permute-done.16.rest_0_ = f32[80,128]{1,0:T(8,128)S(1)} collective-permute-done((f32[80,128]{1,0:T(8,128)S(1)}, f32[80,128]{1,0:T(8,128)S(1)}, u32[]{:S(2)}, u32[]{:S(2)}) %collective-permute-start.16) | collective-permute-done | bytes 40992 | tf_op jit(solution)/shard_map/ppermute | solution.py:77
  58.1 0.1 collective-permute-start.19
  58.1 1.5 %collective-permute-done.19.other_ref = f32[264,256]{1,0:T(8,128)S(1)} collective-permute-done((f32[264,256]{1,0:T(8,128)S(1)}, f32[264,256]{1,0:T(8,128)S(1)}, u32[]{:S(2)}, u32[]{:S(2)}) %collective-permute-start.19) | collective-permute-done | bytes 270368 | tf_op jit(solution)/shard_map/ppermute | solution.py:77
  59.7 2.7 %shard_map.104 = (f32[3,256,256]{2,1,0:T(8,128)}, f32[3,256,256]{2,1,0:T(8,128)}, f32[256,256]{1,0:T(8,128)}, f32[256,256]{1,0:T(8,128)}) custom-call(f32[264,256]{1,0:T(8,128)S(1)} %shard_map.103.mine_ref, f32[264,256]{1,0:T(8,128)S(1)} %collective-permute-done.19.other_ref, f32[3,256,256]{2,1,0:T(8,128)S(1)} %get-tuple-element.52.q_ref, ...), custom_call_target="tpu_custom_call" | custom-call | bytes 369000 | tf_op jit(solution)/shard_map/pallas_call | solution.py:64
  (11 shorter events, 0.2 us)
Async XLA Ops:
  0.6 4.2 %copy-start = (f32[3,256,256]{2,1,0:T(8,128)S(1)}, f32[3,256,256]{2,1,0:T(8,128)}, u32[]{:S(2)}) copy-start(f32[3,256,256]{2,1,0:T(8,128)} %s_ref.11) | copy-start | bytes 2359300
  1.7 19.9 %collective-permute-start.1 = (f32[3,128,256]{2,1,0:T(8,128)S(1)}, f32[3,128,256]{2,1,0:T(8,128)S(1)}, u32[]{:S(2)}, u32[]{:S(2)}) collective-permute-start(f32[3,128,256]{2,1,0:T(8,128)S(1)} %slice.3), channel_id=1, source_target_pairs={{0,8},{8,16},{16,24},{24,0},{1,9},{9,17},{17,25},{25,1},{2,10},{10... | collective-permute-start | bytes 1179656 | tf_op jit(solution)/shard_map/ppermute | solution.py:141
  5.5 1.3 %collective-permute-start = (f32[160,128]{1,0:T(8,128)S(1)}, f32[160,128]{1,0:T(8,128)S(1)}, u32[]{:S(2)}, u32[]{:S(2)}) collective-permute-start(f32[160,128]{1,0:T(8,128)S(1)} %get-tuple-element.33), channel_id=1, source_target_pairs={{0,1},{1,0},{2,3},{3,2},{4,5},{5,4},{6,7},{7,6},{8,9},{9,8},{10,11... | collective-permute-start | bytes 245768 | tf_op jit(solution)/shard_map/ppermute | solution.py:77
  6.9 3.6 %copy-start.1 = (s32[2,1024]{1,0:T(2,128)S(1)}, s32[2,1024]{1,0:T(2,128)}, u32[]{:S(2)}) copy-start(s32[2,1024]{1,0:T(2,128)} %ends_ref.5) | copy-start | bytes 24580
  6.9 3.6 %copy-start.2 = (f32[3,1024]{1,0:T(4,128)S(1)}, f32[3,1024]{1,0:T(4,128)}, u32[]{:S(2)}) copy-start(f32[3,1024]{1,0:T(4,128)} %dir_ref.3) | copy-start | bytes 36868
  6.9 3.6 %copy-start.3 = (f32[1024]{0:T(1024)S(1)}, f32[1024]{0:T(1024)}, u32[]{:S(2)}) copy-start(f32[1024]{0:T(1024)} %param.7) | copy-start | bytes 12292
  6.9 6.0 %collective-permute-start.4 = (f32[160,128]{1,0:T(8,128)S(1)}, f32[160,128]{1,0:T(8,128)S(1)}, u32[]{:S(2)}, u32[]{:S(2)}) collective-permute-start(f32[160,128]{1,0:T(8,128)S(1)} %shard_map.84.tie_ref.refs_0_), channel_id=1, source_target_pairs={{0,6},{1,7},{2,4},{3,5},{4,2},{5,3},{6,0},{7,1},{8,14},{9,15},{10,... | collective-permute-start | bytes 245768 | tf_op jit(solution)/shard_map/ppermute | solution.py:77
  9.4 4.8 %collective-permute-start.3 = (f32[160,128]{1,0:T(8,128)S(1)}, f32[160,128]{1,0:T(8,128)S(1)}, u32[]{:S(2)}, u32[]{:S(2)}) collective-permute-start(f32[160,128]{1,0:T(8,128)S(1)} %shard_map.84.tie_ref.refs_0_), channel_id=1, source_target_pairs={{0,4},{1,5},{2,6},{3,7},{4,0},{5,1},{6,2},{7,3},{8,12},{9,13},{10,... | collective-permute-start | bytes 245768 | tf_op jit(solution)/shard_map/ppermute | solution.py:77
  10.0 4.4 %collective-permute-start.2 = (f32[160,128]{1,0:T(8,128)S(1)}, f32[160,128]{1,0:T(8,128)S(1)}, u32[]{:S(2)}, u32[]{:S(2)}) collective-permute-start(f32[160,128]{1,0:T(8,128)S(1)} %shard_map.84.tie_ref.refs_0_), channel_id=1, source_target_pairs={{0,2},{1,3},{2,0},{3,1},{4,6},{5,7},{6,4},{7,5},{8,10},{9,11},{10,... | collective-permute-start | bytes 245768 | tf_op jit(solution)/shard_map/ppermute | solution.py:77
  14.4 4.5 %collective-permute-start.5 = (f32[160,128]{1,0:T(8,128)S(1)}, f32[160,128]{1,0:T(8,128)S(1)}, u32[]{:S(2)}, u32[]{:S(2)}) collective-permute-start(f32[160,128]{1,0:T(8,128)S(1)} %shard_map.87.refs_0_), channel_id=1, source_target_pairs={{0,8},{1,9},{2,10},{3,11},{4,12},{5,13},{6,14},{7,15},{8,0},{9,1},... | collective-permute-start | bytes 245768 | tf_op jit(solution)/shard_map/ppermute | solution.py:77
  18.9 5.4 %collective-permute-start.6 = (f32[160,128]{1,0:T(8,128)S(1)}, f32[160,128]{1,0:T(8,128)S(1)}, u32[]{:S(2)}, u32[]{:S(2)}) collective-permute-start(f32[160,128]{1,0:T(8,128)S(1)} %shard_map.88.tie_ref.refs_0_), channel_id=1, source_target_pairs={{0,16},{1,17},{2,18},{3,19},{4,20},{5,21},{6,22},{7,23},{8,24},{9,... | collective-permute-start | bytes 245768 | tf_op jit(solution)/shard_map/ppermute | solution.py:77
  24.4 15.9 %collective-permute-start.12 = (f32[408,256]{1,0:T(8,128)S(1)}, f32[408,256]{1,0:T(8,128)S(1)}, u32[]{:S(2)}, u32[]{:S(2)}) collective-permute-start(f32[408,256]{1,0:T(8,128)S(1)} %get-tuple-element.47), channel_id=1, source_target_pairs={{0,24},{8,0},{16,8},{24,16},{1,25},{9,1},{17,9},{25,17},{2,26},{10... | collective-permute-start | bytes 1253384 | tf_op jit(solution)/shard_map/ppermute | solution.py:141
  26.7 1.4 %collective-permute-start.7 = (f32[200,128]{1,0:T(8,128)S(1)}, f32[200,128]{1,0:T(8,128)S(1)}, u32[]{:S(2)}, u32[]{:S(2)}) collective-permute-start(f32[200,128]{1,0:T(8,128)S(1)} %shard_map.92.mine_ref), channel_id=1, source_target_pairs={{0,1},{1,0},{2,3},{3,2},{4,5},{5,4},{6,7},{7,6},{8,9},{9,8},{10,11... | collective-permute-start | bytes 307208 | tf_op jit(solution)/shard_map/ppermute | solution.py:77
  35.2 1.5 %collective-permute-start.8 = (f32[4,80,128]{2,1,0:T(8,128)S(1)}, f32[4,80,128]{2,1,0:T(8,128)S(1)}, u32[]{:S(2)}, u32[]{:S(2)}) collective-permute-start(f32[4,80,128]{2,1,0:T(8,128)S(1)} %get-tuple-element.39), channel_id=1, source_target_pairs={{0,1},{1,0},{2,3},{3,2},{4,5},{5,4},{6,7},{7,6},{8,9},{9,8},{10,11... | collective-permute-start | bytes 491528 | tf_op jit(solution)/shard_map/ppermute | solution.py:77
  36.7 5.4 %collective-permute-start.9 = (f32[80,128]{1,0:T(8,128)S(1)}, f32[80,128]{1,0:T(8,128)S(1)}, u32[]{:S(2)}, u32[]{:S(2)}) collective-permute-start(f32[80,128]{1,0:T(8,128)S(1)} %get-tuple-element.44), channel_id=1, source_target_pairs={{0,2},{1,3},{2,0},{3,1},{4,6},{5,7},{6,4},{7,5},{8,10},{9,11},{10,... | collective-permute-start | bytes 122888 | tf_op jit(solution)/shard_map/ppermute | solution.py:77
  38.4 4.1 %collective-permute-start.10 = (f32[80,128]{1,0:T(8,128)S(1)}, f32[80,128]{1,0:T(8,128)S(1)}, u32[]{:S(2)}, u32[]{:S(2)}) collective-permute-start(f32[80,128]{1,0:T(8,128)S(1)} %get-tuple-element.45), channel_id=1, source_target_pairs={{0,4},{1,5},{2,6},{3,7},{4,0},{5,1},{6,2},{7,3},{8,12},{9,13},{10,... | collective-permute-start | bytes 122888 | tf_op jit(solution)/shard_map/ppermute | solution.py:77
  39.7 4.9 %collective-permute-start.11 = (f32[80,128]{1,0:T(8,128)S(1)}, f32[80,128]{1,0:T(8,128)S(1)}, u32[]{:S(2)}, u32[]{:S(2)}) collective-permute-start(f32[80,128]{1,0:T(8,128)S(1)} %get-tuple-element.46), channel_id=1, source_target_pairs={{0,6},{1,7},{2,4},{3,5},{4,2},{5,3},{6,0},{7,1},{8,14},{9,15},{10,... | collective-permute-start | bytes 122888 | tf_op jit(solution)/shard_map/ppermute | solution.py:77
  44.6 6.8 %collective-permute-start.15 = (f32[80,128]{1,0:T(8,128)S(1)}, f32[80,128]{1,0:T(8,128)S(1)}, u32[]{:S(2)}, u32[]{:S(2)}) collective-permute-start(f32[80,128]{1,0:T(8,128)S(1)} %shard_map.98.tie_ref.refs_0_), channel_id=1, source_target_pairs={{0,24},{1,25},{2,26},{3,27},{4,28},{5,29},{6,30},{7,31},{8,16},{9,... | collective-permute-start | bytes 122888 | tf_op jit(solution)/shard_map/ppermute | solution.py:77
  46.4 5.4 %collective-permute-start.14 = (f32[80,128]{1,0:T(8,128)S(1)}, f32[80,128]{1,0:T(8,128)S(1)}, u32[]{:S(2)}, u32[]{:S(2)}) collective-permute-start(f32[80,128]{1,0:T(8,128)S(1)} %shard_map.98.tie_ref.refs_0_), channel_id=1, source_target_pairs={{0,16},{1,17},{2,18},{3,19},{4,20},{5,21},{6,22},{7,23},{8,24},{9,... | collective-permute-start | bytes 122888 | tf_op jit(solution)/shard_map/ppermute | solution.py:77
  46.4 5.4 %collective-permute-start.13 = (f32[80,128]{1,0:T(8,128)S(1)}, f32[80,128]{1,0:T(8,128)S(1)}, u32[]{:S(2)}, u32[]{:S(2)}) collective-permute-start(f32[80,128]{1,0:T(8,128)S(1)} %shard_map.98.tie_ref.refs_0_), channel_id=1, source_target_pairs={{0,8},{1,9},{2,10},{3,11},{4,12},{5,13},{6,14},{7,15},{8,0},{9,1},... | collective-permute-start | bytes 122888 | tf_op jit(solution)/shard_map/ppermute | solution.py:77
  51.8 5.0 %collective-permute-start.18 = (f32[80,128]{1,0:T(8,128)S(1)}, f32[80,128]{1,0:T(8,128)S(1)}, u32[]{:S(2)}, u32[]{:S(2)}) collective-permute-start(f32[80,128]{1,0:T(8,128)S(1)} %shard_map.100.tie_ref.mine_ref), channel_id=1, source_target_pairs={{0,6},{1,7},{2,4},{3,5},{4,2},{5,3},{6,0},{7,1},{8,14},{9,15},{10,... | collective-permute-start | bytes 122888 | tf_op jit(solution)/shard_map/ppermute | solution.py:77
  52.7 4.2 %collective-permute-start.17 = (f32[80,128]{1,0:T(8,128)S(1)}, f32[80,128]{1,0:T(8,128)S(1)}, u32[]{:S(2)}, u32[]{:S(2)}) collective-permute-start(f32[80,128]{1,0:T(8,128)S(1)} %shard_map.100.tie_ref.mine_ref), channel_id=1, source_target_pairs={{0,4},{1,5},{2,6},{3,7},{4,0},{5,1},{6,2},{7,3},{8,12},{9,13},{10,... | collective-permute-start | bytes 122888 | tf_op jit(solution)/shard_map/ppermute | solution.py:77
  54.0 4.0 %collective-permute-start.16 = (f32[80,128]{1,0:T(8,128)S(1)}, f32[80,128]{1,0:T(8,128)S(1)}, u32[]{:S(2)}, u32[]{:S(2)}) collective-permute-start(f32[80,128]{1,0:T(8,128)S(1)} %shard_map.100.tie_ref.mine_ref), channel_id=1, source_target_pairs={{0,2},{1,3},{2,0},{3,1},{4,6},{5,7},{6,4},{7,5},{8,10},{9,11},{10,... | collective-permute-start | bytes 122888 | tf_op jit(solution)/shard_map/ppermute | solution.py:77
  58.1 1.6 %collective-permute-start.19 = (f32[264,256]{1,0:T(8,128)S(1)}, f32[264,256]{1,0:T(8,128)S(1)}, u32[]{:S(2)}, u32[]{:S(2)}) collective-permute-start(f32[264,256]{1,0:T(8,128)S(1)} %shard_map.103.mine_ref), channel_id=1, source_target_pairs={{0,1},{1,0},{2,3},{3,2},{4,5},{5,4},{6,7},{7,6},{8,9},{9,8},{10,11... | collective-permute-start | bytes 811016 | tf_op jit(solution)/shard_map/ppermute | solution.py:77

commit v8 on v7

--- a/solution.py
+++ b/solution.py
@@ -342,7 +342,7 @@
 def finish_factor(r11, m1, g12, g22, w_ref, r_ref, scratch):
     h = r11.shape[0]
     r12 = dot(m1, g12)
-    r22, m2 = factored(g22 - dot(r12, r12, 0, 0), *scratch)
+    r22, m2 = factored(g22 - gram_of(pieces_of(r12)), *scratch)
     zero = jnp.zeros((h, h), jnp.float32)
     r_ref[:h, :h], r_ref[:h, h:], r_ref[h:, :h], r_ref[h:, h:] = r11, r12, zero, r22
     w_ref[:h, :h], w_ref[h:, h:], w_ref[h:, :h] = m1.T, m2.T, zero

time: 62.7 us -> 62.7 us (level)
  no operation moved by 1% of the time
where the time goes in v8:
time: 62.7 us; the launch traced here: 62.5 us
  starting transfers between devices  25.5 us (41%)
  Pallas kernels  20.5 us (33%)
  waiting for transfers between devices  14.4 us (23%)
  local copies, waits for them, and re-layouts  1.11 us (2%)
  between operations  1 us (2%)
    pallas_call x22, Pallas kernels, call(): pl.pallas_call(kernel, out_shape=tuple((s if isinstance(s, jax.ShapeDtype...  20.5 us
    ppermute x18, starting transfers between devices, exchange(): return lax.ppermute(array, AXES, [(i, i ^ bit) for i in range(count)])  20.2 us
    ppermute x18, waiting for transfers between devices, exchange(): return lax.ppermute(array, AXES, [(i, i ^ bit) for i in range(count)])  14.4 us
    ppermute x2, starting transfers between devices, shifted(): return lax.ppermute(array, axis, pairs)  5.34 us
  transfers between devices with their start and end apart: 20, of which 13 were waited for; matrix products, arithmetic and copies ran while one was open for 0% of the time, Pallas kernels for 28%

profile of v8, /device:TPU:0, one launch (start us, length us, event | category | flops | bytes accessed | tf_op | source)
XLA Modules:
  0.0 62.5 jit_solution(8214243090669119961)
XLA Ops:
  0.6 0.0 copy-start
  0.6 1.1 %slice.3 = f32[3,128,256]{2,1,0:T(8,128)S(1)} slice(f32[3,256,256]{2,1,0:T(8,128)} %s_ref.11), slice={[0:3], [128:256], [0:256]} | slice | bytes 786432 | tf_op jit(solution)/shard_map/slice | solution.py:530
  1.7 3.1 %collective-permute-start.1 = (f32[3,128,256]{2,1,0:T(8,128)S(1)}, f32[3,128,256]{2,1,0:T(8,128)S(1)}, u32[]{:S(2)}, u32[]{:S(2)}) collective-permute-start(f32[3,128,256]{2,1,0:T(8,128)S(1)} %slice.3), channel_id=1, source_target_pairs={{0,8},{8,16},{16,24},{24,0},{1,9},{9,17},{17,25},{25,1},{2,10},{10... | collective-permute-start | bytes 1179656 | tf_op jit(solution)/shard_map/ppermute | solution.py:141
  4.8 0.0 copy-done
  4.8 0.7 %shard_map.83 = (f32[160,128]{1,0:T(8,128)S(1)}, f32[160,128]{1,0:T(8,128)S(1)}) custom-call(f32[3,256,256]{2,1,0:T(8,128)S(1)} %copy-done), custom_call_target="tpu_custom_call" | custom-call | bytes 369000 | tf_op jit(solution)/shard_map/pallas_call | solution.py:64
  5.5 0.1 collective-permute-start
  5.6 1.3 %collective-permute-done.refs_1_ = f32[160,128]{1,0:T(8,128)S(1)} collective-permute-done((f32[160,128]{1,0:T(8,128)S(1)}, f32[160,128]{1,0:T(8,128)S(1)}, u32[]{:S(2)}, u32[]{:S(2)}) %collective-permute-start) | collective-permute-done | bytes 81952 | tf_op jit(solution)/shard_map/ppermute | solution.py:77
  6.9 0.0 copy-start.1
  6.9 0.0 copy-start.2
  6.9 0.0 copy-start.3
  6.9 2.5 %collective-permute-start.4 = (f32[160,128]{1,0:T(8,128)S(1)}, f32[160,128]{1,0:T(8,128)S(1)}, u32[]{:S(2)}, u32[]{:S(2)}) collective-permute-start(f32[160,128]{1,0:T(8,128)S(1)} %shard_map.84.tie_ref.refs_0_), channel_id=1, source_target_pairs={{0,6},{1,7},{2,4},{3,5},{4,2},{5,3},{6,0},{7,1},{8,14},{9,15},{10,... | collective-permute-start | bytes 245768 | tf_op jit(solution)/shard_map/ppermute | solution.py:77
  9.4 0.5 collective-permute-start.3
  10.0 0.5 collective-permute-start.2
  10.5 0.0 copy-done.1
  10.5 0.0 copy-done.2
  10.5 0.0 copy-done.3
  10.5 1.1 %shard_map.85 = (f32[512,256]{1,0:T(8,128)S(1)}, f32[1024,8]{1,0:T(8,128)S(1)}) custom-call(s32[2,1024]{1,0:T(2,128)S(1)} %copy-done.1, f32[3,1024]{1,0:T(4,128)S(1)} %copy-done.2, f32[1,1024]{1,0:T(1,128)S(1)} %bitcast.2, f32[3,256,256]{2,1,0:T(8,128)S(1)} %copy-done, f32[160,128]{1,0:T(8,128)S(1)} %shard_map.84.tie_ref.refs_0_), custom_call_target="tpu_custom_call" | custom-call | bytes 369000 | tf_op jit(solution)/shard_map/pallas_call | solution.py:64
  11.6 0.9 %shard_map.86.refs_5_.second_ref = f32[512,256]{1,0:T(8,128)S(1)} custom-call(f32[1024,8]{1,0:T(8,128)S(1)} %get-tuple-element.34.table_ref, f32[3,256,256]{2,1,0:T(8,128)S(1)} %copy-done, f32[160,128]{1,0:T(8,128)S(1)} %shard_map.84.tie_ref.refs_0_), custom_call_target="tpu_custom_call" | custom-call | bytes 369000 | tf_op jit(solution)/shard_map/pallas_call | solution.py:64
  12.5 0.4 collective-permute-done.4.refs_3_
  12.9 1.3 %collective-permute-done.3.refs_2_ = f32[160,128]{1,0:T(8,128)S(1)} collective-permute-done((f32[160,128]{1,0:T(8,128)S(1)}, f32[160,128]{1,0:T(8,128)S(1)}, u32[]{:S(2)}, u32[]{:S(2)}) %collective-permute-start.3) | collective-permute-done | bytes 81952 | tf_op jit(solution)/shard_map/ppermute | solution.py:77
  14.2 0.2 collective-permute-done.2.refs_1_
  14.4 1.6 %collective-permute-start.5 = (f32[160,128]{1,0:T(8,128)S(1)}, f32[160,128]{1,0:T(8,128)S(1)}, u32[]{:S(2)}, u32[]{:S(2)}) collective-permute-start(f32[160,128]{1,0:T(8,128)S(1)} %shard_map.87.refs_0_), channel_id=1, source_target_pairs={{0,8},{1,9},{2,10},{3,11},{4,12},{5,13},{6,14},{7,15},{8,0},{9,1},... | collective-permute-start | bytes 245768 | tf_op jit(solution)/shard_map/ppermute | solution.py:77
  16.1 2.9 %collective-permute-done.5.refs_1_ = f32[160,128]{1,0:T(8,128)S(1)} collective-permute-done((f32[160,128]{1,0:T(8,128)S(1)}, f32[160,128]{1,0:T(8,128)S(1)}, u32[]{:S(2)}, u32[]{:S(2)}) %collective-permute-start.5) | collective-permute-done | bytes 81952 | tf_op jit(solution)/shard_map/ppermute | solution.py:77
  18.9 2.6 %collective-permute-start.6 = (f32[160,128]{1,0:T(8,128)S(1)}, f32[160,128]{1,0:T(8,128)S(1)}, u32[]{:S(2)}, u32[]{:S(2)}) collective-permute-start(f32[160,128]{1,0:T(8,128)S(1)} %shard_map.88.tie_ref.refs_0_), channel_id=1, source_target_pairs={{0,16},{1,17},{2,18},{3,19},{4,20},{5,21},{6,22},{7,23},{8,24},{9,... | collective-permute-start | bytes 245768 | tf_op jit(solution)/shard_map/ppermute | solution.py:77
  21.6 0.0 collective-permute-done.1.below_ref
  21.6 1.5 %shard_map.89.refs_3_.long_ref = f32[1024,256]{1,0:T(8,128)S(1)} custom-call(f32[1024,8]{1,0:T(8,128)S(1)} %get-tuple-element.34.table_ref, f32[3,128,256]{2,1,0:T(8,128)S(1)} %collective-permute-done.1.below_ref, f32[512,256]{1,0:T(8,128)S(1)} %get-tuple-element.35.refs_4_.first_ref, f32[512,256]{1,0:T(8,128)S(1)} %shard_map.86.refs_5_.second_ref, ...), custom_call_target="tpu_custom_call" | custom-call | bytes 369000 | tf_op jit(solution)/shard_map/pallas_call | solution.py:64
  23.1 1.2 %collective-permute-done.6.refs_1_ = f32[160,128]{1,0:T(8,128)S(1)} collective-permute-done((f32[160,128]{1,0:T(8,128)S(1)}, f32[160,128]{1,0:T(8,128)S(1)}, u32[]{:S(2)}, u32[]{:S(2)}) %collective-permute-start.6) | collective-permute-done | bytes 81952 | tf_op jit(solution)/shard_map/ppermute | solution.py:77
  24.4 2.3 %collective-permute-start.12 = (f32[408,256]{1,0:T(8,128)S(1)}, f32[408,256]{1,0:T(8,128)S(1)}, u32[]{:S(2)}, u32[]{:S(2)}) collective-permute-start(f32[408,256]{1,0:T(8,128)S(1)} %get-tuple-element.47), channel_id=1, source_target_pairs={{0,24},{8,0},{16,8},{24,16},{1,25},{9,1},{17,9},{25,17},{2,26},{10... | collective-permute-start | bytes 1253384 | tf_op jit(solution)/shard_map/ppermute | solution.py:141
  26.7 0.3 collective-permute-start.7
  27.0 1.1 %collective-permute-done.7.other_ref = f32[200,128]{1,0:T(8,128)S(1)} collective-permute-done((f32[200,128]{1,0:T(8,128)S(1)}, f32[200,128]{1,0:T(8,128)S(1)}, u32[]{:S(2)}, u32[]{:S(2)}) %collective-permute-start.7) | collective-permute-done | bytes 102432 | tf_op jit(solution)/shard_map/ppermute | solution.py:77
  28.1 4.8 %shard_map.93 = (f32[256,256]{1,0:T(8,128)S(1)}, f32[256,256]{1,0:T(8,128)S(1)}, f32[1,256]{1,0:T(1,128)S(1)}) custom-call(f32[200,128]{1,0:T(8,128)S(1)} %shard_map.92.mine_ref, f32[200,128]{1,0:T(8,128)S(1)} %collective-permute-done.7.other_ref), custom_call_target="tpu_custom_call" | custom-call | bytes 18450000 | tf_op jit(solution)/shard_map/pallas_call | solution.py:64
  32.9 2.3 %shard_map.94 = (f32[3,256,256]{2,1,0:T(8,128)S(1)}, bf16[2,3,256,256]{3,2,1,0:T(8,128)(2,1)S(1)}, f32[1024,256]{1,0:T(8,128)S(1)}, f32[4,80,128]{2,1,0:T(8,128)S(1)}, f32[4,80,128]{2,1,0:T(8,128)S(1)}) custom-call(f32[3,256,256]{2,1,0:T(8,128)S(1)} %copy-done, f32[1024,256]{1,0:T(8,128)S(1)} %shard_map.89.refs_3_.long_ref, ...), custom_call_target="tpu_custom_call" | custom-call | bytes 11070000 | tf_op jit(solution)/shard_map/pallas_call | solution.py:64
  35.2 0.3 collective-permute-start.8
  35.5 0.6 shard_map.95
  36.1 0.6 collective-permute-done.8.received_ref
  36.7 1.7 %collective-permute-start.9 = (f32[80,128]{1,0:T(8,128)S(1)}, f32[80,128]{1,0:T(8,128)S(1)}, u32[]{:S(2)}, u32[]{:S(2)}) collective-permute-start(f32[80,128]{1,0:T(8,128)S(1)} %get-tuple-element.44), channel_id=1, source_target_pairs={{0,2},{1,3},{2,0},{3,1},{4,6},{5,7},{6,4},{7,5},{8,10},{9,11},{10,... | collective-permute-start | bytes 122888 | tf_op jit(solution)/shard_map/ppermute | solution.py:77
  38.3 1.3 %collective-permute-start.10 = (f32[80,128]{1,0:T(8,128)S(1)}, f32[80,128]{1,0:T(8,128)S(1)}, u32[]{:S(2)}, u32[]{:S(2)}) collective-permute-start(f32[80,128]{1,0:T(8,128)S(1)} %get-tuple-element.45), channel_id=1, source_target_pairs={{0,4},{1,5},{2,6},{3,7},{4,0},{5,1},{6,2},{7,3},{8,12},{9,13},{10,... | collective-permute-start | bytes 122888 | tf_op jit(solution)/shard_map/ppermute | solution.py:77
  39.7 0.6 collective-permute-start.11
  40.3 0.0 collective-permute-done.12.above_ref
  40.3 1.8 %shard_map.97 = (f32[1024,256]{1,0:T(8,128)S(1)}, f32[1024,8]{1,0:T(8,128)S(1)}, f32[8,1024]{1,0:T(8,128)S(1)}) custom-call(f32[408,256]{1,0:T(8,128)S(1)} %collective-permute-done.12.above_ref, f32[3,256,256]{2,1,0:T(8,128)S(1)} %copy-done, f32[80,128]{1,0:T(8,128)S(1)} %get-tuple-element.43.tie_ref.refs_0_), custom_call_target="tpu_custom_call" | custom-call | bytes 7380000 | tf_op jit(solution)/shard_map/pallas_call | solution.py:64
  42.1 0.0 collective-permute-done.9.refs_1_
  42.1 0.4 collective-permute-done.10.refs_2_
  42.5 2.1 %collective-permute-done.11.refs_3_ = f32[80,128]{1,0:T(8,128)S(1)} collective-permute-done((f32[80,128]{1,0:T(8,128)S(1)}, f32[80,128]{1,0:T(8,128)S(1)}, u32[]{:S(2)}, u32[]{:S(2)}) %collective-permute-start.11) | collective-permute-done | bytes 40992 | tf_op jit(solution)/shard_map/ppermute | solution.py:77
  44.6 1.8 %collective-permute-start.15 = (f32[80,128]{1,0:T(8,128)S(1)}, f32[80,128]{1,0:T(8,128)S(1)}, u32[]{:S(2)}, u32[]{:S(2)}) collective-permute-start(f32[80,128]{1,0:T(8,128)S(1)} %shard_map.98.tie_ref.refs_0_), channel_id=1, source_target_pairs={{0,24},{1,25},{2,26},{3,27},{4,28},{5,29},{6,30},{7,31},{8,16},{9,... | collective-permute-start | bytes 122888 | tf_op jit(solution)/shard_map/ppermute | solution.py:77
  46.4 0.0 collective-permute-start.14
  46.4 2.6 %collective-permute-start.13 = (f32[80,128]{1,0:T(8,128)S(1)}, f32[80,128]{1,0:T(8,128)S(1)}, u32[]{:S(2)}, u32[]{:S(2)}) collective-permute-start(f32[80,128]{1,0:T(8,128)S(1)} %shard_map.98.tie_ref.refs_0_), channel_id=1, source_target_pairs={{0,8},{1,9},{2,10},{3,11},{4,12},{5,13},{6,14},{7,15},{8,0},{9,1},... | collective-permute-start | bytes 122888 | tf_op jit(solution)/shard_map/ppermute | solution.py:77
  49.0 2.4 %shard_map.99.refs_4_.top_ref = f32[3,128,256]{2,1,0:T(8,128)S(1)} custom-call(f32[1024,8]{1,0:T(8,128)S(1)} %get-tuple-element.49.table_ref, f32[8,1024]{1,0:T(8,128)S(1)} %get-tuple-element.50.seconds_ref, f32[1024,256]{1,0:T(8,128)S(1)} %get-tuple-element.48.refs_4_.long_ref, f32[256,256]{1,0:T(8,128)S(1)} %get-tuple-element.37.w_ref, ...), custom_call_target="tpu_custom_call" | custom-call | bytes 9225000 | tf_op jit(solution)/shard_map/pallas_call | solution.py:64
  51.4 0.0 collective-permute-done.15.refs_3_
  51.4 0.3 collective-permute-done.14.refs_2_
  51.7 0.0 collective-permute-done.13.refs_1_
  51.8 0.9 %collective-permute-start.18 = (f32[80,128]{1,0:T(8,128)S(1)}, f32[80,128]{1,0:T(8,128)S(1)}, u32[]{:S(2)}, u32[]{:S(2)}) collective-permute-start(f32[80,128]{1,0:T(8,128)S(1)} %shard_map.100.tie_ref.mine_ref), channel_id=1, source_target_pairs={{0,6},{1,7},{2,4},{3,5},{4,2},{5,3},{6,0},{7,1},{8,14},{9,15},{10,... | collective-permute-start | bytes 122888 | tf_op jit(solution)/shard_map/ppermute | solution.py:77
  52.6 1.3 %collective-permute-start.17 = (f32[80,128]{1,0:T(8,128)S(1)}, f32[80,128]{1,0:T(8,128)S(1)}, u32[]{:S(2)}, u32[]{:S(2)}) collective-permute-start(f32[80,128]{1,0:T(8,128)S(1)} %shard_map.100.tie_ref.mine_ref), channel_id=1, source_target_pairs={{0,4},{1,5},{2,6},{3,7},{4,0},{5,1},{6,2},{7,3},{8,12},{9,13},{10,... | collective-permute-start | bytes 122888 | tf_op jit(solution)/shard_map/ppermute | solution.py:77
  53.9 1.4 %collective-permute-start.16 = (f32[80,128]{1,0:T(8,128)S(1)}, f32[80,128]{1,0:T(8,128)S(1)}, u32[]{:S(2)}, u32[]{:S(2)}) collective-permute-start(f32[80,128]{1,0:T(8,128)S(1)} %shard_map.100.tie_ref.mine_ref), channel_id=1, source_target_pairs={{0,2},{1,3},{2,0},{3,1},{4,6},{5,7},{6,4},{7,5},{8,10},{9,11},{10,... | collective-permute-start | bytes 122888 | tf_op jit(solution)/shard_map/ppermute | solution.py:77
  55.3 1.5 %shard_map.101.rest_3_.own_ref = f32[3,256,256]{2,1,0:T(8,128)S(1)} custom-call(f32[1024,8]{1,0:T(8,128)S(1)} %get-tuple-element.34.table_ref, s32[2,1024]{1,0:T(2,128)S(1)} %copy-done.1, f32[1024,256]{1,0:T(8,128)S(1)} %get-tuple-element.51.long_ref, f32[3,128,256]{2,1,0:T(8,128)S(1)} %shard_map.99.refs_4_.top_ref, f32[80,128]{1,0:T(8,128)S(1)} %shard_map.100.tie_ref.mine_ref), custom_call_target="tpu_custom_call" | custom-call | bytes 5535000 | tf_op jit(solution)/shard_map/pallas_call | solution.py:64
  56.8 0.0 collective-permute-done.18.rest_2_
  56.8 0.0 collective-permute-done.17.rest_1_
  56.8 1.1 %collective-permute-done.16.rest_0_ = f32[80,128]{1,0:T(8,128)S(1)} collective-permute-done((f32[80,128]{1,0:T(8,128)S(1)}, f32[80,128]{1,0:T(8,128)S(1)}, u32[]{:S(2)}, u32[]{:S(2)}) %collective-permute-start.16) | collective-permute-done | bytes 40992 | tf_op jit(solution)/shard_map/ppermute | solution.py:77
  58.0 0.1 collective-permute-start.19
  58.1 1.5 %collective-permute-done.19.other_ref = f32[264,256]{1,0:T(8,128)S(1)} collective-permute-done((f32[264,256]{1,0:T(8,128)S(1)}, f32[264,256]{1,0:T(8,128)S(1)}, u32[]{:S(2)}, u32[]{:S(2)}) %collective-permute-start.19) | collective-permute-done | bytes 270368 | tf_op jit(solution)/shard_map/ppermute | solution.py:77
  59.6 2.7 %shard_map.104 = (f32[3,256,256]{2,1,0:T(8,128)}, f32[3,256,256]{2,1,0:T(8,128)}, f32[256,256]{1,0:T(8,128)}, f32[256,256]{1,0:T(8,128)}) custom-call(f32[264,256]{1,0:T(8,128)S(1)} %shard_map.103.mine_ref, f32[264,256]{1,0:T(8,128)S(1)} %collective-permute-done.19.other_ref, f32[3,256,256]{2,1,0:T(8,128)S(1)} %get-tuple-element.52.q_ref, ...), custom_call_target="tpu_custom_call" | custom-call | bytes 369000 | tf_op jit(solution)/shard_map/pallas_call | solution.py:64
  (11 shorter events, 0.2 us)
Async XLA Ops:
  0.6 4.2 %copy-start = (f32[3,256,256]{2,1,0:T(8,128)S(1)}, f32[3,256,256]{2,1,0:T(8,128)}, u32[]{:S(2)}) copy-start(f32[3,256,256]{2,1,0:T(8,128)} %s_ref.11) | copy-start | bytes 2359300
  1.7 19.9 %collective-permute-start.1 = (f32[3,128,256]{2,1,0:T(8,128)S(1)}, f32[3,128,256]{2,1,0:T(8,128)S(1)}, u32[]{:S(2)}, u32[]{:S(2)}) collective-permute-start(f32[3,128,256]{2,1,0:T(8,128)S(1)} %slice.3), channel_id=1, source_target_pairs={{0,8},{8,16},{16,24},{24,0},{1,9},{9,17},{17,25},{25,1},{2,10},{10... | collective-permute-start | bytes 1179656 | tf_op jit(solution)/shard_map/ppermute | solution.py:141
  5.5 1.3 %collective-permute-start = (f32[160,128]{1,0:T(8,128)S(1)}, f32[160,128]{1,0:T(8,128)S(1)}, u32[]{:S(2)}, u32[]{:S(2)}) collective-permute-start(f32[160,128]{1,0:T(8,128)S(1)} %get-tuple-element.33), channel_id=1, source_target_pairs={{0,1},{1,0},{2,3},{3,2},{4,5},{5,4},{6,7},{7,6},{8,9},{9,8},{10,11... | collective-permute-start | bytes 245768 | tf_op jit(solution)/shard_map/ppermute | solution.py:77
  6.9 3.6 %copy-start.1 = (s32[2,1024]{1,0:T(2,128)S(1)}, s32[2,1024]{1,0:T(2,128)}, u32[]{:S(2)}) copy-start(s32[2,1024]{1,0:T(2,128)} %ends_ref.5) | copy-start | bytes 24580
  6.9 3.6 %copy-start.2 = (f32[3,1024]{1,0:T(4,128)S(1)}, f32[3,1024]{1,0:T(4,128)}, u32[]{:S(2)}) copy-start(f32[3,1024]{1,0:T(4,128)} %dir_ref.3) | copy-start | bytes 36868
  6.9 3.6 %copy-start.3 = (f32[1024]{0:T(1024)S(1)}, f32[1024]{0:T(1024)}, u32[]{:S(2)}) copy-start(f32[1024]{0:T(1024)} %param.7) | copy-start | bytes 12292
  6.9 6.0 %collective-permute-start.4 = (f32[160,128]{1,0:T(8,128)S(1)}, f32[160,128]{1,0:T(8,128)S(1)}, u32[]{:S(2)}, u32[]{:S(2)}) collective-permute-start(f32[160,128]{1,0:T(8,128)S(1)} %shard_map.84.tie_ref.refs_0_), channel_id=1, source_target_pairs={{0,6},{1,7},{2,4},{3,5},{4,2},{5,3},{6,0},{7,1},{8,14},{9,15},{10,... | collective-permute-start | bytes 245768 | tf_op jit(solution)/shard_map/ppermute | solution.py:77
  9.4 4.8 %collective-permute-start.3 = (f32[160,128]{1,0:T(8,128)S(1)}, f32[160,128]{1,0:T(8,128)S(1)}, u32[]{:S(2)}, u32[]{:S(2)}) collective-permute-start(f32[160,128]{1,0:T(8,128)S(1)} %shard_map.84.tie_ref.refs_0_), channel_id=1, source_target_pairs={{0,4},{1,5},{2,6},{3,7},{4,0},{5,1},{6,2},{7,3},{8,12},{9,13},{10,... | collective-permute-start | bytes 245768 | tf_op jit(solution)/shard_map/ppermute | solution.py:77
  10.0 4.4 %collective-permute-start.2 = (f32[160,128]{1,0:T(8,128)S(1)}, f32[160,128]{1,0:T(8,128)S(1)}, u32[]{:S(2)}, u32[]{:S(2)}) collective-permute-start(f32[160,128]{1,0:T(8,128)S(1)} %shard_map.84.tie_ref.refs_0_), channel_id=1, source_target_pairs={{0,2},{1,3},{2,0},{3,1},{4,6},{5,7},{6,4},{7,5},{8,10},{9,11},{10,... | collective-permute-start | bytes 245768 | tf_op jit(solution)/shard_map/ppermute | solution.py:77
  14.4 4.5 %collective-permute-start.5 = (f32[160,128]{1,0:T(8,128)S(1)}, f32[160,128]{1,0:T(8,128)S(1)}, u32[]{:S(2)}, u32[]{:S(2)}) collective-permute-start(f32[160,128]{1,0:T(8,128)S(1)} %shard_map.87.refs_0_), channel_id=1, source_target_pairs={{0,8},{1,9},{2,10},{3,11},{4,12},{5,13},{6,14},{7,15},{8,0},{9,1},... | collective-permute-start | bytes 245768 | tf_op jit(solution)/shard_map/ppermute | solution.py:77
  18.9 5.4 %collective-permute-start.6 = (f32[160,128]{1,0:T(8,128)S(1)}, f32[160,128]{1,0:T(8,128)S(1)}, u32[]{:S(2)}, u32[]{:S(2)}) collective-permute-start(f32[160,128]{1,0:T(8,128)S(1)} %shard_map.88.tie_ref.refs_0_), channel_id=1, source_target_pairs={{0,16},{1,17},{2,18},{3,19},{4,20},{5,21},{6,22},{7,23},{8,24},{9,... | collective-permute-start | bytes 245768 | tf_op jit(solution)/shard_map/ppermute | solution.py:77
  24.4 15.8 %collective-permute-start.12 = (f32[408,256]{1,0:T(8,128)S(1)}, f32[408,256]{1,0:T(8,128)S(1)}, u32[]{:S(2)}, u32[]{:S(2)}) collective-permute-start(f32[408,256]{1,0:T(8,128)S(1)} %get-tuple-element.47), channel_id=1, source_target_pairs={{0,24},{8,0},{16,8},{24,16},{1,25},{9,1},{17,9},{25,17},{2,26},{10... | collective-permute-start | bytes 1253384 | tf_op jit(solution)/shard_map/ppermute | solution.py:141
  26.7 1.4 %collective-permute-start.7 = (f32[200,128]{1,0:T(8,128)S(1)}, f32[200,128]{1,0:T(8,128)S(1)}, u32[]{:S(2)}, u32[]{:S(2)}) collective-permute-start(f32[200,128]{1,0:T(8,128)S(1)} %shard_map.92.mine_ref), channel_id=1, source_target_pairs={{0,1},{1,0},{2,3},{3,2},{4,5},{5,4},{6,7},{7,6},{8,9},{9,8},{10,11... | collective-permute-start | bytes 307208 | tf_op jit(solution)/shard_map/ppermute | solution.py:77
  35.2 1.5 %collective-permute-start.8 = (f32[4,80,128]{2,1,0:T(8,128)S(1)}, f32[4,80,128]{2,1,0:T(8,128)S(1)}, u32[]{:S(2)}, u32[]{:S(2)}) collective-permute-start(f32[4,80,128]{2,1,0:T(8,128)S(1)} %get-tuple-element.39), channel_id=1, source_target_pairs={{0,1},{1,0},{2,3},{3,2},{4,5},{5,4},{6,7},{7,6},{8,9},{9,8},{10,11... | collective-permute-start | bytes 491528 | tf_op jit(solution)/shard_map/ppermute | solution.py:77
  36.7 5.4 %collective-permute-start.9 = (f32[80,128]{1,0:T(8,128)S(1)}, f32[80,128]{1,0:T(8,128)S(1)}, u32[]{:S(2)}, u32[]{:S(2)}) collective-permute-start(f32[80,128]{1,0:T(8,128)S(1)} %get-tuple-element.44), channel_id=1, source_target_pairs={{0,2},{1,3},{2,0},{3,1},{4,6},{5,7},{6,4},{7,5},{8,10},{9,11},{10,... | collective-permute-start | bytes 122888 | tf_op jit(solution)/shard_map/ppermute | solution.py:77
  38.3 4.1 %collective-permute-start.10 = (f32[80,128]{1,0:T(8,128)S(1)}, f32[80,128]{1,0:T(8,128)S(1)}, u32[]{:S(2)}, u32[]{:S(2)}) collective-permute-start(f32[80,128]{1,0:T(8,128)S(1)} %get-tuple-element.45), channel_id=1, source_target_pairs={{0,4},{1,5},{2,6},{3,7},{4,0},{5,1},{6,2},{7,3},{8,12},{9,13},{10,... | collective-permute-start | bytes 122888 | tf_op jit(solution)/shard_map/ppermute | solution.py:77
  39.7 4.9 %collective-permute-start.11 = (f32[80,128]{1,0:T(8,128)S(1)}, f32[80,128]{1,0:T(8,128)S(1)}, u32[]{:S(2)}, u32[]{:S(2)}) collective-permute-start(f32[80,128]{1,0:T(8,128)S(1)} %get-tuple-element.46), channel_id=1, source_target_pairs={{0,6},{1,7},{2,4},{3,5},{4,2},{5,3},{6,0},{7,1},{8,14},{9,15},{10,... | collective-permute-start | bytes 122888 | tf_op jit(solution)/shard_map/ppermute | solution.py:77
  44.6 6.8 %collective-permute-start.15 = (f32[80,128]{1,0:T(8,128)S(1)}, f32[80,128]{1,0:T(8,128)S(1)}, u32[]{:S(2)}, u32[]{:S(2)}) collective-permute-start(f32[80,128]{1,0:T(8,128)S(1)} %shard_map.98.tie_ref.refs_0_), channel_id=1, source_target_pairs={{0,24},{1,25},{2,26},{3,27},{4,28},{5,29},{6,30},{7,31},{8,16},{9,... | collective-permute-start | bytes 122888 | tf_op jit(solution)/shard_map/ppermute | solution.py:77
  46.4 5.4 %collective-permute-start.14 = (f32[80,128]{1,0:T(8,128)S(1)}, f32[80,128]{1,0:T(8,128)S(1)}, u32[]{:S(2)}, u32[]{:S(2)}) collective-permute-start(f32[80,128]{1,0:T(8,128)S(1)} %shard_map.98.tie_ref.refs_0_), channel_id=1, source_target_pairs={{0,16},{1,17},{2,18},{3,19},{4,20},{5,21},{6,22},{7,23},{8,24},{9,... | collective-permute-start | bytes 122888 | tf_op jit(solution)/shard_map/ppermute | solution.py:77
  46.4 5.4 %collective-permute-start.13 = (f32[80,128]{1,0:T(8,128)S(1)}, f32[80,128]{1,0:T(8,128)S(1)}, u32[]{:S(2)}, u32[]{:S(2)}) collective-permute-start(f32[80,128]{1,0:T(8,128)S(1)} %shard_map.98.tie_ref.refs_0_), channel_id=1, source_target_pairs={{0,8},{1,9},{2,10},{3,11},{4,12},{5,13},{6,14},{7,15},{8,0},{9,1},... | collective-permute-start | bytes 122888 | tf_op jit(solution)/shard_map/ppermute | solution.py:77
  51.8 5.0 %collective-permute-start.18 = (f32[80,128]{1,0:T(8,128)S(1)}, f32[80,128]{1,0:T(8,128)S(1)}, u32[]{:S(2)}, u32[]{:S(2)}) collective-permute-start(f32[80,128]{1,0:T(8,128)S(1)} %shard_map.100.tie_ref.mine_ref), channel_id=1, source_target_pairs={{0,6},{1,7},{2,4},{3,5},{4,2},{5,3},{6,0},{7,1},{8,14},{9,15},{10,... | collective-permute-start | bytes 122888 | tf_op jit(solution)/shard_map/ppermute | solution.py:77
  52.6 4.2 %collective-permute-start.17 = (f32[80,128]{1,0:T(8,128)S(1)}, f32[80,128]{1,0:T(8,128)S(1)}, u32[]{:S(2)}, u32[]{:S(2)}) collective-permute-start(f32[80,128]{1,0:T(8,128)S(1)} %shard_map.100.tie_ref.mine_ref), channel_id=1, source_target_pairs={{0,4},{1,5},{2,6},{3,7},{4,0},{5,1},{6,2},{7,3},{8,12},{9,13},{10,... | collective-permute-start | bytes 122888 | tf_op jit(solution)/shard_map/ppermute | solution.py:77
  53.9 4.0 %collective-permute-start.16 = (f32[80,128]{1,0:T(8,128)S(1)}, f32[80,128]{1,0:T(8,128)S(1)}, u32[]{:S(2)}, u32[]{:S(2)}) collective-permute-start(f32[80,128]{1,0:T(8,128)S(1)} %shard_map.100.tie_ref.mine_ref), channel_id=1, source_target_pairs={{0,2},{1,3},{2,0},{3,1},{4,6},{5,7},{6,4},{7,5},{8,10},{9,11},{10,... | collective-permute-start | bytes 122888 | tf_op jit(solution)/shard_map/ppermute | solution.py:77
  58.0 1.6 %collective-permute-start.19 = (f32[264,256]{1,0:T(8,128)S(1)}, f32[264,256]{1,0:T(8,128)S(1)}, u32[]{:S(2)}, u32[]{:S(2)}) collective-permute-start(f32[264,256]{1,0:T(8,128)S(1)} %shard_map.103.mine_ref), channel_id=1, source_target_pairs={{0,1},{1,0},{2,3},{3,2},{4,5},{5,4},{6,7},{7,6},{8,9},{9,8},{10,11... | collective-permute-start | bytes 811016 | tf_op jit(solution)/shard_map/ppermute | solution.py:77
